TPU v7x, 512 devices: a whole 4x8x8 slice. The times are simulated.
512 devices in a mesh: row: 16 (over x_lo, z), col: 8 (over y), depth: 4 (over x_hi, core).
Axes of the slice: x: 4 (x_hi: 2, x_lo: 2; x = x_hi * 2 + x_lo), y: 8, z: 8, core: 2. Of those that a mesh axis runs over, the one named last changes fastest.
Arguments:
- left_blocks: bfloat16 [4, 128, 16, 1, 128, 128], P('depth', 'col', 'row'), may hold values from -0.5 to 0.5
- left_rows: int32 [4, 128, 16, 1], P('depth', 'col', 'row'), may hold values from 0 to 3
- right_blocks: bfloat16 [4, 128, 8, 3, 128, 128], P('depth', 'row', 'col'), may hold values from -0.75 to 0.75
- right_cols: int32 [4, 128, 8, 3], P('depth', 'row', 'col'), may hold values from 0 to 5, all different within a row
Outputs:
- product: float32 [8192, 6144], P(('row', 'depth'), 'col')
Inputs may be any that keep to these rules, and one draw needn't show every extreme that they name: For each d, k and r the 1 entries left_rows[d, k, r, :] are distinct. For each d, k and c the 3 entries right_cols[d, k, c, :] are distinct.
All inputs are finite; a program needn't handle non-finite values.
Results may differ from a plain program's by a relative error of at most 0.0003.
Values may be sent and summed in bfloat16 or wider, within the bound.
No kernel may reach another device: no remote copies, remote signals or barrier semaphores. Data moves between devices by JAX's collectives and lax.ppermute only.
A program may use at most 64 MiB of HBM per device.

v0:
```python
import math

import jax
import jax.numpy as jnp
from jax import lax
from jax.sharding import PartitionSpec as P

BR = 4
BC = 6
EA = 1
EB = 3


def accumulate(running, left_part, row_part, right_part, col_part):
    count = left_part.shape[0]
    group = math.gcd(count, 8)
    steps = count // group
    width = left_part.shape[-1]

    def one_group(carried, items):
        left_one, rows_one, right_one, cols_one = items
        products = jnp.einsum(
            "kaxy,kbyz->kabxz", left_one, right_one, preferred_element_type=jnp.float32
        )
        cell_ids = (rows_one[:, :, None] * BC + cols_one[:, None, :]).reshape(-1)
        carried = carried.at[cell_ids].add(products.reshape(-1, width * width))
        return (carried, None)

    items = (
        left_part.reshape((steps, group) + left_part.shape[1:]),
        row_part.reshape((steps, group) + row_part.shape[1:]),
        right_part.reshape((steps, group) + right_part.shape[1:]),
        col_part.reshape((steps, group) + col_part.shape[1:]),
    )
    running, _ = lax.scan(one_group, running, items)
    return running


def per_device(left_blocks, left_rows, right_blocks, right_cols):
    width = left_blocks.shape[-1]
    left_view = left_blocks.reshape((-1, EA, width, width))
    rows_view = left_rows.reshape((-1, EA))
    right_view = right_blocks.reshape((-1, EB, width, width))
    cols_view = right_cols.reshape((-1, EB))
    start = jnp.zeros((BR * BC, width * width), jnp.float32)
    right_all, cols_all = (
        lax.all_gather(right_view, "row", axis=0, tiled=True),
        lax.all_gather(cols_view, "row", axis=0, tiled=True),
    )
    running = accumulate(
        start,
        lax.all_gather(left_view, "col", axis=0, tiled=True),
        lax.all_gather(rows_view, "col", axis=0, tiled=True),
        right_all,
        cols_all,
    )
    tile = (
        running.reshape(BR, BC, width, width).transpose(0, 2, 1, 3).reshape(BR * width, BC * width)
    )
    return lax.psum_scatter(tile, "depth", scatter_dimension=0, tiled=True)


def solution(mesh):
    placed = (
        P("depth", "col", "row", None, None, None),
        P("depth", "col", "row", None),
        P("depth", "row", "col", None, None, None),
        P("depth", "row", "col", None),
    )
    return jax.shard_map(
        per_device,
        mesh=mesh,
        in_specs=placed,
        out_specs=P(("row", "depth"), "col"),
        check_vma=False,
    )
```

profile of v0, /device:TPU:6, one launch (start us, length us, event | category | flops | bytes accessed | tf_op | source)
XLA Modules:
  0.0 403.1 jit_solution(403383234516807297)
XLA Ops:
  11.5 14.1 %all-reduce = s32[128]{0:T(128)S(1)} all-reduce(s32[128]{0:T(128)S(1)} %bitcast_dynamic-update-slice_fusion), channel_id=2, replica_groups=mesh['row'=16,'col'=8,'depth'=4] {'col'}, use_global_device_ids=true, to_apply=%add | all-reduce | flops 128 | bytes 1024
  25.6 39.1 %all-gather.1 = s32[1,128,1,3]{3,2,0,1:T(1,128)S(1)} all-gather(s32[1,8,1,3]{3,2,0,1:T(1,128)S(1)} %copy.16), channel_id=3, replica_groups=mesh['row'=16,'col'=8,'depth'=4] {'row'}, dimensions={1}, use_global_device_ids=true | all-gather | bytes 1632 | tf_op jit(solution)/shard_map/all_gather | solution.py:48
  64.8 6.4 %all-gather.9.cloned.1.call-done = bf16[1,128,1,1,128,128]{5,4,3,2,0,1:T(8,128)(2,1)} async-done(((bf16[1,16,1,1,128,128]{5,4,3,2,0,1:T(8,128)(2,1)}), bf16[1,128,1,1,128,128]{5,4,3,2,0,1:T(8,128)(2,1)}) %all-gather.9.cloned.1.call-update) | async-done | bytes 4194320 | tf_op jit(solution)/shard_map/all_gather | solution.py:52
  71.2 147.1 %all-gather.7.cloned.1.call-done = bf16[1,128,1,3,128,128]{5,4,3,2,0,1:T(8,128)(2,1)} async-done(((bf16[1,8,1,3,128,128]{5,4,3,2,0,1:T(8,128)(2,1)}), bf16[1,128,1,3,128,128]{5,4,3,2,0,1:T(8,128)(2,1)}) %all-gather.7.cloned.1.call-update) | async-done | bytes 12582928 | tf_op jit(solution)/shard_map/all_gather | solution.py:47
  219.6 129.1 %while.10 = (s32[]{:T(128)}, f32[24,16384]{1,0:T(8,128)}, s32[16,8,1]{1,2,0:T(1,128)S(1)}, s32[16,8,3]{2,1,0:T(8,128)S(1)}, bf16[16,8,3,128,128]{4,3,2,1,0:T(8,1...) while((s32[]{:T(128)}, f32[24,16384]{1,0:T(8,128)}, s32[16,8,1]{1,2,0:T(1,128)S(1)}, ...), condition=%wide.region_2.3_spmd, body=%wide.region_0.2_spmd.sunk | while | flops 101056616 | bytes 8915069 | solution.py:35
  221.9 5.7 %scatter_custom_fusion.5 = f32[24,16384]{1,0:T(8,128)} fusion(f32[24,16384]{1,0:T(8,128)} %get-tuple-element.113, s32[24]{0:T(128)S(1)} %fusion.20, f32[3,8,128,128]{3,2,1,0:T(8,128)S(1)} %bitcast.65), kind=kCustom, calls=%fused_computation.1.clone.1 | custom fusion | flops 393216 | bytes 3145728 | tf_op jit(solution)/shard_map/while/body/eval_jaxpr/scatter-add | solution.py:26
  227.9 1.6 convolution_bitcast_fusion.2
  230.0 5.7 %scatter_custom_fusion.5 = f32[24,16384]{1,0:T(8,128)} fusion(f32[24,16384]{1,0:T(8,128)} %get-tuple-element.113, s32[24]{0:T(128)S(1)} %fusion.20, f32[3,8,128,128]{3,2,1,0:T(8,128)S(1)} %bitcast.65), kind=kCustom, calls=%fused_computation.1.clone.1 | custom fusion | flops 393216 | bytes 3145728 | tf_op jit(solution)/shard_map/while/body/eval_jaxpr/scatter-add | solution.py:26
  235.9 1.6 convolution_bitcast_fusion.2
  238.0 5.7 %scatter_custom_fusion.5 = f32[24,16384]{1,0:T(8,128)} fusion(f32[24,16384]{1,0:T(8,128)} %get-tuple-element.113, s32[24]{0:T(128)S(1)} %fusion.20, f32[3,8,128,128]{3,2,1,0:T(8,128)S(1)} %bitcast.65), kind=kCustom, calls=%fused_computation.1.clone.1 | custom fusion | flops 393216 | bytes 3145728 | tf_op jit(solution)/shard_map/while/body/eval_jaxpr/scatter-add | solution.py:26
  246.1 5.7 %scatter_custom_fusion.5 = f32[24,16384]{1,0:T(8,128)} fusion(f32[24,16384]{1,0:T(8,128)} %get-tuple-element.113, s32[24]{0:T(128)S(1)} %fusion.20, f32[3,8,128,128]{3,2,1,0:T(8,128)S(1)} %bitcast.65), kind=kCustom, calls=%fused_computation.1.clone.1 | custom fusion | flops 393216 | bytes 3145728 | tf_op jit(solution)/shard_map/while/body/eval_jaxpr/scatter-add | solution.py:26
  252.1 1.6 convolution_bitcast_fusion.2
  254.2 5.7 %scatter_custom_fusion.5 = f32[24,16384]{1,0:T(8,128)} fusion(f32[24,16384]{1,0:T(8,128)} %get-tuple-element.113, s32[24]{0:T(128)S(1)} %fusion.20, f32[3,8,128,128]{3,2,1,0:T(8,128)S(1)} %bitcast.65), kind=kCustom, calls=%fused_computation.1.clone.1 | custom fusion | flops 393216 | bytes 3145728 | tf_op jit(solution)/shard_map/while/body/eval_jaxpr/scatter-add | solution.py:26
  262.3 5.7 %scatter_custom_fusion.5 = f32[24,16384]{1,0:T(8,128)} fusion(f32[24,16384]{1,0:T(8,128)} %get-tuple-element.113, s32[24]{0:T(128)S(1)} %fusion.20, f32[3,8,128,128]{3,2,1,0:T(8,128)S(1)} %bitcast.65), kind=kCustom, calls=%fused_computation.1.clone.1 | custom fusion | flops 393216 | bytes 3145728 | tf_op jit(solution)/shard_map/while/body/eval_jaxpr/scatter-add | solution.py:26
  268.2 1.6 convolution_bitcast_fusion.2
  270.3 5.7 %scatter_custom_fusion.5 = f32[24,16384]{1,0:T(8,128)} fusion(f32[24,16384]{1,0:T(8,128)} %get-tuple-element.113, s32[24]{0:T(128)S(1)} %fusion.20, f32[3,8,128,128]{3,2,1,0:T(8,128)S(1)} %bitcast.65), kind=kCustom, calls=%fused_computation.1.clone.1 | custom fusion | flops 393216 | bytes 3145728 | tf_op jit(solution)/shard_map/while/body/eval_jaxpr/scatter-add | solution.py:26
  276.3 1.6 convolution_bitcast_fusion.2
  278.4 5.7 %scatter_custom_fusion.5 = f32[24,16384]{1,0:T(8,128)} fusion(f32[24,16384]{1,0:T(8,128)} %get-tuple-element.113, s32[24]{0:T(128)S(1)} %fusion.20, f32[3,8,128,128]{3,2,1,0:T(8,128)S(1)} %bitcast.65), kind=kCustom, calls=%fused_computation.1.clone.1 | custom fusion | flops 393216 | bytes 3145728 | tf_op jit(solution)/shard_map/while/body/eval_jaxpr/scatter-add | solution.py:26
  284.4 1.6 convolution_bitcast_fusion.2
  286.5 5.7 %scatter_custom_fusion.5 = f32[24,16384]{1,0:T(8,128)} fusion(f32[24,16384]{1,0:T(8,128)} %get-tuple-element.113, s32[24]{0:T(128)S(1)} %fusion.20, f32[3,8,128,128]{3,2,1,0:T(8,128)S(1)} %bitcast.65), kind=kCustom, calls=%fused_computation.1.clone.1 | custom fusion | flops 393216 | bytes 3145728 | tf_op jit(solution)/shard_map/while/body/eval_jaxpr/scatter-add | solution.py:26
  292.4 1.6 convolution_bitcast_fusion.2
  294.5 5.7 %scatter_custom_fusion.5 = f32[24,16384]{1,0:T(8,128)} fusion(f32[24,16384]{1,0:T(8,128)} %get-tuple-element.113, s32[24]{0:T(128)S(1)} %fusion.20, f32[3,8,128,128]{3,2,1,0:T(8,128)S(1)} %bitcast.65), kind=kCustom, calls=%fused_computation.1.clone.1 | custom fusion | flops 393216 | bytes 3145728 | tf_op jit(solution)/shard_map/while/body/eval_jaxpr/scatter-add | solution.py:26
  302.6 5.7 %scatter_custom_fusion.5 = f32[24,16384]{1,0:T(8,128)} fusion(f32[24,16384]{1,0:T(8,128)} %get-tuple-element.113, s32[24]{0:T(128)S(1)} %fusion.20, f32[3,8,128,128]{3,2,1,0:T(8,128)S(1)} %bitcast.65), kind=kCustom, calls=%fused_computation.1.clone.1 | custom fusion | flops 393216 | bytes 3145728 | tf_op jit(solution)/shard_map/while/body/eval_jaxpr/scatter-add | solution.py:26
  308.6 1.6 convolution_bitcast_fusion.2
  310.7 5.7 %scatter_custom_fusion.5 = f32[24,16384]{1,0:T(8,128)} fusion(f32[24,16384]{1,0:T(8,128)} %get-tuple-element.113, s32[24]{0:T(128)S(1)} %fusion.20, f32[3,8,128,128]{3,2,1,0:T(8,128)S(1)} %bitcast.65), kind=kCustom, calls=%fused_computation.1.clone.1 | custom fusion | flops 393216 | bytes 3145728 | tf_op jit(solution)/shard_map/while/body/eval_jaxpr/scatter-add | solution.py:26
  318.7 5.7 %scatter_custom_fusion.5 = f32[24,16384]{1,0:T(8,128)} fusion(f32[24,16384]{1,0:T(8,128)} %get-tuple-element.113, s32[24]{0:T(128)S(1)} %fusion.20, f32[3,8,128,128]{3,2,1,0:T(8,128)S(1)} %bitcast.65), kind=kCustom, calls=%fused_computation.1.clone.1 | custom fusion | flops 393216 | bytes 3145728 | tf_op jit(solution)/shard_map/while/body/eval_jaxpr/scatter-add | solution.py:26
  326.8 5.7 %scatter_custom_fusion.5 = f32[24,16384]{1,0:T(8,128)} fusion(f32[24,16384]{1,0:T(8,128)} %get-tuple-element.113, s32[24]{0:T(128)S(1)} %fusion.20, f32[3,8,128,128]{3,2,1,0:T(8,128)S(1)} %bitcast.65), kind=kCustom, calls=%fused_computation.1.clone.1 | custom fusion | flops 393216 | bytes 3145728 | tf_op jit(solution)/shard_map/while/body/eval_jaxpr/scatter-add | solution.py:26
  334.9 5.7 %scatter_custom_fusion.5 = f32[24,16384]{1,0:T(8,128)} fusion(f32[24,16384]{1,0:T(8,128)} %get-tuple-element.113, s32[24]{0:T(128)S(1)} %fusion.20, f32[3,8,128,128]{3,2,1,0:T(8,128)S(1)} %bitcast.65), kind=kCustom, calls=%fused_computation.1.clone.1 | custom fusion | flops 393216 | bytes 3145728 | tf_op jit(solution)/shard_map/while/body/eval_jaxpr/scatter-add | solution.py:26
  343.0 5.7 %scatter_custom_fusion.5 = f32[24,16384]{1,0:T(8,128)} fusion(f32[24,16384]{1,0:T(8,128)} %get-tuple-element.113, s32[24]{0:T(128)S(1)} %fusion.20, f32[3,8,128,128]{3,2,1,0:T(8,128)S(1)} %bitcast.65), kind=kCustom, calls=%fused_computation.1.clone.1 | custom fusion | flops 393216 | bytes 3145728 | tf_op jit(solution)/shard_map/while/body/eval_jaxpr/scatter-add | solution.py:26
  348.7 1.7 copy.27
  352.5 42.2 %reduce-scatter.2.cloned.1.call-done = f32[128,768]{0,1:T(8,128)} async-done(((f32[512,768]{0,1:T(8,128)}), f32[128,768]{0,1:T(8,128)}) %reduce-scatter.2.cloned.1.call-update) | async-done | bytes 393232 | tf_op jit(solution)/shard_map/reduce_scatter | solution.py:60
  394.7 1.9 copy.23
  (134 shorter events, 32.0 us)
Async XLA Ops:
  6.5 64.7 %all-gather.9.cloned.1.call-start = ((), (), s32[]{:S(2)}) async-start(), calls=%async_computation.3 | async-start | bytes 4718592 | tf_op jit(solution)/shard_map/all_gather | solution.py:52
  7.3 211.0 %all-gather.7.cloned.1.call-start = ((), (), s32[]{:S(2)}) async-start(), calls=%async_computation.2 | async-start | bytes 13369344 | tf_op jit(solution)/shard_map/all_gather | solution.py:47
  8.0 386.7 %reduce-scatter.2.cloned.1.call-start = ((), (), s32[]{:S(2)}) async-start(), calls=%async_computation.1 | async-start | bytes 1966080 | tf_op jit(solution)/shard_map/reduce_scatter | solution.py:60
Sparse Core Ops, SparseCore 0:
  9.4 61.7 all-gather.8
  73.3 144.9 all-gather.6
  352.6 42.0 reduce-scatter.1
where the time goes:
time: 407 us; the launch traced here: 403 us
  waiting for transfers between devices  197 us (48%)
  other arithmetic  91.8 us (23%)
  blocking collectives  53.2 us (13%)
  matrix products  25.8 us (6%)
  local copies, waits for them, and re-layouts  21.1 us (5%)
  between operations  13.8 us (3%)
    all_gather x1, waiting for transfers between devices, per_device(): lax.all_gather(right_view, 'row', axis=0, tiled=True)  147 us
    scatter-add x16, other arithmetic, one_group(): carried = carried.at[cell_ids].add(products.reshape(-1, width * width))  91.7 us
    reduce_scatter x1, waiting for transfers between devices, per_device(): return lax.psum_scatter(tile, 'depth', scatter_dimension=0, tiled=True)  42.2 us
    all_gather x1, blocking collectives, per_device(): lax.all_gather(cols_view, 'row', axis=0, tiled=True)  39.1 us
    dot_general x16, matrix products, one_group(): jnp.einsum('kaxy,kbyz->kabxz', left_one, right_one, preferred_element_typ...  25.8 us
    unnamed x1, blocking collectives  14.1 us
  transfers between devices with their start and end apart: 3, of which 3 were waited for; matrix products, arithmetic and copies ran while one was open for 1% of the time, Pallas kernels for 0%

commit v1 on v0

v1 whole, which is shorter than its diff:
```python
import jax
import jax.numpy as jnp
from jax import lax
from jax.experimental import pallas as pl
from jax.experimental.pallas import tpu as pltpu
from jax.sharding import PartitionSpec as P

BR = 4
EB = 3
W = 128
NZ = 8
GROUP = 8
PAD = 16
PARTS = ((4, 4, 3), (4, 3, 4))


def zig(z):
    return ((z + 1) // 2) % 2


def ring_pairs(step):
    pairs = []
    for x_lo in range(2):
        for z in range(NZ):
            to = (z + step) % NZ
            pairs.append((x_lo * NZ + z, (x_lo ^ zig(z) ^ zig(to)) * NZ + to))
    return pairs


def chip_pairs(step):
    pairs = []
    for row in range(16):
        for depth in range(4):
            x = (depth // 2) * 2 + row // NZ
            to = (x + step) % 4
            pairs.append(
                (row * 4 + depth, ((to % 2) * NZ + row % NZ) * 4 + (to // 2) * 2 + depth % 2)
            )
    return pairs


def with_index(blocks, index):
    flat = blocks.reshape(-1, W)
    row = jnp.zeros((PAD, W), flat.dtype)
    row = row.at[0, : index.size].set(index.reshape(-1).astype(flat.dtype))
    return jnp.concatenate([flat, row], axis=0)


def multiply(chunk_sizes, place_ref, cols_ref, slot_ref, *refs):
    n = len(chunk_sizes)
    left_hbm = refs[:2]
    right_hbm = refs[2 : 2 + n]
    keep_hbm, send_hbm = refs[2 + n : 4 + n]
    left_buf, right_buf, acc, left_sem, right_sem, out_sem = refs[4 + n :]
    left_copies = [
        pltpu.make_async_copy(left_hbm[t], left_buf.at[t], left_sem.at[t]) for t in range(2)
    ]
    for copy in left_copies:
        copy.start()
    right_copies = [
        pltpu.make_async_copy(
            right_hbm[c], right_buf.at[c, pl.ds(0, right_hbm[c].shape[0])], right_sem.at[c]
        )
        for c in range(n)
    ]
    for copy in right_copies:
        copy.start()
    acc[...] = jnp.zeros_like(acc)
    for copy in left_copies:
        copy.wait()
    for c, (count, offset) in enumerate(chunk_sizes):
        right_copies[c].wait()
        slot = slot_ref[c]

        def body(j, carry, c=c, offset=offset, slot=slot):
            k = offset + j
            rows = pl.ds(pl.multiple_of(k * W, W), W)
            both = jnp.concatenate(
                [left_buf[0, slot, rows, :], left_buf[1, slot, rows, :]], axis=0
            )
            first = j * (EB * W)
            right = jnp.concatenate(
                [
                    right_buf[c, pl.ds(pl.multiple_of(first + e * W, W), W), :]
                    for e in range(EB)
                ],
                axis=1,
            )
            part = jnp.dot(both, right, preferred_element_type=jnp.float32)
            for e in range(EB):
                col = cols_ref[c, j * EB + e]
                lanes = pl.ds(pl.multiple_of(col * W, W), W)
                for t in range(2):
                    at = place_ref[t, slot * GROUP + k]
                    acc[at, :, lanes] += part[t * W : (t + 1) * W, e * W : (e + 1) * W]
            return carry

        lax.fori_loop(0, count, body, 0, unroll=True)
    keep = pltpu.make_async_copy(acc.at[pl.ds(0, 4)], keep_hbm, out_sem.at[0])
    send = pltpu.make_async_copy(acc.at[pl.ds(4, 4)], send_hbm, out_sem.at[1])
    keep.start()
    send.start()
    keep.wait()
    send.wait()


def per_device(left_blocks, left_rows, right_blocks, right_cols):
    row = lax.axis_index("row")
    y = lax.axis_index("col")
    depth = lax.axis_index("depth")
    x_lo, z = row // NZ, row % NZ
    x_hi, core = depth // 2, depth % 2
    x = x_hi * 2 + x_lo
    half = x_lo ^ zig(z)

    left = left_blocks.reshape(2, GROUP * W, W)
    rows = left_rows.reshape(2, GROUP)
    own = (half + y // 4 + y % 4) % 2
    mine = with_index(
        lax.dynamic_index_in_dim(left, own, 0, False),
        lax.dynamic_index_in_dim(rows, own, 0, False),
    )
    other = with_index(
        lax.dynamic_index_in_dim(left, 1 - own, 0, False),
        lax.dynamic_index_in_dim(rows, 1 - own, 0, False),
    )
    right = right_blocks.reshape(GROUP, EB * W, W)
    cols = right_cols.reshape(GROUP, EB)

    left_own = lax.all_gather(mine, "col", axis=0)
    swapped = lax.ppermute(other, "row", [(r, (r + NZ) % 16) for r in range(16)])
    left_other = lax.all_gather(swapped, "col", axis=0)

    chunks, sizes, sources = [], [], []
    streams = []
    offset = 0
    for count, up, down in PARTS:
        part = with_index(right[offset : offset + count], cols[offset : offset + count])
        chunks.append(part)
        sizes.append((count, offset))
        sources.append(z)
        streams.append([part, 1, up, count, offset])
        streams.append([part, -1, down, count, offset])
        offset += count
    for t in range(1, NZ):
        for stream in streams:
            if t <= stream[2]:
                stream[0] = lax.ppermute(stream[0], "row", ring_pairs(stream[1]))
                chunks.append(stream[0])
                sizes.append((stream[3], stream[4]))
                sources.append((z - stream[1] * t) % NZ)
    source = jnp.stack(sources)
    slots = (4 * (zig(source) ^ half) + source // 2).astype(jnp.int32)

    def places(gathered, tile):
        block_row = gathered[:, GROUP * W, :GROUP].astype(jnp.int32)
        ahead = ((block_row // 2) * 2 + tile - x) % 4
        return (((block_row % 2) ^ core) * 4 + ahead).reshape(-1)

    place = jnp.stack([places(left_own, x_lo), places(left_other, 1 - x_lo)])
    most = max(count for count, _ in sizes)
    col_ids = jnp.stack(
        [
            jnp.pad(
                chunk[count * EB * W, : count * EB].astype(jnp.int32),
                (0, (most - count) * EB),
            )
            for chunk, (count, _) in zip(chunks, sizes)
        ]
    )
    n = len(chunks)
    longest = max(chunk.shape[0] for chunk in chunks)
    flops = 2 * 2 * EB * 64 * W**3
    smem = pl.BlockSpec(memory_space=pltpu.SMEM)
    hbm = pl.BlockSpec(memory_space=pl.ANY)
    keep, send = pl.pallas_call(
        lambda *refs: multiply(sizes, *refs),
        out_shape=[jax.ShapeDtypeStruct((4, W, 6 * W), jnp.float32)] * 2,
        in_specs=[smem] * 3 + [hbm] * (2 + n),
        out_specs=[hbm] * 2,
        scratch_shapes=[
            pltpu.VMEM((2, NZ, GROUP * W + PAD, W), jnp.bfloat16),
            pltpu.VMEM((n, longest, W), jnp.bfloat16),
            pltpu.VMEM((8, W, 6 * W), jnp.float32),
            pltpu.SemaphoreType.DMA((2,)),
            pltpu.SemaphoreType.DMA((n,)),
            pltpu.SemaphoreType.DMA((2,)),
        ],
        compiler_params=pltpu.CompilerParams(vmem_limit_bytes=40 * 2**20),
        cost_estimate=pl.CostEstimate(
            flops=flops, bytes_accessed=14 * 2**20, transcendentals=0
        ),
    )(place, col_ids, slots, left_own, left_other, *chunks)
    got = lax.ppermute(send, "depth", [(0, 1), (1, 0), (2, 3), (3, 2)])
    total = keep + got
    out = total[0]
    for step in (2, 1, 3):
        out = out + lax.ppermute(total[step], ("row", "depth"), chip_pairs(step))
    return out


def solution(mesh):
    placed = (
        P("depth", "col", "row", None, None, None),
        P("depth", "col", "row", None),
        P("depth", "row", "col", None, None, None),
        P("depth", "row", "col", None),
    )
    return jax.shard_map(
        per_device,
        mesh=mesh,
        in_specs=placed,
        out_specs=P(("row", "depth"), "col"),
        check_vma=False,
    )
```

time: 407 us -> 155 us (0.38)
  waiting for transfers between devices: 197 us -> 44.5 us
  other arithmetic: 91.8 us -> 4.01 us
  starting transfers between devices: 0.08 us -> 69.3 us
  blocking collectives: 53.2 us -> 0 us
  matrix products: 25.8 us -> 0 us
  Pallas kernels: 0 us -> 9.87 us
  local copies, waits for them, and re-layouts: 21.1 us -> 11.8 us
    all_gather x2, waiting for transfers between devices: 154 us -> 5.59 us  [the longest x1 5.58 us: per_device(): left_other = lax.all_gather(swapped, 'col', axis=0)]
    scatter-add x16 -> x0, other arithmetic: 91.7 us -> none  [one_group(): carried = carried.at[cell_ids].add(products.reshape(-1, width * width))]
    ppermute x0 -> x19, starting transfers between devices: none -> 69.3 us  [the longest x14 54.2 us: per_device(): stream[0] = lax.ppermute(stream[0], 'row', ring_pairs(stream[1]))]
    reduce_scatter x1 -> x0, waiting for transfers between devices: 42.2 us -> none  [per_device(): return lax.psum_scatter(tile, 'depth', scatter_dimension=0, tiled=True)]
    all_gather x1 -> x0, blocking collectives: 39.1 us -> none  [per_device(): lax.all_gather(cols_view, 'row', axis=0, tiled=True)]
    ppermute x0 -> x19, waiting for transfers between devices: none -> 38.9 us  [the longest x14 15.7 us: per_device(): stream[0] = lax.ppermute(stream[0], 'row', ring_pairs(stream[1]))]
    dot_general x16 -> x0, matrix products: 25.8 us -> none  [one_group(): jnp.einsum('kaxy,kbyz->kabxz', left_one, right_one, preferred_element_typ...]
    unnamed x1 -> x0, blocking collectives: 14.1 us -> none
  transfers between devices with their start and end apart: 3 -> 21, of which waited for: 3 -> 11; matrix products, arithmetic and copies ran while one was open for 1% -> 4% of each run, Pallas kernels for 0% -> 0%
where the time goes in v1:
time: 155 us; the launch traced here: 153 us
  starting transfers between devices  69.3 us (45%)
  waiting for transfers between devices  44.5 us (29%)
  between operations  13.9 us (9%)
  local copies, waits for them, and re-layouts  11.8 us (8%)
  Pallas kernels  9.87 us (6%)
  other arithmetic  4.01 us (3%)
    ppermute x14, starting transfers between devices, per_device(): stream[0] = lax.ppermute(stream[0], 'row', ring_pairs(stream[1]))  54.2 us
    ppermute x14, waiting for transfers between devices, per_device(): stream[0] = lax.ppermute(stream[0], 'row', ring_pairs(stream[1]))  15.7 us
    ppermute x3, waiting for transfers between devices, per_device(): out = out + lax.ppermute(total[step], ('row', 'depth'), chip_pairs(step))  12.5 us
    ppermute x3, starting transfers between devices, per_device(): out = out + lax.ppermute(total[step], ('row', 'depth'), chip_pairs(step))  10.4 us
    pallas_call x1, Pallas kernels, per_device(): pl.pallas_call(lambda *refs: multiply(sizes, *refs), out_shape=[jax.Shape...  9.87 us
    ppermute x1, waiting for transfers between devices, per_device(): lax.ppermute(other, 'row', [(r, (r + NZ) % 16) for r in range(16)])  7.28 us
    all_gather x1, waiting for transfers between devices, per_device(): left_other = lax.all_gather(swapped, 'col', axis=0)  5.58 us
    slice x14, local copies, waits for them, and re-layouts, per_device(): chunk[count * EB * W, :count * EB].astype(jnp.int32)  5.33 us
  transfers between devices with their start and end apart: 21, of which 11 were waited for; matrix products, arithmetic and copies ran while one was open for 4% of the time, Pallas kernels for 0%

profile of v1, /device:TPU:6, one launch (start us, length us, event | category | flops | bytes accessed | tf_op | source)
XLA Modules:
  0.0 153.5 jit_solution(18207393942441134616)
XLA Ops:
  10.4 2.7 %collective-permute-start = (bf16[1040,128]{1,0:T(8,128)(2,1)S(1)}, bf16[1040,128]{1,0:T(8,128)(2,1)S(1)}, u32[]{:S(2)}, u32[]{:S(2)}) collective-permute-start(bf16[1040,128]{1,0:T(8,128)(2,1)S(1)} %fusion.10), channel_id=1, source_target_pairs={{0,256},{32,288},{64,320},{96,352},{128,384},{160,416},{192,448},{... | collective-permute-start | bytes 798728 | tf_op jit(solution)/shard_map/ppermute | solution.py:131
  13.1 7.3 %collective-permute-done = bf16[1040,128]{1,0:T(8,128)(2,1)S(1)} collective-permute-done((bf16[1040,128]{1,0:T(8,128)(2,1)S(1)}, bf16[1040,128]{1,0:T(8,128)(2,1)S(1)}, u32[]{:S(2)}, u32[]{:S(2)}) %collective-permute-start) | collective-permute-done | bytes 266272 | tf_op jit(solution)/shard_map/ppermute | solution.py:131
  21.5 10.9 %collective-permute-start.4 = (bf16[1552,128]{1,0:T(8,128)(2,1)S(1)}, bf16[1552,128]{1,0:T(8,128)(2,1)S(1)}, u32[]{:S(2)}, u32[]{:S(2)}) collective-permute-start(bf16[1552,128]{1,0:T(8,128)(2,1)S(1)} %fusion.5.refs_6_), channel_id=1, source_target_pairs={{0,224},{32,256},{64,32},{96,320},{128,96},{160,384},{192,160},{22... | collective-permute-start | bytes 1191944 | tf_op jit(solution)/shard_map/ppermute | solution.py:148
  32.7 1.9 %collective-permute-start.1 = (bf16[1552,128]{1,0:T(8,128)(2,1)S(1)}, bf16[1552,128]{1,0:T(8,128)(2,1)S(1)}, u32[]{:S(2)}, u32[]{:S(2)}) collective-permute-start(bf16[1552,128]{1,0:T(8,128)(2,1)S(1)} %fusion.4.refs_5_), channel_id=1, source_target_pairs={{0,288},{32,64},{64,352},{96,128},{128,416},{160,192},{192,480},{2... | collective-permute-start | bytes 1191944 | tf_op jit(solution)/shard_map/ppermute | solution.py:148
  34.6 1.9 %collective-permute-start.3 = (bf16[1552,128]{1,0:T(8,128)(2,1)S(1)}, bf16[1552,128]{1,0:T(8,128)(2,1)S(1)}, u32[]{:S(2)}, u32[]{:S(2)}) collective-permute-start(bf16[1552,128]{1,0:T(8,128)(2,1)S(1)} %fusion.5.refs_6_), channel_id=1, source_target_pairs={{0,288},{32,64},{64,352},{96,128},{128,416},{160,192},{192,480},{2... | collective-permute-start | bytes 1191944 | tf_op jit(solution)/shard_map/ppermute | solution.py:148
  36.6 5.1 %collective-permute-start.2 = (bf16[1552,128]{1,0:T(8,128)(2,1)S(1)}, bf16[1552,128]{1,0:T(8,128)(2,1)S(1)}, u32[]{:S(2)}, u32[]{:S(2)}) collective-permute-start(bf16[1552,128]{1,0:T(8,128)(2,1)S(1)} %fusion.4.refs_5_), channel_id=1, source_target_pairs={{0,224},{32,256},{64,32},{96,320},{128,96},{160,384},{192,160},{22... | collective-permute-start | bytes 1191944 | tf_op jit(solution)/shard_map/ppermute | solution.py:148
  41.7 4.8 %collective-permute-start.8 = (bf16[1552,128]{1,0:T(8,128)(2,1)S(1)}, bf16[1552,128]{1,0:T(8,128)(2,1)S(1)}, u32[]{:S(2)}, u32[]{:S(2)}) collective-permute-start(bf16[1552,128]{1,0:T(8,128)(2,1)S(1)} %collective-permute-done.4.refs_10_), channel_id=1, source_target_pairs={{0,224},{32,256},{64,32},{96,320},{128,96},{160,384},{192,160},{22... | collective-permute-start | bytes 1191944 | tf_op jit(solution)/shard_map/ppermute | solution.py:148
  46.5 1.4 collective-permute-done.1.refs_7_
  47.9 1.9 %collective-permute-start.5 = (bf16[1552,128]{1,0:T(8,128)(2,1)S(1)}, bf16[1552,128]{1,0:T(8,128)(2,1)S(1)}, u32[]{:S(2)}, u32[]{:S(2)}) collective-permute-start(bf16[1552,128]{1,0:T(8,128)(2,1)S(1)} %collective-permute-done.1.refs_7_), channel_id=1, source_target_pairs={{0,288},{32,64},{64,352},{96,128},{128,416},{160,192},{192,480},{2... | collective-permute-start | bytes 1191944 | tf_op jit(solution)/shard_map/ppermute | solution.py:148
  49.9 6.6 %collective-permute-done.3.refs_9_ = bf16[1552,128]{1,0:T(8,128)(2,1)S(1)} collective-permute-done((bf16[1552,128]{1,0:T(8,128)(2,1)S(1)}, bf16[1552,128]{1,0:T(8,128)(2,1)S(1)}, u32[]{:S(2)}, u32[]{:S(2)}) %collective-permute-start.3) | collective-permute-done | bytes 397344 | tf_op jit(solution)/shard_map/ppermute | solution.py:148
  56.5 1.9 %collective-permute-start.7 = (bf16[1552,128]{1,0:T(8,128)(2,1)S(1)}, bf16[1552,128]{1,0:T(8,128)(2,1)}, u32[]{:S(2)}, u32[]{:S(2)}) collective-permute-start(bf16[1552,128]{1,0:T(8,128)(2,1)S(1)} %collective-permute-done.3.refs_9_), channel_id=1, source_target_pairs={{0,288},{32,64},{64,352},{96,128},{128,416},{160,192},{192,480},{2... | collective-permute-start | bytes 1191944 | tf_op jit(solution)/shard_map/ppermute | solution.py:148
  58.4 5.1 %collective-permute-start.6 = (bf16[1552,128]{1,0:T(8,128)(2,1)S(1)}, bf16[1552,128]{1,0:T(8,128)(2,1)}, u32[]{:S(2)}, u32[]{:S(2)}) collective-permute-start(bf16[1552,128]{1,0:T(8,128)(2,1)S(1)} %collective-permute-done.2.refs_8_), channel_id=1, source_target_pairs={{0,224},{32,256},{64,32},{96,320},{128,96},{160,384},{192,160},{22... | collective-permute-start | bytes 1191944 | tf_op jit(solution)/shard_map/ppermute | solution.py:148
  63.5 2.1 %collective-permute-start.12 = (bf16[1552,128]{1,0:T(8,128)(2,1)S(1)}, bf16[1552,128]{1,0:T(8,128)(2,1)}, u32[]{:S(2)}, u32[]{:S(2)}) collective-permute-start(bf16[1552,128]{1,0:T(8,128)(2,1)S(1)} %collective-permute-done.8.refs_14_), channel_id=1, source_target_pairs={{0,224},{32,256},{64,32},{96,320},{128,96},{160,384},{192,160},{22... | collective-permute-start | bytes 1191944 | tf_op jit(solution)/shard_map/ppermute | solution.py:148
  65.7 4.6 %collective-permute-start.9 = (bf16[1552,128]{1,0:T(8,128)(2,1)S(1)}, bf16[1552,128]{1,0:T(8,128)(2,1)}, u32[]{:S(2)}, u32[]{:S(2)}) collective-permute-start(bf16[1552,128]{1,0:T(8,128)(2,1)S(1)} %collective-permute-done.5.refs_11_), channel_id=1, source_target_pairs={{0,288},{32,64},{64,352},{96,128},{128,416},{160,192},{192,480},{2... | collective-permute-start | bytes 1191944 | tf_op jit(solution)/shard_map/ppermute | solution.py:148
  70.3 3.3 %collective-permute-done.7.refs_13_ = bf16[1552,128]{1,0:T(8,128)(2,1)} collective-permute-done((bf16[1552,128]{1,0:T(8,128)(2,1)S(1)}, bf16[1552,128]{1,0:T(8,128)(2,1)}, u32[]{:S(2)}, u32[]{:S(2)}) %collective-permute-start.7) | collective-permute-done | bytes 397344 | tf_op jit(solution)/shard_map/ppermute | solution.py:148
  73.6 1.9 %collective-permute-start.11 = (bf16[1552,128]{1,0:T(8,128)(2,1)}, bf16[1552,128]{1,0:T(8,128)(2,1)}, u32[]{:S(2)}, u32[]{:S(2)}) collective-permute-start(bf16[1552,128]{1,0:T(8,128)(2,1)} %collective-permute-done.7.refs_13_), channel_id=1, source_target_pairs={{0,288},{32,64},{64,352},{96,128},{128,416},{160,192},{192,480},{2... | collective-permute-start | bytes 1191944 | tf_op jit(solution)/shard_map/ppermute | solution.py:148
  75.5 5.1 %collective-permute-start.10 = (bf16[1552,128]{1,0:T(8,128)(2,1)}, bf16[1552,128]{1,0:T(8,128)(2,1)}, u32[]{:S(2)}, u32[]{:S(2)}) collective-permute-start(bf16[1552,128]{1,0:T(8,128)(2,1)} %collective-permute-done.6.refs_12_), channel_id=1, source_target_pairs={{0,224},{32,256},{64,32},{96,320},{128,96},{160,384},{192,160},{22... | collective-permute-start | bytes 1191944 | tf_op jit(solution)/shard_map/ppermute | solution.py:148
  80.7 2.1 %collective-permute-start.14 = (bf16[1552,128]{1,0:T(8,128)(2,1)}, bf16[1552,128]{1,0:T(8,128)(2,1)}, u32[]{:S(2)}, u32[]{:S(2)}) collective-permute-start(bf16[1552,128]{1,0:T(8,128)(2,1)} %collective-permute-done.12.refs_18_), channel_id=1, source_target_pairs={{0,224},{32,256},{64,32},{96,320},{128,96},{160,384},{192,160},{22... | collective-permute-start | bytes 1191944 | tf_op jit(solution)/shard_map/ppermute | solution.py:148
  82.8 4.6 %collective-permute-start.13 = (bf16[1552,128]{1,0:T(8,128)(2,1)}, bf16[1552,128]{1,0:T(8,128)(2,1)}, u32[]{:S(2)}, u32[]{:S(2)}) collective-permute-start(bf16[1552,128]{1,0:T(8,128)(2,1)} %collective-permute-done.9.refs_15_), channel_id=1, source_target_pairs={{0,288},{32,64},{64,352},{96,128},{128,416},{160,192},{192,480},{2... | collective-permute-start | bytes 1191944 | tf_op jit(solution)/shard_map/ppermute | solution.py:148
  92.0 2.0 %collective-permute-done.14.refs_20_ = bf16[1552,128]{1,0:T(8,128)(2,1)} collective-permute-done((bf16[1552,128]{1,0:T(8,128)(2,1)}, bf16[1552,128]{1,0:T(8,128)(2,1)}, u32[]{:S(2)}, u32[]{:S(2)}) %collective-permute-start.14) | collective-permute-done | bytes 397344 | tf_op jit(solution)/shard_map/ppermute | solution.py:148
  94.7 2.1 %collective-permute-done.13.refs_19_ = bf16[1552,128]{1,0:T(8,128)(2,1)} collective-permute-done((bf16[1552,128]{1,0:T(8,128)(2,1)}, bf16[1552,128]{1,0:T(8,128)(2,1)}, u32[]{:S(2)}, u32[]{:S(2)}) %collective-permute-start.13) | collective-permute-done | bytes 397344 | tf_op jit(solution)/shard_map/ppermute | solution.py:148
  97.6 5.6 %all-gather.7.cloned.1.call-done = bf16[8320,128]{1,0:T(8,128)(2,1)} async-done(((bf16[1040,128]{1,0:T(8,128)(2,1)}), bf16[8320,128]{1,0:T(8,128)(2,1)}) %all-gather.7.cloned.1.call-update) | async-done | bytes 2129936 | tf_op jit(solution)/shard_map/all_gather | solution.py:132
  104.1 1.6 %copy-done = bf16[8320,128]{1,0:T(8,128)(2,1)S(1)} copy-done((bf16[8320,128]{1,0:T(8,128)(2,1)S(1)}, bf16[8320,128]{1,0:T(8,128)(2,1)}, u32[]{:S(2)}) %copy-start) | copy-done | bytes 2129944
  105.7 1.6 %copy-done.1 = bf16[8320,128]{1,0:T(8,128)(2,1)S(1)} copy-done((bf16[8320,128]{1,0:T(8,128)(2,1)S(1)}, bf16[8320,128]{1,0:T(8,128)(2,1)}, u32[]{:S(2)}) %copy-start.1) | copy-done | bytes 2129944
  107.3 9.9 %shard_map.46 = (f32[4,128,768]{2,1,0:T(8,128)S(1)}, f32[4,128,768]{2,1,0:T(8,128)S(1)}) custom-call(s32[2,64]{1,0:T(2,128)S(1)} %pad_add_fusion.refs_0_, s32[16,12]{1,0:T(8,128)S(1)} %stack.28.refs_1_, s32[16]{0:T(128)S(1)} %fusion.23.refs_2_, bf16[8,1040,128]{2,1,0:T(8,128)(2,1)S(1)} %bitcast.38, bf16[8,1040,128]{2,1,0:T(8,128)(2,1)S(1)} %bitcast.40, ...), custom_call_target="tpu_custom_call" | custom-call | flops 1610612736 | bytes 14680064 | tf_op jit(solution)/shard_map/pallas_call | solution.py:176
  117.2 1.9 %collective-permute-start.15 = (f32[4,128,768]{2,1,0:T(8,128)S(1)}, f32[4,128,768]{2,1,0:T(8,128)S(1)}, u32[]{:S(2)}, u32[]{:S(2)}) collective-permute-start(f32[4,128,768]{2,1,0:T(8,128)S(1)} %get-tuple-element.56), channel_id=1, source_target_pairs={{0,1},{1,0},{2,3},{3,2},{4,5},{5,4},{6,7},{7,6},{8,9},{9,8},{10,11... | collective-permute-start | bytes 4718600 | tf_op jit(solution)/shard_map/ppermute | solution.py:194
  119.1 3.4 %collective-permute-done.15 = f32[4,128,768]{2,1,0:T(8,128)S(1)} collective-permute-done((f32[4,128,768]{2,1,0:T(8,128)S(1)}, f32[4,128,768]{2,1,0:T(8,128)S(1)}, u32[]{:S(2)}, u32[]{:S(2)}) %collective-permute-start.15) | collective-permute-done | bytes 1572896 | tf_op jit(solution)/shard_map/ppermute | solution.py:194
  122.8 3.4 %collective-permute-start.16 = (f32[128,768]{1,0:T(8,128)S(1)}, f32[128,768]{1,0:T(8,128)S(1)}, u32[]{:S(2)}, u32[]{:S(2)}) collective-permute-start(f32[128,768]{1,0:T(8,128)S(1)} %get-tuple-element.57), channel_id=1, source_target_pairs={{0,2},{1,3},{2,0},{3,1},{32,34},{33,35},{34,32},{35,33},{64,66},{6... | collective-permute-start | bytes 1179656 | tf_op jit(solution)/shard_map/ppermute | solution.py:198
  126.2 1.9 %collective-permute-start.18 = (f32[128,768]{1,0:T(8,128)S(1)}, f32[128,768]{1,0:T(8,128)S(1)}, u32[]{:S(2)}, u32[]{:S(2)}) collective-permute-start(f32[128,768]{1,0:T(8,128)S(1)} %get-tuple-element.58), channel_id=1, source_target_pairs={{0,258},{1,259},{2,256},{3,257},{32,290},{33,291},{34,288},{35,289... | collective-permute-start | bytes 1179656 | tf_op jit(solution)/shard_map/ppermute | solution.py:198
  128.1 5.1 %collective-permute-start.17 = (f32[128,768]{1,0:T(8,128)S(1)}, f32[128,768]{1,0:T(8,128)S(1)}, u32[]{:S(2)}, u32[]{:S(2)}) collective-permute-start(f32[128,768]{1,0:T(8,128)S(1)} %get-tuple-element.59), channel_id=1, source_target_pairs={{0,256},{1,257},{2,258},{3,259},{32,288},{33,289},{34,290},{35,291... | collective-permute-start | bytes 1179656 | tf_op jit(solution)/shard_map/ppermute | solution.py:198
  133.2 5.0 %collective-permute-done.16 = f32[128,768]{1,0:T(8,128)S(1)} collective-permute-done((f32[128,768]{1,0:T(8,128)S(1)}, f32[128,768]{1,0:T(8,128)S(1)}, u32[]{:S(2)}, u32[]{:S(2)}) %collective-permute-start.16) | collective-permute-done | bytes 393248 | tf_op jit(solution)/shard_map/ppermute | solution.py:198
  138.2 7.6 %collective-permute-done.18 = f32[128,768]{1,0:T(8,128)S(1)} collective-permute-done((f32[128,768]{1,0:T(8,128)S(1)}, f32[128,768]{1,0:T(8,128)S(1)}, u32[]{:S(2)}, u32[]{:S(2)}) %collective-permute-start.18) | collective-permute-done | bytes 393248 | tf_op jit(solution)/shard_map/ppermute | solution.py:198
  (66 shorter events, 13.0 us)
Async XLA Ops:
  6.5 14.6 %copy-start.4 = (s32[1,8,1,3]{1,2,3,0:T(1,128)S(1)}, s32[1,8,1,3]{1,2,3,0:T(1,128)}, u32[]{:S(2)}) copy-start(s32[1,8,1,3]{1,2,3,0:T(1,128)} %param.15) | copy-start | bytes 292
  6.5 14.9 %copy-start.2 = (bf16[1,8,1,3,128,128]{5,4,3,2,1,0:T(8,128)(2,1)S(1)}, bf16[1,8,1,3,128,128]{5,4,3,2,1,0:T(8,128)(2,1)}, u32[]{:S(2)}) copy-start(bf16[1,8,1,3,128,128]{5,4,3,2,1,0:T(8,128)(2,1)} %param.14) | copy-start | bytes 2359300
  6.5 91.0 %all-gather.5.cloned.1.call-start = ((), (), s32[]{:S(2)}) async-start(), calls=%async_computation | async-start | bytes 2396160 | tf_op jit(solution)/shard_map/all_gather | solution.py:130
  10.3 92.9 %all-gather.7.cloned.1.call-start = ((), (), s32[]{:S(2)}) async-start(), calls=%async_computation.1 | async-start | bytes 2396160 | tf_op jit(solution)/shard_map/all_gather | solution.py:132
  10.4 10.0 %collective-permute-start = (bf16[1040,128]{1,0:T(8,128)(2,1)S(1)}, bf16[1040,128]{1,0:T(8,128)(2,1)S(1)}, u32[]{:S(2)}, u32[]{:S(2)}) collective-permute-start(bf16[1040,128]{1,0:T(8,128)(2,1)S(1)} %fusion.10), channel_id=1, source_target_pairs={{0,256},{32,288},{64,320},{96,352},{128,384},{160,416},{192,448},{... | collective-permute-start | bytes 798728 | tf_op jit(solution)/shard_map/ppermute | solution.py:131
  20.4 0.7 copy-start.3
  21.5 20.2 %collective-permute-start.4 = (bf16[1552,128]{1,0:T(8,128)(2,1)S(1)}, bf16[1552,128]{1,0:T(8,128)(2,1)S(1)}, u32[]{:S(2)}, u32[]{:S(2)}) collective-permute-start(bf16[1552,128]{1,0:T(8,128)(2,1)S(1)} %fusion.5.refs_6_), channel_id=1, source_target_pairs={{0,224},{32,256},{64,32},{96,320},{128,96},{160,384},{192,160},{22... | collective-permute-start | bytes 1191944 | tf_op jit(solution)/shard_map/ppermute | solution.py:148
  32.7 15.2 %collective-permute-start.1 = (bf16[1552,128]{1,0:T(8,128)(2,1)S(1)}, bf16[1552,128]{1,0:T(8,128)(2,1)S(1)}, u32[]{:S(2)}, u32[]{:S(2)}) collective-permute-start(bf16[1552,128]{1,0:T(8,128)(2,1)S(1)} %fusion.4.refs_5_), channel_id=1, source_target_pairs={{0,288},{32,64},{64,352},{96,128},{128,416},{160,192},{192,480},{2... | collective-permute-start | bytes 1191944 | tf_op jit(solution)/shard_map/ppermute | solution.py:148
  34.6 21.8 %collective-permute-start.3 = (bf16[1552,128]{1,0:T(8,128)(2,1)S(1)}, bf16[1552,128]{1,0:T(8,128)(2,1)S(1)}, u32[]{:S(2)}, u32[]{:S(2)}) collective-permute-start(bf16[1552,128]{1,0:T(8,128)(2,1)S(1)} %fusion.5.refs_6_), channel_id=1, source_target_pairs={{0,288},{32,64},{64,352},{96,128},{128,416},{160,192},{192,480},{2... | collective-permute-start | bytes 1191944 | tf_op jit(solution)/shard_map/ppermute | solution.py:148
  36.6 21.8 %collective-permute-start.2 = (bf16[1552,128]{1,0:T(8,128)(2,1)S(1)}, bf16[1552,128]{1,0:T(8,128)(2,1)S(1)}, u32[]{:S(2)}, u32[]{:S(2)}) collective-permute-start(bf16[1552,128]{1,0:T(8,128)(2,1)S(1)} %fusion.4.refs_5_), channel_id=1, source_target_pairs={{0,224},{32,256},{64,32},{96,320},{128,96},{160,384},{192,160},{22... | collective-permute-start | bytes 1191944 | tf_op jit(solution)/shard_map/ppermute | solution.py:148
  41.7 21.8 %collective-permute-start.8 = (bf16[1552,128]{1,0:T(8,128)(2,1)S(1)}, bf16[1552,128]{1,0:T(8,128)(2,1)S(1)}, u32[]{:S(2)}, u32[]{:S(2)}) collective-permute-start(bf16[1552,128]{1,0:T(8,128)(2,1)S(1)} %collective-permute-done.4.refs_10_), channel_id=1, source_target_pairs={{0,224},{32,256},{64,32},{96,320},{128,96},{160,384},{192,160},{22... | collective-permute-start | bytes 1191944 | tf_op jit(solution)/shard_map/ppermute | solution.py:148
  47.9 17.7 %collective-permute-start.5 = (bf16[1552,128]{1,0:T(8,128)(2,1)S(1)}, bf16[1552,128]{1,0:T(8,128)(2,1)S(1)}, u32[]{:S(2)}, u32[]{:S(2)}) collective-permute-start(bf16[1552,128]{1,0:T(8,128)(2,1)S(1)} %collective-permute-done.1.refs_7_), channel_id=1, source_target_pairs={{0,288},{32,64},{64,352},{96,128},{128,416},{160,192},{192,480},{2... | collective-permute-start | bytes 1191944 | tf_op jit(solution)/shard_map/ppermute | solution.py:148
  56.5 17.1 %collective-permute-start.7 = (bf16[1552,128]{1,0:T(8,128)(2,1)S(1)}, bf16[1552,128]{1,0:T(8,128)(2,1)}, u32[]{:S(2)}, u32[]{:S(2)}) collective-permute-start(bf16[1552,128]{1,0:T(8,128)(2,1)S(1)} %collective-permute-done.3.refs_9_), channel_id=1, source_target_pairs={{0,288},{32,64},{64,352},{96,128},{128,416},{160,192},{192,480},{2... | collective-permute-start | bytes 1191944 | tf_op jit(solution)/shard_map/ppermute | solution.py:148
  58.4 17.1 %collective-permute-start.6 = (bf16[1552,128]{1,0:T(8,128)(2,1)S(1)}, bf16[1552,128]{1,0:T(8,128)(2,1)}, u32[]{:S(2)}, u32[]{:S(2)}) collective-permute-start(bf16[1552,128]{1,0:T(8,128)(2,1)S(1)} %collective-permute-done.2.refs_8_), channel_id=1, source_target_pairs={{0,224},{32,256},{64,32},{96,320},{128,96},{160,384},{192,160},{22... | collective-permute-start | bytes 1191944 | tf_op jit(solution)/shard_map/ppermute | solution.py:148
  63.5 17.1 %collective-permute-start.12 = (bf16[1552,128]{1,0:T(8,128)(2,1)S(1)}, bf16[1552,128]{1,0:T(8,128)(2,1)}, u32[]{:S(2)}, u32[]{:S(2)}) collective-permute-start(bf16[1552,128]{1,0:T(8,128)(2,1)S(1)} %collective-permute-done.8.refs_14_), channel_id=1, source_target_pairs={{0,224},{32,256},{64,32},{96,320},{128,96},{160,384},{192,160},{22... | collective-permute-start | bytes 1191944 | tf_op jit(solution)/shard_map/ppermute | solution.py:148
  65.7 17.1 %collective-permute-start.9 = (bf16[1552,128]{1,0:T(8,128)(2,1)S(1)}, bf16[1552,128]{1,0:T(8,128)(2,1)}, u32[]{:S(2)}, u32[]{:S(2)}) collective-permute-start(bf16[1552,128]{1,0:T(8,128)(2,1)S(1)} %collective-permute-done.5.refs_11_), channel_id=1, source_target_pairs={{0,288},{32,64},{64,352},{96,128},{128,416},{160,192},{192,480},{2... | collective-permute-start | bytes 1191944 | tf_op jit(solution)/shard_map/ppermute | solution.py:148
  73.6 17.0 %collective-permute-start.11 = (bf16[1552,128]{1,0:T(8,128)(2,1)}, bf16[1552,128]{1,0:T(8,128)(2,1)}, u32[]{:S(2)}, u32[]{:S(2)}) collective-permute-start(bf16[1552,128]{1,0:T(8,128)(2,1)} %collective-permute-done.7.refs_13_), channel_id=1, source_target_pairs={{0,288},{32,64},{64,352},{96,128},{128,416},{160,192},{192,480},{2... | collective-permute-start | bytes 1191944 | tf_op jit(solution)/shard_map/ppermute | solution.py:148
  75.5 15.8 %collective-permute-start.10 = (bf16[1552,128]{1,0:T(8,128)(2,1)}, bf16[1552,128]{1,0:T(8,128)(2,1)}, u32[]{:S(2)}, u32[]{:S(2)}) collective-permute-start(bf16[1552,128]{1,0:T(8,128)(2,1)} %collective-permute-done.6.refs_12_), channel_id=1, source_target_pairs={{0,224},{32,256},{64,32},{96,320},{128,96},{160,384},{192,160},{22... | collective-permute-start | bytes 1191944 | tf_op jit(solution)/shard_map/ppermute | solution.py:148
  80.7 13.3 %collective-permute-start.14 = (bf16[1552,128]{1,0:T(8,128)(2,1)}, bf16[1552,128]{1,0:T(8,128)(2,1)}, u32[]{:S(2)}, u32[]{:S(2)}) collective-permute-start(bf16[1552,128]{1,0:T(8,128)(2,1)} %collective-permute-done.12.refs_18_), channel_id=1, source_target_pairs={{0,224},{32,256},{64,32},{96,320},{128,96},{160,384},{192,160},{22... | collective-permute-start | bytes 1191944 | tf_op jit(solution)/shard_map/ppermute | solution.py:148
  82.8 14.0 %collective-permute-start.13 = (bf16[1552,128]{1,0:T(8,128)(2,1)}, bf16[1552,128]{1,0:T(8,128)(2,1)}, u32[]{:S(2)}, u32[]{:S(2)}) collective-permute-start(bf16[1552,128]{1,0:T(8,128)(2,1)} %collective-permute-done.9.refs_15_), channel_id=1, source_target_pairs={{0,288},{32,64},{64,352},{96,128},{128,416},{160,192},{192,480},{2... | collective-permute-start | bytes 1191944 | tf_op jit(solution)/shard_map/ppermute | solution.py:148
  104.1 1.6 %copy-start = (bf16[8320,128]{1,0:T(8,128)(2,1)S(1)}, bf16[8320,128]{1,0:T(8,128)(2,1)}, u32[]{:S(2)}) copy-start(bf16[8320,128]{1,0:T(8,128)(2,1)} %all-gather.5.cloned.1.call-done) | copy-start | bytes 6389764
  105.7 1.6 %copy-start.1 = (bf16[8320,128]{1,0:T(8,128)(2,1)S(1)}, bf16[8320,128]{1,0:T(8,128)(2,1)}, u32[]{:S(2)}) copy-start(bf16[8320,128]{1,0:T(8,128)(2,1)} %all-gather.7.cloned.1.call-done) | copy-start | bytes 6389764
  117.2 5.3 %collective-permute-start.15 = (f32[4,128,768]{2,1,0:T(8,128)S(1)}, f32[4,128,768]{2,1,0:T(8,128)S(1)}, u32[]{:S(2)}, u32[]{:S(2)}) collective-permute-start(f32[4,128,768]{2,1,0:T(8,128)S(1)} %get-tuple-element.56), channel_id=1, source_target_pairs={{0,1},{1,0},{2,3},{3,2},{4,5},{5,4},{6,7},{7,6},{8,9},{9,8},{10,11... | collective-permute-start | bytes 4718600 | tf_op jit(solution)/shard_map/ppermute | solution.py:194
  122.8 15.4 %collective-permute-start.16 = (f32[128,768]{1,0:T(8,128)S(1)}, f32[128,768]{1,0:T(8,128)S(1)}, u32[]{:S(2)}, u32[]{:S(2)}) collective-permute-start(f32[128,768]{1,0:T(8,128)S(1)} %get-tuple-element.57), channel_id=1, source_target_pairs={{0,2},{1,3},{2,0},{3,1},{32,34},{33,35},{34,32},{35,33},{64,66},{6... | collective-permute-start | bytes 1179656 | tf_op jit(solution)/shard_map/ppermute | solution.py:198
  126.2 19.6 %collective-permute-start.18 = (f32[128,768]{1,0:T(8,128)S(1)}, f32[128,768]{1,0:T(8,128)S(1)}, u32[]{:S(2)}, u32[]{:S(2)}) collective-permute-start(f32[128,768]{1,0:T(8,128)S(1)} %get-tuple-element.58), channel_id=1, source_target_pairs={{0,258},{1,259},{2,256},{3,257},{32,290},{33,291},{34,288},{35,289... | collective-permute-start | bytes 1179656 | tf_op jit(solution)/shard_map/ppermute | solution.py:198
  128.1 17.7 %collective-permute-start.17 = (f32[128,768]{1,0:T(8,128)S(1)}, f32[128,768]{1,0:T(8,128)S(1)}, u32[]{:S(2)}, u32[]{:S(2)}) collective-permute-start(f32[128,768]{1,0:T(8,128)S(1)} %get-tuple-element.59), channel_id=1, source_target_pairs={{0,256},{1,257},{2,258},{3,259},{32,288},{33,289},{34,290},{35,291... | collective-permute-start | bytes 1179656 | tf_op jit(solution)/shard_map/ppermute | solution.py:198
Sparse Core Ops, SparseCore 0:
  10.4 48.4 all-gather.4
  60.9 42.1 all-gather.6

commit v2 on v1

--- a/solution.py
+++ b/solution.py
@@ -10,6 +10,7 @@
 W = 128
 NZ = 8
 GROUP = 8
+VMEM_LIMIT = 56 * 2**20
 PAD = 16
 PARTS = ((4, 4, 3), (4, 3, 4))
 
@@ -27,18 +28,6 @@
     return pairs
 
 
-def chip_pairs(step):
-    pairs = []
-    for row in range(16):
-        for depth in range(4):
-            x = (depth // 2) * 2 + row // NZ
-            to = (x + step) % 4
-            pairs.append(
-                (row * 4 + depth, ((to % 2) * NZ + row % NZ) * 4 + (to // 2) * 2 + depth % 2)
-            )
-    return pairs
-
-
 def with_index(blocks, index):
     flat = blocks.reshape(-1, W)
     row = jnp.zeros((PAD, W), flat.dtype)
@@ -48,15 +37,12 @@
 
 def multiply(chunk_sizes, place_ref, cols_ref, slot_ref, *refs):
     n = len(chunk_sizes)
-    left_hbm = refs[:2]
-    right_hbm = refs[2 : 2 + n]
-    keep_hbm, send_hbm = refs[2 + n : 4 + n]
-    left_buf, right_buf, acc, left_sem, right_sem, out_sem = refs[4 + n :]
-    left_copies = [
-        pltpu.make_async_copy(left_hbm[t], left_buf.at[t], left_sem.at[t]) for t in range(2)
-    ]
-    for copy in left_copies:
-        copy.start()
+    left_hbm = refs[0]
+    right_hbm = refs[1 : 1 + n]
+    keep_hbm, send_hbm = refs[1 + n : 3 + n]
+    left_buf, right_buf, acc, left_sem, right_sem, out_sem = refs[3 + n :]
+    left_copy = pltpu.make_async_copy(left_hbm, left_buf, left_sem.at[0])
+    left_copy.start()
     right_copies = [
         pltpu.make_async_copy(
             right_hbm[c], right_buf.at[c, pl.ds(0, right_hbm[c].shape[0])], right_sem.at[c]
@@ -66,8 +52,7 @@
     for copy in right_copies:
         copy.start()
     acc[...] = jnp.zeros_like(acc)
-    for copy in left_copies:
-        copy.wait()
+    left_copy.wait()
     for c, (count, offset) in enumerate(chunk_sizes):
         right_copies[c].wait()
         slot = slot_ref[c]
@@ -76,7 +61,7 @@
             k = offset + j
             rows = pl.ds(pl.multiple_of(k * W, W), W)
             both = jnp.concatenate(
-                [left_buf[0, slot, rows, :], left_buf[1, slot, rows, :]], axis=0
+                [left_buf[slot, 0, rows, :], left_buf[slot, 1, rows, :]], axis=0
             )
             first = j * (EB * W)
             right = jnp.concatenate(
@@ -105,12 +90,10 @@
 
 
 def per_device(left_blocks, left_rows, right_blocks, right_cols):
-    row = lax.axis_index("row")
-    y = lax.axis_index("col")
-    depth = lax.axis_index("depth")
-    x_lo, z = row // NZ, row % NZ
-    x_hi, core = depth // 2, depth % 2
-    x = x_hi * 2 + x_lo
+    x_lo = lax.axis_index("x_lo")
+    z = lax.axis_index("z")
+    y = lax.axis_index("y")
+    core = lax.axis_index("core")
     half = x_lo ^ zig(z)
 
     left = left_blocks.reshape(2, GROUP * W, W)
@@ -127,9 +110,7 @@
     right = right_blocks.reshape(GROUP, EB * W, W)
     cols = right_cols.reshape(GROUP, EB)
 
-    left_own = lax.all_gather(mine, "col", axis=0)
-    swapped = lax.ppermute(other, "row", [(r, (r + NZ) % 16) for r in range(16)])
-    left_other = lax.all_gather(swapped, "col", axis=0)
+    swapped = lax.ppermute(other, "x_lo", [(0, 1), (1, 0)])
 
     chunks, sizes, sources = [], [], []
     streams = []
@@ -145,19 +126,20 @@
     for t in range(1, NZ):
         for stream in streams:
             if t <= stream[2]:
-                stream[0] = lax.ppermute(stream[0], "row", ring_pairs(stream[1]))
+                stream[0] = lax.ppermute(stream[0], ("x_lo", "z"), ring_pairs(stream[1]))
                 chunks.append(stream[0])
                 sizes.append((stream[3], stream[4]))
                 sources.append((z - stream[1] * t) % NZ)
+    pair = jnp.stack([mine, swapped])
+    pair = lax.optimization_barrier((pair, *chunks[len(PARTS) : len(PARTS) + 2]))[0]
+    left_all = lax.all_gather(pair, "y", axis=0)
     source = jnp.stack(sources)
     slots = (4 * (zig(source) ^ half) + source // 2).astype(jnp.int32)
 
-    def places(gathered, tile):
-        block_row = gathered[:, GROUP * W, :GROUP].astype(jnp.int32)
-        ahead = ((block_row // 2) * 2 + tile - x) % 4
-        return (((block_row % 2) ^ core) * 4 + ahead).reshape(-1)
-
-    place = jnp.stack([places(left_own, x_lo), places(left_other, 1 - x_lo)])
+    block_row = left_all[:, :, GROUP * W, :GROUP].astype(jnp.int32)
+    tile = jnp.stack([x_lo, 1 - x_lo])[None, :, None]
+    place = ((block_row % 2) ^ core) * 4 + tile * 2 + block_row // 2
+    place = place.transpose(1, 0, 2).reshape(2, NZ * GROUP)
     most = max(count for count, _ in sizes)
     col_ids = jnp.stack(
         [
@@ -176,40 +158,41 @@
     keep, send = pl.pallas_call(
         lambda *refs: multiply(sizes, *refs),
         out_shape=[jax.ShapeDtypeStruct((4, W, 6 * W), jnp.float32)] * 2,
-        in_specs=[smem] * 3 + [hbm] * (2 + n),
+        in_specs=[smem] * 3 + [hbm] * (1 + n),
         out_specs=[hbm] * 2,
         scratch_shapes=[
-            pltpu.VMEM((2, NZ, GROUP * W + PAD, W), jnp.bfloat16),
+            pltpu.VMEM((NZ, 2, GROUP * W + PAD, W), jnp.bfloat16),
             pltpu.VMEM((n, longest, W), jnp.bfloat16),
             pltpu.VMEM((8, W, 6 * W), jnp.float32),
-            pltpu.SemaphoreType.DMA((2,)),
+            pltpu.SemaphoreType.DMA((1,)),
             pltpu.SemaphoreType.DMA((n,)),
             pltpu.SemaphoreType.DMA((2,)),
         ],
-        compiler_params=pltpu.CompilerParams(vmem_limit_bytes=40 * 2**20),
+        compiler_params=pltpu.CompilerParams(vmem_limit_bytes=VMEM_LIMIT),
         cost_estimate=pl.CostEstimate(
             flops=flops, bytes_accessed=14 * 2**20, transcendentals=0
         ),
-    )(place, col_ids, slots, left_own, left_other, *chunks)
-    got = lax.ppermute(send, "depth", [(0, 1), (1, 0), (2, 3), (3, 2)])
+    )(place, col_ids, slots, left_all, *chunks)
+    got = lax.ppermute(send, "core", [(0, 1), (1, 0)])
     total = keep + got
-    out = total[0]
-    for step in (2, 1, 3):
-        out = out + lax.ppermute(total[step], ("row", "depth"), chip_pairs(step))
-    return out
+    return lax.all_to_all(total, ("x_lo", "x_hi"), 0, 0, tiled=True).sum(0)
 
 
 def solution(mesh):
+    split = jax.sharding.Mesh(
+        mesh.devices.reshape(2, NZ, 8, 2, 2), ("x_lo", "z", "y", "x_hi", "core")
+    )
+    row, depth = ("x_lo", "z"), ("x_hi", "core")
     placed = (
-        P("depth", "col", "row", None, None, None),
-        P("depth", "col", "row", None),
-        P("depth", "row", "col", None, None, None),
-        P("depth", "row", "col", None),
+        P(depth, "y", row, None, None, None),
+        P(depth, "y", row, None),
+        P(depth, row, "y", None, None, None),
+        P(depth, row, "y", None),
     )
     return jax.shard_map(
         per_device,
-        mesh=mesh,
+        mesh=split,
         in_specs=placed,
-        out_specs=P(("row", "depth"), "col"),
+        out_specs=P(row + depth, "y"),
         check_vma=False,
     )

time: 155 us -> 155 us (level)
  blocking collectives: 0 us -> 23.2 us
  waiting for transfers between devices: 44.5 us -> 28.7 us
  starting transfers between devices: 69.3 us -> 58.3 us
  Pallas kernels: 9.87 us -> 13.3 us
  local copies, waits for them, and re-layouts: 11.8 us -> 8.43 us
  other arithmetic: 4.01 us -> 6.87 us
    all_to_all x0 -> x1, blocking collectives: none -> 23.2 us  [per_device(): return lax.all_to_all(total, ('x_lo', 'x_hi'), 0, 0, tiled=True).sum(0)]
    ppermute x19 -> x16, starting transfers between devices: 69.3 us -> 58.3 us  [the longest x14 53.6 us: per_device(): stream[0] = lax.ppermute(stream[0], ('x_lo', 'z'), ring_pairs(stream[1]))]
    ppermute x19 -> x16, waiting for transfers between devices: 38.9 us -> 28.6 us  [the longest x14 22.6 us: per_device(): stream[0] = lax.ppermute(stream[0], ('x_lo', 'z'), ring_pairs(stream[1]))]
    all_gather x2 -> x1, waiting for transfers between devices: 5.59 us -> 0.01 us  [per_device(): left_all = lax.all_gather(pair, 'y', axis=0)]
    unnamed x11 -> x21, local copies, waits for them, and re-layouts: 4.41 us -> 0.55 us
    pallas_call x1, Pallas kernels: 9.87 us -> 13.3 us  [per_device(): pl.pallas_call(lambda *refs: multiply(sizes, *refs), out_shape=[jax.Shape...]
  transfers between devices with their start and end apart: 21 -> 17, of which waited for: 11 -> 8; matrix products, arithmetic and copies ran while one was open for 4% -> 5% of each run, Pallas kernels for 0% -> 0%
where the time goes in v2:
time: 155 us; the launch traced here: 153 us
  starting transfers between devices  58.3 us (38%)
  waiting for transfers between devices  28.7 us (19%)
  blocking collectives  23.2 us (15%)
  between operations  13.8 us (9%)
  Pallas kernels  13.3 us (9%)
  local copies, waits for them, and re-layouts  8.43 us (5%)
  other arithmetic  6.87 us (4%)
    ppermute x14, starting transfers between devices, per_device(): stream[0] = lax.ppermute(stream[0], ('x_lo', 'z'), ring_pairs(stream[1]))  53.6 us
    all_to_all x1, blocking collectives, per_device(): return lax.all_to_all(total, ('x_lo', 'x_hi'), 0, 0, tiled=True).sum(0)  23.2 us
    ppermute x14, waiting for transfers between devices, per_device(): stream[0] = lax.ppermute(stream[0], ('x_lo', 'z'), ring_pairs(stream[1]))  22.6 us
    pallas_call x1, Pallas kernels, per_device(): pl.pallas_call(lambda *refs: multiply(sizes, *refs), out_shape=[jax.Shape...  13.3 us
    slice x14, local copies, waits for them, and re-layouts, per_device(): chunk[count * EB * W, :count * EB].astype(jnp.int32)  5.36 us
    ppermute x1, waiting for transfers between devices, per_device(): got = lax.ppermute(send, 'core', [(0, 1), (1, 0)])  3.59 us
  transfers between devices with their start and end apart: 17, of which 8 were waited for; matrix products, arithmetic and copies ran while one was open for 5% of the time, Pallas kernels for 0%

profile of v2, /device:TPU:6, one launch (start us, length us, event | category | flops | bytes accessed | tf_op | source)
XLA Modules:
  0.0 152.5 jit_solution(3348650573255281548)
XLA Ops:
  7.1 1.3 reduce.11
  8.5 1.1 dynamic-slice_bitcast_fusion.1
  9.6 2.7 %collective-permute-start = (bf16[1040,128]{1,0:T(8,128)(2,1)S(1)}, bf16[1040,128]{1,0:T(8,128)(2,1)S(1)}, u32[]{:S(2)}, u32[]{:S(2)}) collective-permute-start(bf16[1040,128]{1,0:T(8,128)(2,1)S(1)} %fusion.8), channel_id=1, source_target_pairs={{0,256},{256,0},{1,257},{257,1},{2,258},{258,2},{3,259},{259,3},{4... | collective-permute-start | bytes 798728 | tf_op jit(solution)/shard_map/ppermute | solution.py:113
  12.7 10.9 %collective-permute-start.2 = (bf16[1552,128]{1,0:T(8,128)(2,1)S(1)}, bf16[1552,128]{1,0:T(8,128)(2,1)S(1)}, u32[]{:S(2)}, u32[]{:S(2)}) collective-permute-start(bf16[1552,128]{1,0:T(8,128)(2,1)S(1)} %fusion.4.refs_4_), channel_id=1, source_target_pairs={{0,224},{32,256},{64,32},{96,320},{128,96},{160,384},{192,160},{22... | collective-permute-start | bytes 1191944 | tf_op jit(solution)/shard_map/ppermute | solution.py:129
  23.7 1.9 %collective-permute-start.1 = (bf16[1552,128]{1,0:T(8,128)(2,1)S(1)}, bf16[1552,128]{1,0:T(8,128)(2,1)S(1)}, u32[]{:S(2)}, u32[]{:S(2)}) collective-permute-start(bf16[1552,128]{1,0:T(8,128)(2,1)S(1)} %fusion.4.refs_4_), channel_id=1, source_target_pairs={{0,288},{32,64},{64,352},{96,128},{128,416},{160,192},{192,480},{2... | collective-permute-start | bytes 1191944 | tf_op jit(solution)/shard_map/ppermute | solution.py:129
  25.6 2.5 %collective-permute-done = bf16[1040,128]{1,0:T(8,128)(2,1)S(1)} collective-permute-done((bf16[1040,128]{1,0:T(8,128)(2,1)S(1)}, bf16[1040,128]{1,0:T(8,128)(2,1)S(1)}, u32[]{:S(2)}, u32[]{:S(2)}) %collective-permute-start) | collective-permute-done | bytes 266272 | tf_op jit(solution)/shard_map/ppermute | solution.py:113
  28.1 0.9 pad_maximum_fusion
  29.0 2.9 %collective-permute-done.2.refs_7_ = bf16[1552,128]{1,0:T(8,128)(2,1)S(1)} collective-permute-done((bf16[1552,128]{1,0:T(8,128)(2,1)S(1)}, bf16[1552,128]{1,0:T(8,128)(2,1)S(1)}, u32[]{:S(2)}, u32[]{:S(2)}) %collective-permute-start.2) | collective-permute-done | bytes 397344 | tf_op jit(solution)/shard_map/ppermute | solution.py:129
  31.8 5.3 %collective-permute-done.1.refs_6_ = bf16[1552,128]{1,0:T(8,128)(2,1)S(1)} collective-permute-done((bf16[1552,128]{1,0:T(8,128)(2,1)S(1)}, bf16[1552,128]{1,0:T(8,128)(2,1)S(1)}, u32[]{:S(2)}, u32[]{:S(2)}) %collective-permute-start.1) | collective-permute-done | bytes 397344 | tf_op jit(solution)/shard_map/ppermute | solution.py:129
  37.4 2.8 %collective-permute-start.4 = (bf16[1552,128]{1,0:T(8,128)(2,1)S(1)}, bf16[1552,128]{1,0:T(8,128)(2,1)S(1)}, u32[]{:S(2)}, u32[]{:S(2)}) collective-permute-start(bf16[1552,128]{1,0:T(8,128)(2,1)S(1)} %fusion.5.refs_5_), channel_id=1, source_target_pairs={{0,224},{32,256},{64,32},{96,320},{128,96},{160,384},{192,160},{22... | collective-permute-start | bytes 1191944 | tf_op jit(solution)/shard_map/ppermute | solution.py:129
  40.2 4.0 %collective-permute-start.3 = (bf16[1552,128]{1,0:T(8,128)(2,1)S(1)}, bf16[1552,128]{1,0:T(8,128)(2,1)S(1)}, u32[]{:S(2)}, u32[]{:S(2)}) collective-permute-start(bf16[1552,128]{1,0:T(8,128)(2,1)S(1)} %fusion.5.refs_5_), channel_id=1, source_target_pairs={{0,288},{32,64},{64,352},{96,128},{128,416},{160,192},{192,480},{2... | collective-permute-start | bytes 1191944 | tf_op jit(solution)/shard_map/ppermute | solution.py:129
  44.2 5.5 %collective-permute-done.4.refs_9_ = bf16[1552,128]{1,0:T(8,128)(2,1)S(1)} collective-permute-done((bf16[1552,128]{1,0:T(8,128)(2,1)S(1)}, bf16[1552,128]{1,0:T(8,128)(2,1)S(1)}, u32[]{:S(2)}, u32[]{:S(2)}) %collective-permute-start.4) | collective-permute-done | bytes 397344 | tf_op jit(solution)/shard_map/ppermute | solution.py:129
  49.7 3.1 %collective-permute-start.8 = (bf16[1552,128]{1,0:T(8,128)(2,1)S(1)}, bf16[1552,128]{1,0:T(8,128)(2,1)S(1)}, u32[]{:S(2)}, u32[]{:S(2)}) collective-permute-start(bf16[1552,128]{1,0:T(8,128)(2,1)S(1)} %collective-permute-done.4.refs_9_), channel_id=1, source_target_pairs={{0,224},{32,256},{64,32},{96,320},{128,96},{160,384},{192,160},{22... | collective-permute-start | bytes 1191944 | tf_op jit(solution)/shard_map/ppermute | solution.py:129
  52.8 3.6 %collective-permute-start.5 = (bf16[1552,128]{1,0:T(8,128)(2,1)S(1)}, bf16[1552,128]{1,0:T(8,128)(2,1)S(1)}, u32[]{:S(2)}, u32[]{:S(2)}) collective-permute-start(bf16[1552,128]{1,0:T(8,128)(2,1)S(1)} %collective-permute-done.1.refs_6_), channel_id=1, source_target_pairs={{0,288},{32,64},{64,352},{96,128},{128,416},{160,192},{192,480},{2... | collective-permute-start | bytes 1191944 | tf_op jit(solution)/shard_map/ppermute | solution.py:129
  56.5 1.9 %collective-permute-start.7 = (bf16[1552,128]{1,0:T(8,128)(2,1)S(1)}, bf16[1552,128]{1,0:T(8,128)(2,1)}, u32[]{:S(2)}, u32[]{:S(2)}) collective-permute-start(bf16[1552,128]{1,0:T(8,128)(2,1)S(1)} %collective-permute-done.3.refs_8_), channel_id=1, source_target_pairs={{0,288},{32,64},{64,352},{96,128},{128,416},{160,192},{192,480},{2... | collective-permute-start | bytes 1191944 | tf_op jit(solution)/shard_map/ppermute | solution.py:129
  58.4 5.1 %collective-permute-start.6 = (bf16[1552,128]{1,0:T(8,128)(2,1)S(1)}, bf16[1552,128]{1,0:T(8,128)(2,1)}, u32[]{:S(2)}, u32[]{:S(2)}) collective-permute-start(bf16[1552,128]{1,0:T(8,128)(2,1)S(1)} %collective-permute-done.2.refs_7_), channel_id=1, source_target_pairs={{0,224},{32,256},{64,32},{96,320},{128,96},{160,384},{192,160},{22... | collective-permute-start | bytes 1191944 | tf_op jit(solution)/shard_map/ppermute | solution.py:129
  63.5 3.1 %collective-permute-start.12 = (bf16[1552,128]{1,0:T(8,128)(2,1)S(1)}, bf16[1552,128]{1,0:T(8,128)(2,1)}, u32[]{:S(2)}, u32[]{:S(2)}) collective-permute-start(bf16[1552,128]{1,0:T(8,128)(2,1)S(1)} %collective-permute-done.8.refs_13_), channel_id=1, source_target_pairs={{0,224},{32,256},{64,32},{96,320},{128,96},{160,384},{192,160},{22... | collective-permute-start | bytes 1191944 | tf_op jit(solution)/shard_map/ppermute | solution.py:129
  66.7 1.4 collective-permute-done.5.refs_10_
  68.0 3.3 %collective-permute-start.9 = (bf16[1552,128]{1,0:T(8,128)(2,1)S(1)}, bf16[1552,128]{1,0:T(8,128)(2,1)}, u32[]{:S(2)}, u32[]{:S(2)}) collective-permute-start(bf16[1552,128]{1,0:T(8,128)(2,1)S(1)} %collective-permute-done.5.refs_10_), channel_id=1, source_target_pairs={{0,288},{32,64},{64,352},{96,128},{128,416},{160,192},{192,480},{2... | collective-permute-start | bytes 1191944 | tf_op jit(solution)/shard_map/ppermute | solution.py:129
  71.4 5.3 %collective-permute-done.7.refs_12_ = bf16[1552,128]{1,0:T(8,128)(2,1)} collective-permute-done((bf16[1552,128]{1,0:T(8,128)(2,1)S(1)}, bf16[1552,128]{1,0:T(8,128)(2,1)}, u32[]{:S(2)}, u32[]{:S(2)}) %collective-permute-start.7) | collective-permute-done | bytes 397344 | tf_op jit(solution)/shard_map/ppermute | solution.py:129
  76.6 3.3 %collective-permute-start.11 = (bf16[1552,128]{1,0:T(8,128)(2,1)}, bf16[1552,128]{1,0:T(8,128)(2,1)}, u32[]{:S(2)}, u32[]{:S(2)}) collective-permute-start(bf16[1552,128]{1,0:T(8,128)(2,1)} %collective-permute-done.7.refs_12_), channel_id=1, source_target_pairs={{0,288},{32,64},{64,352},{96,128},{128,416},{160,192},{192,480},{2... | collective-permute-start | bytes 1191944 | tf_op jit(solution)/shard_map/ppermute | solution.py:129
  80.0 3.7 %collective-permute-start.10 = (bf16[1552,128]{1,0:T(8,128)(2,1)}, bf16[1552,128]{1,0:T(8,128)(2,1)}, u32[]{:S(2)}, u32[]{:S(2)}) collective-permute-start(bf16[1552,128]{1,0:T(8,128)(2,1)} %collective-permute-done.6.refs_11_), channel_id=1, source_target_pairs={{0,224},{32,256},{64,32},{96,320},{128,96},{160,384},{192,160},{22... | collective-permute-start | bytes 1191944 | tf_op jit(solution)/shard_map/ppermute | solution.py:129
  83.7 2.4 %collective-permute-start.14 = (bf16[1552,128]{1,0:T(8,128)(2,1)}, bf16[1552,128]{1,0:T(8,128)(2,1)}, u32[]{:S(2)}, u32[]{:S(2)}) collective-permute-start(bf16[1552,128]{1,0:T(8,128)(2,1)} %collective-permute-done.12.refs_17_), channel_id=1, source_target_pairs={{0,224},{32,256},{64,32},{96,320},{128,96},{160,384},{192,160},{22... | collective-permute-start | bytes 1191944 | tf_op jit(solution)/shard_map/ppermute | solution.py:129
  86.1 4.4 %collective-permute-start.13 = (bf16[1552,128]{1,0:T(8,128)(2,1)}, bf16[1552,128]{1,0:T(8,128)(2,1)}, u32[]{:S(2)}, u32[]{:S(2)}) collective-permute-start(bf16[1552,128]{1,0:T(8,128)(2,1)} %collective-permute-done.9.refs_14_), channel_id=1, source_target_pairs={{0,288},{32,64},{64,352},{96,128},{128,416},{160,192},{192,480},{2... | collective-permute-start | bytes 1191944 | tf_op jit(solution)/shard_map/ppermute | solution.py:129
  96.1 2.2 %collective-permute-done.13.refs_18_ = bf16[1552,128]{1,0:T(8,128)(2,1)} collective-permute-done((bf16[1552,128]{1,0:T(8,128)(2,1)}, bf16[1552,128]{1,0:T(8,128)(2,1)}, u32[]{:S(2)}, u32[]{:S(2)}) %collective-permute-start.13) | collective-permute-done | bytes 397344 | tf_op jit(solution)/shard_map/ppermute | solution.py:129
  99.7 0.8 slice_convert_fusion
  101.2 13.3 %shard_map.46 = (f32[4,128,768]{2,1,0:T(8,128)}, f32[4,128,768]{2,1,0:T(8,128)}) custom-call(s32[2,64]{1,0:T(2,128)} %reshape.178.refs_0_, s32[16,12]{1,0:T(8,128)} %stack.83.refs_1_, s32[16]{0:T(128)} %fusion.23.refs_2_, bf16[8,2,1040,128]{3,2,1,0:T(8,128)(2,1)} %bitcast.50, bf16[1552,128]{1,0:T(8,128)(2,1)} %copy-done, bf16[1552,128]{1,0:T(8,128)(2,1)} %copy-done.1, ...), custom_call_target="tpu_custom_call" | custom-call | flops 1610612736 | bytes 14680064 | tf_op jit(solution)/shard_map/pallas_call | solution.py:158
  114.5 1.9 %collective-permute-start.15 = (f32[4,128,768]{2,1,0:T(8,128)}, f32[4,128,768]{2,1,0:T(8,128)S(1)}, u32[]{:S(2)}, u32[]{:S(2)}) collective-permute-start(f32[4,128,768]{2,1,0:T(8,128)} %get-tuple-element.58), channel_id=1, source_target_pairs={{0,1},{1,0},{2,3},{3,2},{4,5},{5,4},{6,7},{7,6},{8,9},{9,8},{10,11... | collective-permute-start | bytes 4718600 | tf_op jit(solution)/shard_map/ppermute | solution.py:176
  116.5 3.6 %collective-permute-done.15 = f32[4,128,768]{2,1,0:T(8,128)S(1)} collective-permute-done((f32[4,128,768]{2,1,0:T(8,128)}, f32[4,128,768]{2,1,0:T(8,128)S(1)}, u32[]{:S(2)}, u32[]{:S(2)}) %collective-permute-start.15) | collective-permute-done | bytes 1572896 | tf_op jit(solution)/shard_map/ppermute | solution.py:176
  120.1 1.6 %add.144 = f32[4,128,768]{2,1,0:T(8,128)S(1)} add(f32[4,128,768]{2,1,0:T(8,128)} %get-tuple-element.57, f32[4,128,768]{2,1,0:T(8,128)S(1)} %collective-permute-done.15) | non-fusion elementwise | flops 393216 | bytes 4718592 | tf_op jit(solution)/shard_map/add | solution.py:177
  121.7 23.2 %all_to_all.5 = f32[4,128,768]{2,1,0:T(8,128)S(1)} all-to-all(f32[4,128,768]{2,1,0:T(8,128)S(1)} %add.144), channel_id=1, replica_groups=mesh['x_lo'=2,'z'=8,'y'=8,'x_hi'=2,'core'=2] {'x_lo','x_hi'}, dimensions={0} | all-to-all | bytes 3145728 | tf_op jit(solution)/shard_map/all_to_all | solution.py:178
  144.8 0.9 reduce_sum.9
  (66 shorter events, 8.9 us)
Async XLA Ops:
  6.5 5.8 %copy-start.9 = (s32[1,8,1,3]{1,2,3,0:T(1,128)S(1)}, s32[1,8,1,3]{1,2,3,0:T(1,128)}, u32[]{:S(2)}) copy-start(s32[1,8,1,3]{1,2,3,0:T(1,128)} %param.15) | copy-start | bytes 292
  6.5 6.1 %copy-start.2 = (bf16[1,8,1,3,128,128]{5,4,3,2,1,0:T(8,128)(2,1)S(1)}, bf16[1,8,1,3,128,128]{5,4,3,2,1,0:T(8,128)(2,1)}, u32[]{:S(2)}) copy-start(bf16[1,8,1,3,128,128]{5,4,3,2,1,0:T(8,128)(2,1)} %param.14) | copy-start | bytes 2359300
  6.5 93.1 %all-gather.3.cloned.1.call-start = ((), (), s32[]{:S(2)}) async-start(), calls=%async_computation.1 | async-start | bytes 4792320 | tf_op jit(solution)/shard_map/all_gather | solution.py:135
  9.6 18.5 %collective-permute-start = (bf16[1040,128]{1,0:T(8,128)(2,1)S(1)}, bf16[1040,128]{1,0:T(8,128)(2,1)S(1)}, u32[]{:S(2)}, u32[]{:S(2)}) collective-permute-start(bf16[1040,128]{1,0:T(8,128)(2,1)S(1)} %fusion.8), channel_id=1, source_target_pairs={{0,256},{256,0},{1,257},{257,1},{2,258},{258,2},{3,259},{259,3},{4... | collective-permute-start | bytes 798728 | tf_op jit(solution)/shard_map/ppermute | solution.py:113
  12.7 78.0 %copy-start = (bf16[1552,128]{1,0:T(8,128)(2,1)}, bf16[1552,128]{1,0:T(8,128)(2,1)S(1)}, u32[]{:S(2)}) copy-start(bf16[1552,128]{1,0:T(8,128)(2,1)S(1)} %fusion.4.refs_4_) | copy-start | bytes 1191940
  12.7 19.1 %collective-permute-start.2 = (bf16[1552,128]{1,0:T(8,128)(2,1)S(1)}, bf16[1552,128]{1,0:T(8,128)(2,1)S(1)}, u32[]{:S(2)}, u32[]{:S(2)}) collective-permute-start(bf16[1552,128]{1,0:T(8,128)(2,1)S(1)} %fusion.4.refs_4_), channel_id=1, source_target_pairs={{0,224},{32,256},{64,32},{96,320},{128,96},{160,384},{192,160},{22... | collective-permute-start | bytes 1191944 | tf_op jit(solution)/shard_map/ppermute | solution.py:129
  23.7 13.5 %collective-permute-start.1 = (bf16[1552,128]{1,0:T(8,128)(2,1)S(1)}, bf16[1552,128]{1,0:T(8,128)(2,1)S(1)}, u32[]{:S(2)}, u32[]{:S(2)}) collective-permute-start(bf16[1552,128]{1,0:T(8,128)(2,1)S(1)} %fusion.4.refs_4_), channel_id=1, source_target_pairs={{0,288},{32,64},{64,352},{96,128},{128,416},{160,192},{192,480},{2... | collective-permute-start | bytes 1191944 | tf_op jit(solution)/shard_map/ppermute | solution.py:129
  31.8 69.3 %copy-start.3 = (bf16[1552,128]{1,0:T(8,128)(2,1)}, bf16[1552,128]{1,0:T(8,128)(2,1)S(1)}, u32[]{:S(2)}) copy-start(bf16[1552,128]{1,0:T(8,128)(2,1)S(1)} %collective-permute-done.2.refs_7_) | copy-start | bytes 1191940
  37.2 64.0 %copy-start.4 = (bf16[1552,128]{1,0:T(8,128)(2,1)}, bf16[1552,128]{1,0:T(8,128)(2,1)S(1)}, u32[]{:S(2)}) copy-start(bf16[1552,128]{1,0:T(8,128)(2,1)S(1)} %collective-permute-done.1.refs_6_) | copy-start | bytes 1191940
  37.4 63.8 %copy-start.1 = (bf16[1552,128]{1,0:T(8,128)(2,1)}, bf16[1552,128]{1,0:T(8,128)(2,1)S(1)}, u32[]{:S(2)}) copy-start(bf16[1552,128]{1,0:T(8,128)(2,1)S(1)} %fusion.5.refs_5_) | copy-start | bytes 1191940
  37.4 12.2 %collective-permute-start.4 = (bf16[1552,128]{1,0:T(8,128)(2,1)S(1)}, bf16[1552,128]{1,0:T(8,128)(2,1)S(1)}, u32[]{:S(2)}, u32[]{:S(2)}) collective-permute-start(bf16[1552,128]{1,0:T(8,128)(2,1)S(1)} %fusion.5.refs_5_), channel_id=1, source_target_pairs={{0,224},{32,256},{64,32},{96,320},{128,96},{160,384},{192,160},{22... | collective-permute-start | bytes 1191944 | tf_op jit(solution)/shard_map/ppermute | solution.py:129
  40.2 16.2 %collective-permute-start.3 = (bf16[1552,128]{1,0:T(8,128)(2,1)S(1)}, bf16[1552,128]{1,0:T(8,128)(2,1)S(1)}, u32[]{:S(2)}, u32[]{:S(2)}) collective-permute-start(bf16[1552,128]{1,0:T(8,128)(2,1)S(1)} %fusion.5.refs_5_), channel_id=1, source_target_pairs={{0,288},{32,64},{64,352},{96,128},{128,416},{160,192},{192,480},{2... | collective-permute-start | bytes 1191944 | tf_op jit(solution)/shard_map/ppermute | solution.py:129
  49.7 51.5 %copy-start.5 = (bf16[1552,128]{1,0:T(8,128)(2,1)}, bf16[1552,128]{1,0:T(8,128)(2,1)S(1)}, u32[]{:S(2)}) copy-start(bf16[1552,128]{1,0:T(8,128)(2,1)S(1)} %collective-permute-done.4.refs_9_) | copy-start | bytes 1191940
  49.7 13.8 %collective-permute-start.8 = (bf16[1552,128]{1,0:T(8,128)(2,1)S(1)}, bf16[1552,128]{1,0:T(8,128)(2,1)S(1)}, u32[]{:S(2)}, u32[]{:S(2)}) collective-permute-start(bf16[1552,128]{1,0:T(8,128)(2,1)S(1)} %collective-permute-done.4.refs_9_), channel_id=1, source_target_pairs={{0,224},{32,256},{64,32},{96,320},{128,96},{160,384},{192,160},{22... | collective-permute-start | bytes 1191944 | tf_op jit(solution)/shard_map/ppermute | solution.py:129
  52.8 15.2 %collective-permute-start.5 = (bf16[1552,128]{1,0:T(8,128)(2,1)S(1)}, bf16[1552,128]{1,0:T(8,128)(2,1)S(1)}, u32[]{:S(2)}, u32[]{:S(2)}) collective-permute-start(bf16[1552,128]{1,0:T(8,128)(2,1)S(1)} %collective-permute-done.1.refs_6_), channel_id=1, source_target_pairs={{0,288},{32,64},{64,352},{96,128},{128,416},{160,192},{192,480},{2... | collective-permute-start | bytes 1191944 | tf_op jit(solution)/shard_map/ppermute | solution.py:129
  56.4 44.7 %copy-start.6 = (bf16[1552,128]{1,0:T(8,128)(2,1)}, bf16[1552,128]{1,0:T(8,128)(2,1)S(1)}, u32[]{:S(2)}) copy-start(bf16[1552,128]{1,0:T(8,128)(2,1)S(1)} %collective-permute-done.3.refs_8_) | copy-start | bytes 1191940
  56.5 20.2 %collective-permute-start.7 = (bf16[1552,128]{1,0:T(8,128)(2,1)S(1)}, bf16[1552,128]{1,0:T(8,128)(2,1)}, u32[]{:S(2)}, u32[]{:S(2)}) collective-permute-start(bf16[1552,128]{1,0:T(8,128)(2,1)S(1)} %collective-permute-done.3.refs_8_), channel_id=1, source_target_pairs={{0,288},{32,64},{64,352},{96,128},{128,416},{160,192},{192,480},{2... | collective-permute-start | bytes 1191944 | tf_op jit(solution)/shard_map/ppermute | solution.py:129
  58.4 21.6 %collective-permute-start.6 = (bf16[1552,128]{1,0:T(8,128)(2,1)S(1)}, bf16[1552,128]{1,0:T(8,128)(2,1)}, u32[]{:S(2)}, u32[]{:S(2)}) collective-permute-start(bf16[1552,128]{1,0:T(8,128)(2,1)S(1)} %collective-permute-done.2.refs_7_), channel_id=1, source_target_pairs={{0,224},{32,256},{64,32},{96,320},{128,96},{160,384},{192,160},{22... | collective-permute-start | bytes 1191944 | tf_op jit(solution)/shard_map/ppermute | solution.py:129
  63.5 37.7 %copy-start.7 = (bf16[1552,128]{1,0:T(8,128)(2,1)}, bf16[1552,128]{1,0:T(8,128)(2,1)S(1)}, u32[]{:S(2)}) copy-start(bf16[1552,128]{1,0:T(8,128)(2,1)S(1)} %collective-permute-done.8.refs_13_) | copy-start | bytes 1191940
  63.5 20.2 %collective-permute-start.12 = (bf16[1552,128]{1,0:T(8,128)(2,1)S(1)}, bf16[1552,128]{1,0:T(8,128)(2,1)}, u32[]{:S(2)}, u32[]{:S(2)}) collective-permute-start(bf16[1552,128]{1,0:T(8,128)(2,1)S(1)} %collective-permute-done.8.refs_13_), channel_id=1, source_target_pairs={{0,224},{32,256},{64,32},{96,320},{128,96},{160,384},{192,160},{22... | collective-permute-start | bytes 1191944 | tf_op jit(solution)/shard_map/ppermute | solution.py:129
  68.0 33.2 %copy-start.8 = (bf16[1552,128]{1,0:T(8,128)(2,1)}, bf16[1552,128]{1,0:T(8,128)(2,1)S(1)}, u32[]{:S(2)}) copy-start(bf16[1552,128]{1,0:T(8,128)(2,1)S(1)} %collective-permute-done.5.refs_10_) | copy-start | bytes 1191940
  68.0 18.1 %collective-permute-start.9 = (bf16[1552,128]{1,0:T(8,128)(2,1)S(1)}, bf16[1552,128]{1,0:T(8,128)(2,1)}, u32[]{:S(2)}, u32[]{:S(2)}) collective-permute-start(bf16[1552,128]{1,0:T(8,128)(2,1)S(1)} %collective-permute-done.5.refs_10_), channel_id=1, source_target_pairs={{0,288},{32,64},{64,352},{96,128},{128,416},{160,192},{192,480},{2... | collective-permute-start | bytes 1191944 | tf_op jit(solution)/shard_map/ppermute | solution.py:129
  76.6 17.4 %collective-permute-start.11 = (bf16[1552,128]{1,0:T(8,128)(2,1)}, bf16[1552,128]{1,0:T(8,128)(2,1)}, u32[]{:S(2)}, u32[]{:S(2)}) collective-permute-start(bf16[1552,128]{1,0:T(8,128)(2,1)} %collective-permute-done.7.refs_12_), channel_id=1, source_target_pairs={{0,288},{32,64},{64,352},{96,128},{128,416},{160,192},{192,480},{2... | collective-permute-start | bytes 1191944 | tf_op jit(solution)/shard_map/ppermute | solution.py:129
  80.0 14.7 %collective-permute-start.10 = (bf16[1552,128]{1,0:T(8,128)(2,1)}, bf16[1552,128]{1,0:T(8,128)(2,1)}, u32[]{:S(2)}, u32[]{:S(2)}) collective-permute-start(bf16[1552,128]{1,0:T(8,128)(2,1)} %collective-permute-done.6.refs_11_), channel_id=1, source_target_pairs={{0,224},{32,256},{64,32},{96,320},{128,96},{160,384},{192,160},{22... | collective-permute-start | bytes 1191944 | tf_op jit(solution)/shard_map/ppermute | solution.py:129
  83.7 11.7 %collective-permute-start.14 = (bf16[1552,128]{1,0:T(8,128)(2,1)}, bf16[1552,128]{1,0:T(8,128)(2,1)}, u32[]{:S(2)}, u32[]{:S(2)}) collective-permute-start(bf16[1552,128]{1,0:T(8,128)(2,1)} %collective-permute-done.12.refs_17_), channel_id=1, source_target_pairs={{0,224},{32,256},{64,32},{96,320},{128,96},{160,384},{192,160},{22... | collective-permute-start | bytes 1191944 | tf_op jit(solution)/shard_map/ppermute | solution.py:129
  86.1 12.2 %collective-permute-start.13 = (bf16[1552,128]{1,0:T(8,128)(2,1)}, bf16[1552,128]{1,0:T(8,128)(2,1)}, u32[]{:S(2)}, u32[]{:S(2)}) collective-permute-start(bf16[1552,128]{1,0:T(8,128)(2,1)} %collective-permute-done.9.refs_14_), channel_id=1, source_target_pairs={{0,288},{32,64},{64,352},{96,128},{128,416},{160,192},{192,480},{2... | collective-permute-start | bytes 1191944 | tf_op jit(solution)/shard_map/ppermute | solution.py:129
  114.5 5.5 %collective-permute-start.15 = (f32[4,128,768]{2,1,0:T(8,128)}, f32[4,128,768]{2,1,0:T(8,128)S(1)}, u32[]{:S(2)}, u32[]{:S(2)}) collective-permute-start(f32[4,128,768]{2,1,0:T(8,128)} %get-tuple-element.58), channel_id=1, source_target_pairs={{0,1},{1,0},{2,3},{3,2},{4,5},{5,4},{6,7},{7,6},{8,9},{9,8},{10,11... | collective-permute-start | bytes 4718600 | tf_op jit(solution)/shard_map/ppermute | solution.py:176
Sparse Core Ops, SparseCore 0:
  37.3 54.2 all-gather.2

commit v3 on v0

v3 whole, which is shorter than its diff:
```python
import jax
import jax.numpy as jnp
from jax import lax
from jax.experimental import pallas as pl
from jax.experimental.pallas import tpu as pltpu
from jax.sharding import PartitionSpec as P

BR = 4
EB = 3
W = 128
NZ = 8
NY = 8
GROUP = 8
HALF = GROUP // 2
PAD = 16
LPART = GROUP * W + PAD
RPART = HALF * EB * W + PAD
CELL = 6 * W
VMEM_LIMIT = 10 * 2**20


def zig(z):
    return ((z + 1) // 2) % 2


def ring_pairs(step):
    pairs = []
    for x_lo in range(2):
        for z in range(NZ):
            to = (z + step) % NZ
            pairs.append((x_lo * NZ + z, (x_lo ^ zig(z) ^ zig(to)) * NZ + to))
    return pairs


def turn(step):
    return [(y, (y + step) % NY) for y in range(NY)]


def with_index(blocks, index):
    flat = blocks.reshape(-1, W)
    row = jnp.zeros((PAD, W), flat.dtype)
    row = row.at[0, : index.size].set(index.reshape(-1).astype(flat.dtype))
    return jnp.concatenate([flat, row], axis=0)


def load_index(meta, left, slots, held, halves, idx_v, idx_s, sem):
    core, x_lo = meta[0], meta[1]

    def first(ref_rows):
        return ref_rows.astype(jnp.float32)[0:1].astype(jnp.int32)

    for slot in slots:
        for p in range(2):
            rho = first(left[slot, pl.ds(p * LPART + GROUP * W, PAD), :])
            tile = x_lo if p == 0 else 1 - x_lo
            place = ((rho & 1) ^ core) * 4 + tile * 2 + (rho >> 1)
            idx_v[pl.ds(slot * 2 + p, 1), :] = place
    for i, (b, start, _) in enumerate(halves):
        idx_v[pl.ds(2 * NY + i, 1), :] = first(held[b, pl.ds(start + HALF * EB * W, PAD), :])
    copy = pltpu.make_async_copy(idx_v, idx_s, sem)
    copy.start()
    copy.wait()


def add_half(left, acc, idx_s, i, held, entry, slot):
    b, start, half = entry
    for j in range(HALF):
        k = half * HALF + j
        both = jnp.concatenate(
            [left[slot, pl.ds(p * LPART + k * W, W), :] for p in range(2)], axis=0
        )
        right = jnp.concatenate(
            [held[b, pl.ds(start + (j * EB + e) * W, W), :] for e in range(EB)], axis=1
        )
        part = jnp.dot(both, right, preferred_element_type=jnp.float32)
        for e in range(EB):
            lanes = pl.ds(pl.multiple_of(idx_s[2 * NY + i, j * EB + e] * W, W), W)
            for p in range(2):
                at = idx_s[slot * 2 + p, k]
                acc[at, :, lanes] += part[p * W : (p + 1) * W, e * W : (e + 1) * W]


def fetch(pairs, sems):
    copies = [pltpu.make_async_copy(a, b, sems.at[i]) for i, (a, b) in enumerate(pairs)]
    for copy in copies:
        copy.start()
    return copies


def halves_of(count):
    return [(b, h * RPART, h) for b in range(count) for h in range(2)]


def near(meta, *refs):
    lefts, rights, (acc, left, held, idx_v, idx_s, sem, sems) = refs[:7], refs[7:12], refs[12:]
    pairs = [(ref, left.at[slot]) for slot, ref in enumerate(lefts)]
    pairs += [(ref, held.at[b]) for b, ref in enumerate(rights)]
    copies = fetch(pairs, sems)
    acc[...] = jnp.zeros_like(acc)
    for copy in copies:
        copy.wait()
    halves = halves_of(5)
    load_index(meta, left, range(7), held, halves, idx_v, idx_s, sem)
    for c in range(5):

        @pl.when(meta[2 + c] != NY - 1)
        def _(c=c):
            for i in (2 * c, 2 * c + 1):
                add_half(left, acc, idx_s, i, held, halves[i], meta[2 + c])


def mid(meta, *refs):
    lefts, rights, (_, _, acc, left, held, idx_v, idx_s, sem, sems) = refs[:2], refs[2:9], refs[9:]
    pairs = [(ref, left.at[NY - 1, pl.ds(p * LPART, LPART)]) for p, ref in enumerate(lefts)]
    pairs += [(ref, held.at[b]) for b, ref in enumerate(rights[5:])]
    copies = fetch(pairs, sems)
    for c in range(6):
        chosen = meta[10] == 0 if c == 5 else meta[2 + c] == NY - 1

        @pl.when(chosen)
        def _(c=c):
            late = pltpu.make_async_copy(rights[c], held.at[2], sems.at[4])
            late.start()
            late.wait()

    for copy in copies:
        copy.wait()
    halves = halves_of(3)
    load_index(meta, left, range(NY), held, halves, idx_v, idx_s, sem)
    for i in range(4):
        add_half(left, acc, idx_s, i, held, halves[i], meta[7 + i // 2])

    @pl.when(meta[10] != 0)
    def _():
        for i in (4, 5):
            add_half(left, acc, idx_s, i, held, halves[i], NY - 1)


def far(meta, *refs):
    rights, (left, _, acc, held, idx_v, idx_s, sem, sems) = refs[:2], refs[2:]
    copies = fetch([(ref, held.at[b]) for b, ref in enumerate(rights)], sems)
    for copy in copies:
        copy.wait()
    halves = [(h, 0, h) for h in range(2)]
    load_index(meta, left, range(NY), held, halves, idx_v, idx_s, sem)
    for i, entry in enumerate(halves):
        add_half(left, acc, idx_s, i, held, entry, meta[9])


def call(body, meta, operands, near_by, outs, aliases, buffer, blocks):
    smem = pl.BlockSpec(memory_space=pltpu.SMEM)
    vmem = pl.BlockSpec(memory_space=pltpu.VMEM)
    far_off = pl.BlockSpec(memory_space=pl.ANY)
    return pl.pallas_call(
        body,
        out_shape=outs,
        in_specs=[smem] + [far_off] * len(operands) + [vmem] * len(near_by),
        out_specs=[vmem] * len(outs),
        input_output_aliases=aliases,
        scratch_shapes=[
            pltpu.VMEM(buffer, jnp.bfloat16),
            pltpu.VMEM((2 * NY + PAD, W), jnp.int32),
            pltpu.SMEM((2 * NY + PAD, W), jnp.int32),
            pltpu.SemaphoreType.DMA,
            pltpu.SemaphoreType.DMA((12,)),
        ],
        compiler_params=pltpu.CompilerParams(vmem_limit_bytes=VMEM_LIMIT),
        cost_estimate=pl.CostEstimate(
            flops=2 * blocks * W**3, bytes_accessed=2**20, transcendentals=0
        ),
    )(meta, *operands, *near_by)


def per_device(left_blocks, left_rows, right_blocks, right_cols):
    x_lo = lax.axis_index("x_lo")
    z = lax.axis_index("z")
    y = lax.axis_index("y")
    core = lax.axis_index("core")
    side = x_lo ^ zig(z)

    left = left_blocks.reshape(2, GROUP * W, W)
    rows = left_rows.reshape(2, GROUP)
    own = (side + y // 4 + y % 4) % 2

    def group(which):
        return with_index(
            lax.dynamic_index_in_dim(left, which, 0, False),
            lax.dynamic_index_in_dim(rows, which, 0, False),
        )

    swapped = lax.ppermute(group(1 - own), "x_lo", [(0, 1), (1, 0)])
    pair = jnp.concatenate([group(own), swapped], axis=0)
    right = right_blocks.reshape(2, HALF, EB * W, W)
    cols = right_cols.reshape(2, HALF * EB)
    chunk = jnp.concatenate([with_index(right[h], cols[h]) for h in range(2)], axis=0)
    first, _ = lax.optimization_barrier((chunk, swapped))

    row = ("x_lo", "z")
    up = down = first
    fore = back = pair
    rights, lefts = [chunk], [pair]
    for _ in range(3):
        up = lax.ppermute(up, row, ring_pairs(1))
        down = lax.ppermute(down, row, ring_pairs(-1))
        fore = lax.ppermute(fore, "y", turn(1))
        back = lax.ppermute(back, "y", turn(-1))
        rights += [up, down]
        lefts += [fore, back]
    last_left = [
        lax.ppermute(fore[:LPART], "y", turn(1)),
        lax.ppermute(back[LPART:], "y", turn(-1)),
    ]
    last_right = [
        lax.ppermute(up[:RPART], row, ring_pairs(1)),
        lax.ppermute(down[RPART:], row, ring_pairs(-1)),
    ]

    source = (z + jnp.array([0, -1, 1, -2, 2, -3, 3, 4], jnp.int32)) % NZ
    away = (4 * (zig(source) ^ side) + source // 2 - y) % NY
    slot = jnp.where(
        away == 0, 0, jnp.where(away == 4, 7, jnp.where(away < 4, 2 * away, 15 - 2 * away))
    )
    late = (slot[:5] == NY - 1).any()
    meta = jnp.concatenate([jnp.stack([core, x_lo]), slot, late[None]]).astype(jnp.int32)

    sums = jax.ShapeDtypeStruct((8, W, CELL), jnp.float32)
    kept = jax.ShapeDtypeStruct((NY, 2 * LPART, W), jnp.bfloat16)
    chunks = lambda n: (n, 2 * RPART, W)
    acc, left_all = call(near, meta, lefts + rights[:5], [], [sums, kept], {}, chunks(5), 240)
    acc, left_all = call(
        mid,
        meta,
        last_left + rights,
        [acc, left_all],
        [sums, kept],
        {10: 0, 11: 1},
        chunks(3),
        96,
    )
    (acc,) = call(far, meta, last_right, [left_all, acc], [sums], {4: 0}, (2, RPART, W), 48)

    got = lax.ppermute(acc[4:], "core", [(0, 1), (1, 0)])
    total = acc[:4] + got
    return lax.all_to_all(total, ("x_lo", "x_hi"), 0, 0, tiled=True).sum(0)


def solution(mesh):
    split = jax.sharding.Mesh(
        mesh.devices.reshape(2, NZ, NY, 2, 2), ("x_lo", "z", "y", "x_hi", "core")
    )
    row, depth = ("x_lo", "z"), ("x_hi", "core")
    placed = (
        P(depth, "y", row, None, None, None),
        P(depth, "y", row, None),
        P(depth, row, "y", None, None, None),
        P(depth, row, "y", None),
    )
    return jax.shard_map(
        per_device,
        mesh=split,
        in_specs=placed,
        out_specs=P(row + depth, "y"),
        check_vma=False,
    )
```

time: 407 us -> 164 us (0.40)
  waiting for transfers between devices: 197 us -> 36.5 us
  other arithmetic: 91.8 us -> 4.2 us
  starting transfers between devices: 0.08 us -> 67 us
  blocking collectives: 53.2 us -> 23.2 us
  matrix products: 25.8 us -> 0 us
  Pallas kernels: 0 us -> 13.6 us
  between operations: 13.8 us -> 0.99 us
  local copies, waits for them, and re-layouts: 21.1 us -> 15.9 us
    all_gather x2 -> x0, waiting for transfers between devices: 154 us -> none  [the longest x1 147 us: per_device(): lax.all_gather(right_view, 'row', axis=0, tiled=True)]
    scatter-add x16 -> x0, other arithmetic: 91.7 us -> none  [one_group(): carried = carried.at[cell_ids].add(products.reshape(-1, width * width))]
    ppermute x0 -> x18, starting transfers between devices: none -> 67 us  [the longest x3 18.6 us: per_device(): down = lax.ppermute(down, row, ring_pairs(-1))]
    reduce_scatter x1 -> x0, waiting for transfers between devices: 42.2 us -> none  [per_device(): return lax.psum_scatter(tile, 'depth', scatter_dimension=0, tiled=True)]
    all_gather x1 -> x0, blocking collectives: 39.1 us -> none  [per_device(): lax.all_gather(cols_view, 'row', axis=0, tiled=True)]
    ppermute x0 -> x18, waiting for transfers between devices: none -> 36.5 us  [the longest x3 19.1 us: per_device(): up = lax.ppermute(up, row, ring_pairs(1))]
    dot_general x16 -> x0, matrix products: 25.8 us -> none  [one_group(): jnp.einsum('kaxy,kbyz->kabxz', left_one, right_one, preferred_element_typ...]
    all_to_all x0 -> x1, blocking collectives: none -> 23.2 us  [per_device(): return lax.all_to_all(total, ('x_lo', 'x_hi'), 0, 0, tiled=True).sum(0)]
  transfers between devices with their start and end apart: 3 -> 18, of which waited for: 3 -> 5; matrix products, arithmetic and copies ran while one was open for 1% -> 5% of each run, Pallas kernels for 0% -> 6%
where the time goes in v3:
time: 164 us; the launch traced here: 161 us
  starting transfers between devices  67 us (41%)
  waiting for transfers between devices  36.5 us (22%)
  blocking collectives  23.2 us (14%)
  local copies, waits for them, and re-layouts  15.9 us (10%)
  Pallas kernels  13.6 us (8%)
  other arithmetic  4.2 us (3%)
    all_to_all x1, blocking collectives, per_device(): return lax.all_to_all(total, ('x_lo', 'x_hi'), 0, 0, tiled=True).sum(0)  23.2 us
    ppermute x3, waiting for transfers between devices, per_device(): up = lax.ppermute(up, row, ring_pairs(1))  19.1 us
    ppermute x3, starting transfers between devices, per_device(): down = lax.ppermute(down, row, ring_pairs(-1))  18.6 us
    ppermute x3, starting transfers between devices, per_device(): back = lax.ppermute(back, 'y', turn(-1))  14.1 us
    pallas_call x3, Pallas kernels, call(): pl.pallas_call(body, out_shape=outs, in_specs=[smem] + [far_off] * len(op...  13.6 us
    unnamed x33, local copies, waits for them, and re-layouts  9.03 us
    ppermute x3, starting transfers between devices, per_device(): up = lax.ppermute(up, row, ring_pairs(1))  8.35 us
    ppermute x3, starting transfers between devices, per_device(): fore = lax.ppermute(fore, 'y', turn(1))  7.31 us
  transfers between devices with their start and end apart: 18, of which 5 were waited for; matrix products, arithmetic and copies ran while one was open for 5% of the time, Pallas kernels for 6%

profile of v3, /device:TPU:6, one launch (start us, length us, event | category | flops | bytes accessed | tf_op | source)
XLA Modules:
  0.0 161.3 jit_solution(4224008839082454835)
XLA Ops:
  0.5 1.3 reduce.11
  1.9 1.1 dynamic-slice_bitcast_fusion
  3.0 2.7 %collective-permute-start = (bf16[1040,128]{1,0:T(8,128)(2,1)S(1)}, bf16[1040,128]{1,0:T(8,128)(2,1)S(1)}, u32[]{:S(2)}, u32[]{:S(2)}) collective-permute-start(bf16[1040,128]{1,0:T(8,128)(2,1)S(1)} %fusion.11), channel_id=1, source_target_pairs={{0,256},{256,0},{1,257},{257,1},{2,258},{258,2},{3,259},{259,3},{4... | collective-permute-start | bytes 798728 | tf_op jit(solution)/shard_map/ppermute | solution.py:191
  6.4 6.7 %collective-permute-done = bf16[1040,128]{1,0:T(8,128)(2,1)S(1)} collective-permute-done((bf16[1040,128]{1,0:T(8,128)(2,1)S(1)}, bf16[1040,128]{1,0:T(8,128)(2,1)S(1)}, u32[]{:S(2)}, u32[]{:S(2)}) %collective-permute-start) | collective-permute-done | bytes 266272 | tf_op jit(solution)/shard_map/ppermute | solution.py:191
  13.8 4.5 %collective-permute-start.1 = (bf16[3104,128]{1,0:T(8,128)(2,1)S(1)}, bf16[3104,128]{1,0:T(8,128)(2,1)S(1)}, u32[]{:S(2)}, u32[]{:S(2)}) collective-permute-start(bf16[3104,128]{1,0:T(8,128)(2,1)S(1)} %fusion.7.refs_7_.refs_2_), channel_id=1, source_target_pairs={{0,288},{32,64},{64,352},{96,128},{128,416},{160,192},{192,480},{2... | collective-permute-start | bytes 2383880 | tf_op jit(solution)/shard_map/ppermute | solution.py:203
  18.3 8.3 %collective-permute-start.5 = (bf16[3104,128]{1,0:T(8,128)(2,1)S(1)}, bf16[3104,128]{1,0:T(8,128)(2,1)S(1)}, u32[]{:S(2)}, u32[]{:S(2)}) collective-permute-start(bf16[3104,128]{1,0:T(8,128)(2,1)S(1)} %fusion.7.refs_7_.refs_2_), channel_id=1, source_target_pairs={{0,224},{32,256},{64,32},{96,320},{128,96},{160,384},{192,160},{22... | collective-permute-start | bytes 2383880 | tf_op jit(solution)/shard_map/ppermute | solution.py:204
  26.6 14.9 %collective-permute-done.1.refs_8_.refs_3_ = bf16[3104,128]{1,0:T(8,128)(2,1)S(1)} collective-permute-done((bf16[3104,128]{1,0:T(8,128)(2,1)S(1)}, bf16[3104,128]{1,0:T(8,128)(2,1)S(1)}, u32[]{:S(2)}, u32[]{:S(2)}) %collective-permute-start.1) | collective-permute-done | bytes 794656 | tf_op jit(solution)/shard_map/ppermute | solution.py:203
  41.5 1.9 %collective-permute-start.2 = (bf16[3104,128]{1,0:T(8,128)(2,1)S(1)}, bf16[3104,128]{1,0:T(8,128)(2,1)S(1)}, u32[]{:S(2)}, u32[]{:S(2)}) collective-permute-start(bf16[3104,128]{1,0:T(8,128)(2,1)S(1)} %collective-permute-done.1.refs_8_.refs_3_), channel_id=1, source_target_pairs={{0,288},{32,64},{64,352},{96,128},{128,416},{160,192},{192,480},{2... | collective-permute-start | bytes 2383880 | tf_op jit(solution)/shard_map/ppermute | solution.py:203
  43.5 5.1 %collective-permute-start.6 = (bf16[3104,128]{1,0:T(8,128)(2,1)S(1)}, bf16[3104,128]{1,0:T(8,128)(2,1)S(1)}, u32[]{:S(2)}, u32[]{:S(2)}) collective-permute-start(bf16[3104,128]{1,0:T(8,128)(2,1)S(1)} %collective-permute-done.5.refs_9_.refs_4_), channel_id=1, source_target_pairs={{0,224},{32,256},{64,32},{96,320},{128,96},{160,384},{192,160},{22... | collective-permute-start | bytes 2383880 | tf_op jit(solution)/shard_map/ppermute | solution.py:204
  49.6 3.5 %collective-permute-start.9 = (bf16[2080,128]{1,0:T(8,128)(2,1)S(1)}, bf16[2080,128]{1,0:T(8,128)(2,1)S(1)}, u32[]{:S(2)}, u32[]{:S(2)}) collective-permute-start(bf16[2080,128]{1,0:T(8,128)(2,1)S(1)} %fusion.9.refs_0_), channel_id=1, source_target_pairs={{0,4},{4,8},{8,12},{12,16},{16,20},{20,24},{24,28},{28,0},{1,5},{5... | collective-permute-start | bytes 1597448 | tf_op jit(solution)/shard_map/ppermute | solution.py:205
  53.1 3.8 %collective-permute-start.13 = (bf16[2080,128]{1,0:T(8,128)(2,1)S(1)}, bf16[2080,128]{1,0:T(8,128)(2,1)S(1)}, u32[]{:S(2)}, u32[]{:S(2)}) collective-permute-start(bf16[2080,128]{1,0:T(8,128)(2,1)S(1)} %fusion.9.refs_0_), channel_id=1, source_target_pairs={{0,28},{4,0},{8,4},{12,8},{16,12},{20,16},{24,20},{28,24},{1,29},{... | collective-permute-start | bytes 1597448 | tf_op jit(solution)/shard_map/ppermute | solution.py:206
  57.7 7.3 %collective-permute-done.9.refs_1_ = bf16[2080,128]{1,0:T(8,128)(2,1)S(1)} collective-permute-done((bf16[2080,128]{1,0:T(8,128)(2,1)S(1)}, bf16[2080,128]{1,0:T(8,128)(2,1)S(1)}, u32[]{:S(2)}, u32[]{:S(2)}) %collective-permute-start.9) | collective-permute-done | bytes 532512 | tf_op jit(solution)/shard_map/ppermute | solution.py:205
  65.0 1.9 %collective-permute-start.10 = (bf16[2080,128]{1,0:T(8,128)(2,1)S(1)}, bf16[2080,128]{1,0:T(8,128)(2,1)}, u32[]{:S(2)}, u32[]{:S(2)}) collective-permute-start(bf16[2080,128]{1,0:T(8,128)(2,1)S(1)} %collective-permute-done.9.refs_1_), channel_id=1, source_target_pairs={{0,4},{4,8},{8,12},{12,16},{16,20},{20,24},{24,28},{28,0},{1,5},{5... | collective-permute-start | bytes 1597448 | tf_op jit(solution)/shard_map/ppermute | solution.py:205
  67.7 5.1 %collective-permute-start.14 = (bf16[2080,128]{1,0:T(8,128)(2,1)S(1)}, bf16[2080,128]{1,0:T(8,128)(2,1)}, u32[]{:S(2)}, u32[]{:S(2)}) collective-permute-start(bf16[2080,128]{1,0:T(8,128)(2,1)S(1)} %collective-permute-done.13.refs_2_), channel_id=1, source_target_pairs={{0,28},{4,0},{8,4},{12,8},{16,12},{20,16},{24,20},{28,24},{1,29},{... | collective-permute-start | bytes 1597448 | tf_op jit(solution)/shard_map/ppermute | solution.py:206
  73.7 1.9 %collective-permute-start.3 = (bf16[3104,128]{1,0:T(8,128)(2,1)S(1)}, bf16[3104,128]{1,0:T(8,128)(2,1)S(1)}, u32[]{:S(2)}, u32[]{:S(2)}) collective-permute-start(bf16[3104,128]{1,0:T(8,128)(2,1)S(1)} %collective-permute-done.2.refs_10_.refs_5_), channel_id=1, source_target_pairs={{0,288},{32,64},{64,352},{96,128},{128,416},{160,192},{192,480},{2... | collective-permute-start | bytes 2383880 | tf_op jit(solution)/shard_map/ppermute | solution.py:203
  75.6 5.1 %collective-permute-start.7 = (bf16[3104,128]{1,0:T(8,128)(2,1)S(1)}, bf16[3104,128]{1,0:T(8,128)(2,1)S(1)}, u32[]{:S(2)}, u32[]{:S(2)}) collective-permute-start(bf16[3104,128]{1,0:T(8,128)(2,1)S(1)} %collective-permute-done.6.refs_11_.refs_6_), channel_id=1, source_target_pairs={{0,224},{32,256},{64,32},{96,320},{128,96},{160,384},{192,160},{22... | collective-permute-start | bytes 2383880 | tf_op jit(solution)/shard_map/ppermute | solution.py:204
  81.7 1.9 %collective-permute-start.11 = (bf16[2080,128]{1,0:T(8,128)(2,1)}, bf16[2080,128]{1,0:T(8,128)(2,1)}, u32[]{:S(2)}, u32[]{:S(2)}) collective-permute-start(bf16[2080,128]{1,0:T(8,128)(2,1)} %collective-permute-done.10.refs_3_), channel_id=1, source_target_pairs={{0,4},{4,8},{8,12},{12,16},{16,20},{20,24},{24,28},{28,0},{1,5},{5... | collective-permute-start | bytes 1597448 | tf_op jit(solution)/shard_map/ppermute | solution.py:205
  83.6 5.1 %collective-permute-start.15 = (bf16[2080,128]{1,0:T(8,128)(2,1)}, bf16[2080,128]{1,0:T(8,128)(2,1)}, u32[]{:S(2)}, u32[]{:S(2)}) collective-permute-start(bf16[2080,128]{1,0:T(8,128)(2,1)} %collective-permute-done.14.refs_4_), channel_id=1, source_target_pairs={{0,28},{4,0},{8,4},{12,8},{16,12},{20,16},{24,20},{28,24},{1,29},{... | collective-permute-start | bytes 1597448 | tf_op jit(solution)/shard_map/ppermute | solution.py:206
  88.7 4.2 %collective-permute-done.3.refs_7_ = bf16[3104,128]{1,0:T(8,128)(2,1)S(1)} collective-permute-done((bf16[3104,128]{1,0:T(8,128)(2,1)S(1)}, bf16[3104,128]{1,0:T(8,128)(2,1)S(1)}, u32[]{:S(2)}, u32[]{:S(2)}) %collective-permute-start.3) | collective-permute-done | bytes 794656 | tf_op jit(solution)/shard_map/ppermute | solution.py:203
  93.8 1.9 %collective-permute-start.4 = (bf16[1552,128]{1,0:T(8,128)(2,1)}, bf16[1552,128]{1,0:T(8,128)(2,1)}, u32[]{:S(2)}, u32[]{:S(2)}) collective-permute-start(bf16[1552,128]{1,0:T(8,128)(2,1)} %slice.116), channel_id=1, source_target_pairs={{0,288},{32,64},{64,352},{96,128},{128,416},{160,192},{192,480},{2... | collective-permute-start | bytes 1191944 | tf_op jit(solution)/shard_map/ppermute | solution.py:214
  96.8 5.1 %collective-permute-start.8 = (bf16[1552,128]{1,0:T(8,128)(2,1)}, bf16[1552,128]{1,0:T(8,128)(2,1)}, u32[]{:S(2)}, u32[]{:S(2)}) collective-permute-start(bf16[1552,128]{1,0:T(8,128)(2,1)} %slice.117), channel_id=1, source_target_pairs={{0,224},{32,256},{64,32},{96,320},{128,96},{160,384},{192,160},{22... | collective-permute-start | bytes 1191944 | tf_op jit(solution)/shard_map/ppermute | solution.py:215
  102.0 1.7 %slice.118 = bf16[1040,128]{1,0:T(8,128)(2,1)} slice(bf16[2080,128]{1,0:T(8,128)(2,1)} %collective-permute-done.11.refs_5_), slice={[0:1040], [0:128]} | slice | bytes 532480 | tf_op jit(solution)/shard_map/slice | solution.py:210
  103.7 1.9 %collective-permute-start.12 = (bf16[1040,128]{1,0:T(8,128)(2,1)}, bf16[1040,128]{1,0:T(8,128)(2,1)S(1)}, u32[]{:S(2)}, u32[]{:S(2)}) collective-permute-start(bf16[1040,128]{1,0:T(8,128)(2,1)} %slice.118), channel_id=1, source_target_pairs={{0,4},{4,8},{8,12},{12,16},{16,20},{20,24},{24,28},{28,0},{1,5},{5... | collective-permute-start | bytes 798728 | tf_op jit(solution)/shard_map/ppermute | solution.py:210
  105.6 1.7 %slice.119 = bf16[1040,128]{1,0:T(8,128)(2,1)} slice(bf16[2080,128]{1,0:T(8,128)(2,1)} %collective-permute-done.15.refs_6_), slice={[1040:2080], [0:128]} | slice | bytes 532480 | tf_op jit(solution)/shard_map/slice | solution.py:211
  107.3 5.1 %collective-permute-start.16 = (bf16[1040,128]{1,0:T(8,128)(2,1)}, bf16[1040,128]{1,0:T(8,128)(2,1)}, u32[]{:S(2)}, u32[]{:S(2)}) collective-permute-start(bf16[1040,128]{1,0:T(8,128)(2,1)} %slice.119), channel_id=1, source_target_pairs={{0,28},{4,0},{8,4},{12,8},{16,12},{20,16},{24,20},{28,24},{1,29},{... | collective-permute-start | bytes 798728 | tf_op jit(solution)/shard_map/ppermute | solution.py:211
  113.7 1.1 copy-done.1
  118.0 5.9 %shard_map.55 = (f32[8,128,768]{2,1,0:T(8,128)S(1)}, bf16[8,2080,128]{2,1,0:T(8,128)(2,1)S(1)}) custom-call(s32[11]{0:T(128)S(1)} %pad_add_fusion.meta, bf16[2080,128]{1,0:T(8,128)(2,1)S(1)} %copy-done.3, bf16[2080,128]{1,0:T(8,128)(2,1)S(1)} %copy-done.9, bf16[2080,128]{1,0:T(8,128)(2,1)S(1)} %copy-done.11, ...), custom_call_target="tpu_custom_call" | custom-call | flops 1006632960 | bytes 1048576 | tf_op jit(solution)/shard_map/pallas_call | solution.py:154
  124.0 4.4 %shard_map.56 = (f32[8,128,768]{2,1,0:T(8,128)S(1)}, bf16[8,2080,128]{2,1,0:T(8,128)(2,1)S(1)}) custom-call(s32[11]{0:T(128)S(1)} %pad_add_fusion.meta, bf16[1040,128]{1,0:T(8,128)(2,1)S(1)} %collective-permute-done.12.refs_0_, bf16[1040,128]{1,0:T(8,128)(2,1)} %collective-permute-done.16.refs_1_, ...), custom_call_target="tpu_custom_call", output_to_operand_aliasing={{0}: (10, {}), {1}: (11, {})} | custom-call | flops 402653184 | bytes 1048576 | tf_op jit(solution)/shard_map/pallas_call | solution.py:154
  128.4 3.3 %shard_map.57 = f32[8,128,768]{2,1,0:T(8,128)S(1)} custom-call(s32[11]{0:T(128)S(1)} %pad_add_fusion.meta, bf16[1552,128]{1,0:T(8,128)(2,1)} %collective-permute-done.4.refs_0_, bf16[1552,128]{1,0:T(8,128)(2,1)} %collective-permute-done.8.refs_1_, bf16[8,2080,128]{2,1,0:T(8,128)(2,1)S(1)} %get-tuple-element.61.refs_2_, ...), custom_call_target="tpu_custom_call", output_to_operand_aliasing={{}: (4, {})} | custom-call | flops 201326592 | bytes 1048576 | tf_op jit(solution)/shard_map/pallas_call | solution.py:154
  131.8 1.9 %collective-permute-start.17 = (f32[4,128,768]{2,1,0:T(8,128)S(1)}, f32[4,128,768]{2,1,0:T(8,128)S(1)}, u32[]{:S(2)}, u32[]{:S(2)}) collective-permute-start(f32[4,128,768]{2,1,0:T(8,128)S(1)} %slice.121), channel_id=1, source_target_pairs={{0,1},{1,0},{2,3},{3,2},{4,5},{5,4},{6,7},{7,6},{8,9},{9,8},{10,11... | collective-permute-start | bytes 4718600 | tf_op jit(solution)/shard_map/ppermute | solution.py:242
  133.7 3.4 %collective-permute-done.17 = f32[4,128,768]{2,1,0:T(8,128)S(1)} collective-permute-done((f32[4,128,768]{2,1,0:T(8,128)S(1)}, f32[4,128,768]{2,1,0:T(8,128)S(1)}, u32[]{:S(2)}, u32[]{:S(2)}) %collective-permute-start.17) | collective-permute-done | bytes 1572896 | tf_op jit(solution)/shard_map/ppermute | solution.py:242
  137.3 23.2 %all_to_all.5 = f32[4,128,768]{2,1,0:T(8,128)S(1)} all-to-all(f32[4,128,768]{2,1,0:T(8,128)S(1)} %slice_add_fusion), channel_id=1, replica_groups=mesh['x_lo'=2,'z'=8,'y'=8,'x_hi'=2,'core'=2] {'x_lo','x_hi'}, dimensions={0} | all-to-all | bytes 3145728 | tf_op jit(solution)/shard_map/all_to_all | solution.py:244
  (65 shorter events, 13.2 us)
Async XLA Ops:
  0.0 5.8 %copy-start.12 = (bf16[1,8,1,3,128,128]{5,4,3,2,1,0:T(8,128)(2,1)S(1)}, bf16[1,8,1,3,128,128]{5,4,3,2,1,0:T(8,128)(2,1)}, u32[]{:S(2)}) copy-start(bf16[1,8,1,3,128,128]{5,4,3,2,1,0:T(8,128)(2,1)} %param.15) | copy-start | bytes 2359300
  0.0 5.8 %copy-start.14 = (s32[1,8,1,3]{1,2,3,0:T(1,128)S(1)}, s32[1,8,1,3]{1,2,3,0:T(1,128)}, u32[]{:S(2)}) copy-start(s32[1,8,1,3]{1,2,3,0:T(1,128)} %param.16) | copy-start | bytes 292
  3.0 10.0 %collective-permute-start = (bf16[1040,128]{1,0:T(8,128)(2,1)S(1)}, bf16[1040,128]{1,0:T(8,128)(2,1)S(1)}, u32[]{:S(2)}, u32[]{:S(2)}) collective-permute-start(bf16[1040,128]{1,0:T(8,128)(2,1)S(1)} %fusion.11), channel_id=1, source_target_pairs={{0,256},{256,0},{1,257},{257,1},{2,258},{258,2},{3,259},{259,3},{4... | collective-permute-start | bytes 798728 | tf_op jit(solution)/shard_map/ppermute | solution.py:191
  6.4 95.6 %copy-start.15 = (s32[8]{0:T(128)S(1)}, s32[8]{0:T(128)}, u32[]{:S(2)}) copy-start(s32[8]{0:T(128)} %constant.217.clone) | copy-start | bytes 100
  13.8 27.8 %collective-permute-start.1 = (bf16[3104,128]{1,0:T(8,128)(2,1)S(1)}, bf16[3104,128]{1,0:T(8,128)(2,1)S(1)}, u32[]{:S(2)}, u32[]{:S(2)}) collective-permute-start(bf16[3104,128]{1,0:T(8,128)(2,1)S(1)} %fusion.7.refs_7_.refs_2_), channel_id=1, source_target_pairs={{0,288},{32,64},{64,352},{96,128},{128,416},{160,192},{192,480},{2... | collective-permute-start | bytes 2383880 | tf_op jit(solution)/shard_map/ppermute | solution.py:203
  18.3 25.2 %collective-permute-start.5 = (bf16[3104,128]{1,0:T(8,128)(2,1)S(1)}, bf16[3104,128]{1,0:T(8,128)(2,1)S(1)}, u32[]{:S(2)}, u32[]{:S(2)}) collective-permute-start(bf16[3104,128]{1,0:T(8,128)(2,1)S(1)} %fusion.7.refs_7_.refs_2_), channel_id=1, source_target_pairs={{0,224},{32,256},{64,32},{96,320},{128,96},{160,384},{192,160},{22... | collective-permute-start | bytes 2383880 | tf_op jit(solution)/shard_map/ppermute | solution.py:204
  41.5 32.1 %collective-permute-start.2 = (bf16[3104,128]{1,0:T(8,128)(2,1)S(1)}, bf16[3104,128]{1,0:T(8,128)(2,1)S(1)}, u32[]{:S(2)}, u32[]{:S(2)}) collective-permute-start(bf16[3104,128]{1,0:T(8,128)(2,1)S(1)} %collective-permute-done.1.refs_8_.refs_3_), channel_id=1, source_target_pairs={{0,288},{32,64},{64,352},{96,128},{128,416},{160,192},{192,480},{2... | collective-permute-start | bytes 2383880 | tf_op jit(solution)/shard_map/ppermute | solution.py:203
  43.5 32.1 %collective-permute-start.6 = (bf16[3104,128]{1,0:T(8,128)(2,1)S(1)}, bf16[3104,128]{1,0:T(8,128)(2,1)S(1)}, u32[]{:S(2)}, u32[]{:S(2)}) collective-permute-start(bf16[3104,128]{1,0:T(8,128)(2,1)S(1)} %collective-permute-done.5.refs_9_.refs_4_), channel_id=1, source_target_pairs={{0,224},{32,256},{64,32},{96,320},{128,96},{160,384},{192,160},{22... | collective-permute-start | bytes 2383880 | tf_op jit(solution)/shard_map/ppermute | solution.py:204
  49.6 15.4 %collective-permute-start.9 = (bf16[2080,128]{1,0:T(8,128)(2,1)S(1)}, bf16[2080,128]{1,0:T(8,128)(2,1)S(1)}, u32[]{:S(2)}, u32[]{:S(2)}) collective-permute-start(bf16[2080,128]{1,0:T(8,128)(2,1)S(1)} %fusion.9.refs_0_), channel_id=1, source_target_pairs={{0,4},{4,8},{8,12},{12,16},{16,20},{20,24},{24,28},{28,0},{1,5},{5... | collective-permute-start | bytes 1597448 | tf_op jit(solution)/shard_map/ppermute | solution.py:205
  53.1 14.6 %collective-permute-start.13 = (bf16[2080,128]{1,0:T(8,128)(2,1)S(1)}, bf16[2080,128]{1,0:T(8,128)(2,1)S(1)}, u32[]{:S(2)}, u32[]{:S(2)}) collective-permute-start(bf16[2080,128]{1,0:T(8,128)(2,1)S(1)} %fusion.9.refs_0_), channel_id=1, source_target_pairs={{0,28},{4,0},{8,4},{12,8},{16,12},{20,16},{24,20},{28,24},{1,29},{... | collective-permute-start | bytes 1597448 | tf_op jit(solution)/shard_map/ppermute | solution.py:206
  65.0 16.7 %collective-permute-start.10 = (bf16[2080,128]{1,0:T(8,128)(2,1)S(1)}, bf16[2080,128]{1,0:T(8,128)(2,1)}, u32[]{:S(2)}, u32[]{:S(2)}) collective-permute-start(bf16[2080,128]{1,0:T(8,128)(2,1)S(1)} %collective-permute-done.9.refs_1_), channel_id=1, source_target_pairs={{0,4},{4,8},{8,12},{12,16},{16,20},{20,24},{24,28},{28,0},{1,5},{5... | collective-permute-start | bytes 1597448 | tf_op jit(solution)/shard_map/ppermute | solution.py:205
  66.9 0.8 copy-start.8
  67.7 15.9 %collective-permute-start.14 = (bf16[2080,128]{1,0:T(8,128)(2,1)S(1)}, bf16[2080,128]{1,0:T(8,128)(2,1)}, u32[]{:S(2)}, u32[]{:S(2)}) collective-permute-start(bf16[2080,128]{1,0:T(8,128)(2,1)S(1)} %collective-permute-done.13.refs_2_), channel_id=1, source_target_pairs={{0,28},{4,0},{8,4},{12,8},{16,12},{20,16},{24,20},{28,24},{1,29},{... | collective-permute-start | bytes 1597448 | tf_op jit(solution)/shard_map/ppermute | solution.py:206
  72.9 0.8 copy-start.10
  73.7 19.3 %collective-permute-start.3 = (bf16[3104,128]{1,0:T(8,128)(2,1)S(1)}, bf16[3104,128]{1,0:T(8,128)(2,1)S(1)}, u32[]{:S(2)}, u32[]{:S(2)}) collective-permute-start(bf16[3104,128]{1,0:T(8,128)(2,1)S(1)} %collective-permute-done.2.refs_10_.refs_5_), channel_id=1, source_target_pairs={{0,288},{32,64},{64,352},{96,128},{128,416},{160,192},{192,480},{2... | collective-permute-start | bytes 2383880 | tf_op jit(solution)/shard_map/ppermute | solution.py:203
  75.6 20.1 %collective-permute-start.7 = (bf16[3104,128]{1,0:T(8,128)(2,1)S(1)}, bf16[3104,128]{1,0:T(8,128)(2,1)S(1)}, u32[]{:S(2)}, u32[]{:S(2)}) collective-permute-start(bf16[3104,128]{1,0:T(8,128)(2,1)S(1)} %collective-permute-done.6.refs_11_.refs_6_), channel_id=1, source_target_pairs={{0,224},{32,256},{64,32},{96,320},{128,96},{160,384},{192,160},{22... | collective-permute-start | bytes 2383880 | tf_op jit(solution)/shard_map/ppermute | solution.py:204
  80.7 0.9 copy-start
  81.7 20.4 %collective-permute-start.11 = (bf16[2080,128]{1,0:T(8,128)(2,1)}, bf16[2080,128]{1,0:T(8,128)(2,1)}, u32[]{:S(2)}, u32[]{:S(2)}) collective-permute-start(bf16[2080,128]{1,0:T(8,128)(2,1)} %collective-permute-done.10.refs_3_), channel_id=1, source_target_pairs={{0,4},{4,8},{8,12},{12,16},{16,20},{20,24},{24,28},{28,0},{1,5},{5... | collective-permute-start | bytes 1597448 | tf_op jit(solution)/shard_map/ppermute | solution.py:205
  83.6 22.0 %collective-permute-start.15 = (bf16[2080,128]{1,0:T(8,128)(2,1)}, bf16[2080,128]{1,0:T(8,128)(2,1)}, u32[]{:S(2)}, u32[]{:S(2)}) collective-permute-start(bf16[2080,128]{1,0:T(8,128)(2,1)} %collective-permute-done.14.refs_4_), channel_id=1, source_target_pairs={{0,28},{4,0},{8,4},{12,8},{16,12},{20,16},{24,20},{28,24},{1,29},{... | collective-permute-start | bytes 1597448 | tf_op jit(solution)/shard_map/ppermute | solution.py:206
  92.9 2.8 %copy-start.4 = (bf16[3104,128]{1,0:T(8,128)(2,1)}, bf16[3104,128]{1,0:T(8,128)(2,1)S(1)}, u32[]{:S(2)}) copy-start(bf16[3104,128]{1,0:T(8,128)(2,1)S(1)} %collective-permute-done.3.refs_7_) | copy-start | bytes 2383876
  93.8 34.5 %collective-permute-start.4 = (bf16[1552,128]{1,0:T(8,128)(2,1)}, bf16[1552,128]{1,0:T(8,128)(2,1)}, u32[]{:S(2)}, u32[]{:S(2)}) collective-permute-start(bf16[1552,128]{1,0:T(8,128)(2,1)} %slice.116), channel_id=1, source_target_pairs={{0,288},{32,64},{64,352},{96,128},{128,416},{160,192},{192,480},{2... | collective-permute-start | bytes 1191944 | tf_op jit(solution)/shard_map/ppermute | solution.py:214
  95.8 1.1 copy-start.6
  96.8 31.5 %collective-permute-start.8 = (bf16[1552,128]{1,0:T(8,128)(2,1)}, bf16[1552,128]{1,0:T(8,128)(2,1)}, u32[]{:S(2)}, u32[]{:S(2)}) collective-permute-start(bf16[1552,128]{1,0:T(8,128)(2,1)} %slice.117), channel_id=1, source_target_pairs={{0,224},{32,256},{64,32},{96,320},{128,96},{160,384},{192,160},{22... | collective-permute-start | bytes 1191944 | tf_op jit(solution)/shard_map/ppermute | solution.py:215
  103.7 20.2 %collective-permute-start.12 = (bf16[1040,128]{1,0:T(8,128)(2,1)}, bf16[1040,128]{1,0:T(8,128)(2,1)S(1)}, u32[]{:S(2)}, u32[]{:S(2)}) collective-permute-start(bf16[1040,128]{1,0:T(8,128)(2,1)} %slice.118), channel_id=1, source_target_pairs={{0,4},{4,8},{8,12},{12,16},{16,20},{20,24},{24,28},{28,0},{1,5},{5... | collective-permute-start | bytes 798728 | tf_op jit(solution)/shard_map/ppermute | solution.py:210
  107.3 16.6 %collective-permute-start.16 = (bf16[1040,128]{1,0:T(8,128)(2,1)}, bf16[1040,128]{1,0:T(8,128)(2,1)}, u32[]{:S(2)}, u32[]{:S(2)}) collective-permute-start(bf16[1040,128]{1,0:T(8,128)(2,1)} %slice.119), channel_id=1, source_target_pairs={{0,28},{4,0},{8,4},{12,8},{16,12},{20,16},{24,20},{28,24},{1,29},{... | collective-permute-start | bytes 798728 | tf_op jit(solution)/shard_map/ppermute | solution.py:211
  113.7 1.1 copy-start.1
  114.9 1.0 copy-start.3
  115.9 1.0 copy-start.9
  117.0 1.0 copy-start.11
  118.0 5.9 %copy-start.5 = (bf16[3104,128]{1,0:T(8,128)(2,1)S(1)}, bf16[3104,128]{1,0:T(8,128)(2,1)}, u32[]{:S(2)}) copy-start(bf16[3104,128]{1,0:T(8,128)(2,1)} %copy-done.4) | copy-start | bytes 2383876
  118.0 6.0 %copy-start.7 = (bf16[3104,128]{1,0:T(8,128)(2,1)S(1)}, bf16[3104,128]{1,0:T(8,128)(2,1)}, u32[]{:S(2)}) copy-start(bf16[3104,128]{1,0:T(8,128)(2,1)} %copy-done.6) | copy-start | bytes 2383876
  131.8 5.3 %collective-permute-start.17 = (f32[4,128,768]{2,1,0:T(8,128)S(1)}, f32[4,128,768]{2,1,0:T(8,128)S(1)}, u32[]{:S(2)}, u32[]{:S(2)}) collective-permute-start(f32[4,128,768]{2,1,0:T(8,128)S(1)} %slice.121), channel_id=1, source_target_pairs={{0,1},{1,0},{2,3},{3,2},{4,5},{5,4},{6,7},{7,6},{8,9},{9,8},{10,11... | collective-permute-start | bytes 4718600 | tf_op jit(solution)/shard_map/ppermute | solution.py:242
  (2 other events, 1.5 us)

commit v4 on v3

v4 whole, which is shorter than its diff:
```python
import jax
import jax.numpy as jnp
from jax import lax
from jax.experimental import pallas as pl
from jax.experimental.pallas import tpu as pltpu
from jax.sharding import PartitionSpec as P

BR = 4
EB = 3
W = 128
NZ = 8
NY = 8
GROUP = 8
HALF = GROUP // 2
PAD = 16
LPART = GROUP * W + PAD
RPART = HALF * EB * W + PAD
CELL = 6 * W
VMEM_LIMIT = 8 * 2**20


def zig(z):
    return ((z + 1) // 2) % 2


def ring_pairs(step):
    pairs = []
    for x_lo in range(2):
        for z in range(NZ):
            to = (z + step) % NZ
            pairs.append((x_lo * NZ + z, (x_lo ^ zig(z) ^ zig(to)) * NZ + to))
    return pairs


def turn(step):
    return [(y, (y + step) % NY) for y in range(NY)]


def with_index(blocks, index):
    flat = blocks.reshape(-1, W)
    row = jnp.zeros((PAD, W), flat.dtype)
    row = row.at[0, : index.size].set(index.reshape(-1).astype(flat.dtype))
    return jnp.concatenate([flat, row], axis=0)


def load_index(meta, left, right, slots, chunks, idx_v, idx_s, sem):
    core, x_lo = meta[0], meta[1]

    def first(ref_rows):
        return ref_rows.astype(jnp.float32)[0:1].astype(jnp.int32)

    for slot in range(slots):
        for p in range(2):
            rho = first(left[slot, pl.ds(p * LPART + GROUP * W, PAD), :])
            tile = x_lo if p == 0 else 1 - x_lo
            place = ((rho & 1) ^ core) * 4 + tile * 2 + (rho >> 1)
            idx_v[pl.ds(slot * 2 + p, 1), :] = place
    for c in range(chunks):
        for h in range(2):
            row = first(right[c, pl.ds(h * RPART + HALF * EB * W, PAD), :])
            idx_v[pl.ds(2 * NY + 2 * c + h, 1), :] = row
    copy = pltpu.make_async_copy(idx_v, idx_s, sem)
    copy.start()
    copy.wait()


def add_chunk(left, right, acc, idx_s, c, slot):
    for k in range(GROUP):
        half, j = k // HALF, k % HALF
        both = jnp.concatenate(
            [left[slot, pl.ds(p * LPART + k * W, W), :] for p in range(2)], axis=0
        )
        wide = jnp.concatenate(
            [right[c, pl.ds(half * RPART + (j * EB + e) * W, W), :] for e in range(EB)], axis=1
        )
        part = jnp.dot(both, wide, preferred_element_type=jnp.float32)
        for e in range(EB):
            cell = idx_s[2 * NY + 2 * c + half, j * EB + e]
            lanes = pl.ds(pl.multiple_of(cell * W, W), W)
            for p in range(2):
                at = idx_s[slot * 2 + p, k]
                acc[at, :, lanes] += part[p * W : (p + 1) * W, e * W : (e + 1) * W]


def stage(number, new_left, new_right, slots, chunks, meta, *refs):
    n, m = len(new_left), len(new_right)
    arrived = refs[: n + m]
    acc, left, right, token, idx_v, idx_s, sem, sems = refs[-8:]
    token[...] = jnp.zeros_like(token)
    targets = [left.at[at, pl.ds(start, size)] for at, start, size in new_left]
    targets += [right.at[at, pl.ds(start, size)] for at, start, size in new_right]
    copies = [
        pltpu.make_async_copy(ref, target, sems.at[i])
        for i, (ref, target) in enumerate(zip(arrived, targets))
    ]
    for copy in copies:
        copy.start()
    if number == 1:
        acc[...] = jnp.zeros_like(acc)
    for copy in copies:
        copy.wait()
    load_index(meta, left, right, slots, chunks, idx_v, idx_s, sem)

    def body(c, carry):
        @pl.when(meta[10 + c] == number)
        def _():
            add_chunk(left, right, acc, idx_s, c, meta[2 + c])

        return carry

    lax.fori_loop(0, chunks, body, 0)


def run_stage(number, meta, lefts, rights, slots, chunks, state, *after):
    new_left = [(at, start, ref.shape[0]) for at, start, ref in lefts]
    new_right = [(at, start, ref.shape[0]) for at, start, ref in rights]
    operands = [ref for _, _, ref in lefts + rights]
    n = len(operands)
    smem = pl.BlockSpec(memory_space=pltpu.SMEM)
    vmem = pl.BlockSpec(memory_space=pltpu.VMEM)
    far_off = pl.BlockSpec(memory_space=pl.ANY)
    return pl.pallas_call(
        lambda *refs: stage(number, new_left, new_right, slots, chunks, *refs),
        out_shape=[
            jax.ShapeDtypeStruct((8, W, CELL), jnp.float32),
            jax.ShapeDtypeStruct((NY, 2 * LPART, W), jnp.bfloat16),
            jax.ShapeDtypeStruct((NZ, 2 * RPART, W), jnp.bfloat16),
            jax.ShapeDtypeStruct((8, W), jnp.int32),
        ],
        in_specs=[smem] + [far_off] * n + [vmem] * len(state) + [far_off] * len(after),
        out_specs=[vmem] * 4,
        input_output_aliases={1 + n + i: i for i in range(len(state))},
        scratch_shapes=[
            pltpu.VMEM((4 * NY, W), jnp.int32),
            pltpu.SMEM((4 * NY, W), jnp.int32),
            pltpu.SemaphoreType.DMA,
            pltpu.SemaphoreType.DMA((8,)),
        ],
        compiler_params=pltpu.CompilerParams(vmem_limit_bytes=VMEM_LIMIT),
        cost_estimate=pl.CostEstimate(
            flops=8 * 48 * W**3, bytes_accessed=2**20, transcendentals=0
        ),
    )(meta, *operands, *state, *after)


def per_device(left_blocks, left_rows, right_blocks, right_cols):
    x_lo = lax.axis_index("x_lo")
    z = lax.axis_index("z")
    y = lax.axis_index("y")
    core = lax.axis_index("core")
    side = x_lo ^ zig(z)

    left = left_blocks.reshape(2, GROUP * W, W)
    rows = left_rows.reshape(2, GROUP)
    own = (side + y // 4 + y % 4) % 2

    def group(which):
        return with_index(
            lax.dynamic_index_in_dim(left, which, 0, False),
            lax.dynamic_index_in_dim(rows, which, 0, False),
        )

    swapped = lax.ppermute(group(1 - own), "x_lo", [(0, 1), (1, 0)])
    pair = jnp.concatenate([group(own), swapped], axis=0)
    right = right_blocks.reshape(2, HALF, EB * W, W)
    cols = right_cols.reshape(2, HALF * EB)
    chunk = jnp.concatenate([with_index(right[h], cols[h]) for h in range(2)], axis=0)
    first, _ = lax.optimization_barrier((chunk, swapped))

    source = (z + jnp.array([0, -1, 1, -2, 2, -3, 3, 4], jnp.int32)) % NZ
    away = (4 * (zig(source) ^ side) + source // 2 - y) % NY
    slot = jnp.where(
        away == 0, 0, jnp.where(away == 4, 7, jnp.where(away < 4, 2 * away, 15 - 2 * away))
    )
    right_at = jnp.array([1, 1, 1, 2, 2, 3, 3, 4], jnp.int32)
    left_at = jnp.where(slot < 3, 1, jnp.where(slot < 5, 2, 3))
    meta = jnp.concatenate([jnp.stack([core, x_lo]), slot, jnp.maximum(right_at, left_at)])
    meta = meta.astype(jnp.int32)

    def listed(arrays, low, high):
        return [(i, 0, arrays[i]) for i in range(low, high)]

    row = ("x_lo", "z")

    def step_z(up, down):
        return lax.ppermute(up, row, ring_pairs(1)), lax.ppermute(down, row, ring_pairs(-1))

    def step_y(fore, back):
        return lax.ppermute(fore, "y", turn(1)), lax.ppermute(back, "y", turn(-1))

    rights = [chunk, *step_z(first, first)]
    lefts = [pair, *step_y(pair, pair)]
    rights += step_z(*rights[1:3])
    lefts += step_y(*lefts[1:3])
    *state, token = run_stage(1, meta, listed(lefts, 0, 3), listed(rights, 0, 3), 3, 3, [])
    up, down, token = lax.optimization_barrier((*rights[3:5], token))
    rights += step_z(up, down)
    lefts += step_y(*lefts[3:5])
    *state, token = run_stage(2, meta, listed(lefts, 3, 5), listed(rights, 3, 5), 5, 5, state, token)
    last_left = step_y(lefts[5][:LPART], lefts[6][LPART:])
    up, down, token, *last_left = lax.optimization_barrier((*rights[5:7], token, *last_left))
    last_right = step_z(up[:RPART], down[RPART:])
    ends = [(7, 0, last_left[0]), (7, LPART, last_left[1])]
    *state, _ = run_stage(3, meta, listed(lefts, 5, 7) + ends, listed(rights, 5, 7), 8, 7, state, token)
    ends = [(7, 0, last_right[0]), (7, RPART, last_right[1])]
    acc = run_stage(4, meta, [], ends, 8, 8, state)[0]

    got = lax.ppermute(acc[4:], "core", [(0, 1), (1, 0)])
    total = acc[:4] + got
    return lax.all_to_all(total, ("x_lo", "x_hi"), 0, 0, tiled=True).sum(0)


def solution(mesh):
    split = jax.sharding.Mesh(
        mesh.devices.reshape(2, NZ, NY, 2, 2), ("x_lo", "z", "y", "x_hi", "core")
    )
    row, depth = ("x_lo", "z"), ("x_hi", "core")
    placed = (
        P(depth, "y", row, None, None, None),
        P(depth, "y", row, None),
        P(depth, row, "y", None, None, None),
        P(depth, row, "y", None),
    )
    return jax.shard_map(
        per_device,
        mesh=split,
        in_specs=placed,
        out_specs=P(row + depth, "y"),
        check_vma=False,
    )
```

time: 164 us -> 144 us (0.88)
  local copies, waits for them, and re-layouts: 15.9 us -> 2.5 us
  waiting for transfers between devices: 36.5 us -> 29.4 us
  Pallas kernels: 13.6 us -> 16.3 us
    unnamed x33 -> x9, local copies, waits for them, and re-layouts: 9.03 us -> 0.61 us
    ppermute x16, waiting for transfers between devices: 26.4 us -> 19.4 us  [the longest x4 9.13 us: step_z(): lax.ppermute(up, row, ring_pairs(1))]
    slice x4, local copies, waits for them, and re-layouts: 5.07 us -> 0.09 us  [the longest x2 0.05 us: per_device(): last_right = step_z(up[:RPART], down[RPART:])]
    pallas_call x3 -> x4, Pallas kernels: 13.6 us -> 16.3 us  [run_stage(): pl.pallas_call(lambda *refs: stage(number, new_left, new_right, slots, ch...]
  transfers between devices with their start and end apart: 18 -> 18, of which waited for: 5 -> 8; matrix products, arithmetic and copies ran while one was open for 5% -> 1% of each run, Pallas kernels for 6% -> 9%
where the time goes in v4:
time: 144 us; the launch traced here: 142 us
  starting transfers between devices  67.4 us (47%)
  waiting for transfers between devices  29.4 us (20%)
  blocking collectives  23 us (16%)
  Pallas kernels  16.3 us (11%)
  other arithmetic  2.67 us (2%)
  local copies, waits for them, and re-layouts  2.5 us (2%)
    ppermute x8, starting transfers between devices, step_y(): return (lax.ppermute(fore, 'y', turn(1)), lax.ppermute(back, 'y', turn(-1)))  28.7 us
    ppermute x4, starting transfers between devices, step_z(): lax.ppermute(down, row, ring_pairs(-1))  23.8 us
    all_to_all x1, blocking collectives, per_device(): return lax.all_to_all(total, ('x_lo', 'x_hi'), 0, 0, tiled=True).sum(0)  23 us
    pallas_call x4, Pallas kernels, run_stage(): pl.pallas_call(lambda *refs: stage(number, new_left, new_right, slots, ch...  16.3 us
    ppermute x4, starting transfers between devices, step_z(): lax.ppermute(up, row, ring_pairs(1))  10.3 us
    ppermute x4, waiting for transfers between devices, step_z(): lax.ppermute(up, row, ring_pairs(1))  9.13 us
    ppermute x8, waiting for transfers between devices, step_y(): return (lax.ppermute(fore, 'y', turn(1)), lax.ppermute(back, 'y', turn(-1)))  8.37 us
    ppermute x1, waiting for transfers between devices, per_device(): swapped = lax.ppermute(group(1 - own), 'x_lo', [(0, 1), (1, 0)])  6.64 us
  transfers between devices with their start and end apart: 18, of which 8 were waited for; matrix products, arithmetic and copies ran while one was open for 1% of the time, Pallas kernels for 9%

profile of v4, /device:TPU:6, one launch (start us, length us, event | category | flops | bytes accessed | tf_op | source)
XLA Modules:
  0.0 141.6 jit_solution(16252864677243189351)
XLA Ops:
  0.6 1.4 reduce.11
  2.0 1.1 dynamic-slice_bitcast_fusion
  3.2 2.7 %collective-permute-start = (bf16[1040,128]{1,0:T(8,128)(2,1)S(1)}, bf16[1040,128]{1,0:T(8,128)(2,1)S(1)}, u32[]{:S(2)}, u32[]{:S(2)}) collective-permute-start(bf16[1040,128]{1,0:T(8,128)(2,1)S(1)} %fusion.11), channel_id=1, source_target_pairs={{0,256},{256,0},{1,257},{257,1},{2,258},{258,2},{3,259},{259,3},{4... | collective-permute-start | bytes 798728 | tf_op jit(solution)/shard_map/ppermute | solution.py:163
  6.5 6.6 %collective-permute-done = bf16[1040,128]{1,0:T(8,128)(2,1)S(1)} collective-permute-done((bf16[1040,128]{1,0:T(8,128)(2,1)S(1)}, bf16[1040,128]{1,0:T(8,128)(2,1)S(1)}, u32[]{:S(2)}, u32[]{:S(2)}) %collective-permute-start) | collective-permute-done | bytes 266272 | tf_op jit(solution)/shard_map/ppermute | solution.py:163
  13.2 4.5 %collective-permute-start.1 = (bf16[3104,128]{1,0:T(8,128)(2,1)S(1)}, bf16[3104,128]{1,0:T(8,128)(2,1)S(1)}, u32[]{:S(2)}, u32[]{:S(2)}) collective-permute-start(bf16[3104,128]{1,0:T(8,128)(2,1)S(1)} %fusion.7.refs_4_), channel_id=1, source_target_pairs={{0,288},{32,64},{64,352},{96,128},{128,416},{160,192},{192,480},{2... | collective-permute-start | bytes 2383880 | tf_op jit(solution)/shard_map/ppermute | solution.py:186
  17.7 8.3 %collective-permute-start.3 = (bf16[3104,128]{1,0:T(8,128)(2,1)S(1)}, bf16[3104,128]{1,0:T(8,128)(2,1)S(1)}, u32[]{:S(2)}, u32[]{:S(2)}) collective-permute-start(bf16[3104,128]{1,0:T(8,128)(2,1)S(1)} %fusion.7.refs_4_), channel_id=1, source_target_pairs={{0,224},{32,256},{64,32},{96,320},{128,96},{160,384},{192,160},{22... | collective-permute-start | bytes 2383880 | tf_op jit(solution)/shard_map/ppermute | solution.py:186
  26.1 3.5 %collective-permute-start.5 = (bf16[2080,128]{1,0:T(8,128)(2,1)S(1)}, bf16[2080,128]{1,0:T(8,128)(2,1)}, u32[]{:S(2)}, u32[]{:S(2)}) collective-permute-start(bf16[2080,128]{1,0:T(8,128)(2,1)S(1)} %fusion.9.refs_1_), channel_id=1, source_target_pairs={{0,4},{4,8},{8,12},{12,16},{16,20},{20,24},{24,28},{28,0},{1,5},{5... | collective-permute-start | bytes 1597448 | tf_op jit(solution)/shard_map/ppermute | solution.py:189
  29.6 3.8 %collective-permute-start.6 = (bf16[2080,128]{1,0:T(8,128)(2,1)S(1)}, bf16[2080,128]{1,0:T(8,128)(2,1)}, u32[]{:S(2)}, u32[]{:S(2)}) collective-permute-start(bf16[2080,128]{1,0:T(8,128)(2,1)S(1)} %fusion.9.refs_1_), channel_id=1, source_target_pairs={{0,28},{4,0},{8,4},{12,8},{16,12},{20,16},{24,20},{28,24},{1,29},{... | collective-permute-start | bytes 1597448 | tf_op jit(solution)/shard_map/ppermute | solution.py:189
  33.4 7.5 %collective-permute-done.1.refs_5_ = bf16[3104,128]{1,0:T(8,128)(2,1)S(1)} collective-permute-done((bf16[3104,128]{1,0:T(8,128)(2,1)S(1)}, bf16[3104,128]{1,0:T(8,128)(2,1)S(1)}, u32[]{:S(2)}, u32[]{:S(2)}) %collective-permute-start.1) | collective-permute-done | bytes 794656 | tf_op jit(solution)/shard_map/ppermute | solution.py:186
  41.0 1.9 %collective-permute-start.2 = (bf16[3104,128]{1,0:T(8,128)(2,1)S(1)}, bf16[3104,128]{1,0:T(8,128)(2,1)}, u32[]{:S(2)}, u32[]{:S(2)}) collective-permute-start(bf16[3104,128]{1,0:T(8,128)(2,1)S(1)} %collective-permute-done.1.refs_5_), channel_id=1, source_target_pairs={{0,288},{32,64},{64,352},{96,128},{128,416},{160,192},{192,480},{2... | collective-permute-start | bytes 2383880 | tf_op jit(solution)/shard_map/ppermute | solution.py:186
  42.9 5.1 %collective-permute-start.4 = (bf16[3104,128]{1,0:T(8,128)(2,1)S(1)}, bf16[3104,128]{1,0:T(8,128)(2,1)}, u32[]{:S(2)}, u32[]{:S(2)}) collective-permute-start(bf16[3104,128]{1,0:T(8,128)(2,1)S(1)} %collective-permute-done.3.refs_6_), channel_id=1, source_target_pairs={{0,224},{32,256},{64,32},{96,320},{128,96},{160,384},{192,160},{22... | collective-permute-start | bytes 2383880 | tf_op jit(solution)/shard_map/ppermute | solution.py:186
  48.0 3.5 %collective-permute-start.9 = (bf16[2080,128]{1,0:T(8,128)(2,1)}, bf16[2080,128]{1,0:T(8,128)(2,1)S(1)}, u32[]{:S(2)}, u32[]{:S(2)}) collective-permute-start(bf16[2080,128]{1,0:T(8,128)(2,1)} %collective-permute-done.5.refs_2_), channel_id=1, source_target_pairs={{0,4},{4,8},{8,12},{12,16},{16,20},{20,24},{24,28},{28,0},{1,5},{5... | collective-permute-start | bytes 1597448 | tf_op jit(solution)/shard_map/ppermute | solution.py:189
  51.5 3.8 %collective-permute-start.10 = (bf16[2080,128]{1,0:T(8,128)(2,1)}, bf16[2080,128]{1,0:T(8,128)(2,1)}, u32[]{:S(2)}, u32[]{:S(2)}) collective-permute-start(bf16[2080,128]{1,0:T(8,128)(2,1)} %collective-permute-done.6.refs_3_), channel_id=1, source_target_pairs={{0,28},{4,0},{8,4},{12,8},{16,12},{20,16},{24,20},{28,24},{1,29},{... | collective-permute-start | bytes 1597448 | tf_op jit(solution)/shard_map/ppermute | solution.py:189
  55.5 8.2 %collective-permute-done.9.refs_1_ = bf16[2080,128]{1,0:T(8,128)(2,1)S(1)} collective-permute-done((bf16[2080,128]{1,0:T(8,128)(2,1)}, bf16[2080,128]{1,0:T(8,128)(2,1)S(1)}, u32[]{:S(2)}, u32[]{:S(2)}) %collective-permute-start.9) | collective-permute-done | bytes 532512 | tf_op jit(solution)/shard_map/ppermute | solution.py:189
  63.8 1.9 %collective-permute-start.11 = (bf16[2080,128]{1,0:T(8,128)(2,1)S(1)}, bf16[2080,128]{1,0:T(8,128)(2,1)S(1)}, u32[]{:S(2)}, u32[]{:S(2)}) collective-permute-start(bf16[2080,128]{1,0:T(8,128)(2,1)S(1)} %collective-permute-done.9.refs_1_), channel_id=1, source_target_pairs={{0,4},{4,8},{8,12},{12,16},{16,20},{20,24},{24,28},{28,0},{1,5},{5... | collective-permute-start | bytes 1597448 | tf_op jit(solution)/shard_map/ppermute | solution.py:189
  65.7 5.1 %collective-permute-start.13 = (bf16[2080,128]{1,0:T(8,128)(2,1)}, bf16[2080,128]{1,0:T(8,128)(2,1)S(1)}, u32[]{:S(2)}, u32[]{:S(2)}) collective-permute-start(bf16[2080,128]{1,0:T(8,128)(2,1)} %collective-permute-done.10.refs_2_), channel_id=1, source_target_pairs={{0,28},{4,0},{8,4},{12,8},{16,12},{20,16},{24,20},{28,24},{1,29},{... | collective-permute-start | bytes 1597448 | tf_op jit(solution)/shard_map/ppermute | solution.py:189
  70.8 4.1 %shard_map.64 = (f32[8,128,768]{2,1,0:T(8,128)S(1)}, bf16[8,2080,128]{2,1,0:T(8,128)(2,1)S(1)}, bf16[8,3104,128]{2,1,0:T(8,128)(2,1)S(1)}, s32[8,128]{1,0:T(8,128)S(1)}) custom-call(s32[18]{0:T(128)S(1)} %pad_add_fusion.refs_0_, bf16[2080,128]{1,0:T(8,128)(2,1)S(1)} %fusion.9.refs_1_, bf16[2080,128]{1,0:T(8,128)(2,1)} %collective-permute-done.5.refs_2_, ...), custom_call_target="tpu_custom_call" | custom-call | flops 805306368 | bytes 1048576 | tf_op jit(solution)/shard_map/pallas_call | solution.py:122
  75.0 1.9 %collective-permute-start.7 = (bf16[3104,128]{1,0:T(8,128)(2,1)}, bf16[3104,128]{1,0:T(8,128)(2,1)S(1)}, u32[]{:S(2)}, u32[]{:S(2)}) collective-permute-start(bf16[3104,128]{1,0:T(8,128)(2,1)} %collective-permute-done.2.refs_3_), channel_id=1, source_target_pairs={{0,288},{32,64},{64,352},{96,128},{128,416},{160,192},{192,480},{2... | collective-permute-start | bytes 2383880 | tf_op jit(solution)/shard_map/ppermute | solution.py:186
  76.9 5.1 %collective-permute-start.8 = (bf16[3104,128]{1,0:T(8,128)(2,1)}, bf16[3104,128]{1,0:T(8,128)(2,1)S(1)}, u32[]{:S(2)}, u32[]{:S(2)}) collective-permute-start(bf16[3104,128]{1,0:T(8,128)(2,1)} %collective-permute-done.4.refs_4_), channel_id=1, source_target_pairs={{0,224},{32,256},{64,32},{96,320},{128,96},{160,384},{192,160},{22... | collective-permute-start | bytes 2383880 | tf_op jit(solution)/shard_map/ppermute | solution.py:186
  82.1 1.9 %collective-permute-start.12 = (bf16[1040,128]{1,0:T(8,128)(2,1)S(1)}, bf16[1040,128]{1,0:T(8,128)(2,1)S(1)}, u32[]{:S(2)}, u32[]{:S(2)}) collective-permute-start(bf16[1040,128]{1,0:T(8,128)(2,1)S(1)} %slice.112), channel_id=1, source_target_pairs={{0,4},{4,8},{8,12},{12,16},{16,20},{20,24},{24,28},{28,0},{1,5},{5... | collective-permute-start | bytes 798728 | tf_op jit(solution)/shard_map/ppermute | solution.py:189
  84.0 5.1 %collective-permute-start.14 = (bf16[1040,128]{1,0:T(8,128)(2,1)S(1)}, bf16[1040,128]{1,0:T(8,128)(2,1)S(1)}, u32[]{:S(2)}, u32[]{:S(2)}) collective-permute-start(bf16[1040,128]{1,0:T(8,128)(2,1)S(1)} %slice.113), channel_id=1, source_target_pairs={{0,28},{4,0},{8,4},{12,8},{16,12},{20,16},{24,20},{28,24},{1,29},{... | collective-permute-start | bytes 798728 | tf_op jit(solution)/shard_map/ppermute | solution.py:189
  89.2 3.8 %shard_map.65 = (f32[8,128,768]{2,1,0:T(8,128)S(1)}, bf16[8,2080,128]{2,1,0:T(8,128)(2,1)S(1)}, bf16[8,3104,128]{2,1,0:T(8,128)(2,1)S(1)}, s32[8,128]{1,0:T(8,128)S(1)}) custom-call(s32[18]{0:T(128)S(1)} %pad_add_fusion.refs_0_, bf16[2080,128]{1,0:T(8,128)(2,1)S(1)} %collective-permute-done.9.refs_1_, ...), custom_call_target="tpu_custom_call", output_to_operand_aliasing={{0}: (5, {}), {1}: (6, {}), {2}: (7, {})} | custom-call | flops 805306368 | bytes 1048576 | tf_op jit(solution)/shard_map/pallas_call | solution.py:122
  93.1 1.6 %collective-permute-done.7.refs_5_ = bf16[3104,128]{1,0:T(8,128)(2,1)S(1)} collective-permute-done((bf16[3104,128]{1,0:T(8,128)(2,1)}, bf16[3104,128]{1,0:T(8,128)(2,1)S(1)}, u32[]{:S(2)}, u32[]{:S(2)}) %collective-permute-start.7) | collective-permute-done | bytes 794656 | tf_op jit(solution)/shard_map/ppermute | solution.py:186
  94.7 1.6 %collective-permute-done.8.refs_6_ = bf16[3104,128]{1,0:T(8,128)(2,1)S(1)} collective-permute-done((bf16[3104,128]{1,0:T(8,128)(2,1)}, bf16[3104,128]{1,0:T(8,128)(2,1)S(1)}, u32[]{:S(2)}, u32[]{:S(2)}) %collective-permute-start.8) | collective-permute-done | bytes 794656 | tf_op jit(solution)/shard_map/ppermute | solution.py:186
  96.3 1.9 %collective-permute-start.15 = (bf16[1552,128]{1,0:T(8,128)(2,1)S(1)}, bf16[1552,128]{1,0:T(8,128)(2,1)S(1)}, u32[]{:S(2)}, u32[]{:S(2)}) collective-permute-start(bf16[1552,128]{1,0:T(8,128)(2,1)S(1)} %slice.106), channel_id=1, source_target_pairs={{0,288},{32,64},{64,352},{96,128},{128,416},{160,192},{192,480},{2... | collective-permute-start | bytes 1191944 | tf_op jit(solution)/shard_map/ppermute | solution.py:186
  98.3 5.2 %collective-permute-start.16 = (bf16[1552,128]{1,0:T(8,128)(2,1)S(1)}, bf16[1552,128]{1,0:T(8,128)(2,1)S(1)}, u32[]{:S(2)}, u32[]{:S(2)}) collective-permute-start(bf16[1552,128]{1,0:T(8,128)(2,1)S(1)} %slice.107), channel_id=1, source_target_pairs={{0,224},{32,256},{64,32},{96,320},{128,96},{160,384},{192,160},{22... | collective-permute-start | bytes 1191944 | tf_op jit(solution)/shard_map/ppermute | solution.py:186
  103.5 5.2 %shard_map.66 = (f32[8,128,768]{2,1,0:T(8,128)S(1)}, bf16[8,2080,128]{2,1,0:T(8,128)(2,1)S(1)}, bf16[8,3104,128]{2,1,0:T(8,128)(2,1)S(1)}, s32[8,128]{1,0:T(8,128)}) custom-call(s32[18]{0:T(128)S(1)} %pad_add_fusion.refs_0_, bf16[2080,128]{1,0:T(8,128)(2,1)S(1)} %collective-permute-done.11.refs_1_, ...), custom_call_target="tpu_custom_call", output_to_operand_aliasing={{0}: (7, {}), {1}: (8, {}), {2}: (9, {})} | custom-call | flops 805306368 | bytes 1048576 | tf_op jit(solution)/shard_map/pallas_call | solution.py:122
  108.9 3.2 %shard_map.67 = (f32[8,128,768]{2,1,0:T(8,128)S(1)}, bf16[8,2080,128]{2,1,0:T(8,128)(2,1)S(1)}, bf16[8,3104,128]{2,1,0:T(8,128)(2,1)S(1)}, s32[8,128]{1,0:T(8,128)}) custom-call(s32[18]{0:T(128)S(1)} %pad_add_fusion.refs_0_, bf16[1552,128]{1,0:T(8,128)(2,1)S(1)} %collective-permute-done.15.refs_1_, ...), custom_call_target="tpu_custom_call", output_to_operand_aliasing={{0}: (3, {}), {1}: (4, {}), {2}: (5, {})} | custom-call | flops 805306368 | bytes 1048576 | tf_op jit(solution)/shard_map/pallas_call | solution.py:122
  112.3 1.9 %collective-permute-start.17 = (f32[4,128,768]{2,1,0:T(8,128)S(1)}, f32[4,128,768]{2,1,0:T(8,128)S(1)}, u32[]{:S(2)}, u32[]{:S(2)}) collective-permute-start(f32[4,128,768]{2,1,0:T(8,128)S(1)} %slice.109), channel_id=1, source_target_pairs={{0,1},{1,0},{2,3},{3,2},{4,5},{5,4},{6,7},{7,6},{8,9},{9,8},{10,11... | collective-permute-start | bytes 4718600 | tf_op jit(solution)/shard_map/ppermute | solution.py:208
  114.2 3.4 %collective-permute-done.17 = f32[4,128,768]{2,1,0:T(8,128)S(1)} collective-permute-done((f32[4,128,768]{2,1,0:T(8,128)S(1)}, f32[4,128,768]{2,1,0:T(8,128)S(1)}, u32[]{:S(2)}, u32[]{:S(2)}) %collective-permute-start.17) | collective-permute-done | bytes 1572896 | tf_op jit(solution)/shard_map/ppermute | solution.py:208
  117.8 23.0 %all_to_all.5 = f32[4,128,768]{2,1,0:T(8,128)S(1)} all-to-all(f32[4,128,768]{2,1,0:T(8,128)S(1)} %slice_add_fusion), channel_id=1, replica_groups=mesh['x_lo'=2,'z'=8,'y'=8,'x_hi'=2,'core'=2] {'x_lo','x_hi'}, dimensions={0} | all-to-all | bytes 3145728 | tf_op jit(solution)/shard_map/all_to_all | solution.py:210
  140.7 0.9 reduce_sum.9
  (41 shorter events, 2.3 us)
Async XLA Ops:
  0.0 5.9 %copy-start = (bf16[1,8,1,3,128,128]{5,4,3,2,1,0:T(8,128)(2,1)S(1)}, bf16[1,8,1,3,128,128]{5,4,3,2,1,0:T(8,128)(2,1)}, u32[]{:S(2)}) copy-start(bf16[1,8,1,3,128,128]{5,4,3,2,1,0:T(8,128)(2,1)} %param.16) | copy-start | bytes 2359300
  0.0 6.0 %copy-start.1 = (s32[1,8,1,3]{1,2,3,0:T(1,128)S(1)}, s32[1,8,1,3]{1,2,3,0:T(1,128)}, u32[]{:S(2)}) copy-start(s32[1,8,1,3]{1,2,3,0:T(1,128)} %param.17) | copy-start | bytes 292
  3.2 10.0 %collective-permute-start = (bf16[1040,128]{1,0:T(8,128)(2,1)S(1)}, bf16[1040,128]{1,0:T(8,128)(2,1)S(1)}, u32[]{:S(2)}, u32[]{:S(2)}) collective-permute-start(bf16[1040,128]{1,0:T(8,128)(2,1)S(1)} %fusion.11), channel_id=1, source_target_pairs={{0,256},{256,0},{1,257},{257,1},{2,258},{258,2},{3,259},{259,3},{4... | collective-permute-start | bytes 798728 | tf_op jit(solution)/shard_map/ppermute | solution.py:163
  6.0 49.4 %copy-start.2 = (s32[8]{0:T(128)S(1)}, s32[8]{0:T(128)}, u32[]{:S(2)}) copy-start(s32[8]{0:T(128)} %constant.220.clone) | copy-start | bytes 100
  6.0 49.4 %copy-start.3 = (s32[8]{0:T(128)S(1)}, s32[8]{0:T(128)}, u32[]{:S(2)}) copy-start(s32[8]{0:T(128)} %constant.221.clone) | copy-start | bytes 100
  13.2 27.8 %collective-permute-start.1 = (bf16[3104,128]{1,0:T(8,128)(2,1)S(1)}, bf16[3104,128]{1,0:T(8,128)(2,1)S(1)}, u32[]{:S(2)}, u32[]{:S(2)}) collective-permute-start(bf16[3104,128]{1,0:T(8,128)(2,1)S(1)} %fusion.7.refs_4_), channel_id=1, source_target_pairs={{0,288},{32,64},{64,352},{96,128},{128,416},{160,192},{192,480},{2... | collective-permute-start | bytes 2383880 | tf_op jit(solution)/shard_map/ppermute | solution.py:186
  17.7 25.2 %collective-permute-start.3 = (bf16[3104,128]{1,0:T(8,128)(2,1)S(1)}, bf16[3104,128]{1,0:T(8,128)(2,1)S(1)}, u32[]{:S(2)}, u32[]{:S(2)}) collective-permute-start(bf16[3104,128]{1,0:T(8,128)(2,1)S(1)} %fusion.7.refs_4_), channel_id=1, source_target_pairs={{0,224},{32,256},{64,32},{96,320},{128,96},{160,384},{192,160},{22... | collective-permute-start | bytes 2383880 | tf_op jit(solution)/shard_map/ppermute | solution.py:186
  26.1 21.9 %collective-permute-start.5 = (bf16[2080,128]{1,0:T(8,128)(2,1)S(1)}, bf16[2080,128]{1,0:T(8,128)(2,1)}, u32[]{:S(2)}, u32[]{:S(2)}) collective-permute-start(bf16[2080,128]{1,0:T(8,128)(2,1)S(1)} %fusion.9.refs_1_), channel_id=1, source_target_pairs={{0,4},{4,8},{8,12},{12,16},{16,20},{20,24},{24,28},{28,0},{1,5},{5... | collective-permute-start | bytes 1597448 | tf_op jit(solution)/shard_map/ppermute | solution.py:189
  29.6 21.9 %collective-permute-start.6 = (bf16[2080,128]{1,0:T(8,128)(2,1)S(1)}, bf16[2080,128]{1,0:T(8,128)(2,1)}, u32[]{:S(2)}, u32[]{:S(2)}) collective-permute-start(bf16[2080,128]{1,0:T(8,128)(2,1)S(1)} %fusion.9.refs_1_), channel_id=1, source_target_pairs={{0,28},{4,0},{8,4},{12,8},{16,12},{20,16},{24,20},{28,24},{1,29},{... | collective-permute-start | bytes 1597448 | tf_op jit(solution)/shard_map/ppermute | solution.py:189
  41.0 34.0 %collective-permute-start.2 = (bf16[3104,128]{1,0:T(8,128)(2,1)S(1)}, bf16[3104,128]{1,0:T(8,128)(2,1)}, u32[]{:S(2)}, u32[]{:S(2)}) collective-permute-start(bf16[3104,128]{1,0:T(8,128)(2,1)S(1)} %collective-permute-done.1.refs_5_), channel_id=1, source_target_pairs={{0,288},{32,64},{64,352},{96,128},{128,416},{160,192},{192,480},{2... | collective-permute-start | bytes 2383880 | tf_op jit(solution)/shard_map/ppermute | solution.py:186
  42.9 32.1 %collective-permute-start.4 = (bf16[3104,128]{1,0:T(8,128)(2,1)S(1)}, bf16[3104,128]{1,0:T(8,128)(2,1)}, u32[]{:S(2)}, u32[]{:S(2)}) collective-permute-start(bf16[3104,128]{1,0:T(8,128)(2,1)S(1)} %collective-permute-done.3.refs_6_), channel_id=1, source_target_pairs={{0,224},{32,256},{64,32},{96,320},{128,96},{160,384},{192,160},{22... | collective-permute-start | bytes 2383880 | tf_op jit(solution)/shard_map/ppermute | solution.py:186
  48.0 15.7 %collective-permute-start.9 = (bf16[2080,128]{1,0:T(8,128)(2,1)}, bf16[2080,128]{1,0:T(8,128)(2,1)S(1)}, u32[]{:S(2)}, u32[]{:S(2)}) collective-permute-start(bf16[2080,128]{1,0:T(8,128)(2,1)} %collective-permute-done.5.refs_2_), channel_id=1, source_target_pairs={{0,4},{4,8},{8,12},{12,16},{16,20},{20,24},{24,28},{28,0},{1,5},{5... | collective-permute-start | bytes 1597448 | tf_op jit(solution)/shard_map/ppermute | solution.py:189
  51.5 14.1 %collective-permute-start.10 = (bf16[2080,128]{1,0:T(8,128)(2,1)}, bf16[2080,128]{1,0:T(8,128)(2,1)}, u32[]{:S(2)}, u32[]{:S(2)}) collective-permute-start(bf16[2080,128]{1,0:T(8,128)(2,1)} %collective-permute-done.6.refs_3_), channel_id=1, source_target_pairs={{0,28},{4,0},{8,4},{12,8},{16,12},{20,16},{24,20},{28,24},{1,29},{... | collective-permute-start | bytes 1597448 | tf_op jit(solution)/shard_map/ppermute | solution.py:189
  63.8 18.3 %collective-permute-start.11 = (bf16[2080,128]{1,0:T(8,128)(2,1)S(1)}, bf16[2080,128]{1,0:T(8,128)(2,1)S(1)}, u32[]{:S(2)}, u32[]{:S(2)}) collective-permute-start(bf16[2080,128]{1,0:T(8,128)(2,1)S(1)} %collective-permute-done.9.refs_1_), channel_id=1, source_target_pairs={{0,4},{4,8},{8,12},{12,16},{16,20},{20,24},{24,28},{28,0},{1,5},{5... | collective-permute-start | bytes 1597448 | tf_op jit(solution)/shard_map/ppermute | solution.py:189
  65.7 18.3 %collective-permute-start.13 = (bf16[2080,128]{1,0:T(8,128)(2,1)}, bf16[2080,128]{1,0:T(8,128)(2,1)S(1)}, u32[]{:S(2)}, u32[]{:S(2)}) collective-permute-start(bf16[2080,128]{1,0:T(8,128)(2,1)} %collective-permute-done.10.refs_2_), channel_id=1, source_target_pairs={{0,28},{4,0},{8,4},{12,8},{16,12},{20,16},{24,20},{28,24},{1,29},{... | collective-permute-start | bytes 1597448 | tf_op jit(solution)/shard_map/ppermute | solution.py:189
  75.0 19.7 %collective-permute-start.7 = (bf16[3104,128]{1,0:T(8,128)(2,1)}, bf16[3104,128]{1,0:T(8,128)(2,1)S(1)}, u32[]{:S(2)}, u32[]{:S(2)}) collective-permute-start(bf16[3104,128]{1,0:T(8,128)(2,1)} %collective-permute-done.2.refs_3_), channel_id=1, source_target_pairs={{0,288},{32,64},{64,352},{96,128},{128,416},{160,192},{192,480},{2... | collective-permute-start | bytes 2383880 | tf_op jit(solution)/shard_map/ppermute | solution.py:186
  76.9 19.4 %collective-permute-start.8 = (bf16[3104,128]{1,0:T(8,128)(2,1)}, bf16[3104,128]{1,0:T(8,128)(2,1)S(1)}, u32[]{:S(2)}, u32[]{:S(2)}) collective-permute-start(bf16[3104,128]{1,0:T(8,128)(2,1)} %collective-permute-done.4.refs_4_), channel_id=1, source_target_pairs={{0,224},{32,256},{64,32},{96,320},{128,96},{160,384},{192,160},{22... | collective-permute-start | bytes 2383880 | tf_op jit(solution)/shard_map/ppermute | solution.py:186
  82.1 10.9 %collective-permute-start.12 = (bf16[1040,128]{1,0:T(8,128)(2,1)S(1)}, bf16[1040,128]{1,0:T(8,128)(2,1)S(1)}, u32[]{:S(2)}, u32[]{:S(2)}) collective-permute-start(bf16[1040,128]{1,0:T(8,128)(2,1)S(1)} %slice.112), channel_id=1, source_target_pairs={{0,4},{4,8},{8,12},{12,16},{16,20},{20,24},{24,28},{28,0},{1,5},{5... | collective-permute-start | bytes 798728 | tf_op jit(solution)/shard_map/ppermute | solution.py:189
  84.0 9.1 %collective-permute-start.14 = (bf16[1040,128]{1,0:T(8,128)(2,1)S(1)}, bf16[1040,128]{1,0:T(8,128)(2,1)S(1)}, u32[]{:S(2)}, u32[]{:S(2)}) collective-permute-start(bf16[1040,128]{1,0:T(8,128)(2,1)S(1)} %slice.113), channel_id=1, source_target_pairs={{0,28},{4,0},{8,4},{12,8},{16,12},{20,16},{24,20},{28,24},{1,29},{... | collective-permute-start | bytes 798728 | tf_op jit(solution)/shard_map/ppermute | solution.py:189
  96.3 12.3 %collective-permute-start.15 = (bf16[1552,128]{1,0:T(8,128)(2,1)S(1)}, bf16[1552,128]{1,0:T(8,128)(2,1)S(1)}, u32[]{:S(2)}, u32[]{:S(2)}) collective-permute-start(bf16[1552,128]{1,0:T(8,128)(2,1)S(1)} %slice.106), channel_id=1, source_target_pairs={{0,288},{32,64},{64,352},{96,128},{128,416},{160,192},{192,480},{2... | collective-permute-start | bytes 1191944 | tf_op jit(solution)/shard_map/ppermute | solution.py:186
  98.3 10.6 %collective-permute-start.16 = (bf16[1552,128]{1,0:T(8,128)(2,1)S(1)}, bf16[1552,128]{1,0:T(8,128)(2,1)S(1)}, u32[]{:S(2)}, u32[]{:S(2)}) collective-permute-start(bf16[1552,128]{1,0:T(8,128)(2,1)S(1)} %slice.107), channel_id=1, source_target_pairs={{0,224},{32,256},{64,32},{96,320},{128,96},{160,384},{192,160},{22... | collective-permute-start | bytes 1191944 | tf_op jit(solution)/shard_map/ppermute | solution.py:186
  112.3 5.3 %collective-permute-start.17 = (f32[4,128,768]{2,1,0:T(8,128)S(1)}, f32[4,128,768]{2,1,0:T(8,128)S(1)}, u32[]{:S(2)}, u32[]{:S(2)}) collective-permute-start(f32[4,128,768]{2,1,0:T(8,128)S(1)} %slice.109), channel_id=1, source_target_pairs={{0,1},{1,0},{2,3},{3,2},{4,5},{5,4},{6,7},{7,6},{8,9},{9,8},{10,11... | collective-permute-start | bytes 4718600 | tf_op jit(solution)/shard_map/ppermute | solution.py:208

commit v5 on v4

--- a/solution.py
+++ b/solution.py
@@ -16,6 +16,7 @@
 LPART = GROUP * W + PAD
 RPART = HALF * EB * W + PAD
 CELL = 6 * W
+TOP = 32767.0
 VMEM_LIMIT = 8 * 2**20
 
 
@@ -49,13 +50,13 @@
     def first(ref_rows):
         return ref_rows.astype(jnp.float32)[0:1].astype(jnp.int32)
 
-    for slot in range(slots):
+    for i, slot in enumerate(slots):
         for p in range(2):
             rho = first(left[slot, pl.ds(p * LPART + GROUP * W, PAD), :])
             tile = x_lo if p == 0 else 1 - x_lo
             place = ((rho & 1) ^ core) * 4 + tile * 2 + (rho >> 1)
-            idx_v[pl.ds(slot * 2 + p, 1), :] = place
-    for c in range(chunks):
+            idx_v[pl.ds(i * 2 + p, 1), :] = place
+    for c in chunks:
         for h in range(2):
             row = first(right[c, pl.ds(h * RPART + HALF * EB * W, PAD), :])
             idx_v[pl.ds(2 * NY + 2 * c + h, 1), :] = row
@@ -64,7 +65,7 @@
     copy.wait()
 
 
-def add_chunk(left, right, acc, idx_s, c, slot):
+def add_chunk(left, right, acc, idx_s, c, slot, place):
     for k in range(GROUP):
         half, j = k // HALF, k % HALF
         both = jnp.concatenate(
@@ -78,7 +79,7 @@
             cell = idx_s[2 * NY + 2 * c + half, j * EB + e]
             lanes = pl.ds(pl.multiple_of(cell * W, W), W)
             for p in range(2):
-                at = idx_s[slot * 2 + p, k]
+                at = idx_s[place * 2 + p, k]
                 acc[at, :, lanes] += part[p * W : (p + 1) * W, e * W : (e + 1) * W]
 
 
@@ -99,12 +100,16 @@
         acc[...] = jnp.zeros_like(acc)
     for copy in copies:
         copy.wait()
-    load_index(meta, left, right, slots, chunks, idx_v, idx_s, sem)
+    if number == 4:
+        load_index(meta, left, right, [meta[9]], [7], idx_v, idx_s, sem)
+        add_chunk(left, right, acc, idx_s, 7, meta[9], 0)
+        return
+    load_index(meta, left, right, range(slots), range(chunks), idx_v, idx_s, sem)
 
     def body(c, carry):
         @pl.when(meta[10 + c] == number)
         def _():
-            add_chunk(left, right, acc, idx_s, c, meta[2 + c])
+            add_chunk(left, right, acc, idx_s, c, meta[2 + c], meta[2 + c])
 
         return carry
 
@@ -143,6 +148,20 @@
     )(meta, *operands, *state, *after)
 
 
+def encode(total):
+    top = jnp.maximum(jnp.abs(total).max(axis=-1, keepdims=True), 2.0**-100)
+    power = jnp.ceil(jnp.log2(top))
+    whole = jnp.round(total * jnp.exp2(-power) * TOP)
+    whole = jnp.clip(whole, -TOP, TOP).astype(jnp.int16)
+    power = jnp.broadcast_to(power.astype(jnp.int16), total.shape[:-1] + (W,))
+    return jnp.concatenate([whole, power], axis=-1)
+
+
+def decode(moved):
+    power = moved[..., CELL : CELL + 1].astype(jnp.float32)
+    return moved[..., :CELL].astype(jnp.float32) * (jnp.exp2(power) / TOP)
+
+
 def per_device(left_blocks, left_rows, right_blocks, right_cols):
     x_lo = lax.axis_index("x_lo")
     z = lax.axis_index("z")
@@ -165,7 +184,7 @@
     right = right_blocks.reshape(2, HALF, EB * W, W)
     cols = right_cols.reshape(2, HALF * EB)
     chunk = jnp.concatenate([with_index(right[h], cols[h]) for h in range(2)], axis=0)
-    first, _ = lax.optimization_barrier((chunk, swapped))
+    first = chunk
 
     source = (z + jnp.array([0, -1, 1, -2, 2, -3, 3, 4], jnp.int32)) % NZ
     away = (4 * (zig(source) ^ side) + source // 2 - y) % NY
@@ -207,7 +226,8 @@
 
     got = lax.ppermute(acc[4:], "core", [(0, 1), (1, 0)])
     total = acc[:4] + got
-    return lax.all_to_all(total, ("x_lo", "x_hi"), 0, 0, tiled=True).sum(0)
+    moved = lax.all_to_all(encode(total), ("x_lo", "x_hi"), 0, 0, tiled=True)
+    return decode(moved).sum(0)
 
 
 def solution(mesh):

time: 144 us -> 144 us (level)
  starting transfers between devices: 67.4 us -> 78.5 us
  waiting for transfers between devices: 29.4 us -> 22.6 us
  blocking collectives: 23 us -> 17.4 us
  other arithmetic: 2.67 us -> 4.34 us
    ppermute x4, starting transfers between devices: 10.3 us -> 17 us  [step_z(): lax.ppermute(up, row, ring_pairs(1))]
    ppermute x1, waiting for transfers between devices: 6.64 us -> 0.01 us  [per_device(): swapped = lax.ppermute(group(1 - own), 'x_lo', [(0, 1), (1, 0)])]
    all_to_all x1, blocking collectives: 23 us -> 17.4 us  [per_device(): moved = lax.all_to_all(encode(total), ('x_lo', 'x_hi'), 0, 0, tiled=True)]
    ppermute x4, starting transfers between devices: 23.8 us -> 28.4 us  [step_z(): lax.ppermute(down, row, ring_pairs(-1))]
  transfers between devices with their start and end apart: 18 -> 18, of which waited for: 8 -> 7; matrix products, arithmetic and copies ran while one was open for 1% -> 1% of each run, Pallas kernels for 9% -> 9%
where the time goes in v5:
time: 144 us; the launch traced here: 142 us
  starting transfers between devices  78.5 us (55%)
  waiting for transfers between devices  22.6 us (16%)
  blocking collectives  17.4 us (12%)
  Pallas kernels  16.1 us (11%)
  other arithmetic  4.34 us (3%)
  local copies, waits for them, and re-layouts  2.57 us (2%)
    ppermute x8, starting transfers between devices, step_y(): return (lax.ppermute(fore, 'y', turn(1)), lax.ppermute(back, 'y', turn(-1)))  28.4 us
    ppermute x4, starting transfers between devices, step_z(): lax.ppermute(down, row, ring_pairs(-1))  28.4 us
    all_to_all x1, blocking collectives, per_device(): moved = lax.all_to_all(encode(total), ('x_lo', 'x_hi'), 0, 0, tiled=True)  17.4 us
    ppermute x4, starting transfers between devices, step_z(): lax.ppermute(up, row, ring_pairs(1))  17 us
    pallas_call x4, Pallas kernels, run_stage(): pl.pallas_call(lambda *refs: stage(number, new_left, new_right, slots, ch...  16.1 us
    ppermute x4, waiting for transfers between devices, step_z(): lax.ppermute(up, row, ring_pairs(1))  9.21 us
    ppermute x8, waiting for transfers between devices, step_y(): return (lax.ppermute(fore, 'y', turn(1)), lax.ppermute(back, 'y', turn(-1)))  8.61 us
    ppermute x1, waiting for transfers between devices, per_device(): got = lax.ppermute(acc[4:], 'core', [(0, 1), (1, 0)])  3.38 us
  transfers between devices with their start and end apart: 18, of which 7 were waited for; matrix products, arithmetic and copies ran while one was open for 1% of the time, Pallas kernels for 9%

profile of v5, /device:TPU:6, one launch (start us, length us, event | category | flops | bytes accessed | tf_op | source)
XLA Modules:
  0.0 142.0 jit_solution(2096315750997289858)
XLA Ops:
  0.5 1.2 reduce.13
  1.8 1.1 dynamic-slice_bitcast_fusion.1
  3.0 2.7 %collective-permute-start.4 = (bf16[1040,128]{1,0:T(8,128)(2,1)S(1)}, bf16[1040,128]{1,0:T(8,128)(2,1)}, u32[]{:S(2)}, u32[]{:S(2)}) collective-permute-start(bf16[1040,128]{1,0:T(8,128)(2,1)S(1)} %fusion.11), channel_id=1, source_target_pairs={{0,256},{256,0},{1,257},{257,1},{2,258},{258,2},{3,259},{259,3},{4... | collective-permute-start | bytes 798728 | tf_op jit(solution)/shard_map/ppermute | solution.py:182
  6.4 4.9 %collective-permute-start = (bf16[3104,128]{1,0:T(8,128)(2,1)S(1)}, bf16[3104,128]{1,0:T(8,128)(2,1)S(1)}, u32[]{:S(2)}, u32[]{:S(2)}) collective-permute-start(bf16[3104,128]{1,0:T(8,128)(2,1)S(1)} %fusion.7.refs_4_), channel_id=1, source_target_pairs={{0,288},{32,64},{64,352},{96,128},{128,416},{160,192},{192,480},{2... | collective-permute-start | bytes 2383880 | tf_op jit(solution)/shard_map/ppermute | solution.py:205
  11.3 8.0 %collective-permute-start.2 = (bf16[3104,128]{1,0:T(8,128)(2,1)S(1)}, bf16[3104,128]{1,0:T(8,128)(2,1)S(1)}, u32[]{:S(2)}, u32[]{:S(2)}) collective-permute-start(bf16[3104,128]{1,0:T(8,128)(2,1)S(1)} %fusion.7.refs_4_), channel_id=1, source_target_pairs={{0,224},{32,256},{64,32},{96,320},{128,96},{160,384},{192,160},{22... | collective-permute-start | bytes 2383880 | tf_op jit(solution)/shard_map/ppermute | solution.py:205
  19.2 1.0 fusion.9.refs_1_
  20.2 3.5 %collective-permute-start.5 = (bf16[2080,128]{1,0:T(8,128)(2,1)S(1)}, bf16[2080,128]{1,0:T(8,128)(2,1)}, u32[]{:S(2)}, u32[]{:S(2)}) collective-permute-start(bf16[2080,128]{1,0:T(8,128)(2,1)S(1)} %fusion.9.refs_1_), channel_id=1, source_target_pairs={{0,4},{4,8},{8,12},{12,16},{16,20},{20,24},{24,28},{28,0},{1,5},{5... | collective-permute-start | bytes 1597448 | tf_op jit(solution)/shard_map/ppermute | solution.py:208
  23.7 3.8 %collective-permute-start.6 = (bf16[2080,128]{1,0:T(8,128)(2,1)S(1)}, bf16[2080,128]{1,0:T(8,128)(2,1)}, u32[]{:S(2)}, u32[]{:S(2)}) collective-permute-start(bf16[2080,128]{1,0:T(8,128)(2,1)S(1)} %fusion.9.refs_1_), channel_id=1, source_target_pairs={{0,28},{4,0},{8,4},{12,8},{16,12},{20,16},{24,20},{28,24},{1,29},{... | collective-permute-start | bytes 1597448 | tf_op jit(solution)/shard_map/ppermute | solution.py:208
  27.6 7.2 %collective-permute-done.refs_5_ = bf16[3104,128]{1,0:T(8,128)(2,1)S(1)} collective-permute-done((bf16[3104,128]{1,0:T(8,128)(2,1)S(1)}, bf16[3104,128]{1,0:T(8,128)(2,1)S(1)}, u32[]{:S(2)}, u32[]{:S(2)}) %collective-permute-start) | collective-permute-done | bytes 794656 | tf_op jit(solution)/shard_map/ppermute | solution.py:205
  34.7 8.3 %collective-permute-start.1 = (bf16[3104,128]{1,0:T(8,128)(2,1)S(1)}, bf16[3104,128]{1,0:T(8,128)(2,1)}, u32[]{:S(2)}, u32[]{:S(2)}) collective-permute-start(bf16[3104,128]{1,0:T(8,128)(2,1)S(1)} %collective-permute-done.refs_5_), channel_id=1, source_target_pairs={{0,288},{32,64},{64,352},{96,128},{128,416},{160,192},{192,480},{2... | collective-permute-start | bytes 2383880 | tf_op jit(solution)/shard_map/ppermute | solution.py:205
  43.0 8.3 %collective-permute-start.3 = (bf16[3104,128]{1,0:T(8,128)(2,1)S(1)}, bf16[3104,128]{1,0:T(8,128)(2,1)}, u32[]{:S(2)}, u32[]{:S(2)}) collective-permute-start(bf16[3104,128]{1,0:T(8,128)(2,1)S(1)} %collective-permute-done.2.refs_6_), channel_id=1, source_target_pairs={{0,224},{32,256},{64,32},{96,320},{128,96},{160,384},{192,160},{22... | collective-permute-start | bytes 2383880 | tf_op jit(solution)/shard_map/ppermute | solution.py:205
  51.3 2.0 %collective-permute-start.9 = (bf16[2080,128]{1,0:T(8,128)(2,1)}, bf16[2080,128]{1,0:T(8,128)(2,1)S(1)}, u32[]{:S(2)}, u32[]{:S(2)}) collective-permute-start(bf16[2080,128]{1,0:T(8,128)(2,1)} %collective-permute-done.5.refs_2_), channel_id=1, source_target_pairs={{0,4},{4,8},{8,12},{12,16},{16,20},{20,24},{24,28},{28,0},{1,5},{5... | collective-permute-start | bytes 1597448 | tf_op jit(solution)/shard_map/ppermute | solution.py:208
  53.4 5.0 %collective-permute-start.10 = (bf16[2080,128]{1,0:T(8,128)(2,1)}, bf16[2080,128]{1,0:T(8,128)(2,1)}, u32[]{:S(2)}, u32[]{:S(2)}) collective-permute-start(bf16[2080,128]{1,0:T(8,128)(2,1)} %collective-permute-done.6.refs_3_), channel_id=1, source_target_pairs={{0,28},{4,0},{8,4},{12,8},{16,12},{20,16},{24,20},{28,24},{1,29},{... | collective-permute-start | bytes 1597448 | tf_op jit(solution)/shard_map/ppermute | solution.py:208
  58.6 8.5 %collective-permute-done.9.refs_1_ = bf16[2080,128]{1,0:T(8,128)(2,1)S(1)} collective-permute-done((bf16[2080,128]{1,0:T(8,128)(2,1)}, bf16[2080,128]{1,0:T(8,128)(2,1)S(1)}, u32[]{:S(2)}, u32[]{:S(2)}) %collective-permute-start.9) | collective-permute-done | bytes 532512 | tf_op jit(solution)/shard_map/ppermute | solution.py:208
  67.1 1.9 %collective-permute-start.11 = (bf16[2080,128]{1,0:T(8,128)(2,1)S(1)}, bf16[2080,128]{1,0:T(8,128)(2,1)S(1)}, u32[]{:S(2)}, u32[]{:S(2)}) collective-permute-start(bf16[2080,128]{1,0:T(8,128)(2,1)S(1)} %collective-permute-done.9.refs_1_), channel_id=1, source_target_pairs={{0,4},{4,8},{8,12},{12,16},{16,20},{20,24},{24,28},{28,0},{1,5},{5... | collective-permute-start | bytes 1597448 | tf_op jit(solution)/shard_map/ppermute | solution.py:208
  69.0 5.1 %collective-permute-start.13 = (bf16[2080,128]{1,0:T(8,128)(2,1)}, bf16[2080,128]{1,0:T(8,128)(2,1)S(1)}, u32[]{:S(2)}, u32[]{:S(2)}) collective-permute-start(bf16[2080,128]{1,0:T(8,128)(2,1)} %collective-permute-done.10.refs_2_), channel_id=1, source_target_pairs={{0,28},{4,0},{8,4},{12,8},{16,12},{20,16},{24,20},{28,24},{1,29},{... | collective-permute-start | bytes 1597448 | tf_op jit(solution)/shard_map/ppermute | solution.py:208
  74.1 4.1 %shard_map.64 = (f32[8,128,768]{2,1,0:T(8,128)S(1)}, bf16[8,2080,128]{2,1,0:T(8,128)(2,1)S(1)}, bf16[8,3104,128]{2,1,0:T(8,128)(2,1)S(1)}, s32[8,128]{1,0:T(8,128)S(1)}) custom-call(s32[18]{0:T(128)S(1)} %pad_add_fusion.1.refs_0_, bf16[2080,128]{1,0:T(8,128)(2,1)S(1)} %fusion.9.refs_1_, bf16[2080,128]{1,0:T(8,128)(2,1)} %collective-permute-done.5.refs_2_, ...), custom_call_target="tpu_custom_call" | custom-call | flops 805306368 | bytes 1048576 | tf_op jit(solution)/shard_map/pallas_call | solution.py:127
  78.3 1.9 %collective-permute-start.7 = (bf16[3104,128]{1,0:T(8,128)(2,1)}, bf16[3104,128]{1,0:T(8,128)(2,1)S(1)}, u32[]{:S(2)}, u32[]{:S(2)}) collective-permute-start(bf16[3104,128]{1,0:T(8,128)(2,1)} %collective-permute-done.1.refs_3_), channel_id=1, source_target_pairs={{0,288},{32,64},{64,352},{96,128},{128,416},{160,192},{192,480},{2... | collective-permute-start | bytes 2383880 | tf_op jit(solution)/shard_map/ppermute | solution.py:205
  80.2 6.6 %collective-permute-start.8 = (bf16[3104,128]{1,0:T(8,128)(2,1)}, bf16[3104,128]{1,0:T(8,128)(2,1)S(1)}, u32[]{:S(2)}, u32[]{:S(2)}) collective-permute-start(bf16[3104,128]{1,0:T(8,128)(2,1)} %collective-permute-done.3.refs_4_), channel_id=1, source_target_pairs={{0,224},{32,256},{64,32},{96,320},{128,96},{160,384},{192,160},{22... | collective-permute-start | bytes 2383880 | tf_op jit(solution)/shard_map/ppermute | solution.py:205
  86.9 1.9 %collective-permute-start.12 = (bf16[1040,128]{1,0:T(8,128)(2,1)S(1)}, bf16[1040,128]{1,0:T(8,128)(2,1)S(1)}, u32[]{:S(2)}, u32[]{:S(2)}) collective-permute-start(bf16[1040,128]{1,0:T(8,128)(2,1)S(1)} %slice.120), channel_id=1, source_target_pairs={{0,4},{4,8},{8,12},{12,16},{16,20},{20,24},{24,28},{28,0},{1,5},{5... | collective-permute-start | bytes 798728 | tf_op jit(solution)/shard_map/ppermute | solution.py:208
  88.9 5.1 %collective-permute-start.14 = (bf16[1040,128]{1,0:T(8,128)(2,1)S(1)}, bf16[1040,128]{1,0:T(8,128)(2,1)S(1)}, u32[]{:S(2)}, u32[]{:S(2)}) collective-permute-start(bf16[1040,128]{1,0:T(8,128)(2,1)S(1)} %slice.121), channel_id=1, source_target_pairs={{0,28},{4,0},{8,4},{12,8},{16,12},{20,16},{24,20},{28,24},{1,29},{... | collective-permute-start | bytes 798728 | tf_op jit(solution)/shard_map/ppermute | solution.py:208
  94.0 3.8 %shard_map.65 = (f32[8,128,768]{2,1,0:T(8,128)S(1)}, bf16[8,2080,128]{2,1,0:T(8,128)(2,1)S(1)}, bf16[8,3104,128]{2,1,0:T(8,128)(2,1)S(1)}, s32[8,128]{1,0:T(8,128)S(1)}) custom-call(s32[18]{0:T(128)S(1)} %pad_add_fusion.1.refs_0_, bf16[2080,128]{1,0:T(8,128)(2,1)S(1)} %collective-permute-done.9.refs_1_, ...), custom_call_target="tpu_custom_call", output_to_operand_aliasing={{0}: (5, {}), {1}: (6, {}), {2}: (7, {})} | custom-call | flops 805306368 | bytes 1048576 | tf_op jit(solution)/shard_map/pallas_call | solution.py:127
  97.9 2.0 %collective-permute-done.7.refs_5_ = bf16[3104,128]{1,0:T(8,128)(2,1)S(1)} collective-permute-done((bf16[3104,128]{1,0:T(8,128)(2,1)}, bf16[3104,128]{1,0:T(8,128)(2,1)S(1)}, u32[]{:S(2)}, u32[]{:S(2)}) %collective-permute-start.7) | collective-permute-done | bytes 794656 | tf_op jit(solution)/shard_map/ppermute | solution.py:205
  99.9 1.3 collective-permute-done.8.refs_6_
  101.3 1.9 %collective-permute-start.15 = (bf16[1552,128]{1,0:T(8,128)(2,1)S(1)}, bf16[1552,128]{1,0:T(8,128)(2,1)S(1)}, u32[]{:S(2)}, u32[]{:S(2)}) collective-permute-start(bf16[1552,128]{1,0:T(8,128)(2,1)S(1)} %slice.112), channel_id=1, source_target_pairs={{0,288},{32,64},{64,352},{96,128},{128,416},{160,192},{192,480},{2... | collective-permute-start | bytes 1191944 | tf_op jit(solution)/shard_map/ppermute | solution.py:205
  103.2 5.5 %collective-permute-start.16 = (bf16[1552,128]{1,0:T(8,128)(2,1)S(1)}, bf16[1552,128]{1,0:T(8,128)(2,1)S(1)}, u32[]{:S(2)}, u32[]{:S(2)}) collective-permute-start(bf16[1552,128]{1,0:T(8,128)(2,1)S(1)} %slice.113), channel_id=1, source_target_pairs={{0,224},{32,256},{64,32},{96,320},{128,96},{160,384},{192,160},{22... | collective-permute-start | bytes 1191944 | tf_op jit(solution)/shard_map/ppermute | solution.py:205
  108.7 5.2 %shard_map.66 = (f32[8,128,768]{2,1,0:T(8,128)S(1)}, bf16[8,2080,128]{2,1,0:T(8,128)(2,1)S(1)}, bf16[8,3104,128]{2,1,0:T(8,128)(2,1)S(1)}, s32[8,128]{1,0:T(8,128)}) custom-call(s32[18]{0:T(128)S(1)} %pad_add_fusion.1.refs_0_, bf16[2080,128]{1,0:T(8,128)(2,1)S(1)} %collective-permute-done.11.refs_1_, ...), custom_call_target="tpu_custom_call", output_to_operand_aliasing={{0}: (7, {}), {1}: (8, {}), {2}: (9, {})} | custom-call | flops 805306368 | bytes 1048576 | tf_op jit(solution)/shard_map/pallas_call | solution.py:127
  114.0 3.0 %shard_map.67 = (f32[8,128,768]{2,1,0:T(8,128)S(1)}, bf16[8,2080,128]{2,1,0:T(8,128)(2,1)S(1)}, bf16[8,3104,128]{2,1,0:T(8,128)(2,1)S(1)}, s32[8,128]{1,0:T(8,128)}) custom-call(s32[18]{0:T(128)S(1)} %pad_add_fusion.1.refs_0_, bf16[1552,128]{1,0:T(8,128)(2,1)S(1)} %collective-permute-done.15.refs_1_, ...), custom_call_target="tpu_custom_call", output_to_operand_aliasing={{0}: (3, {}), {1}: (4, {}), {2}: (5, {})} | custom-call | flops 805306368 | bytes 1048576 | tf_op jit(solution)/shard_map/pallas_call | solution.py:127
  117.2 1.9 %collective-permute-start.17 = (f32[4,128,768]{2,1,0:T(8,128)S(1)}, f32[4,128,768]{2,1,0:T(8,128)S(1)}, u32[]{:S(2)}, u32[]{:S(2)}) collective-permute-start(f32[4,128,768]{2,1,0:T(8,128)S(1)} %slice.115), channel_id=1, source_target_pairs={{0,1},{1,0},{2,3},{3,2},{4,5},{5,4},{6,7},{7,6},{8,9},{9,8},{10,11... | collective-permute-start | bytes 4718600 | tf_op jit(solution)/shard_map/ppermute | solution.py:227
  119.1 3.4 %collective-permute-done.17 = f32[4,128,768]{2,1,0:T(8,128)S(1)} collective-permute-done((f32[4,128,768]{2,1,0:T(8,128)S(1)}, f32[4,128,768]{2,1,0:T(8,128)S(1)}, u32[]{:S(2)}, u32[]{:S(2)}) %collective-permute-start.17) | collective-permute-done | bytes 1572896 | tf_op jit(solution)/shard_map/ppermute | solution.py:227
  123.3 17.4 %all_to_all.5 = s16[4,128,896]{2,1,0:T(8,128)(2,1)S(1)} all-to-all(s16[4,128,896]{2,1,0:T(8,128)(2,1)S(1)} %pad_add_fusion), channel_id=1, replica_groups=mesh['x_lo'=2,'z'=8,'y'=8,'x_hi'=2,'core'=2] {'x_lo','x_hi'}, dimensions={0} | all-to-all | bytes 1835008 | tf_op jit(solution)/shard_map/all_to_all | solution.py:229
  140.9 1.1 multiply_reduce_fusion
  (46 shorter events, 2.8 us)
Async XLA Ops:
  0.0 5.7 %copy-start = (bf16[1,8,1,3,128,128]{5,4,3,2,1,0:T(8,128)(2,1)S(1)}, bf16[1,8,1,3,128,128]{5,4,3,2,1,0:T(8,128)(2,1)}, u32[]{:S(2)}) copy-start(bf16[1,8,1,3,128,128]{5,4,3,2,1,0:T(8,128)(2,1)} %param.16) | copy-start | bytes 2359300
  1.8 4.0 %copy-start.1 = (s32[1,8,1,3]{1,2,3,0:T(1,128)S(1)}, s32[1,8,1,3]{1,2,3,0:T(1,128)}, u32[]{:S(2)}) copy-start(s32[1,8,1,3]{1,2,3,0:T(1,128)} %param.17) | copy-start | bytes 292
  3.0 16.3 %collective-permute-start.4 = (bf16[1040,128]{1,0:T(8,128)(2,1)S(1)}, bf16[1040,128]{1,0:T(8,128)(2,1)}, u32[]{:S(2)}, u32[]{:S(2)}) collective-permute-start(bf16[1040,128]{1,0:T(8,128)(2,1)S(1)} %fusion.11), channel_id=1, source_target_pairs={{0,256},{256,0},{1,257},{257,1},{2,258},{258,2},{3,259},{259,3},{4... | collective-permute-start | bytes 798728 | tf_op jit(solution)/shard_map/ppermute | solution.py:182
  5.8 52.6 %copy-start.2 = (s32[8]{0:T(128)S(1)}, s32[8]{0:T(128)}, u32[]{:S(2)}) copy-start(s32[8]{0:T(128)} %constant.236.clone) | copy-start | bytes 100
  5.8 52.6 %copy-start.3 = (s32[8]{0:T(128)S(1)}, s32[8]{0:T(128)}, u32[]{:S(2)}) copy-start(s32[8]{0:T(128)} %constant.237.clone) | copy-start | bytes 100
  6.4 28.4 %collective-permute-start = (bf16[3104,128]{1,0:T(8,128)(2,1)S(1)}, bf16[3104,128]{1,0:T(8,128)(2,1)S(1)}, u32[]{:S(2)}, u32[]{:S(2)}) collective-permute-start(bf16[3104,128]{1,0:T(8,128)(2,1)S(1)} %fusion.7.refs_4_), channel_id=1, source_target_pairs={{0,288},{32,64},{64,352},{96,128},{128,416},{160,192},{192,480},{2... | collective-permute-start | bytes 2383880 | tf_op jit(solution)/shard_map/ppermute | solution.py:205
  11.3 31.7 %collective-permute-start.2 = (bf16[3104,128]{1,0:T(8,128)(2,1)S(1)}, bf16[3104,128]{1,0:T(8,128)(2,1)S(1)}, u32[]{:S(2)}, u32[]{:S(2)}) collective-permute-start(bf16[3104,128]{1,0:T(8,128)(2,1)S(1)} %fusion.7.refs_4_), channel_id=1, source_target_pairs={{0,224},{32,256},{64,32},{96,320},{128,96},{160,384},{192,160},{22... | collective-permute-start | bytes 2383880 | tf_op jit(solution)/shard_map/ppermute | solution.py:205
  20.2 31.1 %collective-permute-start.5 = (bf16[2080,128]{1,0:T(8,128)(2,1)S(1)}, bf16[2080,128]{1,0:T(8,128)(2,1)}, u32[]{:S(2)}, u32[]{:S(2)}) collective-permute-start(bf16[2080,128]{1,0:T(8,128)(2,1)S(1)} %fusion.9.refs_1_), channel_id=1, source_target_pairs={{0,4},{4,8},{8,12},{12,16},{16,20},{20,24},{24,28},{28,0},{1,5},{5... | collective-permute-start | bytes 1597448 | tf_op jit(solution)/shard_map/ppermute | solution.py:208
  23.7 29.7 %collective-permute-start.6 = (bf16[2080,128]{1,0:T(8,128)(2,1)S(1)}, bf16[2080,128]{1,0:T(8,128)(2,1)}, u32[]{:S(2)}, u32[]{:S(2)}) collective-permute-start(bf16[2080,128]{1,0:T(8,128)(2,1)S(1)} %fusion.9.refs_1_), channel_id=1, source_target_pairs={{0,28},{4,0},{8,4},{12,8},{16,12},{20,16},{24,20},{28,24},{1,29},{... | collective-permute-start | bytes 1597448 | tf_op jit(solution)/shard_map/ppermute | solution.py:208
  34.7 43.5 %collective-permute-start.1 = (bf16[3104,128]{1,0:T(8,128)(2,1)S(1)}, bf16[3104,128]{1,0:T(8,128)(2,1)}, u32[]{:S(2)}, u32[]{:S(2)}) collective-permute-start(bf16[3104,128]{1,0:T(8,128)(2,1)S(1)} %collective-permute-done.refs_5_), channel_id=1, source_target_pairs={{0,288},{32,64},{64,352},{96,128},{128,416},{160,192},{192,480},{2... | collective-permute-start | bytes 2383880 | tf_op jit(solution)/shard_map/ppermute | solution.py:205
  43.0 35.3 %collective-permute-start.3 = (bf16[3104,128]{1,0:T(8,128)(2,1)S(1)}, bf16[3104,128]{1,0:T(8,128)(2,1)}, u32[]{:S(2)}, u32[]{:S(2)}) collective-permute-start(bf16[3104,128]{1,0:T(8,128)(2,1)S(1)} %collective-permute-done.2.refs_6_), channel_id=1, source_target_pairs={{0,224},{32,256},{64,32},{96,320},{128,96},{160,384},{192,160},{22... | collective-permute-start | bytes 2383880 | tf_op jit(solution)/shard_map/ppermute | solution.py:205
  51.3 15.7 %collective-permute-start.9 = (bf16[2080,128]{1,0:T(8,128)(2,1)}, bf16[2080,128]{1,0:T(8,128)(2,1)S(1)}, u32[]{:S(2)}, u32[]{:S(2)}) collective-permute-start(bf16[2080,128]{1,0:T(8,128)(2,1)} %collective-permute-done.5.refs_2_), channel_id=1, source_target_pairs={{0,4},{4,8},{8,12},{12,16},{16,20},{20,24},{24,28},{28,0},{1,5},{5... | collective-permute-start | bytes 1597448 | tf_op jit(solution)/shard_map/ppermute | solution.py:208
  53.4 15.6 %collective-permute-start.10 = (bf16[2080,128]{1,0:T(8,128)(2,1)}, bf16[2080,128]{1,0:T(8,128)(2,1)}, u32[]{:S(2)}, u32[]{:S(2)}) collective-permute-start(bf16[2080,128]{1,0:T(8,128)(2,1)} %collective-permute-done.6.refs_3_), channel_id=1, source_target_pairs={{0,28},{4,0},{8,4},{12,8},{16,12},{20,16},{24,20},{28,24},{1,29},{... | collective-permute-start | bytes 1597448 | tf_op jit(solution)/shard_map/ppermute | solution.py:208
  67.1 19.8 %collective-permute-start.11 = (bf16[2080,128]{1,0:T(8,128)(2,1)S(1)}, bf16[2080,128]{1,0:T(8,128)(2,1)S(1)}, u32[]{:S(2)}, u32[]{:S(2)}) collective-permute-start(bf16[2080,128]{1,0:T(8,128)(2,1)S(1)} %collective-permute-done.9.refs_1_), channel_id=1, source_target_pairs={{0,4},{4,8},{8,12},{12,16},{16,20},{20,24},{24,28},{28,0},{1,5},{5... | collective-permute-start | bytes 1597448 | tf_op jit(solution)/shard_map/ppermute | solution.py:208
  69.0 19.8 %collective-permute-start.13 = (bf16[2080,128]{1,0:T(8,128)(2,1)}, bf16[2080,128]{1,0:T(8,128)(2,1)S(1)}, u32[]{:S(2)}, u32[]{:S(2)}) collective-permute-start(bf16[2080,128]{1,0:T(8,128)(2,1)} %collective-permute-done.10.refs_2_), channel_id=1, source_target_pairs={{0,28},{4,0},{8,4},{12,8},{16,12},{20,16},{24,20},{28,24},{1,29},{... | collective-permute-start | bytes 1597448 | tf_op jit(solution)/shard_map/ppermute | solution.py:208
  78.3 21.6 %collective-permute-start.7 = (bf16[3104,128]{1,0:T(8,128)(2,1)}, bf16[3104,128]{1,0:T(8,128)(2,1)S(1)}, u32[]{:S(2)}, u32[]{:S(2)}) collective-permute-start(bf16[3104,128]{1,0:T(8,128)(2,1)} %collective-permute-done.1.refs_3_), channel_id=1, source_target_pairs={{0,288},{32,64},{64,352},{96,128},{128,416},{160,192},{192,480},{2... | collective-permute-start | bytes 2383880 | tf_op jit(solution)/shard_map/ppermute | solution.py:205
  80.2 21.0 %collective-permute-start.8 = (bf16[3104,128]{1,0:T(8,128)(2,1)}, bf16[3104,128]{1,0:T(8,128)(2,1)S(1)}, u32[]{:S(2)}, u32[]{:S(2)}) collective-permute-start(bf16[3104,128]{1,0:T(8,128)(2,1)} %collective-permute-done.3.refs_4_), channel_id=1, source_target_pairs={{0,224},{32,256},{64,32},{96,320},{128,96},{160,384},{192,160},{22... | collective-permute-start | bytes 2383880 | tf_op jit(solution)/shard_map/ppermute | solution.py:205
  86.9 10.9 %collective-permute-start.12 = (bf16[1040,128]{1,0:T(8,128)(2,1)S(1)}, bf16[1040,128]{1,0:T(8,128)(2,1)S(1)}, u32[]{:S(2)}, u32[]{:S(2)}) collective-permute-start(bf16[1040,128]{1,0:T(8,128)(2,1)S(1)} %slice.120), channel_id=1, source_target_pairs={{0,4},{4,8},{8,12},{12,16},{16,20},{20,24},{24,28},{28,0},{1,5},{5... | collective-permute-start | bytes 798728 | tf_op jit(solution)/shard_map/ppermute | solution.py:208
  88.9 9.1 %collective-permute-start.14 = (bf16[1040,128]{1,0:T(8,128)(2,1)S(1)}, bf16[1040,128]{1,0:T(8,128)(2,1)S(1)}, u32[]{:S(2)}, u32[]{:S(2)}) collective-permute-start(bf16[1040,128]{1,0:T(8,128)(2,1)S(1)} %slice.121), channel_id=1, source_target_pairs={{0,28},{4,0},{8,4},{12,8},{16,12},{20,16},{24,20},{28,24},{1,29},{... | collective-permute-start | bytes 798728 | tf_op jit(solution)/shard_map/ppermute | solution.py:208
  101.3 12.6 %collective-permute-start.15 = (bf16[1552,128]{1,0:T(8,128)(2,1)S(1)}, bf16[1552,128]{1,0:T(8,128)(2,1)S(1)}, u32[]{:S(2)}, u32[]{:S(2)}) collective-permute-start(bf16[1552,128]{1,0:T(8,128)(2,1)S(1)} %slice.112), channel_id=1, source_target_pairs={{0,288},{32,64},{64,352},{96,128},{128,416},{160,192},{192,480},{2... | collective-permute-start | bytes 1191944 | tf_op jit(solution)/shard_map/ppermute | solution.py:205
  103.2 10.8 %collective-permute-start.16 = (bf16[1552,128]{1,0:T(8,128)(2,1)S(1)}, bf16[1552,128]{1,0:T(8,128)(2,1)S(1)}, u32[]{:S(2)}, u32[]{:S(2)}) collective-permute-start(bf16[1552,128]{1,0:T(8,128)(2,1)S(1)} %slice.113), channel_id=1, source_target_pairs={{0,224},{32,256},{64,32},{96,320},{128,96},{160,384},{192,160},{22... | collective-permute-start | bytes 1191944 | tf_op jit(solution)/shard_map/ppermute | solution.py:205
  117.2 5.3 %collective-permute-start.17 = (f32[4,128,768]{2,1,0:T(8,128)S(1)}, f32[4,128,768]{2,1,0:T(8,128)S(1)}, u32[]{:S(2)}, u32[]{:S(2)}) collective-permute-start(f32[4,128,768]{2,1,0:T(8,128)S(1)} %slice.115), channel_id=1, source_target_pairs={{0,1},{1,0},{2,3},{3,2},{4,5},{5,4},{6,7},{7,6},{8,9},{9,8},{10,11... | collective-permute-start | bytes 4718600 | tf_op jit(solution)/shard_map/ppermute | solution.py:227

commit v6 on v5

--- a/solution.py
+++ b/solution.py
@@ -37,6 +37,13 @@
     return [(y, (y + step) % NY) for y in range(NY)]
 
 
+def chip_pairs(step):
+    def other(i):
+        return (i % 2) * 2 + i // 2
+
+    return [(i, other((other(i) + step) % 4)) for i in range(4)]
+
+
 def with_index(blocks, index):
     flat = blocks.reshape(-1, W)
     row = jnp.zeros((PAD, W), flat.dtype)
@@ -54,7 +61,8 @@
         for p in range(2):
             rho = first(left[slot, pl.ds(p * LPART + GROUP * W, PAD), :])
             tile = x_lo if p == 0 else 1 - x_lo
-            place = ((rho & 1) ^ core) * 4 + tile * 2 + (rho >> 1)
+            ahead = ((rho >> 1) * 2 + tile - meta[18]) & 3
+            place = ((rho & 1) ^ core) * 4 + ahead
             idx_v[pl.ds(i * 2 + p, 1), :] = place
     for c in chunks:
         for h in range(2):
@@ -184,7 +192,7 @@
     right = right_blocks.reshape(2, HALF, EB * W, W)
     cols = right_cols.reshape(2, HALF * EB)
     chunk = jnp.concatenate([with_index(right[h], cols[h]) for h in range(2)], axis=0)
-    first = chunk
+    first, _ = lax.optimization_barrier((chunk, swapped))
 
     source = (z + jnp.array([0, -1, 1, -2, 2, -3, 3, 4], jnp.int32)) % NZ
     away = (4 * (zig(source) ^ side) + source // 2 - y) % NY
@@ -193,7 +201,10 @@
     )
     right_at = jnp.array([1, 1, 1, 2, 2, 3, 3, 4], jnp.int32)
     left_at = jnp.where(slot < 3, 1, jnp.where(slot < 5, 2, 3))
-    meta = jnp.concatenate([jnp.stack([core, x_lo]), slot, jnp.maximum(right_at, left_at)])
+    x = lax.axis_index("x_hi") * 2 + x_lo
+    meta = jnp.concatenate(
+        [jnp.stack([core, x_lo]), slot, jnp.maximum(right_at, left_at), x[None]]
+    )
     meta = meta.astype(jnp.int32)
 
     def listed(arrays, low, high):
@@ -226,8 +237,11 @@
 
     got = lax.ppermute(acc[4:], "core", [(0, 1), (1, 0)])
     total = acc[:4] + got
-    moved = lax.all_to_all(encode(total), ("x_lo", "x_hi"), 0, 0, tiled=True)
-    return decode(moved).sum(0)
+    out = total[0]
+    for step in (2, 1, 3):
+        moved = lax.ppermute(encode(total[step]), ("x_lo", "x_hi"), chip_pairs(step))
+        out = out + decode(moved)
+    return out
 
 
 def solution(mesh):

time: 144 us -> 137 us (0.951); the launches traced: 142 us -> 137 us
  blocking collectives: 17.4 us -> 0 us
  waiting for transfers between devices: 22.6 us -> 37.2 us
  starting transfers between devices: 78.5 us -> 76.5 us
    all_to_all x1 -> x0, blocking collectives: 17.4 us -> none  [per_device(): moved = lax.all_to_all(encode(total), ('x_lo', 'x_hi'), 0, 0, tiled=True)]
    ppermute x0 -> x3, starting transfers between devices: none -> 9.14 us  [per_device(): lax.ppermute(encode(total[step]), ('x_lo', 'x_hi'), chip_pairs(step))]
    ppermute x0 -> x3, waiting for transfers between devices: none -> 7.89 us  [per_device(): lax.ppermute(encode(total[step]), ('x_lo', 'x_hi'), chip_pairs(step))]
    ppermute x4, starting transfers between devices: 17 us -> 10.3 us  [step_z(): lax.ppermute(up, row, ring_pairs(1))]
    ppermute x1, waiting for transfers between devices: 0.01 us -> 6.64 us  [per_device(): swapped = lax.ppermute(group(1 - own), 'x_lo', [(0, 1), (1, 0)])]
    ppermute x4, starting transfers between devices: 28.4 us -> 23.8 us  [step_z(): lax.ppermute(down, row, ring_pairs(-1))]
  transfers between devices with their start and end apart: 18 -> 21, of which waited for: 7 -> 11; matrix products, arithmetic and copies ran while one was open for 1% -> 1% of each run, Pallas kernels for 9% -> 10%
where the time goes in v6:
time: 137 us
  starting transfers between devices  76.5 us (56%)
  waiting for transfers between devices  37.2 us (27%)
  Pallas kernels  16.1 us (12%)
  other arithmetic  3.58 us (3%)
  local copies, waits for them, and re-layouts  2.73 us (2%)
    ppermute x8, starting transfers between devices, step_y(): return (lax.ppermute(fore, 'y', turn(1)), lax.ppermute(back, 'y', turn(-1)))  28.7 us
    ppermute x4, starting transfers between devices, step_z(): lax.ppermute(down, row, ring_pairs(-1))  23.8 us
    pallas_call x4, Pallas kernels, run_stage(): pl.pallas_call(lambda *refs: stage(number, new_left, new_right, slots, ch...  16.1 us
    ppermute x4, starting transfers between devices, step_z(): lax.ppermute(up, row, ring_pairs(1))  10.3 us
    ppermute x3, starting transfers between devices, per_device(): lax.ppermute(encode(total[step]), ('x_lo', 'x_hi'), chip_pairs(step))  9.14 us
    ppermute x4, waiting for transfers between devices, step_z(): lax.ppermute(up, row, ring_pairs(1))  9.12 us
    ppermute x8, waiting for transfers between devices, step_y(): return (lax.ppermute(fore, 'y', turn(1)), lax.ppermute(back, 'y', turn(-1)))  8.35 us
    ppermute x3, waiting for transfers between devices, per_device(): lax.ppermute(encode(total[step]), ('x_lo', 'x_hi'), chip_pairs(step))  7.89 us
  transfers between devices with their start and end apart: 21, of which 11 were waited for; matrix products, arithmetic and copies ran while one was open for 1% of the time, Pallas kernels for 10%

profile of v6, /device:TPU:6, one launch (start us, length us, event | category | flops | bytes accessed | tf_op | source)
XLA Modules:
  0.0 136.7 jit_solution(4894376077986128708)
XLA Ops:
  3.0 2.7 %collective-permute-start = (bf16[1040,128]{1,0:T(8,128)(2,1)S(1)}, bf16[1040,128]{1,0:T(8,128)(2,1)S(1)}, u32[]{:S(2)}, u32[]{:S(2)}) collective-permute-start(bf16[1040,128]{1,0:T(8,128)(2,1)S(1)} %fusion.14), channel_id=1, source_target_pairs={{0,256},{256,0},{1,257},{257,1},{2,258},{258,2},{3,259},{259,3},{4... | collective-permute-start | bytes 798728 | tf_op jit(solution)/shard_map/ppermute | solution.py:190
  6.4 6.6 %collective-permute-done = bf16[1040,128]{1,0:T(8,128)(2,1)S(1)} collective-permute-done((bf16[1040,128]{1,0:T(8,128)(2,1)S(1)}, bf16[1040,128]{1,0:T(8,128)(2,1)S(1)}, u32[]{:S(2)}, u32[]{:S(2)}) %collective-permute-start) | collective-permute-done | bytes 266272 | tf_op jit(solution)/shard_map/ppermute | solution.py:190
  13.1 4.5 %collective-permute-start.1 = (bf16[3104,128]{1,0:T(8,128)(2,1)S(1)}, bf16[3104,128]{1,0:T(8,128)(2,1)S(1)}, u32[]{:S(2)}, u32[]{:S(2)}) collective-permute-start(bf16[3104,128]{1,0:T(8,128)(2,1)S(1)} %fusion.7.refs_4_), channel_id=1, source_target_pairs={{0,288},{32,64},{64,352},{96,128},{128,416},{160,192},{192,480},{2... | collective-permute-start | bytes 2383880 | tf_op jit(solution)/shard_map/ppermute | solution.py:216
  17.6 8.3 %collective-permute-start.3 = (bf16[3104,128]{1,0:T(8,128)(2,1)S(1)}, bf16[3104,128]{1,0:T(8,128)(2,1)S(1)}, u32[]{:S(2)}, u32[]{:S(2)}) collective-permute-start(bf16[3104,128]{1,0:T(8,128)(2,1)S(1)} %fusion.7.refs_4_), channel_id=1, source_target_pairs={{0,224},{32,256},{64,32},{96,320},{128,96},{160,384},{192,160},{22... | collective-permute-start | bytes 2383880 | tf_op jit(solution)/shard_map/ppermute | solution.py:216
  26.0 3.5 %collective-permute-start.5 = (bf16[2080,128]{1,0:T(8,128)(2,1)S(1)}, bf16[2080,128]{1,0:T(8,128)(2,1)}, u32[]{:S(2)}, u32[]{:S(2)}) collective-permute-start(bf16[2080,128]{1,0:T(8,128)(2,1)S(1)} %fusion.9.refs_1_), channel_id=1, source_target_pairs={{0,4},{4,8},{8,12},{12,16},{16,20},{20,24},{24,28},{28,0},{1,5},{5... | collective-permute-start | bytes 1597448 | tf_op jit(solution)/shard_map/ppermute | solution.py:219
  29.5 3.8 %collective-permute-start.6 = (bf16[2080,128]{1,0:T(8,128)(2,1)S(1)}, bf16[2080,128]{1,0:T(8,128)(2,1)}, u32[]{:S(2)}, u32[]{:S(2)}) collective-permute-start(bf16[2080,128]{1,0:T(8,128)(2,1)S(1)} %fusion.9.refs_1_), channel_id=1, source_target_pairs={{0,28},{4,0},{8,4},{12,8},{16,12},{20,16},{24,20},{28,24},{1,29},{... | collective-permute-start | bytes 1597448 | tf_op jit(solution)/shard_map/ppermute | solution.py:219
  33.3 7.5 %collective-permute-done.1.refs_5_ = bf16[3104,128]{1,0:T(8,128)(2,1)S(1)} collective-permute-done((bf16[3104,128]{1,0:T(8,128)(2,1)S(1)}, bf16[3104,128]{1,0:T(8,128)(2,1)S(1)}, u32[]{:S(2)}, u32[]{:S(2)}) %collective-permute-start.1) | collective-permute-done | bytes 794656 | tf_op jit(solution)/shard_map/ppermute | solution.py:216
  40.8 1.9 %collective-permute-start.2 = (bf16[3104,128]{1,0:T(8,128)(2,1)S(1)}, bf16[3104,128]{1,0:T(8,128)(2,1)}, u32[]{:S(2)}, u32[]{:S(2)}) collective-permute-start(bf16[3104,128]{1,0:T(8,128)(2,1)S(1)} %collective-permute-done.1.refs_5_), channel_id=1, source_target_pairs={{0,288},{32,64},{64,352},{96,128},{128,416},{160,192},{192,480},{2... | collective-permute-start | bytes 2383880 | tf_op jit(solution)/shard_map/ppermute | solution.py:216
  42.8 5.1 %collective-permute-start.4 = (bf16[3104,128]{1,0:T(8,128)(2,1)S(1)}, bf16[3104,128]{1,0:T(8,128)(2,1)}, u32[]{:S(2)}, u32[]{:S(2)}) collective-permute-start(bf16[3104,128]{1,0:T(8,128)(2,1)S(1)} %collective-permute-done.3.refs_6_), channel_id=1, source_target_pairs={{0,224},{32,256},{64,32},{96,320},{128,96},{160,384},{192,160},{22... | collective-permute-start | bytes 2383880 | tf_op jit(solution)/shard_map/ppermute | solution.py:216
  47.9 3.5 %collective-permute-start.9 = (bf16[2080,128]{1,0:T(8,128)(2,1)}, bf16[2080,128]{1,0:T(8,128)(2,1)S(1)}, u32[]{:S(2)}, u32[]{:S(2)}) collective-permute-start(bf16[2080,128]{1,0:T(8,128)(2,1)} %collective-permute-done.5.refs_2_), channel_id=1, source_target_pairs={{0,4},{4,8},{8,12},{12,16},{16,20},{20,24},{24,28},{28,0},{1,5},{5... | collective-permute-start | bytes 1597448 | tf_op jit(solution)/shard_map/ppermute | solution.py:219
  51.4 3.8 %collective-permute-start.10 = (bf16[2080,128]{1,0:T(8,128)(2,1)}, bf16[2080,128]{1,0:T(8,128)(2,1)}, u32[]{:S(2)}, u32[]{:S(2)}) collective-permute-start(bf16[2080,128]{1,0:T(8,128)(2,1)} %collective-permute-done.6.refs_3_), channel_id=1, source_target_pairs={{0,28},{4,0},{8,4},{12,8},{16,12},{20,16},{24,20},{28,24},{1,29},{... | collective-permute-start | bytes 1597448 | tf_op jit(solution)/shard_map/ppermute | solution.py:219
  55.4 8.2 %collective-permute-done.9.refs_1_ = bf16[2080,128]{1,0:T(8,128)(2,1)S(1)} collective-permute-done((bf16[2080,128]{1,0:T(8,128)(2,1)}, bf16[2080,128]{1,0:T(8,128)(2,1)S(1)}, u32[]{:S(2)}, u32[]{:S(2)}) %collective-permute-start.9) | collective-permute-done | bytes 532512 | tf_op jit(solution)/shard_map/ppermute | solution.py:219
  63.6 1.9 %collective-permute-start.11 = (bf16[2080,128]{1,0:T(8,128)(2,1)S(1)}, bf16[2080,128]{1,0:T(8,128)(2,1)S(1)}, u32[]{:S(2)}, u32[]{:S(2)}) collective-permute-start(bf16[2080,128]{1,0:T(8,128)(2,1)S(1)} %collective-permute-done.9.refs_1_), channel_id=1, source_target_pairs={{0,4},{4,8},{8,12},{12,16},{16,20},{20,24},{24,28},{28,0},{1,5},{5... | collective-permute-start | bytes 1597448 | tf_op jit(solution)/shard_map/ppermute | solution.py:219
  65.6 5.1 %collective-permute-start.13 = (bf16[2080,128]{1,0:T(8,128)(2,1)}, bf16[2080,128]{1,0:T(8,128)(2,1)S(1)}, u32[]{:S(2)}, u32[]{:S(2)}) collective-permute-start(bf16[2080,128]{1,0:T(8,128)(2,1)} %collective-permute-done.10.refs_2_), channel_id=1, source_target_pairs={{0,28},{4,0},{8,4},{12,8},{16,12},{20,16},{24,20},{28,24},{1,29},{... | collective-permute-start | bytes 1597448 | tf_op jit(solution)/shard_map/ppermute | solution.py:219
  70.7 4.1 %shard_map.64 = (f32[8,128,768]{2,1,0:T(8,128)S(1)}, bf16[8,2080,128]{2,1,0:T(8,128)(2,1)S(1)}, bf16[8,3104,128]{2,1,0:T(8,128)(2,1)S(1)}, s32[8,128]{1,0:T(8,128)S(1)}) custom-call(s32[19]{0:T(128)S(1)} %concatenate.29.refs_0_, bf16[2080,128]{1,0:T(8,128)(2,1)S(1)} %fusion.9.refs_1_, bf16[2080,128]{1,0:T(8,128)(2,1)} %collective-permute-done.5.refs_2_, ...), custom_call_target="tpu_custom_call" | custom-call | flops 805306368 | bytes 1048576 | tf_op jit(solution)/shard_map/pallas_call | solution.py:135
  74.9 1.9 %collective-permute-start.7 = (bf16[3104,128]{1,0:T(8,128)(2,1)}, bf16[3104,128]{1,0:T(8,128)(2,1)S(1)}, u32[]{:S(2)}, u32[]{:S(2)}) collective-permute-start(bf16[3104,128]{1,0:T(8,128)(2,1)} %collective-permute-done.2.refs_3_), channel_id=1, source_target_pairs={{0,288},{32,64},{64,352},{96,128},{128,416},{160,192},{192,480},{2... | collective-permute-start | bytes 2383880 | tf_op jit(solution)/shard_map/ppermute | solution.py:216
  76.8 5.1 %collective-permute-start.8 = (bf16[3104,128]{1,0:T(8,128)(2,1)}, bf16[3104,128]{1,0:T(8,128)(2,1)S(1)}, u32[]{:S(2)}, u32[]{:S(2)}) collective-permute-start(bf16[3104,128]{1,0:T(8,128)(2,1)} %collective-permute-done.4.refs_4_), channel_id=1, source_target_pairs={{0,224},{32,256},{64,32},{96,320},{128,96},{160,384},{192,160},{22... | collective-permute-start | bytes 2383880 | tf_op jit(solution)/shard_map/ppermute | solution.py:216
  82.0 1.9 %collective-permute-start.12 = (bf16[1040,128]{1,0:T(8,128)(2,1)S(1)}, bf16[1040,128]{1,0:T(8,128)(2,1)S(1)}, u32[]{:S(2)}, u32[]{:S(2)}) collective-permute-start(bf16[1040,128]{1,0:T(8,128)(2,1)S(1)} %slice.152), channel_id=1, source_target_pairs={{0,4},{4,8},{8,12},{12,16},{16,20},{20,24},{24,28},{28,0},{1,5},{5... | collective-permute-start | bytes 798728 | tf_op jit(solution)/shard_map/ppermute | solution.py:219
  83.9 5.1 %collective-permute-start.14 = (bf16[1040,128]{1,0:T(8,128)(2,1)S(1)}, bf16[1040,128]{1,0:T(8,128)(2,1)S(1)}, u32[]{:S(2)}, u32[]{:S(2)}) collective-permute-start(bf16[1040,128]{1,0:T(8,128)(2,1)S(1)} %slice.153), channel_id=1, source_target_pairs={{0,28},{4,0},{8,4},{12,8},{16,12},{20,16},{24,20},{28,24},{1,29},{... | collective-permute-start | bytes 798728 | tf_op jit(solution)/shard_map/ppermute | solution.py:219
  89.1 3.8 %shard_map.65 = (f32[8,128,768]{2,1,0:T(8,128)S(1)}, bf16[8,2080,128]{2,1,0:T(8,128)(2,1)S(1)}, bf16[8,3104,128]{2,1,0:T(8,128)(2,1)S(1)}, s32[8,128]{1,0:T(8,128)S(1)}) custom-call(s32[19]{0:T(128)S(1)} %concatenate.29.refs_0_, bf16[2080,128]{1,0:T(8,128)(2,1)S(1)} %collective-permute-done.9.refs_1_, ...), custom_call_target="tpu_custom_call", output_to_operand_aliasing={{0}: (5, {}), {1}: (6, {}), {2}: (7, {})} | custom-call | flops 805306368 | bytes 1048576 | tf_op jit(solution)/shard_map/pallas_call | solution.py:135
  96.2 1.9 %collective-permute-start.15 = (bf16[1552,128]{1,0:T(8,128)(2,1)S(1)}, bf16[1552,128]{1,0:T(8,128)(2,1)S(1)}, u32[]{:S(2)}, u32[]{:S(2)}) collective-permute-start(bf16[1552,128]{1,0:T(8,128)(2,1)S(1)} %slice.136), channel_id=1, source_target_pairs={{0,288},{32,64},{64,352},{96,128},{128,416},{160,192},{192,480},{2... | collective-permute-start | bytes 1191944 | tf_op jit(solution)/shard_map/ppermute | solution.py:216
  98.2 5.2 %collective-permute-start.16 = (bf16[1552,128]{1,0:T(8,128)(2,1)S(1)}, bf16[1552,128]{1,0:T(8,128)(2,1)S(1)}, u32[]{:S(2)}, u32[]{:S(2)}) collective-permute-start(bf16[1552,128]{1,0:T(8,128)(2,1)S(1)} %slice.137), channel_id=1, source_target_pairs={{0,224},{32,256},{64,32},{96,320},{128,96},{160,384},{192,160},{22... | collective-permute-start | bytes 1191944 | tf_op jit(solution)/shard_map/ppermute | solution.py:216
  103.3 5.2 %shard_map.66 = (f32[8,128,768]{2,1,0:T(8,128)S(1)}, bf16[8,2080,128]{2,1,0:T(8,128)(2,1)S(1)}, bf16[8,3104,128]{2,1,0:T(8,128)(2,1)S(1)}, s32[8,128]{1,0:T(8,128)}) custom-call(s32[19]{0:T(128)S(1)} %concatenate.29.refs_0_, bf16[2080,128]{1,0:T(8,128)(2,1)S(1)} %collective-permute-done.11.refs_1_, ...), custom_call_target="tpu_custom_call", output_to_operand_aliasing={{0}: (7, {}), {1}: (8, {}), {2}: (9, {})} | custom-call | flops 805306368 | bytes 1048576 | tf_op jit(solution)/shard_map/pallas_call | solution.py:135
  108.8 3.0 %shard_map.67 = (f32[8,128,768]{2,1,0:T(8,128)S(1)}, bf16[8,2080,128]{2,1,0:T(8,128)(2,1)S(1)}, bf16[8,3104,128]{2,1,0:T(8,128)(2,1)S(1)}, s32[8,128]{1,0:T(8,128)}) custom-call(s32[19]{0:T(128)S(1)} %concatenate.29.refs_0_, bf16[1552,128]{1,0:T(8,128)(2,1)S(1)} %collective-permute-done.15.refs_1_, ...), custom_call_target="tpu_custom_call", output_to_operand_aliasing={{0}: (3, {}), {1}: (4, {}), {2}: (5, {})} | custom-call | flops 805306368 | bytes 1048576 | tf_op jit(solution)/shard_map/pallas_call | solution.py:135
  111.9 1.9 %collective-permute-start.17 = (f32[4,128,768]{2,1,0:T(8,128)S(1)}, f32[4,128,768]{2,1,0:T(8,128)S(1)}, u32[]{:S(2)}, u32[]{:S(2)}) collective-permute-start(f32[4,128,768]{2,1,0:T(8,128)S(1)} %slice.139), channel_id=1, source_target_pairs={{0,1},{1,0},{2,3},{3,2},{4,5},{5,4},{6,7},{7,6},{8,9},{9,8},{10,11... | collective-permute-start | bytes 4718600 | tf_op jit(solution)/shard_map/ppermute | solution.py:238
  113.8 3.4 %collective-permute-done.17 = f32[4,128,768]{2,1,0:T(8,128)S(1)} collective-permute-done((f32[4,128,768]{2,1,0:T(8,128)S(1)}, f32[4,128,768]{2,1,0:T(8,128)S(1)}, u32[]{:S(2)}, u32[]{:S(2)}) %collective-permute-start.17) | collective-permute-done | bytes 1572896 | tf_op jit(solution)/shard_map/ppermute | solution.py:238
  118.0 3.3 %collective-permute-start.18 = (s16[128,896]{1,0:T(8,128)(2,1)S(1)}, s16[128,896]{1,0:T(8,128)(2,1)S(1)}, u32[]{:S(2)}, u32[]{:S(2)}) collective-permute-start(s16[128,896]{1,0:T(8,128)(2,1)S(1)} %pad_add_fusion), channel_id=1, source_target_pairs={{0,2},{2,0},{256,258},{258,256},{1,3},{3,1},{257,259},{259,257},{4... | collective-permute-start | bytes 688136 | tf_op jit(solution)/shard_map/ppermute | solution.py:242
  121.4 3.8 %collective-permute-start.19 = (s16[128,896]{1,0:T(8,128)(2,1)S(1)}, s16[128,896]{1,0:T(8,128)(2,1)S(1)}, u32[]{:S(2)}, u32[]{:S(2)}) collective-permute-start(s16[128,896]{1,0:T(8,128)(2,1)S(1)} %pad_add_fusion.1), channel_id=1, source_target_pairs={{0,256},{2,258},{256,2},{258,0},{1,257},{3,259},{257,3},{259,1},{4... | collective-permute-start | bytes 688136 | tf_op jit(solution)/shard_map/ppermute | solution.py:242
  125.3 2.1 %collective-permute-start.20 = (s16[128,896]{1,0:T(8,128)(2,1)S(1)}, s16[128,896]{1,0:T(8,128)(2,1)S(1)}, u32[]{:S(2)}, u32[]{:S(2)}) collective-permute-start(s16[128,896]{1,0:T(8,128)(2,1)S(1)} %pad_add_fusion.2), channel_id=1, source_target_pairs={{0,258},{2,256},{256,0},{258,2},{1,259},{3,257},{257,1},{259,3},{4... | collective-permute-start | bytes 688136 | tf_op jit(solution)/shard_map/ppermute | solution.py:242
  127.4 1.6 %collective-permute-done.18 = s16[128,896]{1,0:T(8,128)(2,1)S(1)} collective-permute-done((s16[128,896]{1,0:T(8,128)(2,1)S(1)}, s16[128,896]{1,0:T(8,128)(2,1)S(1)}, u32[]{:S(2)}, u32[]{:S(2)}) %collective-permute-start.18) | collective-permute-done | bytes 229408 | tf_op jit(solution)/shard_map/ppermute | solution.py:242
  129.2 2.4 %collective-permute-done.19 = s16[128,896]{1,0:T(8,128)(2,1)S(1)} collective-permute-done((s16[128,896]{1,0:T(8,128)(2,1)S(1)}, s16[128,896]{1,0:T(8,128)(2,1)S(1)}, u32[]{:S(2)}, u32[]{:S(2)}) %collective-permute-start.19) | collective-permute-done | bytes 229408 | tf_op jit(solution)/shard_map/ppermute | solution.py:242
  131.7 3.9 %collective-permute-done.20 = s16[128,896]{1,0:T(8,128)(2,1)S(1)} collective-permute-done((s16[128,896]{1,0:T(8,128)(2,1)S(1)}, s16[128,896]{1,0:T(8,128)(2,1)S(1)}, u32[]{:S(2)}, u32[]{:S(2)}) %collective-permute-start.20) | collective-permute-done | bytes 229408 | tf_op jit(solution)/shard_map/ppermute | solution.py:242
  (59 shorter events, 9.9 us)
Async XLA Ops:
  0.0 5.8 %copy-start = (bf16[1,8,1,3,128,128]{5,4,3,2,1,0:T(8,128)(2,1)S(1)}, bf16[1,8,1,3,128,128]{5,4,3,2,1,0:T(8,128)(2,1)}, u32[]{:S(2)}) copy-start(bf16[1,8,1,3,128,128]{5,4,3,2,1,0:T(8,128)(2,1)} %param.16) | copy-start | bytes 2359300
  0.0 5.8 %copy-start.1 = (s32[1,8,1,3]{1,2,3,0:T(1,128)S(1)}, s32[1,8,1,3]{1,2,3,0:T(1,128)}, u32[]{:S(2)}) copy-start(s32[1,8,1,3]{1,2,3,0:T(1,128)} %param.17) | copy-start | bytes 292
  3.0 10.0 %collective-permute-start = (bf16[1040,128]{1,0:T(8,128)(2,1)S(1)}, bf16[1040,128]{1,0:T(8,128)(2,1)S(1)}, u32[]{:S(2)}, u32[]{:S(2)}) collective-permute-start(bf16[1040,128]{1,0:T(8,128)(2,1)S(1)} %fusion.14), channel_id=1, source_target_pairs={{0,256},{256,0},{1,257},{257,1},{2,258},{258,2},{3,259},{259,3},{4... | collective-permute-start | bytes 798728 | tf_op jit(solution)/shard_map/ppermute | solution.py:190
  5.9 49.4 %copy-start.2 = (s32[8]{0:T(128)S(1)}, s32[8]{0:T(128)}, u32[]{:S(2)}) copy-start(s32[8]{0:T(128)} %constant.238.clone) | copy-start | bytes 100
  5.9 49.4 %copy-start.3 = (s32[8]{0:T(128)S(1)}, s32[8]{0:T(128)}, u32[]{:S(2)}) copy-start(s32[8]{0:T(128)} %constant.239.clone) | copy-start | bytes 100
  13.1 27.8 %collective-permute-start.1 = (bf16[3104,128]{1,0:T(8,128)(2,1)S(1)}, bf16[3104,128]{1,0:T(8,128)(2,1)S(1)}, u32[]{:S(2)}, u32[]{:S(2)}) collective-permute-start(bf16[3104,128]{1,0:T(8,128)(2,1)S(1)} %fusion.7.refs_4_), channel_id=1, source_target_pairs={{0,288},{32,64},{64,352},{96,128},{128,416},{160,192},{192,480},{2... | collective-permute-start | bytes 2383880 | tf_op jit(solution)/shard_map/ppermute | solution.py:216
  17.6 25.2 %collective-permute-start.3 = (bf16[3104,128]{1,0:T(8,128)(2,1)S(1)}, bf16[3104,128]{1,0:T(8,128)(2,1)S(1)}, u32[]{:S(2)}, u32[]{:S(2)}) collective-permute-start(bf16[3104,128]{1,0:T(8,128)(2,1)S(1)} %fusion.7.refs_4_), channel_id=1, source_target_pairs={{0,224},{32,256},{64,32},{96,320},{128,96},{160,384},{192,160},{22... | collective-permute-start | bytes 2383880 | tf_op jit(solution)/shard_map/ppermute | solution.py:216
  26.0 21.9 %collective-permute-start.5 = (bf16[2080,128]{1,0:T(8,128)(2,1)S(1)}, bf16[2080,128]{1,0:T(8,128)(2,1)}, u32[]{:S(2)}, u32[]{:S(2)}) collective-permute-start(bf16[2080,128]{1,0:T(8,128)(2,1)S(1)} %fusion.9.refs_1_), channel_id=1, source_target_pairs={{0,4},{4,8},{8,12},{12,16},{16,20},{20,24},{24,28},{28,0},{1,5},{5... | collective-permute-start | bytes 1597448 | tf_op jit(solution)/shard_map/ppermute | solution.py:219
  29.5 21.9 %collective-permute-start.6 = (bf16[2080,128]{1,0:T(8,128)(2,1)S(1)}, bf16[2080,128]{1,0:T(8,128)(2,1)}, u32[]{:S(2)}, u32[]{:S(2)}) collective-permute-start(bf16[2080,128]{1,0:T(8,128)(2,1)S(1)} %fusion.9.refs_1_), channel_id=1, source_target_pairs={{0,28},{4,0},{8,4},{12,8},{16,12},{20,16},{24,20},{28,24},{1,29},{... | collective-permute-start | bytes 1597448 | tf_op jit(solution)/shard_map/ppermute | solution.py:219
  40.8 34.0 %collective-permute-start.2 = (bf16[3104,128]{1,0:T(8,128)(2,1)S(1)}, bf16[3104,128]{1,0:T(8,128)(2,1)}, u32[]{:S(2)}, u32[]{:S(2)}) collective-permute-start(bf16[3104,128]{1,0:T(8,128)(2,1)S(1)} %collective-permute-done.1.refs_5_), channel_id=1, source_target_pairs={{0,288},{32,64},{64,352},{96,128},{128,416},{160,192},{192,480},{2... | collective-permute-start | bytes 2383880 | tf_op jit(solution)/shard_map/ppermute | solution.py:216
  42.8 32.1 %collective-permute-start.4 = (bf16[3104,128]{1,0:T(8,128)(2,1)S(1)}, bf16[3104,128]{1,0:T(8,128)(2,1)}, u32[]{:S(2)}, u32[]{:S(2)}) collective-permute-start(bf16[3104,128]{1,0:T(8,128)(2,1)S(1)} %collective-permute-done.3.refs_6_), channel_id=1, source_target_pairs={{0,224},{32,256},{64,32},{96,320},{128,96},{160,384},{192,160},{22... | collective-permute-start | bytes 2383880 | tf_op jit(solution)/shard_map/ppermute | solution.py:216
  47.9 15.7 %collective-permute-start.9 = (bf16[2080,128]{1,0:T(8,128)(2,1)}, bf16[2080,128]{1,0:T(8,128)(2,1)S(1)}, u32[]{:S(2)}, u32[]{:S(2)}) collective-permute-start(bf16[2080,128]{1,0:T(8,128)(2,1)} %collective-permute-done.5.refs_2_), channel_id=1, source_target_pairs={{0,4},{4,8},{8,12},{12,16},{16,20},{20,24},{24,28},{28,0},{1,5},{5... | collective-permute-start | bytes 1597448 | tf_op jit(solution)/shard_map/ppermute | solution.py:219
  51.4 14.1 %collective-permute-start.10 = (bf16[2080,128]{1,0:T(8,128)(2,1)}, bf16[2080,128]{1,0:T(8,128)(2,1)}, u32[]{:S(2)}, u32[]{:S(2)}) collective-permute-start(bf16[2080,128]{1,0:T(8,128)(2,1)} %collective-permute-done.6.refs_3_), channel_id=1, source_target_pairs={{0,28},{4,0},{8,4},{12,8},{16,12},{20,16},{24,20},{28,24},{1,29},{... | collective-permute-start | bytes 1597448 | tf_op jit(solution)/shard_map/ppermute | solution.py:219
  63.6 18.3 %collective-permute-start.11 = (bf16[2080,128]{1,0:T(8,128)(2,1)S(1)}, bf16[2080,128]{1,0:T(8,128)(2,1)S(1)}, u32[]{:S(2)}, u32[]{:S(2)}) collective-permute-start(bf16[2080,128]{1,0:T(8,128)(2,1)S(1)} %collective-permute-done.9.refs_1_), channel_id=1, source_target_pairs={{0,4},{4,8},{8,12},{12,16},{16,20},{20,24},{24,28},{28,0},{1,5},{5... | collective-permute-start | bytes 1597448 | tf_op jit(solution)/shard_map/ppermute | solution.py:219
  65.6 18.3 %collective-permute-start.13 = (bf16[2080,128]{1,0:T(8,128)(2,1)}, bf16[2080,128]{1,0:T(8,128)(2,1)S(1)}, u32[]{:S(2)}, u32[]{:S(2)}) collective-permute-start(bf16[2080,128]{1,0:T(8,128)(2,1)} %collective-permute-done.10.refs_2_), channel_id=1, source_target_pairs={{0,28},{4,0},{8,4},{12,8},{16,12},{20,16},{24,20},{28,24},{1,29},{... | collective-permute-start | bytes 1597448 | tf_op jit(solution)/shard_map/ppermute | solution.py:219
  74.9 19.7 %collective-permute-start.7 = (bf16[3104,128]{1,0:T(8,128)(2,1)}, bf16[3104,128]{1,0:T(8,128)(2,1)S(1)}, u32[]{:S(2)}, u32[]{:S(2)}) collective-permute-start(bf16[3104,128]{1,0:T(8,128)(2,1)} %collective-permute-done.2.refs_3_), channel_id=1, source_target_pairs={{0,288},{32,64},{64,352},{96,128},{128,416},{160,192},{192,480},{2... | collective-permute-start | bytes 2383880 | tf_op jit(solution)/shard_map/ppermute | solution.py:216
  76.8 19.4 %collective-permute-start.8 = (bf16[3104,128]{1,0:T(8,128)(2,1)}, bf16[3104,128]{1,0:T(8,128)(2,1)S(1)}, u32[]{:S(2)}, u32[]{:S(2)}) collective-permute-start(bf16[3104,128]{1,0:T(8,128)(2,1)} %collective-permute-done.4.refs_4_), channel_id=1, source_target_pairs={{0,224},{32,256},{64,32},{96,320},{128,96},{160,384},{192,160},{22... | collective-permute-start | bytes 2383880 | tf_op jit(solution)/shard_map/ppermute | solution.py:216
  82.0 10.9 %collective-permute-start.12 = (bf16[1040,128]{1,0:T(8,128)(2,1)S(1)}, bf16[1040,128]{1,0:T(8,128)(2,1)S(1)}, u32[]{:S(2)}, u32[]{:S(2)}) collective-permute-start(bf16[1040,128]{1,0:T(8,128)(2,1)S(1)} %slice.152), channel_id=1, source_target_pairs={{0,4},{4,8},{8,12},{12,16},{16,20},{20,24},{24,28},{28,0},{1,5},{5... | collective-permute-start | bytes 798728 | tf_op jit(solution)/shard_map/ppermute | solution.py:219
  83.9 9.1 %collective-permute-start.14 = (bf16[1040,128]{1,0:T(8,128)(2,1)S(1)}, bf16[1040,128]{1,0:T(8,128)(2,1)S(1)}, u32[]{:S(2)}, u32[]{:S(2)}) collective-permute-start(bf16[1040,128]{1,0:T(8,128)(2,1)S(1)} %slice.153), channel_id=1, source_target_pairs={{0,28},{4,0},{8,4},{12,8},{16,12},{20,16},{24,20},{28,24},{1,29},{... | collective-permute-start | bytes 798728 | tf_op jit(solution)/shard_map/ppermute | solution.py:219
  96.2 12.3 %collective-permute-start.15 = (bf16[1552,128]{1,0:T(8,128)(2,1)S(1)}, bf16[1552,128]{1,0:T(8,128)(2,1)S(1)}, u32[]{:S(2)}, u32[]{:S(2)}) collective-permute-start(bf16[1552,128]{1,0:T(8,128)(2,1)S(1)} %slice.136), channel_id=1, source_target_pairs={{0,288},{32,64},{64,352},{96,128},{128,416},{160,192},{192,480},{2... | collective-permute-start | bytes 1191944 | tf_op jit(solution)/shard_map/ppermute | solution.py:216
  98.2 10.6 %collective-permute-start.16 = (bf16[1552,128]{1,0:T(8,128)(2,1)S(1)}, bf16[1552,128]{1,0:T(8,128)(2,1)S(1)}, u32[]{:S(2)}, u32[]{:S(2)}) collective-permute-start(bf16[1552,128]{1,0:T(8,128)(2,1)S(1)} %slice.137), channel_id=1, source_target_pairs={{0,224},{32,256},{64,32},{96,320},{128,96},{160,384},{192,160},{22... | collective-permute-start | bytes 1191944 | tf_op jit(solution)/shard_map/ppermute | solution.py:216
  111.9 5.3 %collective-permute-start.17 = (f32[4,128,768]{2,1,0:T(8,128)S(1)}, f32[4,128,768]{2,1,0:T(8,128)S(1)}, u32[]{:S(2)}, u32[]{:S(2)}) collective-permute-start(f32[4,128,768]{2,1,0:T(8,128)S(1)} %slice.139), channel_id=1, source_target_pairs={{0,1},{1,0},{2,3},{3,2},{4,5},{5,4},{6,7},{7,6},{8,9},{9,8},{10,11... | collective-permute-start | bytes 4718600 | tf_op jit(solution)/shard_map/ppermute | solution.py:238
  118.0 11.0 %collective-permute-start.18 = (s16[128,896]{1,0:T(8,128)(2,1)S(1)}, s16[128,896]{1,0:T(8,128)(2,1)S(1)}, u32[]{:S(2)}, u32[]{:S(2)}) collective-permute-start(s16[128,896]{1,0:T(8,128)(2,1)S(1)} %pad_add_fusion), channel_id=1, source_target_pairs={{0,2},{2,0},{256,258},{258,256},{1,3},{3,1},{257,259},{259,257},{4... | collective-permute-start | bytes 688136 | tf_op jit(solution)/shard_map/ppermute | solution.py:242
  121.4 10.1 %collective-permute-start.19 = (s16[128,896]{1,0:T(8,128)(2,1)S(1)}, s16[128,896]{1,0:T(8,128)(2,1)S(1)}, u32[]{:S(2)}, u32[]{:S(2)}) collective-permute-start(s16[128,896]{1,0:T(8,128)(2,1)S(1)} %pad_add_fusion.1), channel_id=1, source_target_pairs={{0,256},{2,258},{256,2},{258,0},{1,257},{3,259},{257,3},{259,1},{4... | collective-permute-start | bytes 688136 | tf_op jit(solution)/shard_map/ppermute | solution.py:242
  125.3 10.2 %collective-permute-start.20 = (s16[128,896]{1,0:T(8,128)(2,1)S(1)}, s16[128,896]{1,0:T(8,128)(2,1)S(1)}, u32[]{:S(2)}, u32[]{:S(2)}) collective-permute-start(s16[128,896]{1,0:T(8,128)(2,1)S(1)} %pad_add_fusion.2), channel_id=1, source_target_pairs={{0,258},{2,256},{256,0},{258,2},{1,259},{3,257},{257,1},{259,3},{4... | collective-permute-start | bytes 688136 | tf_op jit(solution)/shard_map/ppermute | solution.py:242

commit v7 on v6

--- a/solution.py
+++ b/solution.py
@@ -223,9 +223,9 @@
     rights += step_z(*rights[1:3])
     lefts += step_y(*lefts[1:3])
     *state, token = run_stage(1, meta, listed(lefts, 0, 3), listed(rights, 0, 3), 3, 3, [])
-    up, down, token = lax.optimization_barrier((*rights[3:5], token))
-    rights += step_z(up, down)
-    lefts += step_y(*lefts[3:5])
+    fore, back, token = lax.optimization_barrier((*lefts[3:5], token))
+    rights += step_z(*rights[3:5])
+    lefts += step_y(fore, back)
     *state, token = run_stage(2, meta, listed(lefts, 3, 5), listed(rights, 3, 5), 5, 5, state, token)
     last_left = step_y(lefts[5][:LPART], lefts[6][LPART:])
     up, down, token, *last_left = lax.optimization_barrier((*rights[5:7], token, *last_left))

time: 137 us -> 138 us (level)
  transfers between devices with their start and end apart: 21 -> 21, of which waited for: 11 -> 12; matrix products, arithmetic and copies ran while one was open for 1% -> 1% of each run, Pallas kernels for 10% -> 10%
where the time goes in v7:
time: 138 us; the launch traced here: 137 us
  starting transfers between devices  77.1 us (56%)
  waiting for transfers between devices  37.3 us (27%)
  Pallas kernels  16 us (12%)
  other arithmetic  3.58 us (3%)
  local copies, waits for them, and re-layouts  2.73 us (2%)
    ppermute x8, starting transfers between devices, step_y(): return (lax.ppermute(fore, 'y', turn(1)), lax.ppermute(back, 'y', turn(-1)))  28.7 us
    ppermute x4, starting transfers between devices, step_z(): lax.ppermute(down, row, ring_pairs(-1))  23.8 us
    pallas_call x4, Pallas kernels, run_stage(): pl.pallas_call(lambda *refs: stage(number, new_left, new_right, slots, ch...  16 us
    ppermute x4, starting transfers between devices, step_z(): lax.ppermute(up, row, ring_pairs(1))  10.3 us
    ppermute x3, starting transfers between devices, per_device(): lax.ppermute(encode(total[step]), ('x_lo', 'x_hi'), chip_pairs(step))  9.69 us
    ppermute x8, waiting for transfers between devices, step_y(): return (lax.ppermute(fore, 'y', turn(1)), lax.ppermute(back, 'y', turn(-1)))  8.95 us
    ppermute x4, waiting for transfers between devices, step_z(): lax.ppermute(up, row, ring_pairs(1))  8.45 us
    ppermute x3, waiting for transfers between devices, per_device(): lax.ppermute(encode(total[step]), ('x_lo', 'x_hi'), chip_pairs(step))  8.02 us
  transfers between devices with their start and end apart: 21, of which 12 were waited for; matrix products, arithmetic and copies ran while one was open for 1% of the time, Pallas kernels for 10%

profile of v7, /device:TPU:6, one launch (start us, length us, event | category | flops | bytes accessed | tf_op | source)
XLA Modules:
  0.0 137.2 jit_solution(16860978648100914957)
XLA Ops:
  3.0 2.7 %collective-permute-start = (bf16[1040,128]{1,0:T(8,128)(2,1)S(1)}, bf16[1040,128]{1,0:T(8,128)(2,1)S(1)}, u32[]{:S(2)}, u32[]{:S(2)}) collective-permute-start(bf16[1040,128]{1,0:T(8,128)(2,1)S(1)} %fusion.14), channel_id=1, source_target_pairs={{0,256},{256,0},{1,257},{257,1},{2,258},{258,2},{3,259},{259,3},{4... | collective-permute-start | bytes 798728 | tf_op jit(solution)/shard_map/ppermute | solution.py:190
  6.4 6.6 %collective-permute-done = bf16[1040,128]{1,0:T(8,128)(2,1)S(1)} collective-permute-done((bf16[1040,128]{1,0:T(8,128)(2,1)S(1)}, bf16[1040,128]{1,0:T(8,128)(2,1)S(1)}, u32[]{:S(2)}, u32[]{:S(2)}) %collective-permute-start) | collective-permute-done | bytes 266272 | tf_op jit(solution)/shard_map/ppermute | solution.py:190
  13.1 4.5 %collective-permute-start.1 = (bf16[3104,128]{1,0:T(8,128)(2,1)S(1)}, bf16[3104,128]{1,0:T(8,128)(2,1)S(1)}, u32[]{:S(2)}, u32[]{:S(2)}) collective-permute-start(bf16[3104,128]{1,0:T(8,128)(2,1)S(1)} %fusion.7.refs_4_), channel_id=1, source_target_pairs={{0,288},{32,64},{64,352},{96,128},{128,416},{160,192},{192,480},{2... | collective-permute-start | bytes 2383880 | tf_op jit(solution)/shard_map/ppermute | solution.py:216
  17.6 8.3 %collective-permute-start.4 = (bf16[3104,128]{1,0:T(8,128)(2,1)S(1)}, bf16[3104,128]{1,0:T(8,128)(2,1)S(1)}, u32[]{:S(2)}, u32[]{:S(2)}) collective-permute-start(bf16[3104,128]{1,0:T(8,128)(2,1)S(1)} %fusion.7.refs_4_), channel_id=1, source_target_pairs={{0,224},{32,256},{64,32},{96,320},{128,96},{160,384},{192,160},{22... | collective-permute-start | bytes 2383880 | tf_op jit(solution)/shard_map/ppermute | solution.py:216
  26.0 5.4 %collective-permute-start.9 = (bf16[2080,128]{1,0:T(8,128)(2,1)S(1)}, bf16[2080,128]{1,0:T(8,128)(2,1)}, u32[]{:S(2)}, u32[]{:S(2)}) collective-permute-start(bf16[2080,128]{1,0:T(8,128)(2,1)S(1)} %fusion.9.refs_1_), channel_id=1, source_target_pairs={{0,28},{4,0},{8,4},{12,8},{16,12},{20,16},{24,20},{28,24},{1,29},{... | collective-permute-start | bytes 1597448 | tf_op jit(solution)/shard_map/ppermute | solution.py:219
  31.4 1.9 %collective-permute-start.7 = (bf16[2080,128]{1,0:T(8,128)(2,1)S(1)}, bf16[2080,128]{1,0:T(8,128)(2,1)}, u32[]{:S(2)}, u32[]{:S(2)}) collective-permute-start(bf16[2080,128]{1,0:T(8,128)(2,1)S(1)} %fusion.9.refs_1_), channel_id=1, source_target_pairs={{0,4},{4,8},{8,12},{12,16},{16,20},{20,24},{24,28},{28,0},{1,5},{5... | collective-permute-start | bytes 1597448 | tf_op jit(solution)/shard_map/ppermute | solution.py:219
  33.3 7.5 %collective-permute-done.1.refs_5_ = bf16[3104,128]{1,0:T(8,128)(2,1)S(1)} collective-permute-done((bf16[3104,128]{1,0:T(8,128)(2,1)S(1)}, bf16[3104,128]{1,0:T(8,128)(2,1)S(1)}, u32[]{:S(2)}, u32[]{:S(2)}) %collective-permute-start.1) | collective-permute-done | bytes 794656 | tf_op jit(solution)/shard_map/ppermute | solution.py:216
  40.8 1.9 %collective-permute-start.2 = (bf16[3104,128]{1,0:T(8,128)(2,1)S(1)}, bf16[3104,128]{1,0:T(8,128)(2,1)}, u32[]{:S(2)}, u32[]{:S(2)}) collective-permute-start(bf16[3104,128]{1,0:T(8,128)(2,1)S(1)} %collective-permute-done.1.refs_5_), channel_id=1, source_target_pairs={{0,288},{32,64},{64,352},{96,128},{128,416},{160,192},{192,480},{2... | collective-permute-start | bytes 2383880 | tf_op jit(solution)/shard_map/ppermute | solution.py:216
  42.8 5.1 %collective-permute-start.5 = (bf16[3104,128]{1,0:T(8,128)(2,1)S(1)}, bf16[3104,128]{1,0:T(8,128)(2,1)}, u32[]{:S(2)}, u32[]{:S(2)}) collective-permute-start(bf16[3104,128]{1,0:T(8,128)(2,1)S(1)} %collective-permute-done.4.refs_6_), channel_id=1, source_target_pairs={{0,224},{32,256},{64,32},{96,320},{128,96},{160,384},{192,160},{22... | collective-permute-start | bytes 2383880 | tf_op jit(solution)/shard_map/ppermute | solution.py:216
  47.9 5.4 %collective-permute-start.10 = (bf16[2080,128]{1,0:T(8,128)(2,1)}, bf16[2080,128]{1,0:T(8,128)(2,1)S(1)}, u32[]{:S(2)}, u32[]{:S(2)}) collective-permute-start(bf16[2080,128]{1,0:T(8,128)(2,1)} %collective-permute-done.9.refs_3_), channel_id=1, source_target_pairs={{0,28},{4,0},{8,4},{12,8},{16,12},{20,16},{24,20},{28,24},{1,29},{... | collective-permute-start | bytes 1597448 | tf_op jit(solution)/shard_map/ppermute | solution.py:219
  53.3 1.9 %collective-permute-start.8 = (bf16[2080,128]{1,0:T(8,128)(2,1)}, bf16[2080,128]{1,0:T(8,128)(2,1)}, u32[]{:S(2)}, u32[]{:S(2)}) collective-permute-start(bf16[2080,128]{1,0:T(8,128)(2,1)} %collective-permute-done.7.refs_2_), channel_id=1, source_target_pairs={{0,4},{4,8},{8,12},{12,16},{16,20},{20,24},{24,28},{28,0},{1,5},{5... | collective-permute-start | bytes 1597448 | tf_op jit(solution)/shard_map/ppermute | solution.py:219
  55.4 4.1 %shard_map.64 = (f32[8,128,768]{2,1,0:T(8,128)S(1)}, bf16[8,2080,128]{2,1,0:T(8,128)(2,1)S(1)}, bf16[8,3104,128]{2,1,0:T(8,128)(2,1)S(1)}, s32[8,128]{1,0:T(8,128)S(1)}) custom-call(s32[19]{0:T(128)S(1)} %concatenate.29.refs_0_, bf16[2080,128]{1,0:T(8,128)(2,1)S(1)} %fusion.9.refs_1_, bf16[2080,128]{1,0:T(8,128)(2,1)} %collective-permute-done.7.refs_2_, ...), custom_call_target="tpu_custom_call" | custom-call | flops 805306368 | bytes 1048576 | tf_op jit(solution)/shard_map/pallas_call | solution.py:135
  59.5 3.5 %collective-permute-done.10.refs_2_ = bf16[2080,128]{1,0:T(8,128)(2,1)S(1)} collective-permute-done((bf16[2080,128]{1,0:T(8,128)(2,1)}, bf16[2080,128]{1,0:T(8,128)(2,1)S(1)}, u32[]{:S(2)}, u32[]{:S(2)}) %collective-permute-start.10) | collective-permute-done | bytes 532512 | tf_op jit(solution)/shard_map/ppermute | solution.py:219
  63.0 5.3 %collective-permute-done.8.refs_1_ = bf16[2080,128]{1,0:T(8,128)(2,1)} collective-permute-done((bf16[2080,128]{1,0:T(8,128)(2,1)}, bf16[2080,128]{1,0:T(8,128)(2,1)}, u32[]{:S(2)}, u32[]{:S(2)}) %collective-permute-start.8) | collective-permute-done | bytes 532512 | tf_op jit(solution)/shard_map/ppermute | solution.py:219
  68.3 1.9 %collective-permute-start.11 = (bf16[2080,128]{1,0:T(8,128)(2,1)}, bf16[2080,128]{1,0:T(8,128)(2,1)S(1)}, u32[]{:S(2)}, u32[]{:S(2)}) collective-permute-start(bf16[2080,128]{1,0:T(8,128)(2,1)} %collective-permute-done.8.refs_1_), channel_id=1, source_target_pairs={{0,4},{4,8},{8,12},{12,16},{16,20},{20,24},{24,28},{28,0},{1,5},{5... | collective-permute-start | bytes 1597448 | tf_op jit(solution)/shard_map/ppermute | solution.py:219
  70.2 5.1 %collective-permute-start.13 = (bf16[2080,128]{1,0:T(8,128)(2,1)S(1)}, bf16[2080,128]{1,0:T(8,128)(2,1)S(1)}, u32[]{:S(2)}, u32[]{:S(2)}) collective-permute-start(bf16[2080,128]{1,0:T(8,128)(2,1)S(1)} %collective-permute-done.10.refs_2_), channel_id=1, source_target_pairs={{0,28},{4,0},{8,4},{12,8},{16,12},{20,16},{24,20},{28,24},{1,29},{... | collective-permute-start | bytes 1597448 | tf_op jit(solution)/shard_map/ppermute | solution.py:219
  75.4 1.9 %collective-permute-start.3 = (bf16[3104,128]{1,0:T(8,128)(2,1)}, bf16[3104,128]{1,0:T(8,128)(2,1)S(1)}, u32[]{:S(2)}, u32[]{:S(2)}) collective-permute-start(bf16[3104,128]{1,0:T(8,128)(2,1)} %collective-permute-done.2.refs_3_), channel_id=1, source_target_pairs={{0,288},{32,64},{64,352},{96,128},{128,416},{160,192},{192,480},{2... | collective-permute-start | bytes 2383880 | tf_op jit(solution)/shard_map/ppermute | solution.py:216
  77.3 5.1 %collective-permute-start.6 = (bf16[3104,128]{1,0:T(8,128)(2,1)}, bf16[3104,128]{1,0:T(8,128)(2,1)S(1)}, u32[]{:S(2)}, u32[]{:S(2)}) collective-permute-start(bf16[3104,128]{1,0:T(8,128)(2,1)} %collective-permute-done.5.refs_4_), channel_id=1, source_target_pairs={{0,224},{32,256},{64,32},{96,320},{128,96},{160,384},{192,160},{22... | collective-permute-start | bytes 2383880 | tf_op jit(solution)/shard_map/ppermute | solution.py:216
  82.5 1.9 %collective-permute-start.12 = (bf16[1040,128]{1,0:T(8,128)(2,1)S(1)}, bf16[1040,128]{1,0:T(8,128)(2,1)S(1)}, u32[]{:S(2)}, u32[]{:S(2)}) collective-permute-start(bf16[1040,128]{1,0:T(8,128)(2,1)S(1)} %slice.152), channel_id=1, source_target_pairs={{0,4},{4,8},{8,12},{12,16},{16,20},{20,24},{24,28},{28,0},{1,5},{5... | collective-permute-start | bytes 798728 | tf_op jit(solution)/shard_map/ppermute | solution.py:219
  84.5 5.1 %collective-permute-start.14 = (bf16[1040,128]{1,0:T(8,128)(2,1)S(1)}, bf16[1040,128]{1,0:T(8,128)(2,1)S(1)}, u32[]{:S(2)}, u32[]{:S(2)}) collective-permute-start(bf16[1040,128]{1,0:T(8,128)(2,1)S(1)} %slice.153), channel_id=1, source_target_pairs={{0,28},{4,0},{8,4},{12,8},{16,12},{20,16},{24,20},{28,24},{1,29},{... | collective-permute-start | bytes 798728 | tf_op jit(solution)/shard_map/ppermute | solution.py:219
  89.6 3.8 %shard_map.65 = (f32[8,128,768]{2,1,0:T(8,128)S(1)}, bf16[8,2080,128]{2,1,0:T(8,128)(2,1)S(1)}, bf16[8,3104,128]{2,1,0:T(8,128)(2,1)S(1)}, s32[8,128]{1,0:T(8,128)S(1)}) custom-call(s32[19]{0:T(128)S(1)} %concatenate.29.refs_0_, bf16[2080,128]{1,0:T(8,128)(2,1)} %collective-permute-done.8.refs_1_, ...), custom_call_target="tpu_custom_call", output_to_operand_aliasing={{0}: (5, {}), {1}: (6, {}), {2}: (7, {})} | custom-call | flops 805306368 | bytes 1048576 | tf_op jit(solution)/shard_map/pallas_call | solution.py:135
  96.1 1.9 %collective-permute-start.15 = (bf16[1552,128]{1,0:T(8,128)(2,1)S(1)}, bf16[1552,128]{1,0:T(8,128)(2,1)S(1)}, u32[]{:S(2)}, u32[]{:S(2)}) collective-permute-start(bf16[1552,128]{1,0:T(8,128)(2,1)S(1)} %slice.136), channel_id=1, source_target_pairs={{0,288},{32,64},{64,352},{96,128},{128,416},{160,192},{192,480},{2... | collective-permute-start | bytes 1191944 | tf_op jit(solution)/shard_map/ppermute | solution.py:216
  98.1 5.2 %collective-permute-start.16 = (bf16[1552,128]{1,0:T(8,128)(2,1)S(1)}, bf16[1552,128]{1,0:T(8,128)(2,1)S(1)}, u32[]{:S(2)}, u32[]{:S(2)}) collective-permute-start(bf16[1552,128]{1,0:T(8,128)(2,1)S(1)} %slice.137), channel_id=1, source_target_pairs={{0,224},{32,256},{64,32},{96,320},{128,96},{160,384},{192,160},{22... | collective-permute-start | bytes 1191944 | tf_op jit(solution)/shard_map/ppermute | solution.py:216
  103.2 5.2 %shard_map.66 = (f32[8,128,768]{2,1,0:T(8,128)S(1)}, bf16[8,2080,128]{2,1,0:T(8,128)(2,1)S(1)}, bf16[8,3104,128]{2,1,0:T(8,128)(2,1)S(1)}, s32[8,128]{1,0:T(8,128)}) custom-call(s32[19]{0:T(128)S(1)} %concatenate.29.refs_0_, bf16[2080,128]{1,0:T(8,128)(2,1)S(1)} %collective-permute-done.11.refs_1_, ...), custom_call_target="tpu_custom_call", output_to_operand_aliasing={{0}: (7, {}), {1}: (8, {}), {2}: (9, {})} | custom-call | flops 805306368 | bytes 1048576 | tf_op jit(solution)/shard_map/pallas_call | solution.py:135
  108.7 3.0 %shard_map.67 = (f32[8,128,768]{2,1,0:T(8,128)S(1)}, bf16[8,2080,128]{2,1,0:T(8,128)(2,1)S(1)}, bf16[8,3104,128]{2,1,0:T(8,128)(2,1)S(1)}, s32[8,128]{1,0:T(8,128)}) custom-call(s32[19]{0:T(128)S(1)} %concatenate.29.refs_0_, bf16[1552,128]{1,0:T(8,128)(2,1)S(1)} %collective-permute-done.15.refs_1_, ...), custom_call_target="tpu_custom_call", output_to_operand_aliasing={{0}: (3, {}), {1}: (4, {}), {2}: (5, {})} | custom-call | flops 805306368 | bytes 1048576 | tf_op jit(solution)/shard_map/pallas_call | solution.py:135
  111.8 1.9 %collective-permute-start.17 = (f32[4,128,768]{2,1,0:T(8,128)S(1)}, f32[4,128,768]{2,1,0:T(8,128)S(1)}, u32[]{:S(2)}, u32[]{:S(2)}) collective-permute-start(f32[4,128,768]{2,1,0:T(8,128)S(1)} %slice.139), channel_id=1, source_target_pairs={{0,1},{1,0},{2,3},{3,2},{4,5},{5,4},{6,7},{7,6},{8,9},{9,8},{10,11... | collective-permute-start | bytes 4718600 | tf_op jit(solution)/shard_map/ppermute | solution.py:238
  113.7 3.4 %collective-permute-done.17 = f32[4,128,768]{2,1,0:T(8,128)S(1)} collective-permute-done((f32[4,128,768]{2,1,0:T(8,128)S(1)}, f32[4,128,768]{2,1,0:T(8,128)S(1)}, u32[]{:S(2)}, u32[]{:S(2)}) %collective-permute-start.17) | collective-permute-done | bytes 1572896 | tf_op jit(solution)/shard_map/ppermute | solution.py:238
  117.9 3.3 %collective-permute-start.18 = (s16[128,896]{1,0:T(8,128)(2,1)S(1)}, s16[128,896]{1,0:T(8,128)(2,1)S(1)}, u32[]{:S(2)}, u32[]{:S(2)}) collective-permute-start(s16[128,896]{1,0:T(8,128)(2,1)S(1)} %pad_add_fusion), channel_id=1, source_target_pairs={{0,2},{2,0},{256,258},{258,256},{1,3},{3,1},{257,259},{259,257},{4... | collective-permute-start | bytes 688136 | tf_op jit(solution)/shard_map/ppermute | solution.py:242
  121.3 4.5 %collective-permute-start.19 = (s16[128,896]{1,0:T(8,128)(2,1)S(1)}, s16[128,896]{1,0:T(8,128)(2,1)S(1)}, u32[]{:S(2)}, u32[]{:S(2)}) collective-permute-start(s16[128,896]{1,0:T(8,128)(2,1)S(1)} %pad_add_fusion.1), channel_id=1, source_target_pairs={{0,256},{2,258},{256,2},{258,0},{1,257},{3,259},{257,3},{259,1},{4... | collective-permute-start | bytes 688136 | tf_op jit(solution)/shard_map/ppermute | solution.py:242
  125.9 1.9 %collective-permute-start.20 = (s16[128,896]{1,0:T(8,128)(2,1)S(1)}, s16[128,896]{1,0:T(8,128)(2,1)S(1)}, u32[]{:S(2)}, u32[]{:S(2)}) collective-permute-start(s16[128,896]{1,0:T(8,128)(2,1)S(1)} %pad_add_fusion.2), channel_id=1, source_target_pairs={{0,258},{2,256},{256,0},{258,2},{1,259},{3,257},{257,1},{259,3},{4... | collective-permute-start | bytes 688136 | tf_op jit(solution)/shard_map/ppermute | solution.py:242
  129.0 3.1 %collective-permute-done.19 = s16[128,896]{1,0:T(8,128)(2,1)S(1)} collective-permute-done((s16[128,896]{1,0:T(8,128)(2,1)S(1)}, s16[128,896]{1,0:T(8,128)(2,1)S(1)}, u32[]{:S(2)}, u32[]{:S(2)}) %collective-permute-start.19) | collective-permute-done | bytes 229408 | tf_op jit(solution)/shard_map/ppermute | solution.py:242
  132.2 3.9 %collective-permute-done.20 = s16[128,896]{1,0:T(8,128)(2,1)S(1)} collective-permute-done((s16[128,896]{1,0:T(8,128)(2,1)S(1)}, s16[128,896]{1,0:T(8,128)(2,1)S(1)}, u32[]{:S(2)}, u32[]{:S(2)}) %collective-permute-start.20) | collective-permute-done | bytes 229408 | tf_op jit(solution)/shard_map/ppermute | solution.py:242
  (59 shorter events, 10.3 us)
Async XLA Ops:
  0.0 5.8 %copy-start = (bf16[1,8,1,3,128,128]{5,4,3,2,1,0:T(8,128)(2,1)S(1)}, bf16[1,8,1,3,128,128]{5,4,3,2,1,0:T(8,128)(2,1)}, u32[]{:S(2)}) copy-start(bf16[1,8,1,3,128,128]{5,4,3,2,1,0:T(8,128)(2,1)} %param.16) | copy-start | bytes 2359300
  0.0 5.8 %copy-start.1 = (s32[1,8,1,3]{1,2,3,0:T(1,128)S(1)}, s32[1,8,1,3]{1,2,3,0:T(1,128)}, u32[]{:S(2)}) copy-start(s32[1,8,1,3]{1,2,3,0:T(1,128)} %param.17) | copy-start | bytes 292
  3.0 10.0 %collective-permute-start = (bf16[1040,128]{1,0:T(8,128)(2,1)S(1)}, bf16[1040,128]{1,0:T(8,128)(2,1)S(1)}, u32[]{:S(2)}, u32[]{:S(2)}) collective-permute-start(bf16[1040,128]{1,0:T(8,128)(2,1)S(1)} %fusion.14), channel_id=1, source_target_pairs={{0,256},{256,0},{1,257},{257,1},{2,258},{258,2},{3,259},{259,3},{4... | collective-permute-start | bytes 798728 | tf_op jit(solution)/shard_map/ppermute | solution.py:190
  5.9 49.4 %copy-start.2 = (s32[8]{0:T(128)S(1)}, s32[8]{0:T(128)}, u32[]{:S(2)}) copy-start(s32[8]{0:T(128)} %constant.238.clone) | copy-start | bytes 100
  5.9 49.4 %copy-start.3 = (s32[8]{0:T(128)S(1)}, s32[8]{0:T(128)}, u32[]{:S(2)}) copy-start(s32[8]{0:T(128)} %constant.239.clone) | copy-start | bytes 100
  13.1 27.8 %collective-permute-start.1 = (bf16[3104,128]{1,0:T(8,128)(2,1)S(1)}, bf16[3104,128]{1,0:T(8,128)(2,1)S(1)}, u32[]{:S(2)}, u32[]{:S(2)}) collective-permute-start(bf16[3104,128]{1,0:T(8,128)(2,1)S(1)} %fusion.7.refs_4_), channel_id=1, source_target_pairs={{0,288},{32,64},{64,352},{96,128},{128,416},{160,192},{192,480},{2... | collective-permute-start | bytes 2383880 | tf_op jit(solution)/shard_map/ppermute | solution.py:216
  17.6 25.2 %collective-permute-start.4 = (bf16[3104,128]{1,0:T(8,128)(2,1)S(1)}, bf16[3104,128]{1,0:T(8,128)(2,1)S(1)}, u32[]{:S(2)}, u32[]{:S(2)}) collective-permute-start(bf16[3104,128]{1,0:T(8,128)(2,1)S(1)} %fusion.7.refs_4_), channel_id=1, source_target_pairs={{0,224},{32,256},{64,32},{96,320},{128,96},{160,384},{192,160},{22... | collective-permute-start | bytes 2383880 | tf_op jit(solution)/shard_map/ppermute | solution.py:216
  26.0 21.9 %collective-permute-start.9 = (bf16[2080,128]{1,0:T(8,128)(2,1)S(1)}, bf16[2080,128]{1,0:T(8,128)(2,1)}, u32[]{:S(2)}, u32[]{:S(2)}) collective-permute-start(bf16[2080,128]{1,0:T(8,128)(2,1)S(1)} %fusion.9.refs_1_), channel_id=1, source_target_pairs={{0,28},{4,0},{8,4},{12,8},{16,12},{20,16},{24,20},{28,24},{1,29},{... | collective-permute-start | bytes 1597448 | tf_op jit(solution)/shard_map/ppermute | solution.py:219
  31.4 21.9 %collective-permute-start.7 = (bf16[2080,128]{1,0:T(8,128)(2,1)S(1)}, bf16[2080,128]{1,0:T(8,128)(2,1)}, u32[]{:S(2)}, u32[]{:S(2)}) collective-permute-start(bf16[2080,128]{1,0:T(8,128)(2,1)S(1)} %fusion.9.refs_1_), channel_id=1, source_target_pairs={{0,4},{4,8},{8,12},{12,16},{16,20},{20,24},{24,28},{28,0},{1,5},{5... | collective-permute-start | bytes 1597448 | tf_op jit(solution)/shard_map/ppermute | solution.py:219
  40.8 34.5 %collective-permute-start.2 = (bf16[3104,128]{1,0:T(8,128)(2,1)S(1)}, bf16[3104,128]{1,0:T(8,128)(2,1)}, u32[]{:S(2)}, u32[]{:S(2)}) collective-permute-start(bf16[3104,128]{1,0:T(8,128)(2,1)S(1)} %collective-permute-done.1.refs_5_), channel_id=1, source_target_pairs={{0,288},{32,64},{64,352},{96,128},{128,416},{160,192},{192,480},{2... | collective-permute-start | bytes 2383880 | tf_op jit(solution)/shard_map/ppermute | solution.py:216
  42.8 34.6 %collective-permute-start.5 = (bf16[3104,128]{1,0:T(8,128)(2,1)S(1)}, bf16[3104,128]{1,0:T(8,128)(2,1)}, u32[]{:S(2)}, u32[]{:S(2)}) collective-permute-start(bf16[3104,128]{1,0:T(8,128)(2,1)S(1)} %collective-permute-done.4.refs_6_), channel_id=1, source_target_pairs={{0,224},{32,256},{64,32},{96,320},{128,96},{160,384},{192,160},{22... | collective-permute-start | bytes 2383880 | tf_op jit(solution)/shard_map/ppermute | solution.py:216
  47.9 15.1 %collective-permute-start.10 = (bf16[2080,128]{1,0:T(8,128)(2,1)}, bf16[2080,128]{1,0:T(8,128)(2,1)S(1)}, u32[]{:S(2)}, u32[]{:S(2)}) collective-permute-start(bf16[2080,128]{1,0:T(8,128)(2,1)} %collective-permute-done.9.refs_3_), channel_id=1, source_target_pairs={{0,28},{4,0},{8,4},{12,8},{16,12},{20,16},{24,20},{28,24},{1,29},{... | collective-permute-start | bytes 1597448 | tf_op jit(solution)/shard_map/ppermute | solution.py:219
  53.3 15.0 %collective-permute-start.8 = (bf16[2080,128]{1,0:T(8,128)(2,1)}, bf16[2080,128]{1,0:T(8,128)(2,1)}, u32[]{:S(2)}, u32[]{:S(2)}) collective-permute-start(bf16[2080,128]{1,0:T(8,128)(2,1)} %collective-permute-done.7.refs_2_), channel_id=1, source_target_pairs={{0,4},{4,8},{8,12},{12,16},{16,20},{20,24},{24,28},{28,0},{1,5},{5... | collective-permute-start | bytes 1597448 | tf_op jit(solution)/shard_map/ppermute | solution.py:219
  68.3 14.1 %collective-permute-start.11 = (bf16[2080,128]{1,0:T(8,128)(2,1)}, bf16[2080,128]{1,0:T(8,128)(2,1)S(1)}, u32[]{:S(2)}, u32[]{:S(2)}) collective-permute-start(bf16[2080,128]{1,0:T(8,128)(2,1)} %collective-permute-done.8.refs_1_), channel_id=1, source_target_pairs={{0,4},{4,8},{8,12},{12,16},{16,20},{20,24},{24,28},{28,0},{1,5},{5... | collective-permute-start | bytes 1597448 | tf_op jit(solution)/shard_map/ppermute | solution.py:219
  70.2 14.2 %collective-permute-start.13 = (bf16[2080,128]{1,0:T(8,128)(2,1)S(1)}, bf16[2080,128]{1,0:T(8,128)(2,1)S(1)}, u32[]{:S(2)}, u32[]{:S(2)}) collective-permute-start(bf16[2080,128]{1,0:T(8,128)(2,1)S(1)} %collective-permute-done.10.refs_2_), channel_id=1, source_target_pairs={{0,28},{4,0},{8,4},{12,8},{16,12},{20,16},{24,20},{28,24},{1,29},{... | collective-permute-start | bytes 1597448 | tf_op jit(solution)/shard_map/ppermute | solution.py:219
  75.4 19.0 %collective-permute-start.3 = (bf16[3104,128]{1,0:T(8,128)(2,1)}, bf16[3104,128]{1,0:T(8,128)(2,1)S(1)}, u32[]{:S(2)}, u32[]{:S(2)}) collective-permute-start(bf16[3104,128]{1,0:T(8,128)(2,1)} %collective-permute-done.2.refs_3_), channel_id=1, source_target_pairs={{0,288},{32,64},{64,352},{96,128},{128,416},{160,192},{192,480},{2... | collective-permute-start | bytes 2383880 | tf_op jit(solution)/shard_map/ppermute | solution.py:216
  77.3 18.7 %collective-permute-start.6 = (bf16[3104,128]{1,0:T(8,128)(2,1)}, bf16[3104,128]{1,0:T(8,128)(2,1)S(1)}, u32[]{:S(2)}, u32[]{:S(2)}) collective-permute-start(bf16[3104,128]{1,0:T(8,128)(2,1)} %collective-permute-done.5.refs_4_), channel_id=1, source_target_pairs={{0,224},{32,256},{64,32},{96,320},{128,96},{160,384},{192,160},{22... | collective-permute-start | bytes 2383880 | tf_op jit(solution)/shard_map/ppermute | solution.py:216
  82.5 10.9 %collective-permute-start.12 = (bf16[1040,128]{1,0:T(8,128)(2,1)S(1)}, bf16[1040,128]{1,0:T(8,128)(2,1)S(1)}, u32[]{:S(2)}, u32[]{:S(2)}) collective-permute-start(bf16[1040,128]{1,0:T(8,128)(2,1)S(1)} %slice.152), channel_id=1, source_target_pairs={{0,4},{4,8},{8,12},{12,16},{16,20},{20,24},{24,28},{28,0},{1,5},{5... | collective-permute-start | bytes 798728 | tf_op jit(solution)/shard_map/ppermute | solution.py:219
  84.5 9.1 %collective-permute-start.14 = (bf16[1040,128]{1,0:T(8,128)(2,1)S(1)}, bf16[1040,128]{1,0:T(8,128)(2,1)S(1)}, u32[]{:S(2)}, u32[]{:S(2)}) collective-permute-start(bf16[1040,128]{1,0:T(8,128)(2,1)S(1)} %slice.153), channel_id=1, source_target_pairs={{0,28},{4,0},{8,4},{12,8},{16,12},{20,16},{24,20},{28,24},{1,29},{... | collective-permute-start | bytes 798728 | tf_op jit(solution)/shard_map/ppermute | solution.py:219
  96.1 12.3 %collective-permute-start.15 = (bf16[1552,128]{1,0:T(8,128)(2,1)S(1)}, bf16[1552,128]{1,0:T(8,128)(2,1)S(1)}, u32[]{:S(2)}, u32[]{:S(2)}) collective-permute-start(bf16[1552,128]{1,0:T(8,128)(2,1)S(1)} %slice.136), channel_id=1, source_target_pairs={{0,288},{32,64},{64,352},{96,128},{128,416},{160,192},{192,480},{2... | collective-permute-start | bytes 1191944 | tf_op jit(solution)/shard_map/ppermute | solution.py:216
  98.1 10.6 %collective-permute-start.16 = (bf16[1552,128]{1,0:T(8,128)(2,1)S(1)}, bf16[1552,128]{1,0:T(8,128)(2,1)S(1)}, u32[]{:S(2)}, u32[]{:S(2)}) collective-permute-start(bf16[1552,128]{1,0:T(8,128)(2,1)S(1)} %slice.137), channel_id=1, source_target_pairs={{0,224},{32,256},{64,32},{96,320},{128,96},{160,384},{192,160},{22... | collective-permute-start | bytes 1191944 | tf_op jit(solution)/shard_map/ppermute | solution.py:216
  111.8 5.3 %collective-permute-start.17 = (f32[4,128,768]{2,1,0:T(8,128)S(1)}, f32[4,128,768]{2,1,0:T(8,128)S(1)}, u32[]{:S(2)}, u32[]{:S(2)}) collective-permute-start(f32[4,128,768]{2,1,0:T(8,128)S(1)} %slice.139), channel_id=1, source_target_pairs={{0,1},{1,0},{2,3},{3,2},{4,5},{5,4},{6,7},{7,6},{8,9},{9,8},{10,11... | collective-permute-start | bytes 4718600 | tf_op jit(solution)/shard_map/ppermute | solution.py:238
  117.9 11.0 %collective-permute-start.18 = (s16[128,896]{1,0:T(8,128)(2,1)S(1)}, s16[128,896]{1,0:T(8,128)(2,1)S(1)}, u32[]{:S(2)}, u32[]{:S(2)}) collective-permute-start(s16[128,896]{1,0:T(8,128)(2,1)S(1)} %pad_add_fusion), channel_id=1, source_target_pairs={{0,2},{2,0},{256,258},{258,256},{1,3},{3,1},{257,259},{259,257},{4... | collective-permute-start | bytes 688136 | tf_op jit(solution)/shard_map/ppermute | solution.py:242
  121.3 10.8 %collective-permute-start.19 = (s16[128,896]{1,0:T(8,128)(2,1)S(1)}, s16[128,896]{1,0:T(8,128)(2,1)S(1)}, u32[]{:S(2)}, u32[]{:S(2)}) collective-permute-start(s16[128,896]{1,0:T(8,128)(2,1)S(1)} %pad_add_fusion.1), channel_id=1, source_target_pairs={{0,256},{2,258},{256,2},{258,0},{1,257},{3,259},{257,3},{259,1},{4... | collective-permute-start | bytes 688136 | tf_op jit(solution)/shard_map/ppermute | solution.py:242
  125.9 10.2 %collective-permute-start.20 = (s16[128,896]{1,0:T(8,128)(2,1)S(1)}, s16[128,896]{1,0:T(8,128)(2,1)S(1)}, u32[]{:S(2)}, u32[]{:S(2)}) collective-permute-start(s16[128,896]{1,0:T(8,128)(2,1)S(1)} %pad_add_fusion.2), channel_id=1, source_target_pairs={{0,258},{2,256},{256,0},{258,2},{1,259},{3,257},{257,1},{259,3},{4... | collective-permute-start | bytes 688136 | tf_op jit(solution)/shard_map/ppermute | solution.py:242

commit v8 on v6

--- a/solution.py
+++ b/solution.py
@@ -108,10 +108,6 @@
         acc[...] = jnp.zeros_like(acc)
     for copy in copies:
         copy.wait()
-    if number == 4:
-        load_index(meta, left, right, [meta[9]], [7], idx_v, idx_s, sem)
-        add_chunk(left, right, acc, idx_s, 7, meta[9], 0)
-        return
     load_index(meta, left, right, range(slots), range(chunks), idx_v, idx_s, sem)
 
     def body(c, carry):
@@ -200,7 +196,7 @@
         away == 0, 0, jnp.where(away == 4, 7, jnp.where(away < 4, 2 * away, 15 - 2 * away))
     )
     right_at = jnp.array([1, 1, 1, 2, 2, 3, 3, 4], jnp.int32)
-    left_at = jnp.where(slot < 3, 1, jnp.where(slot < 5, 2, 3))
+    left_at = jnp.where(slot < 3, 1, jnp.where(slot < 5, 2, jnp.where(slot < 7, 3, 4)))
     x = lax.axis_index("x_hi") * 2 + x_lo
     meta = jnp.concatenate(
         [jnp.stack([core, x_lo]), slot, jnp.maximum(right_at, left_at), x[None]]
@@ -228,12 +224,12 @@
     lefts += step_y(*lefts[3:5])
     *state, token = run_stage(2, meta, listed(lefts, 3, 5), listed(rights, 3, 5), 5, 5, state, token)
     last_left = step_y(lefts[5][:LPART], lefts[6][LPART:])
-    up, down, token, *last_left = lax.optimization_barrier((*rights[5:7], token, *last_left))
+    up, down, token = lax.optimization_barrier((*rights[5:7], token))
     last_right = step_z(up[:RPART], down[RPART:])
-    ends = [(7, 0, last_left[0]), (7, LPART, last_left[1])]
-    *state, _ = run_stage(3, meta, listed(lefts, 5, 7) + ends, listed(rights, 5, 7), 8, 7, state, token)
-    ends = [(7, 0, last_right[0]), (7, RPART, last_right[1])]
-    acc = run_stage(4, meta, [], ends, 8, 8, state)[0]
+    *state, _ = run_stage(3, meta, listed(lefts, 5, 7), listed(rights, 5, 7), 7, 7, state, token)
+    last = [(7, i * LPART, part) for i, part in enumerate(last_left)]
+    ends = [(7, i * RPART, part) for i, part in enumerate(last_right)]
+    acc = run_stage(4, meta, last, ends, 8, 8, state)[0]
 
     got = lax.ppermute(acc[4:], "core", [(0, 1), (1, 0)])
     total = acc[:4] + got

time: 137 us -> 137 us (level); the launches traced: 137 us -> 135 us
  waiting for transfers between devices: 37.2 us -> 33.6 us
  starting transfers between devices: 76.5 us -> 77.9 us
    ppermute x8, waiting for transfers between devices: 8.35 us -> 0.02 us  [step_y(): return (lax.ppermute(fore, 'y', turn(1)), lax.ppermute(back, 'y', turn(-1)))]
    ppermute x4, waiting for transfers between devices: 9.12 us -> 12.4 us  [step_z(): lax.ppermute(up, row, ring_pairs(1))]
    ppermute x4, starting transfers between devices: 10.3 us -> 12 us  [step_z(): lax.ppermute(up, row, ring_pairs(1))]
    ppermute x4, starting transfers between devices: 23.8 us -> 22.1 us  [step_z(): lax.ppermute(down, row, ring_pairs(-1))]
  transfers between devices with their start and end apart: 21 -> 21, of which waited for: 11 -> 10; matrix products, arithmetic and copies ran while one was open for 1% -> 1% of each run, Pallas kernels for 10% -> 9%
where the time goes in v8:
time: 137 us; the launch traced here: 135 us
  starting transfers between devices  77.9 us (57%)
  waiting for transfers between devices  33.6 us (25%)
  Pallas kernels  16.3 us (12%)
  other arithmetic  3.58 us (3%)
  local copies, waits for them, and re-layouts  2.73 us (2%)
    ppermute x8, starting transfers between devices, step_y(): return (lax.ppermute(fore, 'y', turn(1)), lax.ppermute(back, 'y', turn(-1)))  29.2 us
    ppermute x4, starting transfers between devices, step_z(): lax.ppermute(down, row, ring_pairs(-1))  22.1 us
    pallas_call x4, Pallas kernels, run_stage(): pl.pallas_call(lambda *refs: stage(number, new_left, new_right, slots, ch...  16.3 us
    ppermute x4, waiting for transfers between devices, step_z(): lax.ppermute(up, row, ring_pairs(1))  12.4 us
    ppermute x4, starting transfers between devices, step_z(): lax.ppermute(up, row, ring_pairs(1))  12 us
    ppermute x3, starting transfers between devices, per_device(): lax.ppermute(encode(total[step]), ('x_lo', 'x_hi'), chip_pairs(step))  9.94 us
    ppermute x3, waiting for transfers between devices, per_device(): lax.ppermute(encode(total[step]), ('x_lo', 'x_hi'), chip_pairs(step))  8.02 us
    ppermute x1, waiting for transfers between devices, per_device(): swapped = lax.ppermute(group(1 - own), 'x_lo', [(0, 1), (1, 0)])  6.64 us
  transfers between devices with their start and end apart: 21, of which 10 were waited for; matrix products, arithmetic and copies ran while one was open for 1% of the time, Pallas kernels for 9%

profile of v8, /device:TPU:6, one launch (start us, length us, event | category | flops | bytes accessed | tf_op | source)
XLA Modules:
  0.0 134.7 jit_solution(13248135263746678144)
XLA Ops:
  3.0 2.7 %collective-permute-start = (bf16[1040,128]{1,0:T(8,128)(2,1)S(1)}, bf16[1040,128]{1,0:T(8,128)(2,1)S(1)}, u32[]{:S(2)}, u32[]{:S(2)}) collective-permute-start(bf16[1040,128]{1,0:T(8,128)(2,1)S(1)} %fusion.14), channel_id=1, source_target_pairs={{0,256},{256,0},{1,257},{257,1},{2,258},{258,2},{3,259},{259,3},{4... | collective-permute-start | bytes 798728 | tf_op jit(solution)/shard_map/ppermute | solution.py:186
  6.4 6.6 %collective-permute-done = bf16[1040,128]{1,0:T(8,128)(2,1)S(1)} collective-permute-done((bf16[1040,128]{1,0:T(8,128)(2,1)S(1)}, bf16[1040,128]{1,0:T(8,128)(2,1)S(1)}, u32[]{:S(2)}, u32[]{:S(2)}) %collective-permute-start) | collective-permute-done | bytes 266272 | tf_op jit(solution)/shard_map/ppermute | solution.py:186
  13.1 4.5 %collective-permute-start.9 = (bf16[3104,128]{1,0:T(8,128)(2,1)S(1)}, bf16[3104,128]{1,0:T(8,128)(2,1)S(1)}, u32[]{:S(2)}, u32[]{:S(2)}) collective-permute-start(bf16[3104,128]{1,0:T(8,128)(2,1)S(1)} %fusion.7.refs_4_), channel_id=1, source_target_pairs={{0,288},{32,64},{64,352},{96,128},{128,416},{160,192},{192,480},{2... | collective-permute-start | bytes 2383880 | tf_op jit(solution)/shard_map/ppermute | solution.py:212
  17.6 8.3 %collective-permute-start.11 = (bf16[3104,128]{1,0:T(8,128)(2,1)S(1)}, bf16[3104,128]{1,0:T(8,128)(2,1)S(1)}, u32[]{:S(2)}, u32[]{:S(2)}) collective-permute-start(bf16[3104,128]{1,0:T(8,128)(2,1)S(1)} %fusion.7.refs_4_), channel_id=1, source_target_pairs={{0,224},{32,256},{64,32},{96,320},{128,96},{160,384},{192,160},{22... | collective-permute-start | bytes 2383880 | tf_op jit(solution)/shard_map/ppermute | solution.py:212
  26.0 3.5 %collective-permute-start.1 = (bf16[2080,128]{1,0:T(8,128)(2,1)S(1)}, bf16[2080,128]{1,0:T(8,128)(2,1)}, u32[]{:S(2)}, u32[]{:S(2)}) collective-permute-start(bf16[2080,128]{1,0:T(8,128)(2,1)S(1)} %fusion.9.refs_1_), channel_id=1, source_target_pairs={{0,4},{4,8},{8,12},{12,16},{16,20},{20,24},{24,28},{28,0},{1,5},{5... | collective-permute-start | bytes 1597448 | tf_op jit(solution)/shard_map/ppermute | solution.py:215
  29.5 3.8 %collective-permute-start.5 = (bf16[2080,128]{1,0:T(8,128)(2,1)S(1)}, bf16[2080,128]{1,0:T(8,128)(2,1)}, u32[]{:S(2)}, u32[]{:S(2)}) collective-permute-start(bf16[2080,128]{1,0:T(8,128)(2,1)S(1)} %fusion.9.refs_1_), channel_id=1, source_target_pairs={{0,28},{4,0},{8,4},{12,8},{16,12},{20,16},{24,20},{28,24},{1,29},{... | collective-permute-start | bytes 1597448 | tf_op jit(solution)/shard_map/ppermute | solution.py:215
  33.3 7.5 %collective-permute-done.9.refs_5_ = bf16[3104,128]{1,0:T(8,128)(2,1)S(1)} collective-permute-done((bf16[3104,128]{1,0:T(8,128)(2,1)S(1)}, bf16[3104,128]{1,0:T(8,128)(2,1)S(1)}, u32[]{:S(2)}, u32[]{:S(2)}) %collective-permute-start.9) | collective-permute-done | bytes 794656 | tf_op jit(solution)/shard_map/ppermute | solution.py:212
  40.8 1.9 %collective-permute-start.10 = (bf16[3104,128]{1,0:T(8,128)(2,1)S(1)}, bf16[3104,128]{1,0:T(8,128)(2,1)}, u32[]{:S(2)}, u32[]{:S(2)}) collective-permute-start(bf16[3104,128]{1,0:T(8,128)(2,1)S(1)} %collective-permute-done.9.refs_5_), channel_id=1, source_target_pairs={{0,288},{32,64},{64,352},{96,128},{128,416},{160,192},{192,480},{2... | collective-permute-start | bytes 2383880 | tf_op jit(solution)/shard_map/ppermute | solution.py:212
  42.8 5.1 %collective-permute-start.12 = (bf16[3104,128]{1,0:T(8,128)(2,1)S(1)}, bf16[3104,128]{1,0:T(8,128)(2,1)}, u32[]{:S(2)}, u32[]{:S(2)}) collective-permute-start(bf16[3104,128]{1,0:T(8,128)(2,1)S(1)} %collective-permute-done.11.refs_6_), channel_id=1, source_target_pairs={{0,224},{32,256},{64,32},{96,320},{128,96},{160,384},{192,160},{22... | collective-permute-start | bytes 2383880 | tf_op jit(solution)/shard_map/ppermute | solution.py:212
  47.9 3.5 %collective-permute-start.2 = (bf16[2080,128]{1,0:T(8,128)(2,1)}, bf16[2080,128]{1,0:T(8,128)(2,1)}, u32[]{:S(2)}, u32[]{:S(2)}) collective-permute-start(bf16[2080,128]{1,0:T(8,128)(2,1)} %collective-permute-done.1.refs_2_), channel_id=1, source_target_pairs={{0,4},{4,8},{8,12},{12,16},{16,20},{20,24},{24,28},{28,0},{1,5},{5... | collective-permute-start | bytes 1597448 | tf_op jit(solution)/shard_map/ppermute | solution.py:215
  51.4 3.8 %collective-permute-start.6 = (bf16[2080,128]{1,0:T(8,128)(2,1)}, bf16[2080,128]{1,0:T(8,128)(2,1)S(1)}, u32[]{:S(2)}, u32[]{:S(2)}) collective-permute-start(bf16[2080,128]{1,0:T(8,128)(2,1)} %collective-permute-done.5.refs_3_), channel_id=1, source_target_pairs={{0,28},{4,0},{8,4},{12,8},{16,12},{20,16},{24,20},{28,24},{1,29},{... | collective-permute-start | bytes 1597448 | tf_op jit(solution)/shard_map/ppermute | solution.py:215
  55.4 4.1 %shard_map.64 = (f32[8,128,768]{2,1,0:T(8,128)S(1)}, bf16[8,2080,128]{2,1,0:T(8,128)(2,1)S(1)}, bf16[8,3104,128]{2,1,0:T(8,128)(2,1)S(1)}, s32[8,128]{1,0:T(8,128)S(1)}) custom-call(s32[19]{0:T(128)S(1)} %concatenate.29.refs_0_, bf16[2080,128]{1,0:T(8,128)(2,1)S(1)} %fusion.9.refs_1_, bf16[2080,128]{1,0:T(8,128)(2,1)} %collective-permute-done.1.refs_2_, ...), custom_call_target="tpu_custom_call" | custom-call | flops 805306368 | bytes 1048576 | tf_op jit(solution)/shard_map/pallas_call | solution.py:131
  59.5 2.6 %collective-permute-done.10.refs_3_ = bf16[3104,128]{1,0:T(8,128)(2,1)} collective-permute-done((bf16[3104,128]{1,0:T(8,128)(2,1)S(1)}, bf16[3104,128]{1,0:T(8,128)(2,1)}, u32[]{:S(2)}, u32[]{:S(2)}) %collective-permute-start.10) | collective-permute-done | bytes 794656 | tf_op jit(solution)/shard_map/ppermute | solution.py:212
  63.7 1.9 %collective-permute-start.13 = (bf16[3104,128]{1,0:T(8,128)(2,1)}, bf16[3104,128]{1,0:T(8,128)(2,1)S(1)}, u32[]{:S(2)}, u32[]{:S(2)}) collective-permute-start(bf16[3104,128]{1,0:T(8,128)(2,1)} %collective-permute-done.10.refs_3_), channel_id=1, source_target_pairs={{0,288},{32,64},{64,352},{96,128},{128,416},{160,192},{192,480},{2... | collective-permute-start | bytes 2383880 | tf_op jit(solution)/shard_map/ppermute | solution.py:212
  65.6 5.2 %collective-permute-start.14 = (bf16[3104,128]{1,0:T(8,128)(2,1)}, bf16[3104,128]{1,0:T(8,128)(2,1)S(1)}, u32[]{:S(2)}, u32[]{:S(2)}) collective-permute-start(bf16[3104,128]{1,0:T(8,128)(2,1)} %collective-permute-done.12.refs_4_), channel_id=1, source_target_pairs={{0,224},{32,256},{64,32},{96,320},{128,96},{160,384},{192,160},{22... | collective-permute-start | bytes 2383880 | tf_op jit(solution)/shard_map/ppermute | solution.py:212
  70.8 3.4 %collective-permute-start.3 = (bf16[2080,128]{1,0:T(8,128)(2,1)}, bf16[2080,128]{1,0:T(8,128)(2,1)S(1)}, u32[]{:S(2)}, u32[]{:S(2)}) collective-permute-start(bf16[2080,128]{1,0:T(8,128)(2,1)} %collective-permute-done.2.refs_1_), channel_id=1, source_target_pairs={{0,4},{4,8},{8,12},{12,16},{16,20},{20,24},{24,28},{28,0},{1,5},{5... | collective-permute-start | bytes 1597448 | tf_op jit(solution)/shard_map/ppermute | solution.py:215
  74.2 3.9 %collective-permute-start.7 = (bf16[2080,128]{1,0:T(8,128)(2,1)S(1)}, bf16[2080,128]{1,0:T(8,128)(2,1)S(1)}, u32[]{:S(2)}, u32[]{:S(2)}) collective-permute-start(bf16[2080,128]{1,0:T(8,128)(2,1)S(1)} %collective-permute-done.6.refs_2_), channel_id=1, source_target_pairs={{0,28},{4,0},{8,4},{12,8},{16,12},{20,16},{24,20},{28,24},{1,29},{... | collective-permute-start | bytes 1597448 | tf_op jit(solution)/shard_map/ppermute | solution.py:215
  78.1 3.8 %shard_map.65 = (f32[8,128,768]{2,1,0:T(8,128)S(1)}, bf16[8,2080,128]{2,1,0:T(8,128)(2,1)S(1)}, bf16[8,3104,128]{2,1,0:T(8,128)(2,1)S(1)}, s32[8,128]{1,0:T(8,128)S(1)}) custom-call(s32[19]{0:T(128)S(1)} %concatenate.29.refs_0_, bf16[2080,128]{1,0:T(8,128)(2,1)} %collective-permute-done.2.refs_1_, ...), custom_call_target="tpu_custom_call", output_to_operand_aliasing={{0}: (5, {}), {1}: (6, {}), {2}: (7, {})} | custom-call | flops 805306368 | bytes 1048576 | tf_op jit(solution)/shard_map/pallas_call | solution.py:131
  81.9 2.3 %collective-permute-done.13.refs_3_ = bf16[3104,128]{1,0:T(8,128)(2,1)S(1)} collective-permute-done((bf16[3104,128]{1,0:T(8,128)(2,1)}, bf16[3104,128]{1,0:T(8,128)(2,1)S(1)}, u32[]{:S(2)}, u32[]{:S(2)}) %collective-permute-start.13) | collective-permute-done | bytes 794656 | tf_op jit(solution)/shard_map/ppermute | solution.py:212
  85.8 3.7 %collective-permute-start.15 = (bf16[1552,128]{1,0:T(8,128)(2,1)S(1)}, bf16[1552,128]{1,0:T(8,128)(2,1)S(1)}, u32[]{:S(2)}, u32[]{:S(2)}) collective-permute-start(bf16[1552,128]{1,0:T(8,128)(2,1)S(1)} %slice.136), channel_id=1, source_target_pairs={{0,288},{32,64},{64,352},{96,128},{128,416},{160,192},{192,480},{2... | collective-permute-start | bytes 1191944 | tf_op jit(solution)/shard_map/ppermute | solution.py:212
  89.5 3.5 %collective-permute-start.16 = (bf16[1552,128]{1,0:T(8,128)(2,1)S(1)}, bf16[1552,128]{1,0:T(8,128)(2,1)S(1)}, u32[]{:S(2)}, u32[]{:S(2)}) collective-permute-start(bf16[1552,128]{1,0:T(8,128)(2,1)S(1)} %slice.137), channel_id=1, source_target_pairs={{0,224},{32,256},{64,32},{96,320},{128,96},{160,384},{192,160},{22... | collective-permute-start | bytes 1191944 | tf_op jit(solution)/shard_map/ppermute | solution.py:212
  93.0 3.3 %collective-permute-start.4 = (bf16[1040,128]{1,0:T(8,128)(2,1)S(1)}, bf16[1040,128]{1,0:T(8,128)(2,1)S(1)}, u32[]{:S(2)}, u32[]{:S(2)}) collective-permute-start(bf16[1040,128]{1,0:T(8,128)(2,1)S(1)} %slice.150), channel_id=1, source_target_pairs={{0,4},{4,8},{8,12},{12,16},{16,20},{20,24},{24,28},{28,0},{1,5},{5... | collective-permute-start | bytes 798728 | tf_op jit(solution)/shard_map/ppermute | solution.py:215
  96.3 4.0 %collective-permute-start.8 = (bf16[1040,128]{1,0:T(8,128)(2,1)S(1)}, bf16[1040,128]{1,0:T(8,128)(2,1)S(1)}, u32[]{:S(2)}, u32[]{:S(2)}) collective-permute-start(bf16[1040,128]{1,0:T(8,128)(2,1)S(1)} %slice.151), channel_id=1, source_target_pairs={{0,28},{4,0},{8,4},{12,8},{16,12},{20,16},{24,20},{28,24},{1,29},{... | collective-permute-start | bytes 798728 | tf_op jit(solution)/shard_map/ppermute | solution.py:215
  100.3 4.4 %shard_map.66 = (f32[8,128,768]{2,1,0:T(8,128)S(1)}, bf16[8,2080,128]{2,1,0:T(8,128)(2,1)S(1)}, bf16[8,3104,128]{2,1,0:T(8,128)(2,1)S(1)}, s32[8,128]{1,0:T(8,128)}) custom-call(s32[19]{0:T(128)S(1)} %concatenate.29.refs_0_, bf16[2080,128]{1,0:T(8,128)(2,1)S(1)} %collective-permute-done.3.refs_1_, ...), custom_call_target="tpu_custom_call", output_to_operand_aliasing={{0}: (5, {}), {1}: (6, {}), {2}: (7, {})} | custom-call | flops 805306368 | bytes 1048576 | tf_op jit(solution)/shard_map/pallas_call | solution.py:131
  104.8 4.0 %shard_map.67 = (f32[8,128,768]{2,1,0:T(8,128)S(1)}, bf16[8,2080,128]{2,1,0:T(8,128)(2,1)S(1)}, bf16[8,3104,128]{2,1,0:T(8,128)(2,1)S(1)}, s32[8,128]{1,0:T(8,128)}) custom-call(s32[19]{0:T(128)S(1)} %concatenate.29.refs_0_, bf16[1040,128]{1,0:T(8,128)(2,1)S(1)} %collective-permute-done.4.refs_1_, ...), custom_call_target="tpu_custom_call", output_to_operand_aliasing={{0}: (5, {}), {1}: (6, {}), {2}: (7, {})} | custom-call | flops 805306368 | bytes 1048576 | tf_op jit(solution)/shard_map/pallas_call | solution.py:131
  109.0 1.9 %collective-permute-start.17 = (f32[4,128,768]{2,1,0:T(8,128)S(1)}, f32[4,128,768]{2,1,0:T(8,128)S(1)}, u32[]{:S(2)}, u32[]{:S(2)}) collective-permute-start(f32[4,128,768]{2,1,0:T(8,128)S(1)} %slice.139), channel_id=1, source_target_pairs={{0,1},{1,0},{2,3},{3,2},{4,5},{5,4},{6,7},{7,6},{8,9},{9,8},{10,11... | collective-permute-start | bytes 4718600 | tf_op jit(solution)/shard_map/ppermute | solution.py:234
  110.9 3.4 %collective-permute-done.17 = f32[4,128,768]{2,1,0:T(8,128)S(1)} collective-permute-done((f32[4,128,768]{2,1,0:T(8,128)S(1)}, f32[4,128,768]{2,1,0:T(8,128)S(1)}, u32[]{:S(2)}, u32[]{:S(2)}) %collective-permute-start.17) | collective-permute-done | bytes 1572896 | tf_op jit(solution)/shard_map/ppermute | solution.py:234
  115.1 3.3 %collective-permute-start.18 = (s16[128,896]{1,0:T(8,128)(2,1)S(1)}, s16[128,896]{1,0:T(8,128)(2,1)S(1)}, u32[]{:S(2)}, u32[]{:S(2)}) collective-permute-start(s16[128,896]{1,0:T(8,128)(2,1)S(1)} %pad_add_fusion), channel_id=1, source_target_pairs={{0,2},{2,0},{256,258},{258,256},{1,3},{3,1},{257,259},{259,257},{4... | collective-permute-start | bytes 688136 | tf_op jit(solution)/shard_map/ppermute | solution.py:238
  118.5 4.7 %collective-permute-start.19 = (s16[128,896]{1,0:T(8,128)(2,1)S(1)}, s16[128,896]{1,0:T(8,128)(2,1)S(1)}, u32[]{:S(2)}, u32[]{:S(2)}) collective-permute-start(s16[128,896]{1,0:T(8,128)(2,1)S(1)} %pad_add_fusion.1), channel_id=1, source_target_pairs={{0,256},{2,258},{256,2},{258,0},{1,257},{3,259},{257,3},{259,1},{4... | collective-permute-start | bytes 688136 | tf_op jit(solution)/shard_map/ppermute | solution.py:238
  123.3 1.9 %collective-permute-start.20 = (s16[128,896]{1,0:T(8,128)(2,1)S(1)}, s16[128,896]{1,0:T(8,128)(2,1)S(1)}, u32[]{:S(2)}, u32[]{:S(2)}) collective-permute-start(s16[128,896]{1,0:T(8,128)(2,1)S(1)} %pad_add_fusion.2), channel_id=1, source_target_pairs={{0,258},{2,256},{256,0},{258,2},{1,259},{3,257},{257,1},{259,3},{4... | collective-permute-start | bytes 688136 | tf_op jit(solution)/shard_map/ppermute | solution.py:238
  126.2 3.3 %collective-permute-done.19 = s16[128,896]{1,0:T(8,128)(2,1)S(1)} collective-permute-done((s16[128,896]{1,0:T(8,128)(2,1)S(1)}, s16[128,896]{1,0:T(8,128)(2,1)S(1)}, u32[]{:S(2)}, u32[]{:S(2)}) %collective-permute-start.19) | collective-permute-done | bytes 229408 | tf_op jit(solution)/shard_map/ppermute | solution.py:238
  129.6 3.9 %collective-permute-done.20 = s16[128,896]{1,0:T(8,128)(2,1)S(1)} collective-permute-done((s16[128,896]{1,0:T(8,128)(2,1)S(1)}, s16[128,896]{1,0:T(8,128)(2,1)S(1)}, u32[]{:S(2)}, u32[]{:S(2)}) %collective-permute-start.20) | collective-permute-done | bytes 229408 | tf_op jit(solution)/shard_map/ppermute | solution.py:238
  (59 shorter events, 10.4 us)
Async XLA Ops:
  0.0 5.8 %copy-start = (bf16[1,8,1,3,128,128]{5,4,3,2,1,0:T(8,128)(2,1)S(1)}, bf16[1,8,1,3,128,128]{5,4,3,2,1,0:T(8,128)(2,1)}, u32[]{:S(2)}) copy-start(bf16[1,8,1,3,128,128]{5,4,3,2,1,0:T(8,128)(2,1)} %param.16) | copy-start | bytes 2359300
  0.0 5.8 %copy-start.1 = (s32[1,8,1,3]{1,2,3,0:T(1,128)S(1)}, s32[1,8,1,3]{1,2,3,0:T(1,128)}, u32[]{:S(2)}) copy-start(s32[1,8,1,3]{1,2,3,0:T(1,128)} %param.17) | copy-start | bytes 292
  3.0 10.0 %collective-permute-start = (bf16[1040,128]{1,0:T(8,128)(2,1)S(1)}, bf16[1040,128]{1,0:T(8,128)(2,1)S(1)}, u32[]{:S(2)}, u32[]{:S(2)}) collective-permute-start(bf16[1040,128]{1,0:T(8,128)(2,1)S(1)} %fusion.14), channel_id=1, source_target_pairs={{0,256},{256,0},{1,257},{257,1},{2,258},{258,2},{3,259},{259,3},{4... | collective-permute-start | bytes 798728 | tf_op jit(solution)/shard_map/ppermute | solution.py:186
  5.9 49.4 %copy-start.2 = (s32[8]{0:T(128)S(1)}, s32[8]{0:T(128)}, u32[]{:S(2)}) copy-start(s32[8]{0:T(128)} %constant.239.clone) | copy-start | bytes 100
  5.9 49.4 %copy-start.3 = (s32[8]{0:T(128)S(1)}, s32[8]{0:T(128)}, u32[]{:S(2)}) copy-start(s32[8]{0:T(128)} %constant.240.clone) | copy-start | bytes 100
  13.1 27.8 %collective-permute-start.9 = (bf16[3104,128]{1,0:T(8,128)(2,1)S(1)}, bf16[3104,128]{1,0:T(8,128)(2,1)S(1)}, u32[]{:S(2)}, u32[]{:S(2)}) collective-permute-start(bf16[3104,128]{1,0:T(8,128)(2,1)S(1)} %fusion.7.refs_4_), channel_id=1, source_target_pairs={{0,288},{32,64},{64,352},{96,128},{128,416},{160,192},{192,480},{2... | collective-permute-start | bytes 2383880 | tf_op jit(solution)/shard_map/ppermute | solution.py:212
  17.6 25.2 %collective-permute-start.11 = (bf16[3104,128]{1,0:T(8,128)(2,1)S(1)}, bf16[3104,128]{1,0:T(8,128)(2,1)S(1)}, u32[]{:S(2)}, u32[]{:S(2)}) collective-permute-start(bf16[3104,128]{1,0:T(8,128)(2,1)S(1)} %fusion.7.refs_4_), channel_id=1, source_target_pairs={{0,224},{32,256},{64,32},{96,320},{128,96},{160,384},{192,160},{22... | collective-permute-start | bytes 2383880 | tf_op jit(solution)/shard_map/ppermute | solution.py:212
  26.0 21.9 %collective-permute-start.1 = (bf16[2080,128]{1,0:T(8,128)(2,1)S(1)}, bf16[2080,128]{1,0:T(8,128)(2,1)}, u32[]{:S(2)}, u32[]{:S(2)}) collective-permute-start(bf16[2080,128]{1,0:T(8,128)(2,1)S(1)} %fusion.9.refs_1_), channel_id=1, source_target_pairs={{0,4},{4,8},{8,12},{12,16},{16,20},{20,24},{24,28},{28,0},{1,5},{5... | collective-permute-start | bytes 1597448 | tf_op jit(solution)/shard_map/ppermute | solution.py:215
  29.5 21.9 %collective-permute-start.5 = (bf16[2080,128]{1,0:T(8,128)(2,1)S(1)}, bf16[2080,128]{1,0:T(8,128)(2,1)}, u32[]{:S(2)}, u32[]{:S(2)}) collective-permute-start(bf16[2080,128]{1,0:T(8,128)(2,1)S(1)} %fusion.9.refs_1_), channel_id=1, source_target_pairs={{0,28},{4,0},{8,4},{12,8},{16,12},{20,16},{24,20},{28,24},{1,29},{... | collective-permute-start | bytes 1597448 | tf_op jit(solution)/shard_map/ppermute | solution.py:215
  40.8 21.2 %collective-permute-start.10 = (bf16[3104,128]{1,0:T(8,128)(2,1)S(1)}, bf16[3104,128]{1,0:T(8,128)(2,1)}, u32[]{:S(2)}, u32[]{:S(2)}) collective-permute-start(bf16[3104,128]{1,0:T(8,128)(2,1)S(1)} %collective-permute-done.9.refs_5_), channel_id=1, source_target_pairs={{0,288},{32,64},{64,352},{96,128},{128,416},{160,192},{192,480},{2... | collective-permute-start | bytes 2383880 | tf_op jit(solution)/shard_map/ppermute | solution.py:212
  42.8 20.9 %collective-permute-start.12 = (bf16[3104,128]{1,0:T(8,128)(2,1)S(1)}, bf16[3104,128]{1,0:T(8,128)(2,1)}, u32[]{:S(2)}, u32[]{:S(2)}) collective-permute-start(bf16[3104,128]{1,0:T(8,128)(2,1)S(1)} %collective-permute-done.11.refs_6_), channel_id=1, source_target_pairs={{0,224},{32,256},{64,32},{96,320},{128,96},{160,384},{192,160},{22... | collective-permute-start | bytes 2383880 | tf_op jit(solution)/shard_map/ppermute | solution.py:212
  47.9 22.9 %collective-permute-start.2 = (bf16[2080,128]{1,0:T(8,128)(2,1)}, bf16[2080,128]{1,0:T(8,128)(2,1)}, u32[]{:S(2)}, u32[]{:S(2)}) collective-permute-start(bf16[2080,128]{1,0:T(8,128)(2,1)} %collective-permute-done.1.refs_2_), channel_id=1, source_target_pairs={{0,4},{4,8},{8,12},{12,16},{16,20},{20,24},{24,28},{28,0},{1,5},{5... | collective-permute-start | bytes 1597448 | tf_op jit(solution)/shard_map/ppermute | solution.py:215
  51.4 22.8 %collective-permute-start.6 = (bf16[2080,128]{1,0:T(8,128)(2,1)}, bf16[2080,128]{1,0:T(8,128)(2,1)S(1)}, u32[]{:S(2)}, u32[]{:S(2)}) collective-permute-start(bf16[2080,128]{1,0:T(8,128)(2,1)} %collective-permute-done.5.refs_3_), channel_id=1, source_target_pairs={{0,28},{4,0},{8,4},{12,8},{16,12},{20,16},{24,20},{28,24},{1,29},{... | collective-permute-start | bytes 1597448 | tf_op jit(solution)/shard_map/ppermute | solution.py:215
  63.7 20.5 %collective-permute-start.13 = (bf16[3104,128]{1,0:T(8,128)(2,1)}, bf16[3104,128]{1,0:T(8,128)(2,1)S(1)}, u32[]{:S(2)}, u32[]{:S(2)}) collective-permute-start(bf16[3104,128]{1,0:T(8,128)(2,1)} %collective-permute-done.10.refs_3_), channel_id=1, source_target_pairs={{0,288},{32,64},{64,352},{96,128},{128,416},{160,192},{192,480},{2... | collective-permute-start | bytes 2383880 | tf_op jit(solution)/shard_map/ppermute | solution.py:212
  65.6 20.1 %collective-permute-start.14 = (bf16[3104,128]{1,0:T(8,128)(2,1)}, bf16[3104,128]{1,0:T(8,128)(2,1)S(1)}, u32[]{:S(2)}, u32[]{:S(2)}) collective-permute-start(bf16[3104,128]{1,0:T(8,128)(2,1)} %collective-permute-done.12.refs_4_), channel_id=1, source_target_pairs={{0,224},{32,256},{64,32},{96,320},{128,96},{160,384},{192,160},{22... | collective-permute-start | bytes 2383880 | tf_op jit(solution)/shard_map/ppermute | solution.py:212
  70.8 22.1 %collective-permute-start.3 = (bf16[2080,128]{1,0:T(8,128)(2,1)}, bf16[2080,128]{1,0:T(8,128)(2,1)S(1)}, u32[]{:S(2)}, u32[]{:S(2)}) collective-permute-start(bf16[2080,128]{1,0:T(8,128)(2,1)} %collective-permute-done.2.refs_1_), channel_id=1, source_target_pairs={{0,4},{4,8},{8,12},{12,16},{16,20},{20,24},{24,28},{28,0},{1,5},{5... | collective-permute-start | bytes 1597448 | tf_op jit(solution)/shard_map/ppermute | solution.py:215
  74.2 22.1 %collective-permute-start.7 = (bf16[2080,128]{1,0:T(8,128)(2,1)S(1)}, bf16[2080,128]{1,0:T(8,128)(2,1)S(1)}, u32[]{:S(2)}, u32[]{:S(2)}) collective-permute-start(bf16[2080,128]{1,0:T(8,128)(2,1)S(1)} %collective-permute-done.6.refs_2_), channel_id=1, source_target_pairs={{0,28},{4,0},{8,4},{12,8},{16,12},{20,16},{24,20},{28,24},{1,29},{... | collective-permute-start | bytes 1597448 | tf_op jit(solution)/shard_map/ppermute | solution.py:215
  85.8 19.0 %collective-permute-start.15 = (bf16[1552,128]{1,0:T(8,128)(2,1)S(1)}, bf16[1552,128]{1,0:T(8,128)(2,1)S(1)}, u32[]{:S(2)}, u32[]{:S(2)}) collective-permute-start(bf16[1552,128]{1,0:T(8,128)(2,1)S(1)} %slice.136), channel_id=1, source_target_pairs={{0,288},{32,64},{64,352},{96,128},{128,416},{160,192},{192,480},{2... | collective-permute-start | bytes 1191944 | tf_op jit(solution)/shard_map/ppermute | solution.py:212
  89.5 15.3 %collective-permute-start.16 = (bf16[1552,128]{1,0:T(8,128)(2,1)S(1)}, bf16[1552,128]{1,0:T(8,128)(2,1)S(1)}, u32[]{:S(2)}, u32[]{:S(2)}) collective-permute-start(bf16[1552,128]{1,0:T(8,128)(2,1)S(1)} %slice.137), channel_id=1, source_target_pairs={{0,224},{32,256},{64,32},{96,320},{128,96},{160,384},{192,160},{22... | collective-permute-start | bytes 1191944 | tf_op jit(solution)/shard_map/ppermute | solution.py:212
  93.0 11.8 %collective-permute-start.4 = (bf16[1040,128]{1,0:T(8,128)(2,1)S(1)}, bf16[1040,128]{1,0:T(8,128)(2,1)S(1)}, u32[]{:S(2)}, u32[]{:S(2)}) collective-permute-start(bf16[1040,128]{1,0:T(8,128)(2,1)S(1)} %slice.150), channel_id=1, source_target_pairs={{0,4},{4,8},{8,12},{12,16},{16,20},{20,24},{24,28},{28,0},{1,5},{5... | collective-permute-start | bytes 798728 | tf_op jit(solution)/shard_map/ppermute | solution.py:215
  96.3 8.5 %collective-permute-start.8 = (bf16[1040,128]{1,0:T(8,128)(2,1)S(1)}, bf16[1040,128]{1,0:T(8,128)(2,1)S(1)}, u32[]{:S(2)}, u32[]{:S(2)}) collective-permute-start(bf16[1040,128]{1,0:T(8,128)(2,1)S(1)} %slice.151), channel_id=1, source_target_pairs={{0,28},{4,0},{8,4},{12,8},{16,12},{20,16},{24,20},{28,24},{1,29},{... | collective-permute-start | bytes 798728 | tf_op jit(solution)/shard_map/ppermute | solution.py:215
  109.0 5.3 %collective-permute-start.17 = (f32[4,128,768]{2,1,0:T(8,128)S(1)}, f32[4,128,768]{2,1,0:T(8,128)S(1)}, u32[]{:S(2)}, u32[]{:S(2)}) collective-permute-start(f32[4,128,768]{2,1,0:T(8,128)S(1)} %slice.139), channel_id=1, source_target_pairs={{0,1},{1,0},{2,3},{3,2},{4,5},{5,4},{6,7},{7,6},{8,9},{9,8},{10,11... | collective-permute-start | bytes 4718600 | tf_op jit(solution)/shard_map/ppermute | solution.py:234
  115.1 11.0 %collective-permute-start.18 = (s16[128,896]{1,0:T(8,128)(2,1)S(1)}, s16[128,896]{1,0:T(8,128)(2,1)S(1)}, u32[]{:S(2)}, u32[]{:S(2)}) collective-permute-start(s16[128,896]{1,0:T(8,128)(2,1)S(1)} %pad_add_fusion), channel_id=1, source_target_pairs={{0,2},{2,0},{256,258},{258,256},{1,3},{3,1},{257,259},{259,257},{4... | collective-permute-start | bytes 688136 | tf_op jit(solution)/shard_map/ppermute | solution.py:238
  118.5 11.0 %collective-permute-start.19 = (s16[128,896]{1,0:T(8,128)(2,1)S(1)}, s16[128,896]{1,0:T(8,128)(2,1)S(1)}, u32[]{:S(2)}, u32[]{:S(2)}) collective-permute-start(s16[128,896]{1,0:T(8,128)(2,1)S(1)} %pad_add_fusion.1), channel_id=1, source_target_pairs={{0,256},{2,258},{256,2},{258,0},{1,257},{3,259},{257,3},{259,1},{4... | collective-permute-start | bytes 688136 | tf_op jit(solution)/shard_map/ppermute | solution.py:238
  123.3 10.2 %collective-permute-start.20 = (s16[128,896]{1,0:T(8,128)(2,1)S(1)}, s16[128,896]{1,0:T(8,128)(2,1)S(1)}, u32[]{:S(2)}, u32[]{:S(2)}) collective-permute-start(s16[128,896]{1,0:T(8,128)(2,1)S(1)} %pad_add_fusion.2), channel_id=1, source_target_pairs={{0,258},{2,256},{256,0},{258,2},{1,259},{3,257},{257,1},{259,3},{4... | collective-permute-start | bytes 688136 | tf_op jit(solution)/shard_map/ppermute | solution.py:238

commit v9 on v8

--- a/solution.py
+++ b/solution.py
@@ -74,21 +74,34 @@
 
 
 def add_chunk(left, right, acc, idx_s, c, slot, place):
-    for k in range(GROUP):
-        half, j = k // HALF, k % HALF
+    none = jnp.zeros((W, W), jnp.bfloat16)
+    for pair in range(GROUP // 2):
+        ks = (2 * pair, 2 * pair + 1)
         both = jnp.concatenate(
-            [left[slot, pl.ds(p * LPART + k * W, W), :] for p in range(2)], axis=0
+            [
+                jnp.concatenate(
+                    [left[slot, pl.ds(p * LPART + k * W, W), :] for p in range(2)], axis=0
+                )
+                for k in ks
+            ],
+            axis=1,
         )
-        wide = jnp.concatenate(
-            [right[c, pl.ds(half * RPART + (j * EB + e) * W, W), :] for e in range(EB)], axis=1
-        )
-        part = jnp.dot(both, wide, preferred_element_type=jnp.float32)
+        half = ks[0] // HALF
         for e in range(EB):
-            cell = idx_s[2 * NY + 2 * c + half, j * EB + e]
-            lanes = pl.ds(pl.multiple_of(cell * W, W), W)
-            for p in range(2):
-                at = idx_s[place * 2 + p, k]
-                acc[at, :, lanes] += part[p * W : (p + 1) * W, e * W : (e + 1) * W]
+            one, two = (
+                right[c, pl.ds(half * RPART + ((k % HALF) * EB + e) * W, W), :] for k in ks
+            )
+            wide = jnp.concatenate(
+                [jnp.concatenate([one, none], axis=1), jnp.concatenate([none, two], axis=1)],
+                axis=0,
+            )
+            part = jnp.dot(both, wide, preferred_element_type=jnp.float32)
+            for i, k in enumerate(ks):
+                cell = idx_s[2 * NY + 2 * c + half, (k % HALF) * EB + e]
+                lanes = pl.ds(pl.multiple_of(cell * W, W), W)
+                for p in range(2):
+                    at = idx_s[place * 2 + p, k]
+                    acc[at, :, lanes] += part[p * W : (p + 1) * W, i * W : (i + 1) * W]
 
 
 def stage(number, new_left, new_right, slots, chunks, meta, *refs):
@@ -178,17 +191,21 @@
     own = (side + y // 4 + y % 4) % 2
 
     def group(which):
-        return with_index(
-            lax.dynamic_index_in_dim(left, which, 0, False),
-            lax.dynamic_index_in_dim(rows, which, 0, False),
-        )
-
-    swapped = lax.ppermute(group(1 - own), "x_lo", [(0, 1), (1, 0)])
-    pair = jnp.concatenate([group(own), swapped], axis=0)
+        return lax.dynamic_index_in_dim(left, which, 0, False)
+
+    def group_index(which):
+        picked = lax.dynamic_index_in_dim(rows, which, 0, False).astype(left.dtype)
+        return jnp.zeros((PAD, W), left.dtype).at[0, :GROUP].set(picked)
+
     right = right_blocks.reshape(2, HALF, EB * W, W)
     cols = right_cols.reshape(2, HALF * EB)
     chunk = jnp.concatenate([with_index(right[h], cols[h]) for h in range(2)], axis=0)
-    first, _ = lax.optimization_barrier((chunk, swapped))
+    swap = [(0, 1), (1, 0)]
+    swapped = lax.ppermute(group(1 - own), "x_lo", swap)
+    chunk, other = lax.optimization_barrier((chunk, group_index(1 - own)))
+    swapped_index = lax.ppermute(other, "x_lo", swap)
+    first, swapped, swapped_index = lax.optimization_barrier((chunk, swapped, swapped_index))
+    pair = jnp.concatenate([group(own), group_index(own), swapped, swapped_index], axis=0)
 
     source = (z + jnp.array([0, -1, 1, -2, 2, -3, 3, 4], jnp.int32)) % NZ
     away = (4 * (zig(source) ^ side) + source // 2 - y) % NY

time: 137 us -> 136 us (level)
  waiting for transfers between devices: 33.6 us -> 28.9 us
  starting transfers between devices: 77.9 us -> 81.4 us
    ppermute x1 -> x2, waiting for transfers between devices: 6.64 us -> 2.39 us  [the longest x1 2.39 us: per_device(): swapped_index = lax.ppermute(other, 'x_lo', swap)]
    ppermute x1 -> x2, starting transfers between devices: 2.74 us -> 5.84 us  [the longest x1 3.11 us: per_device(): swapped_index = lax.ppermute(other, 'x_lo', swap)]
  transfers between devices with their start and end apart: 21 -> 22, of which waited for: 10 -> 10; matrix products, arithmetic and copies ran while one was open for 1% -> 2% of each run, Pallas kernels for 9% -> 9%
where the time goes in v9:
time: 136 us; the launch traced here: 134 us
  starting transfers between devices  81.4 us (60%)
  waiting for transfers between devices  28.9 us (21%)
  Pallas kernels  16.5 us (12%)
  other arithmetic  3.56 us (3%)
  local copies, waits for them, and re-layouts  2.81 us (2%)
    ppermute x8, starting transfers between devices, step_y(): return (lax.ppermute(fore, 'y', turn(1)), lax.ppermute(back, 'y', turn(-1)))  29.2 us
    ppermute x4, starting transfers between devices, step_z(): lax.ppermute(down, row, ring_pairs(-1))  21.7 us
    pallas_call x4, Pallas kernels, run_stage(): pl.pallas_call(lambda *refs: stage(number, new_left, new_right, slots, ch...  16.5 us
    ppermute x4, starting transfers between devices, step_z(): lax.ppermute(up, row, ring_pairs(1))  12.4 us
    ppermute x4, waiting for transfers between devices, step_z(): lax.ppermute(up, row, ring_pairs(1))  11.9 us
    ppermute x3, starting transfers between devices, per_device(): lax.ppermute(encode(total[step]), ('x_lo', 'x_hi'), chip_pairs(step))  10.3 us
    ppermute x3, waiting for transfers between devices, per_device(): lax.ppermute(encode(total[step]), ('x_lo', 'x_hi'), chip_pairs(step))  8.02 us
    ppermute x1, waiting for transfers between devices, per_device(): got = lax.ppermute(acc[4:], 'core', [(0, 1), (1, 0)])  3.38 us
  transfers between devices with their start and end apart: 22, of which 10 were waited for; matrix products, arithmetic and copies ran while one was open for 2% of the time, Pallas kernels for 9%

profile of v9, /device:TPU:6, one launch (start us, length us, event | category | flops | bytes accessed | tf_op | source)
XLA Modules:
  0.0 133.6 jit_solution(2096475646096772235)
XLA Ops:
  1.1 2.7 %collective-permute-start = (bf16[1024,128]{1,0:T(8,128)(2,1)S(1)}, bf16[1024,128]{1,0:T(8,128)(2,1)S(1)}, u32[]{:S(2)}, u32[]{:S(2)}) collective-permute-start(bf16[1024,128]{1,0:T(8,128)(2,1)S(1)} %get-tuple-element.110), channel_id=1, source_target_pairs={{0,256},{256,0},{1,257},{257,1},{2,258},{258,2},{3,259},{259,3},{4... | collective-permute-start | bytes 786440 | tf_op jit(solution)/shard_map/ppermute | solution.py:204
  6.5 3.1 %collective-permute-start.1 = (bf16[16,128]{1,0:T(8,128)(2,1)S(1)}, bf16[16,128]{1,0:T(8,128)(2,1)S(1)}, u32[]{:S(2)}, u32[]{:S(2)}) collective-permute-start(bf16[16,128]{1,0:T(8,128)(2,1)S(1)} %scatter.19), channel_id=1, source_target_pairs={{0,256},{256,0},{1,257},{257,1},{2,258},{258,2},{3,259},{259,3},{4... | collective-permute-start | bytes 12296 | tf_op jit(solution)/shard_map/ppermute | solution.py:206
  9.6 2.4 %collective-permute-done.1 = bf16[16,128]{1,0:T(8,128)(2,1)S(1)} collective-permute-done((bf16[16,128]{1,0:T(8,128)(2,1)S(1)}, bf16[16,128]{1,0:T(8,128)(2,1)S(1)}, u32[]{:S(2)}, u32[]{:S(2)}) %collective-permute-start.1) | collective-permute-done | bytes 4128 | tf_op jit(solution)/shard_map/ppermute | solution.py:206
  12.0 4.9 %collective-permute-start.10 = (bf16[3104,128]{1,0:T(8,128)(2,1)S(1)}, bf16[3104,128]{1,0:T(8,128)(2,1)S(1)}, u32[]{:S(2)}, u32[]{:S(2)}) collective-permute-start(bf16[3104,128]{1,0:T(8,128)(2,1)S(1)} %fusion.7.refs_4_), channel_id=1, source_target_pairs={{0,288},{32,64},{64,352},{96,128},{128,416},{160,192},{192,480},{2... | collective-permute-start | bytes 2383880 | tf_op jit(solution)/shard_map/ppermute | solution.py:229
  16.9 8.0 %collective-permute-start.12 = (bf16[3104,128]{1,0:T(8,128)(2,1)S(1)}, bf16[3104,128]{1,0:T(8,128)(2,1)S(1)}, u32[]{:S(2)}, u32[]{:S(2)}) collective-permute-start(bf16[3104,128]{1,0:T(8,128)(2,1)S(1)} %fusion.7.refs_4_), channel_id=1, source_target_pairs={{0,224},{32,256},{64,32},{96,320},{128,96},{160,384},{192,160},{22... | collective-permute-start | bytes 2383880 | tf_op jit(solution)/shard_map/ppermute | solution.py:229
  24.9 3.5 %collective-permute-start.2 = (bf16[2080,128]{1,0:T(8,128)(2,1)S(1)}, bf16[2080,128]{1,0:T(8,128)(2,1)}, u32[]{:S(2)}, u32[]{:S(2)}) collective-permute-start(bf16[2080,128]{1,0:T(8,128)(2,1)S(1)} %fusion.10.refs_1_), channel_id=1, source_target_pairs={{0,4},{4,8},{8,12},{12,16},{16,20},{20,24},{24,28},{28,0},{1,5},{5... | collective-permute-start | bytes 1597448 | tf_op jit(solution)/shard_map/ppermute | solution.py:232
  28.4 3.8 %collective-permute-start.6 = (bf16[2080,128]{1,0:T(8,128)(2,1)S(1)}, bf16[2080,128]{1,0:T(8,128)(2,1)}, u32[]{:S(2)}, u32[]{:S(2)}) collective-permute-start(bf16[2080,128]{1,0:T(8,128)(2,1)S(1)} %fusion.10.refs_1_), channel_id=1, source_target_pairs={{0,28},{4,0},{8,4},{12,8},{16,12},{20,16},{24,20},{28,24},{1,29},{... | collective-permute-start | bytes 1597448 | tf_op jit(solution)/shard_map/ppermute | solution.py:232
  32.2 7.4 %collective-permute-done.10.refs_5_ = bf16[3104,128]{1,0:T(8,128)(2,1)S(1)} collective-permute-done((bf16[3104,128]{1,0:T(8,128)(2,1)S(1)}, bf16[3104,128]{1,0:T(8,128)(2,1)S(1)}, u32[]{:S(2)}, u32[]{:S(2)}) %collective-permute-start.10) | collective-permute-done | bytes 794656 | tf_op jit(solution)/shard_map/ppermute | solution.py:229
  39.6 1.9 %collective-permute-start.11 = (bf16[3104,128]{1,0:T(8,128)(2,1)S(1)}, bf16[3104,128]{1,0:T(8,128)(2,1)}, u32[]{:S(2)}, u32[]{:S(2)}) collective-permute-start(bf16[3104,128]{1,0:T(8,128)(2,1)S(1)} %collective-permute-done.10.refs_5_), channel_id=1, source_target_pairs={{0,288},{32,64},{64,352},{96,128},{128,416},{160,192},{192,480},{2... | collective-permute-start | bytes 2383880 | tf_op jit(solution)/shard_map/ppermute | solution.py:229
  41.5 5.1 %collective-permute-start.13 = (bf16[3104,128]{1,0:T(8,128)(2,1)S(1)}, bf16[3104,128]{1,0:T(8,128)(2,1)}, u32[]{:S(2)}, u32[]{:S(2)}) collective-permute-start(bf16[3104,128]{1,0:T(8,128)(2,1)S(1)} %collective-permute-done.12.refs_6_), channel_id=1, source_target_pairs={{0,224},{32,256},{64,32},{96,320},{128,96},{160,384},{192,160},{22... | collective-permute-start | bytes 2383880 | tf_op jit(solution)/shard_map/ppermute | solution.py:229
  46.7 3.5 %collective-permute-start.3 = (bf16[2080,128]{1,0:T(8,128)(2,1)}, bf16[2080,128]{1,0:T(8,128)(2,1)}, u32[]{:S(2)}, u32[]{:S(2)}) collective-permute-start(bf16[2080,128]{1,0:T(8,128)(2,1)} %collective-permute-done.2.refs_2_), channel_id=1, source_target_pairs={{0,4},{4,8},{8,12},{12,16},{16,20},{20,24},{24,28},{28,0},{1,5},{5... | collective-permute-start | bytes 1597448 | tf_op jit(solution)/shard_map/ppermute | solution.py:232
  50.2 3.8 %collective-permute-start.7 = (bf16[2080,128]{1,0:T(8,128)(2,1)}, bf16[2080,128]{1,0:T(8,128)(2,1)S(1)}, u32[]{:S(2)}, u32[]{:S(2)}) collective-permute-start(bf16[2080,128]{1,0:T(8,128)(2,1)} %collective-permute-done.6.refs_3_), channel_id=1, source_target_pairs={{0,28},{4,0},{8,4},{12,8},{16,12},{20,16},{24,20},{28,24},{1,29},{... | collective-permute-start | bytes 1597448 | tf_op jit(solution)/shard_map/ppermute | solution.py:232
  54.1 4.2 %shard_map.64 = (f32[8,128,768]{2,1,0:T(8,128)S(1)}, bf16[8,2080,128]{2,1,0:T(8,128)(2,1)S(1)}, bf16[8,3104,128]{2,1,0:T(8,128)(2,1)S(1)}, s32[8,128]{1,0:T(8,128)S(1)}) custom-call(s32[19]{0:T(128)S(1)} %concatenate.26.refs_0_, bf16[2080,128]{1,0:T(8,128)(2,1)S(1)} %fusion.10.refs_1_, bf16[2080,128]{1,0:T(8,128)(2,1)} %collective-permute-done.2.refs_2_, ...), custom_call_target="tpu_custom_call" | custom-call | flops 805306368 | bytes 1048576 | tf_op jit(solution)/shard_map/pallas_call | solution.py:144
  58.3 2.4 %collective-permute-done.11.refs_3_ = bf16[3104,128]{1,0:T(8,128)(2,1)} collective-permute-done((bf16[3104,128]{1,0:T(8,128)(2,1)S(1)}, bf16[3104,128]{1,0:T(8,128)(2,1)}, u32[]{:S(2)}, u32[]{:S(2)}) %collective-permute-start.11) | collective-permute-done | bytes 794656 | tf_op jit(solution)/shard_map/ppermute | solution.py:229
  64.2 5.2 %collective-permute-start.15 = (bf16[3104,128]{1,0:T(8,128)(2,1)}, bf16[3104,128]{1,0:T(8,128)(2,1)S(1)}, u32[]{:S(2)}, u32[]{:S(2)}) collective-permute-start(bf16[3104,128]{1,0:T(8,128)(2,1)} %collective-permute-done.13.refs_4_), channel_id=1, source_target_pairs={{0,224},{32,256},{64,32},{96,320},{128,96},{160,384},{192,160},{22... | collective-permute-start | bytes 2383880 | tf_op jit(solution)/shard_map/ppermute | solution.py:229
  69.4 3.4 %collective-permute-start.4 = (bf16[2080,128]{1,0:T(8,128)(2,1)}, bf16[2080,128]{1,0:T(8,128)(2,1)S(1)}, u32[]{:S(2)}, u32[]{:S(2)}) collective-permute-start(bf16[2080,128]{1,0:T(8,128)(2,1)} %collective-permute-done.3.refs_1_), channel_id=1, source_target_pairs={{0,4},{4,8},{8,12},{12,16},{16,20},{20,24},{24,28},{28,0},{1,5},{5... | collective-permute-start | bytes 1597448 | tf_op jit(solution)/shard_map/ppermute | solution.py:232
  72.8 3.9 %collective-permute-start.8 = (bf16[2080,128]{1,0:T(8,128)(2,1)S(1)}, bf16[2080,128]{1,0:T(8,128)(2,1)S(1)}, u32[]{:S(2)}, u32[]{:S(2)}) collective-permute-start(bf16[2080,128]{1,0:T(8,128)(2,1)S(1)} %collective-permute-done.7.refs_2_), channel_id=1, source_target_pairs={{0,28},{4,0},{8,4},{12,8},{16,12},{20,16},{24,20},{28,24},{1,29},{... | collective-permute-start | bytes 1597448 | tf_op jit(solution)/shard_map/ppermute | solution.py:232
  76.7 3.8 %shard_map.65 = (f32[8,128,768]{2,1,0:T(8,128)S(1)}, bf16[8,2080,128]{2,1,0:T(8,128)(2,1)S(1)}, bf16[8,3104,128]{2,1,0:T(8,128)(2,1)S(1)}, s32[8,128]{1,0:T(8,128)S(1)}) custom-call(s32[19]{0:T(128)S(1)} %concatenate.26.refs_0_, bf16[2080,128]{1,0:T(8,128)(2,1)} %collective-permute-done.3.refs_1_, ...), custom_call_target="tpu_custom_call", output_to_operand_aliasing={{0}: (5, {}), {1}: (6, {}), {2}: (7, {})} | custom-call | flops 805306368 | bytes 1048576 | tf_op jit(solution)/shard_map/pallas_call | solution.py:144
  80.5 2.1 %collective-permute-done.14.refs_3_ = bf16[3104,128]{1,0:T(8,128)(2,1)S(1)} collective-permute-done((bf16[3104,128]{1,0:T(8,128)(2,1)}, bf16[3104,128]{1,0:T(8,128)(2,1)S(1)}, u32[]{:S(2)}, u32[]{:S(2)}) %collective-permute-start.14) | collective-permute-done | bytes 794656 | tf_op jit(solution)/shard_map/ppermute | solution.py:229
  84.2 3.7 %collective-permute-start.16 = (bf16[1552,128]{1,0:T(8,128)(2,1)S(1)}, bf16[1552,128]{1,0:T(8,128)(2,1)S(1)}, u32[]{:S(2)}, u32[]{:S(2)}) collective-permute-start(bf16[1552,128]{1,0:T(8,128)(2,1)S(1)} %slice.136), channel_id=1, source_target_pairs={{0,288},{32,64},{64,352},{96,128},{128,416},{160,192},{192,480},{2... | collective-permute-start | bytes 1191944 | tf_op jit(solution)/shard_map/ppermute | solution.py:229
  87.9 3.4 %collective-permute-start.17 = (bf16[1552,128]{1,0:T(8,128)(2,1)S(1)}, bf16[1552,128]{1,0:T(8,128)(2,1)S(1)}, u32[]{:S(2)}, u32[]{:S(2)}) collective-permute-start(bf16[1552,128]{1,0:T(8,128)(2,1)S(1)} %slice.137), channel_id=1, source_target_pairs={{0,224},{32,256},{64,32},{96,320},{128,96},{160,384},{192,160},{22... | collective-permute-start | bytes 1191944 | tf_op jit(solution)/shard_map/ppermute | solution.py:229
  91.4 3.3 %collective-permute-start.5 = (bf16[1040,128]{1,0:T(8,128)(2,1)S(1)}, bf16[1040,128]{1,0:T(8,128)(2,1)S(1)}, u32[]{:S(2)}, u32[]{:S(2)}) collective-permute-start(bf16[1040,128]{1,0:T(8,128)(2,1)S(1)} %slice.152), channel_id=1, source_target_pairs={{0,4},{4,8},{8,12},{12,16},{16,20},{20,24},{24,28},{28,0},{1,5},{5... | collective-permute-start | bytes 798728 | tf_op jit(solution)/shard_map/ppermute | solution.py:232
  94.7 4.0 %collective-permute-start.9 = (bf16[1040,128]{1,0:T(8,128)(2,1)S(1)}, bf16[1040,128]{1,0:T(8,128)(2,1)S(1)}, u32[]{:S(2)}, u32[]{:S(2)}) collective-permute-start(bf16[1040,128]{1,0:T(8,128)(2,1)S(1)} %slice.153), channel_id=1, source_target_pairs={{0,28},{4,0},{8,4},{12,8},{16,12},{20,16},{24,20},{28,24},{1,29},{... | collective-permute-start | bytes 798728 | tf_op jit(solution)/shard_map/ppermute | solution.py:232
  98.8 4.5 %shard_map.66 = (f32[8,128,768]{2,1,0:T(8,128)S(1)}, bf16[8,2080,128]{2,1,0:T(8,128)(2,1)S(1)}, bf16[8,3104,128]{2,1,0:T(8,128)(2,1)S(1)}, s32[8,128]{1,0:T(8,128)}) custom-call(s32[19]{0:T(128)S(1)} %concatenate.26.refs_0_, bf16[2080,128]{1,0:T(8,128)(2,1)S(1)} %collective-permute-done.4.refs_1_, ...), custom_call_target="tpu_custom_call", output_to_operand_aliasing={{0}: (5, {}), {1}: (6, {}), {2}: (7, {})} | custom-call | flops 805306368 | bytes 1048576 | tf_op jit(solution)/shard_map/pallas_call | solution.py:144
  103.4 4.0 %shard_map.67 = (f32[8,128,768]{2,1,0:T(8,128)S(1)}, bf16[8,2080,128]{2,1,0:T(8,128)(2,1)S(1)}, bf16[8,3104,128]{2,1,0:T(8,128)(2,1)S(1)}, s32[8,128]{1,0:T(8,128)}) custom-call(s32[19]{0:T(128)S(1)} %concatenate.26.refs_0_, bf16[1040,128]{1,0:T(8,128)(2,1)S(1)} %collective-permute-done.5.refs_1_, ...), custom_call_target="tpu_custom_call", output_to_operand_aliasing={{0}: (5, {}), {1}: (6, {}), {2}: (7, {})} | custom-call | flops 805306368 | bytes 1048576 | tf_op jit(solution)/shard_map/pallas_call | solution.py:144
  107.5 1.9 %collective-permute-start.18 = (f32[4,128,768]{2,1,0:T(8,128)S(1)}, f32[4,128,768]{2,1,0:T(8,128)S(1)}, u32[]{:S(2)}, u32[]{:S(2)}) collective-permute-start(f32[4,128,768]{2,1,0:T(8,128)S(1)} %slice.139), channel_id=1, source_target_pairs={{0,1},{1,0},{2,3},{3,2},{4,5},{5,4},{6,7},{7,6},{8,9},{9,8},{10,11... | collective-permute-start | bytes 4718600 | tf_op jit(solution)/shard_map/ppermute | solution.py:251
  109.5 3.4 %collective-permute-done.18 = f32[4,128,768]{2,1,0:T(8,128)S(1)} collective-permute-done((f32[4,128,768]{2,1,0:T(8,128)S(1)}, f32[4,128,768]{2,1,0:T(8,128)S(1)}, u32[]{:S(2)}, u32[]{:S(2)}) %collective-permute-start.18) | collective-permute-done | bytes 1572896 | tf_op jit(solution)/shard_map/ppermute | solution.py:251
  113.6 3.0 %collective-permute-start.19 = (s16[128,896]{1,0:T(8,128)(2,1)S(1)}, s16[128,896]{1,0:T(8,128)(2,1)S(1)}, u32[]{:S(2)}, u32[]{:S(2)}) collective-permute-start(s16[128,896]{1,0:T(8,128)(2,1)S(1)} %pad_add_fusion), channel_id=1, source_target_pairs={{0,2},{2,0},{256,258},{258,256},{1,3},{3,1},{257,259},{259,257},{4... | collective-permute-start | bytes 688136 | tf_op jit(solution)/shard_map/ppermute | solution.py:255
  116.8 5.4 %collective-permute-start.20 = (s16[128,896]{1,0:T(8,128)(2,1)S(1)}, s16[128,896]{1,0:T(8,128)(2,1)S(1)}, u32[]{:S(2)}, u32[]{:S(2)}) collective-permute-start(s16[128,896]{1,0:T(8,128)(2,1)S(1)} %pad_add_fusion.1), channel_id=1, source_target_pairs={{0,256},{2,258},{256,2},{258,0},{1,257},{3,259},{257,3},{259,1},{4... | collective-permute-start | bytes 688136 | tf_op jit(solution)/shard_map/ppermute | solution.py:255
  122.3 1.9 %collective-permute-start.21 = (s16[128,896]{1,0:T(8,128)(2,1)S(1)}, s16[128,896]{1,0:T(8,128)(2,1)S(1)}, u32[]{:S(2)}, u32[]{:S(2)}) collective-permute-start(s16[128,896]{1,0:T(8,128)(2,1)S(1)} %pad_add_fusion.2), channel_id=1, source_target_pairs={{0,258},{2,256},{256,0},{258,2},{1,259},{3,257},{257,1},{259,3},{4... | collective-permute-start | bytes 688136 | tf_op jit(solution)/shard_map/ppermute | solution.py:255
  124.8 3.5 %collective-permute-done.20 = s16[128,896]{1,0:T(8,128)(2,1)S(1)} collective-permute-done((s16[128,896]{1,0:T(8,128)(2,1)S(1)}, s16[128,896]{1,0:T(8,128)(2,1)S(1)}, u32[]{:S(2)}, u32[]{:S(2)}) %collective-permute-start.20) | collective-permute-done | bytes 229408 | tf_op jit(solution)/shard_map/ppermute | solution.py:255
  128.4 4.1 %collective-permute-done.21 = s16[128,896]{1,0:T(8,128)(2,1)S(1)} collective-permute-done((s16[128,896]{1,0:T(8,128)(2,1)S(1)}, s16[128,896]{1,0:T(8,128)(2,1)S(1)}, u32[]{:S(2)}, u32[]{:S(2)}) %collective-permute-start.21) | collective-permute-done | bytes 229408 | tf_op jit(solution)/shard_map/ppermute | solution.py:255
  (61 shorter events, 12.0 us)
Async XLA Ops:
  0.0 5.8 %copy-start = (bf16[1,8,1,3,128,128]{5,4,3,2,1,0:T(8,128)(2,1)S(1)}, bf16[1,8,1,3,128,128]{5,4,3,2,1,0:T(8,128)(2,1)}, u32[]{:S(2)}) copy-start(bf16[1,8,1,3,128,128]{5,4,3,2,1,0:T(8,128)(2,1)} %param.16) | copy-start | bytes 2359300
  0.0 5.9 %copy-start.1 = (s32[1,8,1,3]{1,2,3,0:T(1,128)S(1)}, s32[1,8,1,3]{1,2,3,0:T(1,128)}, u32[]{:S(2)}) copy-start(s32[1,8,1,3]{1,2,3,0:T(1,128)} %param.17) | copy-start | bytes 292
  1.1 10.8 %collective-permute-start = (bf16[1024,128]{1,0:T(8,128)(2,1)S(1)}, bf16[1024,128]{1,0:T(8,128)(2,1)S(1)}, u32[]{:S(2)}, u32[]{:S(2)}) collective-permute-start(bf16[1024,128]{1,0:T(8,128)(2,1)S(1)} %get-tuple-element.110), channel_id=1, source_target_pairs={{0,256},{256,0},{1,257},{257,1},{2,258},{258,2},{3,259},{259,3},{4... | collective-permute-start | bytes 786440 | tf_op jit(solution)/shard_map/ppermute | solution.py:204
  5.9 48.1 %copy-start.2 = (s32[8]{0:T(128)S(1)}, s32[8]{0:T(128)}, u32[]{:S(2)}) copy-start(s32[8]{0:T(128)} %constant.239.clone) | copy-start | bytes 100
  5.9 48.1 %copy-start.3 = (s32[8]{0:T(128)S(1)}, s32[8]{0:T(128)}, u32[]{:S(2)}) copy-start(s32[8]{0:T(128)} %constant.240.clone) | copy-start | bytes 100
  6.5 5.5 %collective-permute-start.1 = (bf16[16,128]{1,0:T(8,128)(2,1)S(1)}, bf16[16,128]{1,0:T(8,128)(2,1)S(1)}, u32[]{:S(2)}, u32[]{:S(2)}) collective-permute-start(bf16[16,128]{1,0:T(8,128)(2,1)S(1)} %scatter.19), channel_id=1, source_target_pairs={{0,256},{256,0},{1,257},{257,1},{2,258},{258,2},{3,259},{259,3},{4... | collective-permute-start | bytes 12296 | tf_op jit(solution)/shard_map/ppermute | solution.py:206
  12.0 27.6 %collective-permute-start.10 = (bf16[3104,128]{1,0:T(8,128)(2,1)S(1)}, bf16[3104,128]{1,0:T(8,128)(2,1)S(1)}, u32[]{:S(2)}, u32[]{:S(2)}) collective-permute-start(bf16[3104,128]{1,0:T(8,128)(2,1)S(1)} %fusion.7.refs_4_), channel_id=1, source_target_pairs={{0,288},{32,64},{64,352},{96,128},{128,416},{160,192},{192,480},{2... | collective-permute-start | bytes 2383880 | tf_op jit(solution)/shard_map/ppermute | solution.py:229
  16.9 24.6 %collective-permute-start.12 = (bf16[3104,128]{1,0:T(8,128)(2,1)S(1)}, bf16[3104,128]{1,0:T(8,128)(2,1)S(1)}, u32[]{:S(2)}, u32[]{:S(2)}) collective-permute-start(bf16[3104,128]{1,0:T(8,128)(2,1)S(1)} %fusion.7.refs_4_), channel_id=1, source_target_pairs={{0,224},{32,256},{64,32},{96,320},{128,96},{160,384},{192,160},{22... | collective-permute-start | bytes 2383880 | tf_op jit(solution)/shard_map/ppermute | solution.py:229
  24.9 21.8 %collective-permute-start.2 = (bf16[2080,128]{1,0:T(8,128)(2,1)S(1)}, bf16[2080,128]{1,0:T(8,128)(2,1)}, u32[]{:S(2)}, u32[]{:S(2)}) collective-permute-start(bf16[2080,128]{1,0:T(8,128)(2,1)S(1)} %fusion.10.refs_1_), channel_id=1, source_target_pairs={{0,4},{4,8},{8,12},{12,16},{16,20},{20,24},{24,28},{28,0},{1,5},{5... | collective-permute-start | bytes 1597448 | tf_op jit(solution)/shard_map/ppermute | solution.py:232
  28.4 21.8 %collective-permute-start.6 = (bf16[2080,128]{1,0:T(8,128)(2,1)S(1)}, bf16[2080,128]{1,0:T(8,128)(2,1)}, u32[]{:S(2)}, u32[]{:S(2)}) collective-permute-start(bf16[2080,128]{1,0:T(8,128)(2,1)S(1)} %fusion.10.refs_1_), channel_id=1, source_target_pairs={{0,28},{4,0},{8,4},{12,8},{16,12},{20,16},{24,20},{28,24},{1,29},{... | collective-permute-start | bytes 1597448 | tf_op jit(solution)/shard_map/ppermute | solution.py:232
  39.6 21.1 %collective-permute-start.11 = (bf16[3104,128]{1,0:T(8,128)(2,1)S(1)}, bf16[3104,128]{1,0:T(8,128)(2,1)}, u32[]{:S(2)}, u32[]{:S(2)}) collective-permute-start(bf16[3104,128]{1,0:T(8,128)(2,1)S(1)} %collective-permute-done.10.refs_5_), channel_id=1, source_target_pairs={{0,288},{32,64},{64,352},{96,128},{128,416},{160,192},{192,480},{2... | collective-permute-start | bytes 2383880 | tf_op jit(solution)/shard_map/ppermute | solution.py:229
  41.5 20.8 %collective-permute-start.13 = (bf16[3104,128]{1,0:T(8,128)(2,1)S(1)}, bf16[3104,128]{1,0:T(8,128)(2,1)}, u32[]{:S(2)}, u32[]{:S(2)}) collective-permute-start(bf16[3104,128]{1,0:T(8,128)(2,1)S(1)} %collective-permute-done.12.refs_6_), channel_id=1, source_target_pairs={{0,224},{32,256},{64,32},{96,320},{128,96},{160,384},{192,160},{22... | collective-permute-start | bytes 2383880 | tf_op jit(solution)/shard_map/ppermute | solution.py:229
  46.7 22.7 %collective-permute-start.3 = (bf16[2080,128]{1,0:T(8,128)(2,1)}, bf16[2080,128]{1,0:T(8,128)(2,1)}, u32[]{:S(2)}, u32[]{:S(2)}) collective-permute-start(bf16[2080,128]{1,0:T(8,128)(2,1)} %collective-permute-done.2.refs_2_), channel_id=1, source_target_pairs={{0,4},{4,8},{8,12},{12,16},{16,20},{20,24},{24,28},{28,0},{1,5},{5... | collective-permute-start | bytes 1597448 | tf_op jit(solution)/shard_map/ppermute | solution.py:232
  50.2 22.6 %collective-permute-start.7 = (bf16[2080,128]{1,0:T(8,128)(2,1)}, bf16[2080,128]{1,0:T(8,128)(2,1)S(1)}, u32[]{:S(2)}, u32[]{:S(2)}) collective-permute-start(bf16[2080,128]{1,0:T(8,128)(2,1)} %collective-permute-done.6.refs_3_), channel_id=1, source_target_pairs={{0,28},{4,0},{8,4},{12,8},{16,12},{20,16},{24,20},{28,24},{1,29},{... | collective-permute-start | bytes 1597448 | tf_op jit(solution)/shard_map/ppermute | solution.py:232
  62.3 20.3 %collective-permute-start.14 = (bf16[3104,128]{1,0:T(8,128)(2,1)}, bf16[3104,128]{1,0:T(8,128)(2,1)S(1)}, u32[]{:S(2)}, u32[]{:S(2)}) collective-permute-start(bf16[3104,128]{1,0:T(8,128)(2,1)} %collective-permute-done.11.refs_3_), channel_id=1, source_target_pairs={{0,288},{32,64},{64,352},{96,128},{128,416},{160,192},{192,480},{2... | collective-permute-start | bytes 2383880 | tf_op jit(solution)/shard_map/ppermute | solution.py:229
  64.2 20.0 %collective-permute-start.15 = (bf16[3104,128]{1,0:T(8,128)(2,1)}, bf16[3104,128]{1,0:T(8,128)(2,1)S(1)}, u32[]{:S(2)}, u32[]{:S(2)}) collective-permute-start(bf16[3104,128]{1,0:T(8,128)(2,1)} %collective-permute-done.13.refs_4_), channel_id=1, source_target_pairs={{0,224},{32,256},{64,32},{96,320},{128,96},{160,384},{192,160},{22... | collective-permute-start | bytes 2383880 | tf_op jit(solution)/shard_map/ppermute | solution.py:229
  69.4 22.0 %collective-permute-start.4 = (bf16[2080,128]{1,0:T(8,128)(2,1)}, bf16[2080,128]{1,0:T(8,128)(2,1)S(1)}, u32[]{:S(2)}, u32[]{:S(2)}) collective-permute-start(bf16[2080,128]{1,0:T(8,128)(2,1)} %collective-permute-done.3.refs_1_), channel_id=1, source_target_pairs={{0,4},{4,8},{8,12},{12,16},{16,20},{20,24},{24,28},{28,0},{1,5},{5... | collective-permute-start | bytes 1597448 | tf_op jit(solution)/shard_map/ppermute | solution.py:232
  72.8 21.9 %collective-permute-start.8 = (bf16[2080,128]{1,0:T(8,128)(2,1)S(1)}, bf16[2080,128]{1,0:T(8,128)(2,1)S(1)}, u32[]{:S(2)}, u32[]{:S(2)}) collective-permute-start(bf16[2080,128]{1,0:T(8,128)(2,1)S(1)} %collective-permute-done.7.refs_2_), channel_id=1, source_target_pairs={{0,28},{4,0},{8,4},{12,8},{16,12},{20,16},{24,20},{28,24},{1,29},{... | collective-permute-start | bytes 1597448 | tf_op jit(solution)/shard_map/ppermute | solution.py:232
  84.2 19.1 %collective-permute-start.16 = (bf16[1552,128]{1,0:T(8,128)(2,1)S(1)}, bf16[1552,128]{1,0:T(8,128)(2,1)S(1)}, u32[]{:S(2)}, u32[]{:S(2)}) collective-permute-start(bf16[1552,128]{1,0:T(8,128)(2,1)S(1)} %slice.136), channel_id=1, source_target_pairs={{0,288},{32,64},{64,352},{96,128},{128,416},{160,192},{192,480},{2... | collective-permute-start | bytes 1191944 | tf_op jit(solution)/shard_map/ppermute | solution.py:229
  87.9 15.4 %collective-permute-start.17 = (bf16[1552,128]{1,0:T(8,128)(2,1)S(1)}, bf16[1552,128]{1,0:T(8,128)(2,1)S(1)}, u32[]{:S(2)}, u32[]{:S(2)}) collective-permute-start(bf16[1552,128]{1,0:T(8,128)(2,1)S(1)} %slice.137), channel_id=1, source_target_pairs={{0,224},{32,256},{64,32},{96,320},{128,96},{160,384},{192,160},{22... | collective-permute-start | bytes 1191944 | tf_op jit(solution)/shard_map/ppermute | solution.py:229
  91.4 11.9 %collective-permute-start.5 = (bf16[1040,128]{1,0:T(8,128)(2,1)S(1)}, bf16[1040,128]{1,0:T(8,128)(2,1)S(1)}, u32[]{:S(2)}, u32[]{:S(2)}) collective-permute-start(bf16[1040,128]{1,0:T(8,128)(2,1)S(1)} %slice.152), channel_id=1, source_target_pairs={{0,4},{4,8},{8,12},{12,16},{16,20},{20,24},{24,28},{28,0},{1,5},{5... | collective-permute-start | bytes 798728 | tf_op jit(solution)/shard_map/ppermute | solution.py:232
  94.7 8.6 %collective-permute-start.9 = (bf16[1040,128]{1,0:T(8,128)(2,1)S(1)}, bf16[1040,128]{1,0:T(8,128)(2,1)S(1)}, u32[]{:S(2)}, u32[]{:S(2)}) collective-permute-start(bf16[1040,128]{1,0:T(8,128)(2,1)S(1)} %slice.153), channel_id=1, source_target_pairs={{0,28},{4,0},{8,4},{12,8},{16,12},{20,16},{24,20},{28,24},{1,29},{... | collective-permute-start | bytes 798728 | tf_op jit(solution)/shard_map/ppermute | solution.py:232
  107.5 5.3 %collective-permute-start.18 = (f32[4,128,768]{2,1,0:T(8,128)S(1)}, f32[4,128,768]{2,1,0:T(8,128)S(1)}, u32[]{:S(2)}, u32[]{:S(2)}) collective-permute-start(f32[4,128,768]{2,1,0:T(8,128)S(1)} %slice.139), channel_id=1, source_target_pairs={{0,1},{1,0},{2,3},{3,2},{4,5},{5,4},{6,7},{7,6},{8,9},{9,8},{10,11... | collective-permute-start | bytes 4718600 | tf_op jit(solution)/shard_map/ppermute | solution.py:251
  113.6 11.0 %collective-permute-start.19 = (s16[128,896]{1,0:T(8,128)(2,1)S(1)}, s16[128,896]{1,0:T(8,128)(2,1)S(1)}, u32[]{:S(2)}, u32[]{:S(2)}) collective-permute-start(s16[128,896]{1,0:T(8,128)(2,1)S(1)} %pad_add_fusion), channel_id=1, source_target_pairs={{0,2},{2,0},{256,258},{258,256},{1,3},{3,1},{257,259},{259,257},{4... | collective-permute-start | bytes 688136 | tf_op jit(solution)/shard_map/ppermute | solution.py:255
  116.8 11.5 %collective-permute-start.20 = (s16[128,896]{1,0:T(8,128)(2,1)S(1)}, s16[128,896]{1,0:T(8,128)(2,1)S(1)}, u32[]{:S(2)}, u32[]{:S(2)}) collective-permute-start(s16[128,896]{1,0:T(8,128)(2,1)S(1)} %pad_add_fusion.1), channel_id=1, source_target_pairs={{0,256},{2,258},{256,2},{258,0},{1,257},{3,259},{257,3},{259,1},{4... | collective-permute-start | bytes 688136 | tf_op jit(solution)/shard_map/ppermute | solution.py:255
  122.3 10.2 %collective-permute-start.21 = (s16[128,896]{1,0:T(8,128)(2,1)S(1)}, s16[128,896]{1,0:T(8,128)(2,1)S(1)}, u32[]{:S(2)}, u32[]{:S(2)}) collective-permute-start(s16[128,896]{1,0:T(8,128)(2,1)S(1)} %pad_add_fusion.2), channel_id=1, source_target_pairs={{0,258},{2,256},{256,0},{258,2},{1,259},{3,257},{257,1},{259,3},{4... | collective-permute-start | bytes 688136 | tf_op jit(solution)/shard_map/ppermute | solution.py:255

commit v10 on v8

--- a/solution.py
+++ b/solution.py
@@ -178,17 +178,21 @@
     own = (side + y // 4 + y % 4) % 2
 
     def group(which):
-        return with_index(
-            lax.dynamic_index_in_dim(left, which, 0, False),
-            lax.dynamic_index_in_dim(rows, which, 0, False),
-        )
-
-    swapped = lax.ppermute(group(1 - own), "x_lo", [(0, 1), (1, 0)])
-    pair = jnp.concatenate([group(own), swapped], axis=0)
+        return lax.dynamic_index_in_dim(left, which, 0, False)
+
+    def group_index(which):
+        picked = lax.dynamic_index_in_dim(rows, which, 0, False).astype(left.dtype)
+        return jnp.zeros((PAD, W), left.dtype).at[0, :GROUP].set(picked)
+
     right = right_blocks.reshape(2, HALF, EB * W, W)
     cols = right_cols.reshape(2, HALF * EB)
     chunk = jnp.concatenate([with_index(right[h], cols[h]) for h in range(2)], axis=0)
-    first, _ = lax.optimization_barrier((chunk, swapped))
+    swap = [(0, 1), (1, 0)]
+    swapped = lax.ppermute(group(1 - own), "x_lo", swap)
+    chunk, other = lax.optimization_barrier((chunk, group_index(1 - own)))
+    swapped_index = lax.ppermute(other, "x_lo", swap)
+    first, swapped = lax.optimization_barrier((chunk, swapped))
+    pair = jnp.concatenate([group(own), group_index(own), swapped, swapped_index], axis=0)
 
     source = (z + jnp.array([0, -1, 1, -2, 2, -3, 3, 4], jnp.int32)) % NZ
     away = (4 * (zig(source) ^ side) + source // 2 - y) % NY

time: 137 us -> 135 us (0.985)
  the two profiles are of different devices: /device:TPU:6 before, /device:TPU:30 now
where the time goes in v10:
time: 135 us; the launch traced here: 134 us
  starting transfers between devices  77.5 us (57%)
  waiting for transfers between devices  33.7 us (25%)
  Pallas kernels  16.3 us (12%)
  other arithmetic  3.55 us (3%)
  local copies, waits for them, and re-layouts  2.81 us (2%)
    ppermute x8, starting transfers between devices, step_y(): return (lax.ppermute(fore, 'y', turn(1)), lax.ppermute(back, 'y', turn(-1)))  26.8 us
    ppermute x4, starting transfers between devices, step_z(): lax.ppermute(down, row, ring_pairs(-1))  22.1 us
    pallas_call x4, Pallas kernels, run_stage(): pl.pallas_call(lambda *refs: stage(number, new_left, new_right, slots, ch...  16.3 us
    ppermute x4, starting transfers between devices, step_z(): lax.ppermute(up, row, ring_pairs(1))  12 us
    ppermute x3, starting transfers between devices, per_device(): lax.ppermute(encode(total[step]), ('x_lo', 'x_hi'), chip_pairs(step))  9.26 us
    ppermute x4, waiting for transfers between devices, step_z(): lax.ppermute(up, row, ring_pairs(1))  8.27 us
    ppermute x3, waiting for transfers between devices, per_device(): lax.ppermute(encode(total[step]), ('x_lo', 'x_hi'), chip_pairs(step))  8.02 us
    ppermute x1, waiting for transfers between devices, per_device(): swapped = lax.ppermute(group(1 - own), 'x_lo', swap)  4.62 us
  transfers between devices with their start and end apart: 22, of which 12 were waited for; matrix products, arithmetic and copies ran while one was open for 2% of the time, Pallas kernels for 9%

profile of v10, /device:TPU:30, one launch (start us, length us, event | category | flops | bytes accessed | tf_op | source)
XLA Modules:
  0.0 134.4 jit_solution(3659126072739347917)
XLA Ops:
  1.1 2.7 %collective-permute-start = (bf16[1024,128]{1,0:T(8,128)(2,1)S(1)}, bf16[1024,128]{1,0:T(8,128)(2,1)S(1)}, u32[]{:S(2)}, u32[]{:S(2)}) collective-permute-start(bf16[1024,128]{1,0:T(8,128)(2,1)S(1)} %get-tuple-element.108), channel_id=1, source_target_pairs={{0,256},{256,0},{1,257},{257,1},{2,258},{258,2},{3,259},{259,3},{4... | collective-permute-start | bytes 786440 | tf_op jit(solution)/shard_map/ppermute | solution.py:191
  6.5 4.6 %collective-permute-done = bf16[1024,128]{1,0:T(8,128)(2,1)S(1)} collective-permute-done((bf16[1024,128]{1,0:T(8,128)(2,1)S(1)}, bf16[1024,128]{1,0:T(8,128)(2,1)S(1)}, u32[]{:S(2)}, u32[]{:S(2)}) %collective-permute-start) | collective-permute-done | bytes 262176 | tf_op jit(solution)/shard_map/ppermute | solution.py:191
  11.1 4.5 %collective-permute-start.10 = (bf16[3104,128]{1,0:T(8,128)(2,1)S(1)}, bf16[3104,128]{1,0:T(8,128)(2,1)S(1)}, u32[]{:S(2)}, u32[]{:S(2)}) collective-permute-start(bf16[3104,128]{1,0:T(8,128)(2,1)S(1)} %fusion.7.refs_4_), channel_id=1, source_target_pairs={{0,288},{32,64},{64,352},{96,128},{128,416},{160,192},{192,480},{2... | collective-permute-start | bytes 2383880 | tf_op jit(solution)/shard_map/ppermute | solution.py:216
  15.6 8.3 %collective-permute-start.12 = (bf16[3104,128]{1,0:T(8,128)(2,1)S(1)}, bf16[3104,128]{1,0:T(8,128)(2,1)S(1)}, u32[]{:S(2)}, u32[]{:S(2)}) collective-permute-start(bf16[3104,128]{1,0:T(8,128)(2,1)S(1)} %fusion.7.refs_4_), channel_id=1, source_target_pairs={{0,224},{32,256},{64,32},{96,320},{128,96},{160,384},{192,160},{22... | collective-permute-start | bytes 2383880 | tf_op jit(solution)/shard_map/ppermute | solution.py:216
  24.0 2.7 %collective-permute-start.1 = (bf16[16,128]{1,0:T(8,128)(2,1)S(1)}, bf16[16,128]{1,0:T(8,128)(2,1)S(1)}, u32[]{:S(2)}, u32[]{:S(2)}) collective-permute-start(bf16[16,128]{1,0:T(8,128)(2,1)S(1)} %scatter.19), channel_id=1, source_target_pairs={{0,256},{256,0},{1,257},{257,1},{2,258},{258,2},{3,259},{259,3},{4... | collective-permute-start | bytes 12296 | tf_op jit(solution)/shard_map/ppermute | solution.py:193
  26.7 3.1 %collective-permute-done.1 = bf16[16,128]{1,0:T(8,128)(2,1)S(1)} collective-permute-done((bf16[16,128]{1,0:T(8,128)(2,1)S(1)}, bf16[16,128]{1,0:T(8,128)(2,1)S(1)}, u32[]{:S(2)}, u32[]{:S(2)}) %collective-permute-start.1) | collective-permute-done | bytes 4128 | tf_op jit(solution)/shard_map/ppermute | solution.py:193
  29.8 4.7 %collective-permute-start.2 = (bf16[2080,128]{1,0:T(8,128)(2,1)S(1)}, bf16[2080,128]{1,0:T(8,128)(2,1)}, u32[]{:S(2)}, u32[]{:S(2)}) collective-permute-start(bf16[2080,128]{1,0:T(8,128)(2,1)S(1)} %fusion.10.refs_1_), channel_id=1, source_target_pairs={{0,4},{4,8},{8,12},{12,16},{16,20},{20,24},{24,28},{28,0},{1,5},{5... | collective-permute-start | bytes 1597448 | tf_op jit(solution)/shard_map/ppermute | solution.py:219
  34.5 1.9 %collective-permute-start.6 = (bf16[2080,128]{1,0:T(8,128)(2,1)S(1)}, bf16[2080,128]{1,0:T(8,128)(2,1)}, u32[]{:S(2)}, u32[]{:S(2)}) collective-permute-start(bf16[2080,128]{1,0:T(8,128)(2,1)S(1)} %fusion.10.refs_1_), channel_id=1, source_target_pairs={{0,28},{4,0},{8,4},{12,8},{16,12},{20,16},{24,20},{28,24},{1,29},{... | collective-permute-start | bytes 1597448 | tf_op jit(solution)/shard_map/ppermute | solution.py:219
  36.5 2.4 %collective-permute-done.10.refs_5_ = bf16[3104,128]{1,0:T(8,128)(2,1)S(1)} collective-permute-done((bf16[3104,128]{1,0:T(8,128)(2,1)S(1)}, bf16[3104,128]{1,0:T(8,128)(2,1)S(1)}, u32[]{:S(2)}, u32[]{:S(2)}) %collective-permute-start.10) | collective-permute-done | bytes 794656 | tf_op jit(solution)/shard_map/ppermute | solution.py:216
  40.8 5.1 %collective-permute-start.13 = (bf16[3104,128]{1,0:T(8,128)(2,1)S(1)}, bf16[3104,128]{1,0:T(8,128)(2,1)}, u32[]{:S(2)}, u32[]{:S(2)}) collective-permute-start(bf16[3104,128]{1,0:T(8,128)(2,1)S(1)} %collective-permute-done.12.refs_6_), channel_id=1, source_target_pairs={{0,224},{32,256},{64,32},{96,320},{128,96},{160,384},{192,160},{22... | collective-permute-start | bytes 2383880 | tf_op jit(solution)/shard_map/ppermute | solution.py:216
  45.9 4.7 %collective-permute-start.3 = (bf16[2080,128]{1,0:T(8,128)(2,1)}, bf16[2080,128]{1,0:T(8,128)(2,1)}, u32[]{:S(2)}, u32[]{:S(2)}) collective-permute-start(bf16[2080,128]{1,0:T(8,128)(2,1)} %collective-permute-done.2.refs_2_), channel_id=1, source_target_pairs={{0,4},{4,8},{8,12},{12,16},{16,20},{20,24},{24,28},{28,0},{1,5},{5... | collective-permute-start | bytes 1597448 | tf_op jit(solution)/shard_map/ppermute | solution.py:219
  52.7 3.4 %shard_map.64 = (f32[8,128,768]{2,1,0:T(8,128)S(1)}, bf16[8,2080,128]{2,1,0:T(8,128)(2,1)S(1)}, bf16[8,3104,128]{2,1,0:T(8,128)(2,1)S(1)}, s32[8,128]{1,0:T(8,128)S(1)}) custom-call(s32[19]{0:T(128)S(1)} %concatenate.26.refs_0_, bf16[2080,128]{1,0:T(8,128)(2,1)S(1)} %fusion.10.refs_1_, bf16[2080,128]{1,0:T(8,128)(2,1)} %collective-permute-done.2.refs_2_, ...), custom_call_target="tpu_custom_call" | custom-call | flops 805306368 | bytes 1048576 | tf_op jit(solution)/shard_map/pallas_call | solution.py:131
  56.2 3.8 %collective-permute-done.11.refs_3_ = bf16[3104,128]{1,0:T(8,128)(2,1)} collective-permute-done((bf16[3104,128]{1,0:T(8,128)(2,1)S(1)}, bf16[3104,128]{1,0:T(8,128)(2,1)}, u32[]{:S(2)}, u32[]{:S(2)}) %collective-permute-start.11) | collective-permute-done | bytes 794656 | tf_op jit(solution)/shard_map/ppermute | solution.py:216
  63.5 5.2 %collective-permute-start.15 = (bf16[3104,128]{1,0:T(8,128)(2,1)}, bf16[3104,128]{1,0:T(8,128)(2,1)S(1)}, u32[]{:S(2)}, u32[]{:S(2)}) collective-permute-start(bf16[3104,128]{1,0:T(8,128)(2,1)} %collective-permute-done.13.refs_4_), channel_id=1, source_target_pairs={{0,224},{32,256},{64,32},{96,320},{128,96},{160,384},{192,160},{22... | collective-permute-start | bytes 2383880 | tf_op jit(solution)/shard_map/ppermute | solution.py:216
  68.7 4.8 %collective-permute-start.4 = (bf16[2080,128]{1,0:T(8,128)(2,1)}, bf16[2080,128]{1,0:T(8,128)(2,1)S(1)}, u32[]{:S(2)}, u32[]{:S(2)}) collective-permute-start(bf16[2080,128]{1,0:T(8,128)(2,1)} %collective-permute-done.3.refs_1_), channel_id=1, source_target_pairs={{0,4},{4,8},{8,12},{12,16},{16,20},{20,24},{24,28},{28,0},{1,5},{5... | collective-permute-start | bytes 1597448 | tf_op jit(solution)/shard_map/ppermute | solution.py:219
  73.5 1.9 %collective-permute-start.8 = (bf16[2080,128]{1,0:T(8,128)(2,1)S(1)}, bf16[2080,128]{1,0:T(8,128)(2,1)S(1)}, u32[]{:S(2)}, u32[]{:S(2)}) collective-permute-start(bf16[2080,128]{1,0:T(8,128)(2,1)S(1)} %collective-permute-done.7.refs_2_), channel_id=1, source_target_pairs={{0,28},{4,0},{8,4},{12,8},{16,12},{20,16},{24,20},{28,24},{1,29},{... | collective-permute-start | bytes 1597448 | tf_op jit(solution)/shard_map/ppermute | solution.py:219
  75.5 4.5 %shard_map.65 = (f32[8,128,768]{2,1,0:T(8,128)S(1)}, bf16[8,2080,128]{2,1,0:T(8,128)(2,1)S(1)}, bf16[8,3104,128]{2,1,0:T(8,128)(2,1)S(1)}, s32[8,128]{1,0:T(8,128)S(1)}) custom-call(s32[19]{0:T(128)S(1)} %concatenate.26.refs_0_, bf16[2080,128]{1,0:T(8,128)(2,1)} %collective-permute-done.3.refs_1_, ...), custom_call_target="tpu_custom_call", output_to_operand_aliasing={{0}: (5, {}), {1}: (6, {}), {2}: (7, {})} | custom-call | flops 805306368 | bytes 1048576 | tf_op jit(solution)/shard_map/pallas_call | solution.py:131
  79.9 2.1 %collective-permute-done.14.refs_3_ = bf16[3104,128]{1,0:T(8,128)(2,1)S(1)} collective-permute-done((bf16[3104,128]{1,0:T(8,128)(2,1)}, bf16[3104,128]{1,0:T(8,128)(2,1)S(1)}, u32[]{:S(2)}, u32[]{:S(2)}) %collective-permute-start.14) | collective-permute-done | bytes 794656 | tf_op jit(solution)/shard_map/ppermute | solution.py:216
  83.6 3.7 %collective-permute-start.16 = (bf16[1552,128]{1,0:T(8,128)(2,1)S(1)}, bf16[1552,128]{1,0:T(8,128)(2,1)S(1)}, u32[]{:S(2)}, u32[]{:S(2)}) collective-permute-start(bf16[1552,128]{1,0:T(8,128)(2,1)S(1)} %slice.136), channel_id=1, source_target_pairs={{0,288},{32,64},{64,352},{96,128},{128,416},{160,192},{192,480},{2... | collective-permute-start | bytes 1191944 | tf_op jit(solution)/shard_map/ppermute | solution.py:216
  87.3 3.5 %collective-permute-start.17 = (bf16[1552,128]{1,0:T(8,128)(2,1)S(1)}, bf16[1552,128]{1,0:T(8,128)(2,1)S(1)}, u32[]{:S(2)}, u32[]{:S(2)}) collective-permute-start(bf16[1552,128]{1,0:T(8,128)(2,1)S(1)} %slice.137), channel_id=1, source_target_pairs={{0,224},{32,256},{64,32},{96,320},{128,96},{160,384},{192,160},{22... | collective-permute-start | bytes 1191944 | tf_op jit(solution)/shard_map/ppermute | solution.py:216
  90.8 4.9 %collective-permute-start.5 = (bf16[1040,128]{1,0:T(8,128)(2,1)S(1)}, bf16[1040,128]{1,0:T(8,128)(2,1)S(1)}, u32[]{:S(2)}, u32[]{:S(2)}) collective-permute-start(bf16[1040,128]{1,0:T(8,128)(2,1)S(1)} %slice.152), channel_id=1, source_target_pairs={{0,4},{4,8},{8,12},{12,16},{16,20},{20,24},{24,28},{28,0},{1,5},{5... | collective-permute-start | bytes 798728 | tf_op jit(solution)/shard_map/ppermute | solution.py:219
  95.8 1.9 %collective-permute-start.9 = (bf16[1040,128]{1,0:T(8,128)(2,1)S(1)}, bf16[1040,128]{1,0:T(8,128)(2,1)S(1)}, u32[]{:S(2)}, u32[]{:S(2)}) collective-permute-start(bf16[1040,128]{1,0:T(8,128)(2,1)S(1)} %slice.153), channel_id=1, source_target_pairs={{0,28},{4,0},{8,4},{12,8},{16,12},{20,16},{24,20},{28,24},{1,29},{... | collective-permute-start | bytes 798728 | tf_op jit(solution)/shard_map/ppermute | solution.py:219
  97.7 4.4 %shard_map.66 = (f32[8,128,768]{2,1,0:T(8,128)S(1)}, bf16[8,2080,128]{2,1,0:T(8,128)(2,1)S(1)}, bf16[8,3104,128]{2,1,0:T(8,128)(2,1)S(1)}, s32[8,128]{1,0:T(8,128)}) custom-call(s32[19]{0:T(128)S(1)} %concatenate.26.refs_0_, bf16[2080,128]{1,0:T(8,128)(2,1)S(1)} %collective-permute-done.4.refs_1_, ...), custom_call_target="tpu_custom_call", output_to_operand_aliasing={{0}: (5, {}), {1}: (6, {}), {2}: (7, {})} | custom-call | flops 805306368 | bytes 1048576 | tf_op jit(solution)/shard_map/pallas_call | solution.py:131
  102.2 3.1 %collective-permute-done.9.refs_2_ = bf16[1040,128]{1,0:T(8,128)(2,1)S(1)} collective-permute-done((bf16[1040,128]{1,0:T(8,128)(2,1)S(1)}, bf16[1040,128]{1,0:T(8,128)(2,1)S(1)}, u32[]{:S(2)}, u32[]{:S(2)}) %collective-permute-start.9) | collective-permute-done | bytes 266272 | tf_op jit(solution)/shard_map/ppermute | solution.py:219
  105.3 4.0 %shard_map.67 = (f32[8,128,768]{2,1,0:T(8,128)S(1)}, bf16[8,2080,128]{2,1,0:T(8,128)(2,1)S(1)}, bf16[8,3104,128]{2,1,0:T(8,128)(2,1)S(1)}, s32[8,128]{1,0:T(8,128)}) custom-call(s32[19]{0:T(128)S(1)} %concatenate.26.refs_0_, bf16[1040,128]{1,0:T(8,128)(2,1)S(1)} %collective-permute-done.5.refs_1_, ...), custom_call_target="tpu_custom_call", output_to_operand_aliasing={{0}: (5, {}), {1}: (6, {}), {2}: (7, {})} | custom-call | flops 805306368 | bytes 1048576 | tf_op jit(solution)/shard_map/pallas_call | solution.py:131
  109.4 1.9 %collective-permute-start.18 = (f32[4,128,768]{2,1,0:T(8,128)S(1)}, f32[4,128,768]{2,1,0:T(8,128)S(1)}, u32[]{:S(2)}, u32[]{:S(2)}) collective-permute-start(f32[4,128,768]{2,1,0:T(8,128)S(1)} %slice.139), channel_id=1, source_target_pairs={{0,1},{1,0},{2,3},{3,2},{4,5},{5,4},{6,7},{7,6},{8,9},{9,8},{10,11... | collective-permute-start | bytes 4718600 | tf_op jit(solution)/shard_map/ppermute | solution.py:238
  111.3 3.4 %collective-permute-done.18 = f32[4,128,768]{2,1,0:T(8,128)S(1)} collective-permute-done((f32[4,128,768]{2,1,0:T(8,128)S(1)}, f32[4,128,768]{2,1,0:T(8,128)S(1)}, u32[]{:S(2)}, u32[]{:S(2)}) %collective-permute-start.18) | collective-permute-done | bytes 1572896 | tf_op jit(solution)/shard_map/ppermute | solution.py:238
  115.5 3.3 %collective-permute-start.19 = (s16[128,896]{1,0:T(8,128)(2,1)S(1)}, s16[128,896]{1,0:T(8,128)(2,1)S(1)}, u32[]{:S(2)}, u32[]{:S(2)}) collective-permute-start(s16[128,896]{1,0:T(8,128)(2,1)S(1)} %pad_add_fusion), channel_id=1, source_target_pairs={{0,2},{2,0},{256,258},{258,256},{1,3},{3,1},{257,259},{259,257},{4... | collective-permute-start | bytes 688136 | tf_op jit(solution)/shard_map/ppermute | solution.py:242
  118.9 4.0 %collective-permute-start.20 = (s16[128,896]{1,0:T(8,128)(2,1)S(1)}, s16[128,896]{1,0:T(8,128)(2,1)S(1)}, u32[]{:S(2)}, u32[]{:S(2)}) collective-permute-start(s16[128,896]{1,0:T(8,128)(2,1)S(1)} %pad_add_fusion.1), channel_id=1, source_target_pairs={{0,256},{2,258},{256,2},{258,0},{1,257},{3,259},{257,3},{259,1},{4... | collective-permute-start | bytes 688136 | tf_op jit(solution)/shard_map/ppermute | solution.py:242
  123.1 1.9 %collective-permute-start.21 = (s16[128,896]{1,0:T(8,128)(2,1)S(1)}, s16[128,896]{1,0:T(8,128)(2,1)S(1)}, u32[]{:S(2)}, u32[]{:S(2)}) collective-permute-start(s16[128,896]{1,0:T(8,128)(2,1)S(1)} %pad_add_fusion.2), channel_id=1, source_target_pairs={{0,258},{2,256},{256,0},{258,2},{1,259},{3,257},{257,1},{259,3},{4... | collective-permute-start | bytes 688136 | tf_op jit(solution)/shard_map/ppermute | solution.py:242
  126.6 2.6 %collective-permute-done.20 = s16[128,896]{1,0:T(8,128)(2,1)S(1)} collective-permute-done((s16[128,896]{1,0:T(8,128)(2,1)S(1)}, s16[128,896]{1,0:T(8,128)(2,1)S(1)}, u32[]{:S(2)}, u32[]{:S(2)}) %collective-permute-start.20) | collective-permute-done | bytes 229408 | tf_op jit(solution)/shard_map/ppermute | solution.py:242
  129.4 3.9 %collective-permute-done.21 = s16[128,896]{1,0:T(8,128)(2,1)S(1)} collective-permute-done((s16[128,896]{1,0:T(8,128)(2,1)S(1)}, s16[128,896]{1,0:T(8,128)(2,1)S(1)}, u32[]{:S(2)}, u32[]{:S(2)}) %collective-permute-start.21) | collective-permute-done | bytes 229408 | tf_op jit(solution)/shard_map/ppermute | solution.py:242
  (61 shorter events, 16.9 us)
Async XLA Ops:
  0.0 5.8 %copy-start = (bf16[1,8,1,3,128,128]{5,4,3,2,1,0:T(8,128)(2,1)S(1)}, bf16[1,8,1,3,128,128]{5,4,3,2,1,0:T(8,128)(2,1)}, u32[]{:S(2)}) copy-start(bf16[1,8,1,3,128,128]{5,4,3,2,1,0:T(8,128)(2,1)} %param.16) | copy-start | bytes 2359300
  0.0 5.9 %copy-start.1 = (s32[1,8,1,3]{1,2,3,0:T(1,128)S(1)}, s32[1,8,1,3]{1,2,3,0:T(1,128)}, u32[]{:S(2)}) copy-start(s32[1,8,1,3]{1,2,3,0:T(1,128)} %param.17) | copy-start | bytes 292
  1.1 9.9 %collective-permute-start = (bf16[1024,128]{1,0:T(8,128)(2,1)S(1)}, bf16[1024,128]{1,0:T(8,128)(2,1)S(1)}, u32[]{:S(2)}, u32[]{:S(2)}) collective-permute-start(bf16[1024,128]{1,0:T(8,128)(2,1)S(1)} %get-tuple-element.108), channel_id=1, source_target_pairs={{0,256},{256,0},{1,257},{257,1},{2,258},{258,2},{3,259},{259,3},{4... | collective-permute-start | bytes 786440 | tf_op jit(solution)/shard_map/ppermute | solution.py:191
  5.9 46.7 %copy-start.2 = (s32[8]{0:T(128)S(1)}, s32[8]{0:T(128)}, u32[]{:S(2)}) copy-start(s32[8]{0:T(128)} %constant.239.clone) | copy-start | bytes 100
  5.9 46.7 %copy-start.3 = (s32[8]{0:T(128)S(1)}, s32[8]{0:T(128)}, u32[]{:S(2)}) copy-start(s32[8]{0:T(128)} %constant.240.clone) | copy-start | bytes 100
  11.1 27.8 %collective-permute-start.10 = (bf16[3104,128]{1,0:T(8,128)(2,1)S(1)}, bf16[3104,128]{1,0:T(8,128)(2,1)S(1)}, u32[]{:S(2)}, u32[]{:S(2)}) collective-permute-start(bf16[3104,128]{1,0:T(8,128)(2,1)S(1)} %fusion.7.refs_4_), channel_id=1, source_target_pairs={{0,288},{32,64},{64,352},{96,128},{128,416},{160,192},{192,480},{2... | collective-permute-start | bytes 2383880 | tf_op jit(solution)/shard_map/ppermute | solution.py:216
  15.6 25.2 %collective-permute-start.12 = (bf16[3104,128]{1,0:T(8,128)(2,1)S(1)}, bf16[3104,128]{1,0:T(8,128)(2,1)S(1)}, u32[]{:S(2)}, u32[]{:S(2)}) collective-permute-start(bf16[3104,128]{1,0:T(8,128)(2,1)S(1)} %fusion.7.refs_4_), channel_id=1, source_target_pairs={{0,224},{32,256},{64,32},{96,320},{128,96},{160,384},{192,160},{22... | collective-permute-start | bytes 2383880 | tf_op jit(solution)/shard_map/ppermute | solution.py:216
  24.0 5.8 %collective-permute-start.1 = (bf16[16,128]{1,0:T(8,128)(2,1)S(1)}, bf16[16,128]{1,0:T(8,128)(2,1)S(1)}, u32[]{:S(2)}, u32[]{:S(2)}) collective-permute-start(bf16[16,128]{1,0:T(8,128)(2,1)S(1)} %scatter.19), channel_id=1, source_target_pairs={{0,256},{256,0},{1,257},{257,1},{2,258},{258,2},{3,259},{259,3},{4... | collective-permute-start | bytes 12296 | tf_op jit(solution)/shard_map/ppermute | solution.py:193
  29.8 16.1 %collective-permute-start.2 = (bf16[2080,128]{1,0:T(8,128)(2,1)S(1)}, bf16[2080,128]{1,0:T(8,128)(2,1)}, u32[]{:S(2)}, u32[]{:S(2)}) collective-permute-start(bf16[2080,128]{1,0:T(8,128)(2,1)S(1)} %fusion.10.refs_1_), channel_id=1, source_target_pairs={{0,4},{4,8},{8,12},{12,16},{16,20},{20,24},{24,28},{28,0},{1,5},{5... | collective-permute-start | bytes 1597448 | tf_op jit(solution)/shard_map/ppermute | solution.py:219
  34.5 16.1 %collective-permute-start.6 = (bf16[2080,128]{1,0:T(8,128)(2,1)S(1)}, bf16[2080,128]{1,0:T(8,128)(2,1)}, u32[]{:S(2)}, u32[]{:S(2)}) collective-permute-start(bf16[2080,128]{1,0:T(8,128)(2,1)S(1)} %fusion.10.refs_1_), channel_id=1, source_target_pairs={{0,28},{4,0},{8,4},{12,8},{16,12},{20,16},{24,20},{28,24},{1,29},{... | collective-permute-start | bytes 1597448 | tf_op jit(solution)/shard_map/ppermute | solution.py:219
  38.9 21.1 %collective-permute-start.11 = (bf16[3104,128]{1,0:T(8,128)(2,1)S(1)}, bf16[3104,128]{1,0:T(8,128)(2,1)}, u32[]{:S(2)}, u32[]{:S(2)}) collective-permute-start(bf16[3104,128]{1,0:T(8,128)(2,1)S(1)} %collective-permute-done.10.refs_5_), channel_id=1, source_target_pairs={{0,288},{32,64},{64,352},{96,128},{128,416},{160,192},{192,480},{2... | collective-permute-start | bytes 2383880 | tf_op jit(solution)/shard_map/ppermute | solution.py:216
  40.8 20.8 %collective-permute-start.13 = (bf16[3104,128]{1,0:T(8,128)(2,1)S(1)}, bf16[3104,128]{1,0:T(8,128)(2,1)}, u32[]{:S(2)}, u32[]{:S(2)}) collective-permute-start(bf16[3104,128]{1,0:T(8,128)(2,1)S(1)} %collective-permute-done.12.refs_6_), channel_id=1, source_target_pairs={{0,224},{32,256},{64,32},{96,320},{128,96},{160,384},{192,160},{22... | collective-permute-start | bytes 2383880 | tf_op jit(solution)/shard_map/ppermute | solution.py:216
  45.9 22.8 %collective-permute-start.3 = (bf16[2080,128]{1,0:T(8,128)(2,1)}, bf16[2080,128]{1,0:T(8,128)(2,1)}, u32[]{:S(2)}, u32[]{:S(2)}) collective-permute-start(bf16[2080,128]{1,0:T(8,128)(2,1)} %collective-permute-done.2.refs_2_), channel_id=1, source_target_pairs={{0,4},{4,8},{8,12},{12,16},{16,20},{20,24},{24,28},{28,0},{1,5},{5... | collective-permute-start | bytes 1597448 | tf_op jit(solution)/shard_map/ppermute | solution.py:219
  50.7 22.9 %collective-permute-start.7 = (bf16[2080,128]{1,0:T(8,128)(2,1)}, bf16[2080,128]{1,0:T(8,128)(2,1)S(1)}, u32[]{:S(2)}, u32[]{:S(2)}) collective-permute-start(bf16[2080,128]{1,0:T(8,128)(2,1)} %collective-permute-done.6.refs_3_), channel_id=1, source_target_pairs={{0,28},{4,0},{8,4},{12,8},{16,12},{20,16},{24,20},{28,24},{1,29},{... | collective-permute-start | bytes 1597448 | tf_op jit(solution)/shard_map/ppermute | solution.py:219
  61.6 20.4 %collective-permute-start.14 = (bf16[3104,128]{1,0:T(8,128)(2,1)}, bf16[3104,128]{1,0:T(8,128)(2,1)S(1)}, u32[]{:S(2)}, u32[]{:S(2)}) collective-permute-start(bf16[3104,128]{1,0:T(8,128)(2,1)} %collective-permute-done.11.refs_3_), channel_id=1, source_target_pairs={{0,288},{32,64},{64,352},{96,128},{128,416},{160,192},{192,480},{2... | collective-permute-start | bytes 2383880 | tf_op jit(solution)/shard_map/ppermute | solution.py:216
  63.5 20.0 %collective-permute-start.15 = (bf16[3104,128]{1,0:T(8,128)(2,1)}, bf16[3104,128]{1,0:T(8,128)(2,1)S(1)}, u32[]{:S(2)}, u32[]{:S(2)}) collective-permute-start(bf16[3104,128]{1,0:T(8,128)(2,1)} %collective-permute-done.13.refs_4_), channel_id=1, source_target_pairs={{0,224},{32,256},{64,32},{96,320},{128,96},{160,384},{192,160},{22... | collective-permute-start | bytes 2383880 | tf_op jit(solution)/shard_map/ppermute | solution.py:216
  68.7 22.0 %collective-permute-start.4 = (bf16[2080,128]{1,0:T(8,128)(2,1)}, bf16[2080,128]{1,0:T(8,128)(2,1)S(1)}, u32[]{:S(2)}, u32[]{:S(2)}) collective-permute-start(bf16[2080,128]{1,0:T(8,128)(2,1)} %collective-permute-done.3.refs_1_), channel_id=1, source_target_pairs={{0,4},{4,8},{8,12},{12,16},{16,20},{20,24},{24,28},{28,0},{1,5},{5... | collective-permute-start | bytes 1597448 | tf_op jit(solution)/shard_map/ppermute | solution.py:219
  73.5 22.2 %collective-permute-start.8 = (bf16[2080,128]{1,0:T(8,128)(2,1)S(1)}, bf16[2080,128]{1,0:T(8,128)(2,1)S(1)}, u32[]{:S(2)}, u32[]{:S(2)}) collective-permute-start(bf16[2080,128]{1,0:T(8,128)(2,1)S(1)} %collective-permute-done.7.refs_2_), channel_id=1, source_target_pairs={{0,28},{4,0},{8,4},{12,8},{16,12},{20,16},{24,20},{28,24},{1,29},{... | collective-permute-start | bytes 1597448 | tf_op jit(solution)/shard_map/ppermute | solution.py:219
  83.6 21.7 %collective-permute-start.16 = (bf16[1552,128]{1,0:T(8,128)(2,1)S(1)}, bf16[1552,128]{1,0:T(8,128)(2,1)S(1)}, u32[]{:S(2)}, u32[]{:S(2)}) collective-permute-start(bf16[1552,128]{1,0:T(8,128)(2,1)S(1)} %slice.136), channel_id=1, source_target_pairs={{0,288},{32,64},{64,352},{96,128},{128,416},{160,192},{192,480},{2... | collective-permute-start | bytes 1191944 | tf_op jit(solution)/shard_map/ppermute | solution.py:216
  87.3 18.0 %collective-permute-start.17 = (bf16[1552,128]{1,0:T(8,128)(2,1)S(1)}, bf16[1552,128]{1,0:T(8,128)(2,1)S(1)}, u32[]{:S(2)}, u32[]{:S(2)}) collective-permute-start(bf16[1552,128]{1,0:T(8,128)(2,1)S(1)} %slice.137), channel_id=1, source_target_pairs={{0,224},{32,256},{64,32},{96,320},{128,96},{160,384},{192,160},{22... | collective-permute-start | bytes 1191944 | tf_op jit(solution)/shard_map/ppermute | solution.py:216
  90.8 11.3 %collective-permute-start.5 = (bf16[1040,128]{1,0:T(8,128)(2,1)S(1)}, bf16[1040,128]{1,0:T(8,128)(2,1)S(1)}, u32[]{:S(2)}, u32[]{:S(2)}) collective-permute-start(bf16[1040,128]{1,0:T(8,128)(2,1)S(1)} %slice.152), channel_id=1, source_target_pairs={{0,4},{4,8},{8,12},{12,16},{16,20},{20,24},{24,28},{28,0},{1,5},{5... | collective-permute-start | bytes 798728 | tf_op jit(solution)/shard_map/ppermute | solution.py:219
  95.8 9.5 %collective-permute-start.9 = (bf16[1040,128]{1,0:T(8,128)(2,1)S(1)}, bf16[1040,128]{1,0:T(8,128)(2,1)S(1)}, u32[]{:S(2)}, u32[]{:S(2)}) collective-permute-start(bf16[1040,128]{1,0:T(8,128)(2,1)S(1)} %slice.153), channel_id=1, source_target_pairs={{0,28},{4,0},{8,4},{12,8},{16,12},{20,16},{24,20},{28,24},{1,29},{... | collective-permute-start | bytes 798728 | tf_op jit(solution)/shard_map/ppermute | solution.py:219
  109.4 5.3 %collective-permute-start.18 = (f32[4,128,768]{2,1,0:T(8,128)S(1)}, f32[4,128,768]{2,1,0:T(8,128)S(1)}, u32[]{:S(2)}, u32[]{:S(2)}) collective-permute-start(f32[4,128,768]{2,1,0:T(8,128)S(1)} %slice.139), channel_id=1, source_target_pairs={{0,1},{1,0},{2,3},{3,2},{4,5},{5,4},{6,7},{7,6},{8,9},{9,8},{10,11... | collective-permute-start | bytes 4718600 | tf_op jit(solution)/shard_map/ppermute | solution.py:238
  115.5 11.0 %collective-permute-start.19 = (s16[128,896]{1,0:T(8,128)(2,1)S(1)}, s16[128,896]{1,0:T(8,128)(2,1)S(1)}, u32[]{:S(2)}, u32[]{:S(2)}) collective-permute-start(s16[128,896]{1,0:T(8,128)(2,1)S(1)} %pad_add_fusion), channel_id=1, source_target_pairs={{0,2},{2,0},{256,258},{258,256},{1,3},{3,1},{257,259},{259,257},{4... | collective-permute-start | bytes 688136 | tf_op jit(solution)/shard_map/ppermute | solution.py:242
  118.9 10.4 %collective-permute-start.20 = (s16[128,896]{1,0:T(8,128)(2,1)S(1)}, s16[128,896]{1,0:T(8,128)(2,1)S(1)}, u32[]{:S(2)}, u32[]{:S(2)}) collective-permute-start(s16[128,896]{1,0:T(8,128)(2,1)S(1)} %pad_add_fusion.1), channel_id=1, source_target_pairs={{0,256},{2,258},{256,2},{258,0},{1,257},{3,259},{257,3},{259,1},{4... | collective-permute-start | bytes 688136 | tf_op jit(solution)/shard_map/ppermute | solution.py:242
  123.1 10.2 %collective-permute-start.21 = (s16[128,896]{1,0:T(8,128)(2,1)S(1)}, s16[128,896]{1,0:T(8,128)(2,1)S(1)}, u32[]{:S(2)}, u32[]{:S(2)}) collective-permute-start(s16[128,896]{1,0:T(8,128)(2,1)S(1)} %pad_add_fusion.2), channel_id=1, source_target_pairs={{0,258},{2,256},{256,0},{258,2},{1,259},{3,257},{257,1},{259,3},{4... | collective-permute-start | bytes 688136 | tf_op jit(solution)/shard_map/ppermute | solution.py:242

commit v11 on v8

--- a/solution.py
+++ b/solution.py
@@ -16,6 +16,7 @@
 LPART = GROUP * W + PAD
 RPART = HALF * EB * W + PAD
 CELL = 6 * W
+BASE = 2 * NY * GROUP
 TOP = 32767.0
 VMEM_LIMIT = 8 * 2**20
 
@@ -59,15 +60,16 @@
 
     for i, slot in enumerate(slots):
         for p in range(2):
-            rho = first(left[slot, pl.ds(p * LPART + GROUP * W, PAD), :])
+            held = left[slot, pl.ds(p * LPART + GROUP * W, PAD), :]
+            rho = held.astype(jnp.float32)[0:GROUP].astype(jnp.int32)
             tile = x_lo if p == 0 else 1 - x_lo
             ahead = ((rho >> 1) * 2 + tile - meta[18]) & 3
             place = ((rho & 1) ^ core) * 4 + ahead
-            idx_v[pl.ds(i * 2 + p, 1), :] = place
+            idx_v[pl.ds((slot * 2 + p) * GROUP, GROUP), :] = place
     for c in chunks:
         for h in range(2):
             row = first(right[c, pl.ds(h * RPART + HALF * EB * W, PAD), :])
-            idx_v[pl.ds(2 * NY + 2 * c + h, 1), :] = row
+            idx_v[pl.ds(BASE + 2 * c + h, 1), :] = row
     copy = pltpu.make_async_copy(idx_v, idx_s, sem)
     copy.start()
     copy.wait()
@@ -84,10 +86,10 @@
         )
         part = jnp.dot(both, wide, preferred_element_type=jnp.float32)
         for e in range(EB):
-            cell = idx_s[2 * NY + 2 * c + half, j * EB + e]
+            cell = idx_s[BASE + 2 * c + half, j * EB + e]
             lanes = pl.ds(pl.multiple_of(cell * W, W), W)
             for p in range(2):
-                at = idx_s[place * 2 + p, k]
+                at = idx_s[(place * 2 + p) * GROUP + k, 0]
                 acc[at, :, lanes] += part[p * W : (p + 1) * W, e * W : (e + 1) * W]
 
 
@@ -140,8 +142,8 @@
         out_specs=[vmem] * 4,
         input_output_aliases={1 + n + i: i for i in range(len(state))},
         scratch_shapes=[
-            pltpu.VMEM((4 * NY, W), jnp.int32),
-            pltpu.SMEM((4 * NY, W), jnp.int32),
+            pltpu.VMEM((BASE + 2 * NZ, W), jnp.int32),
+            pltpu.SMEM((BASE + 2 * NZ, W), jnp.int32),
             pltpu.SemaphoreType.DMA,
             pltpu.SemaphoreType.DMA((8,)),
         ],
@@ -174,14 +176,13 @@
     side = x_lo ^ zig(z)
 
     left = left_blocks.reshape(2, GROUP * W, W)
-    rows = left_rows.reshape(2, GROUP)
+    rows = jnp.broadcast_to(left_rows[0, :, 0, :].astype(left.dtype), (2 * GROUP, W))
     own = (side + y // 4 + y % 4) % 2
 
     def group(which):
-        return with_index(
-            lax.dynamic_index_in_dim(left, which, 0, False),
-            lax.dynamic_index_in_dim(rows, which, 0, False),
-        )
+        picked = lax.dynamic_slice_in_dim(rows, which * GROUP, GROUP, 0)
+        blocks = lax.dynamic_index_in_dim(left, which, 0, False)
+        return jnp.concatenate([blocks, picked, jnp.zeros_like(picked)], axis=0)
 
     swapped = lax.ppermute(group(1 - own), "x_lo", [(0, 1), (1, 0)])
     pair = jnp.concatenate([group(own), swapped], axis=0)

time: 137 us -> 137 us (level)
  Pallas kernels: 16.3 us -> 20.1 us
  waiting for transfers between devices: 33.6 us -> 31.4 us
    pallas_call x4, Pallas kernels: 16.3 us -> 20.1 us  [run_stage(): pl.pallas_call(lambda *refs: stage(number, new_left, new_right, slots, ch...]
    ppermute x4, waiting for transfers between devices: 12.4 us -> 10.2 us  [step_z(): lax.ppermute(up, row, ring_pairs(1))]
  transfers between devices with their start and end apart: 21 -> 21, of which waited for: 10 -> 10; matrix products, arithmetic and copies ran while one was open for 1% -> 1% of each run, Pallas kernels for 9% -> 11%
where the time goes in v11:
time: 137 us; the launch traced here: 136 us
  starting transfers between devices  77.8 us (57%)
  waiting for transfers between devices  31.4 us (23%)
  Pallas kernels  20.1 us (15%)
  other arithmetic  3.47 us (3%)
  local copies, waits for them, and re-layouts  2.23 us (2%)
    ppermute x8, starting transfers between devices, step_y(): return (lax.ppermute(fore, 'y', turn(1)), lax.ppermute(back, 'y', turn(-1)))  29.2 us
    ppermute x4, starting transfers between devices, step_z(): lax.ppermute(down, row, ring_pairs(-1))  22.1 us
    pallas_call x4, Pallas kernels, run_stage(): pl.pallas_call(lambda *refs: stage(number, new_left, new_right, slots, ch...  20.1 us
    ppermute x4, starting transfers between devices, step_z(): lax.ppermute(up, row, ring_pairs(1))  12 us
    ppermute x4, waiting for transfers between devices, step_z(): lax.ppermute(up, row, ring_pairs(1))  10.2 us
    ppermute x3, starting transfers between devices, per_device(): lax.ppermute(encode(total[step]), ('x_lo', 'x_hi'), chip_pairs(step))  9.91 us
    ppermute x3, waiting for transfers between devices, per_device(): lax.ppermute(encode(total[step]), ('x_lo', 'x_hi'), chip_pairs(step))  8.02 us
    ppermute x1, waiting for transfers between devices, per_device(): swapped = lax.ppermute(group(1 - own), 'x_lo', [(0, 1), (1, 0)])  6.64 us
  transfers between devices with their start and end apart: 21, of which 10 were waited for; matrix products, arithmetic and copies ran while one was open for 1% of the time, Pallas kernels for 11%

profile of v11, /device:TPU:6, one launch (start us, length us, event | category | flops | bytes accessed | tf_op | source)
XLA Modules:
  0.0 135.6 jit_solution(17174709171395718070)
XLA Ops:
  2.1 2.7 %collective-permute-start = (bf16[1040,128]{1,0:T(8,128)(2,1)S(1)}, bf16[1040,128]{1,0:T(8,128)(2,1)S(1)}, u32[]{:S(2)}, u32[]{:S(2)}) collective-permute-start(bf16[1040,128]{1,0:T(8,128)(2,1)S(1)} %pad_maximum_fusion.1), channel_id=1, source_target_pairs={{0,256},{256,0},{1,257},{257,1},{2,258},{258,2},{3,259},{259,3},{4... | collective-permute-start | bytes 798728 | tf_op jit(solution)/shard_map/ppermute | solution.py:187
  5.5 6.6 %collective-permute-done = bf16[1040,128]{1,0:T(8,128)(2,1)S(1)} collective-permute-done((bf16[1040,128]{1,0:T(8,128)(2,1)S(1)}, bf16[1040,128]{1,0:T(8,128)(2,1)S(1)}, u32[]{:S(2)}, u32[]{:S(2)}) %collective-permute-start) | collective-permute-done | bytes 266272 | tf_op jit(solution)/shard_map/ppermute | solution.py:187
  12.1 4.5 %collective-permute-start.9 = (bf16[3104,128]{1,0:T(8,128)(2,1)S(1)}, bf16[3104,128]{1,0:T(8,128)(2,1)S(1)}, u32[]{:S(2)}, u32[]{:S(2)}) collective-permute-start(bf16[3104,128]{1,0:T(8,128)(2,1)S(1)} %fusion.5.refs_4_), channel_id=1, source_target_pairs={{0,288},{32,64},{64,352},{96,128},{128,416},{160,192},{192,480},{2... | collective-permute-start | bytes 2383880 | tf_op jit(solution)/shard_map/ppermute | solution.py:213
  16.7 8.3 %collective-permute-start.11 = (bf16[3104,128]{1,0:T(8,128)(2,1)S(1)}, bf16[3104,128]{1,0:T(8,128)(2,1)S(1)}, u32[]{:S(2)}, u32[]{:S(2)}) collective-permute-start(bf16[3104,128]{1,0:T(8,128)(2,1)S(1)} %fusion.5.refs_4_), channel_id=1, source_target_pairs={{0,224},{32,256},{64,32},{96,320},{128,96},{160,384},{192,160},{22... | collective-permute-start | bytes 2383880 | tf_op jit(solution)/shard_map/ppermute | solution.py:213
  25.4 3.5 %collective-permute-start.1 = (bf16[2080,128]{1,0:T(8,128)(2,1)S(1)}, bf16[2080,128]{1,0:T(8,128)(2,1)}, u32[]{:S(2)}, u32[]{:S(2)}) collective-permute-start(bf16[2080,128]{1,0:T(8,128)(2,1)S(1)} %pad_maximum_fusion.refs_1_), channel_id=1, source_target_pairs={{0,4},{4,8},{8,12},{12,16},{16,20},{20,24},{24,28},{28,0},{1,5},{5... | collective-permute-start | bytes 1597448 | tf_op jit(solution)/shard_map/ppermute | solution.py:216
  28.9 3.8 %collective-permute-start.5 = (bf16[2080,128]{1,0:T(8,128)(2,1)S(1)}, bf16[2080,128]{1,0:T(8,128)(2,1)}, u32[]{:S(2)}, u32[]{:S(2)}) collective-permute-start(bf16[2080,128]{1,0:T(8,128)(2,1)S(1)} %pad_maximum_fusion.refs_1_), channel_id=1, source_target_pairs={{0,28},{4,0},{8,4},{12,8},{16,12},{20,16},{24,20},{28,24},{1,29},{... | collective-permute-start | bytes 1597448 | tf_op jit(solution)/shard_map/ppermute | solution.py:216
  32.7 7.2 %collective-permute-done.9.refs_5_ = bf16[3104,128]{1,0:T(8,128)(2,1)S(1)} collective-permute-done((bf16[3104,128]{1,0:T(8,128)(2,1)S(1)}, bf16[3104,128]{1,0:T(8,128)(2,1)S(1)}, u32[]{:S(2)}, u32[]{:S(2)}) %collective-permute-start.9) | collective-permute-done | bytes 794656 | tf_op jit(solution)/shard_map/ppermute | solution.py:213
  39.9 1.9 %collective-permute-start.10 = (bf16[3104,128]{1,0:T(8,128)(2,1)S(1)}, bf16[3104,128]{1,0:T(8,128)(2,1)}, u32[]{:S(2)}, u32[]{:S(2)}) collective-permute-start(bf16[3104,128]{1,0:T(8,128)(2,1)S(1)} %collective-permute-done.9.refs_5_), channel_id=1, source_target_pairs={{0,288},{32,64},{64,352},{96,128},{128,416},{160,192},{192,480},{2... | collective-permute-start | bytes 2383880 | tf_op jit(solution)/shard_map/ppermute | solution.py:213
  41.8 5.1 %collective-permute-start.12 = (bf16[3104,128]{1,0:T(8,128)(2,1)S(1)}, bf16[3104,128]{1,0:T(8,128)(2,1)}, u32[]{:S(2)}, u32[]{:S(2)}) collective-permute-start(bf16[3104,128]{1,0:T(8,128)(2,1)S(1)} %collective-permute-done.11.refs_6_), channel_id=1, source_target_pairs={{0,224},{32,256},{64,32},{96,320},{128,96},{160,384},{192,160},{22... | collective-permute-start | bytes 2383880 | tf_op jit(solution)/shard_map/ppermute | solution.py:213
  47.0 3.5 %collective-permute-start.2 = (bf16[2080,128]{1,0:T(8,128)(2,1)}, bf16[2080,128]{1,0:T(8,128)(2,1)}, u32[]{:S(2)}, u32[]{:S(2)}) collective-permute-start(bf16[2080,128]{1,0:T(8,128)(2,1)} %collective-permute-done.1.refs_2_), channel_id=1, source_target_pairs={{0,4},{4,8},{8,12},{12,16},{16,20},{20,24},{24,28},{28,0},{1,5},{5... | collective-permute-start | bytes 1597448 | tf_op jit(solution)/shard_map/ppermute | solution.py:216
  50.5 3.8 %collective-permute-start.6 = (bf16[2080,128]{1,0:T(8,128)(2,1)}, bf16[2080,128]{1,0:T(8,128)(2,1)S(1)}, u32[]{:S(2)}, u32[]{:S(2)}) collective-permute-start(bf16[2080,128]{1,0:T(8,128)(2,1)} %collective-permute-done.5.refs_3_), channel_id=1, source_target_pairs={{0,28},{4,0},{8,4},{12,8},{16,12},{20,16},{24,20},{28,24},{1,29},{... | collective-permute-start | bytes 1597448 | tf_op jit(solution)/shard_map/ppermute | solution.py:216
  54.5 5.1 %shard_map.64 = (f32[8,128,768]{2,1,0:T(8,128)S(1)}, bf16[8,2080,128]{2,1,0:T(8,128)(2,1)S(1)}, bf16[8,3104,128]{2,1,0:T(8,128)(2,1)S(1)}, s32[8,128]{1,0:T(8,128)S(1)}) custom-call(s32[19]{0:T(128)S(1)} %concatenate.25.refs_0_, bf16[2080,128]{1,0:T(8,128)(2,1)S(1)} %pad_maximum_fusion.refs_1_, bf16[2080,128]{1,0:T(8,128)(2,1)} %collective-permute-done.1.refs_2_, ...), custom_call_target="tpu_custom_call" | custom-call | flops 805306368 | bytes 1048576 | tf_op jit(solution)/shard_map/pallas_call | solution.py:133
  59.6 1.6 %collective-permute-done.10.refs_3_ = bf16[3104,128]{1,0:T(8,128)(2,1)} collective-permute-done((bf16[3104,128]{1,0:T(8,128)(2,1)S(1)}, bf16[3104,128]{1,0:T(8,128)(2,1)}, u32[]{:S(2)}, u32[]{:S(2)}) %collective-permute-start.10) | collective-permute-done | bytes 794656 | tf_op jit(solution)/shard_map/ppermute | solution.py:213
  61.2 1.6 %collective-permute-done.12.refs_4_ = bf16[3104,128]{1,0:T(8,128)(2,1)} collective-permute-done((bf16[3104,128]{1,0:T(8,128)(2,1)S(1)}, bf16[3104,128]{1,0:T(8,128)(2,1)}, u32[]{:S(2)}, u32[]{:S(2)}) %collective-permute-start.12) | collective-permute-done | bytes 794656 | tf_op jit(solution)/shard_map/ppermute | solution.py:213
  62.8 1.9 %collective-permute-start.13 = (bf16[3104,128]{1,0:T(8,128)(2,1)}, bf16[3104,128]{1,0:T(8,128)(2,1)S(1)}, u32[]{:S(2)}, u32[]{:S(2)}) collective-permute-start(bf16[3104,128]{1,0:T(8,128)(2,1)} %collective-permute-done.10.refs_3_), channel_id=1, source_target_pairs={{0,288},{32,64},{64,352},{96,128},{128,416},{160,192},{192,480},{2... | collective-permute-start | bytes 2383880 | tf_op jit(solution)/shard_map/ppermute | solution.py:213
  64.7 5.2 %collective-permute-start.14 = (bf16[3104,128]{1,0:T(8,128)(2,1)}, bf16[3104,128]{1,0:T(8,128)(2,1)S(1)}, u32[]{:S(2)}, u32[]{:S(2)}) collective-permute-start(bf16[3104,128]{1,0:T(8,128)(2,1)} %collective-permute-done.12.refs_4_), channel_id=1, source_target_pairs={{0,224},{32,256},{64,32},{96,320},{128,96},{160,384},{192,160},{22... | collective-permute-start | bytes 2383880 | tf_op jit(solution)/shard_map/ppermute | solution.py:213
  69.9 3.4 %collective-permute-start.3 = (bf16[2080,128]{1,0:T(8,128)(2,1)}, bf16[2080,128]{1,0:T(8,128)(2,1)S(1)}, u32[]{:S(2)}, u32[]{:S(2)}) collective-permute-start(bf16[2080,128]{1,0:T(8,128)(2,1)} %collective-permute-done.2.refs_1_), channel_id=1, source_target_pairs={{0,4},{4,8},{8,12},{12,16},{16,20},{20,24},{24,28},{28,0},{1,5},{5... | collective-permute-start | bytes 1597448 | tf_op jit(solution)/shard_map/ppermute | solution.py:216
  73.3 3.9 %collective-permute-start.7 = (bf16[2080,128]{1,0:T(8,128)(2,1)S(1)}, bf16[2080,128]{1,0:T(8,128)(2,1)S(1)}, u32[]{:S(2)}, u32[]{:S(2)}) collective-permute-start(bf16[2080,128]{1,0:T(8,128)(2,1)S(1)} %collective-permute-done.6.refs_2_), channel_id=1, source_target_pairs={{0,28},{4,0},{8,4},{12,8},{16,12},{20,16},{24,20},{28,24},{1,29},{... | collective-permute-start | bytes 1597448 | tf_op jit(solution)/shard_map/ppermute | solution.py:216
  77.2 4.7 %shard_map.65 = (f32[8,128,768]{2,1,0:T(8,128)S(1)}, bf16[8,2080,128]{2,1,0:T(8,128)(2,1)S(1)}, bf16[8,3104,128]{2,1,0:T(8,128)(2,1)S(1)}, s32[8,128]{1,0:T(8,128)S(1)}) custom-call(s32[19]{0:T(128)S(1)} %concatenate.25.refs_0_, bf16[2080,128]{1,0:T(8,128)(2,1)} %collective-permute-done.2.refs_1_, ...), custom_call_target="tpu_custom_call", output_to_operand_aliasing={{0}: (5, {}), {1}: (6, {}), {2}: (7, {})} | custom-call | flops 805306368 | bytes 1048576 | tf_op jit(solution)/shard_map/pallas_call | solution.py:133
  84.9 3.7 %collective-permute-start.15 = (bf16[1552,128]{1,0:T(8,128)(2,1)S(1)}, bf16[1552,128]{1,0:T(8,128)(2,1)S(1)}, u32[]{:S(2)}, u32[]{:S(2)}) collective-permute-start(bf16[1552,128]{1,0:T(8,128)(2,1)S(1)} %slice.104), channel_id=1, source_target_pairs={{0,288},{32,64},{64,352},{96,128},{128,416},{160,192},{192,480},{2... | collective-permute-start | bytes 1191944 | tf_op jit(solution)/shard_map/ppermute | solution.py:213
  88.6 3.5 %collective-permute-start.16 = (bf16[1552,128]{1,0:T(8,128)(2,1)S(1)}, bf16[1552,128]{1,0:T(8,128)(2,1)S(1)}, u32[]{:S(2)}, u32[]{:S(2)}) collective-permute-start(bf16[1552,128]{1,0:T(8,128)(2,1)S(1)} %slice.105), channel_id=1, source_target_pairs={{0,224},{32,256},{64,32},{96,320},{128,96},{160,384},{192,160},{22... | collective-permute-start | bytes 1191944 | tf_op jit(solution)/shard_map/ppermute | solution.py:213
  92.1 3.3 %collective-permute-start.4 = (bf16[1040,128]{1,0:T(8,128)(2,1)S(1)}, bf16[1040,128]{1,0:T(8,128)(2,1)S(1)}, u32[]{:S(2)}, u32[]{:S(2)}) collective-permute-start(bf16[1040,128]{1,0:T(8,128)(2,1)S(1)} %slice.118), channel_id=1, source_target_pairs={{0,4},{4,8},{8,12},{12,16},{16,20},{20,24},{24,28},{28,0},{1,5},{5... | collective-permute-start | bytes 798728 | tf_op jit(solution)/shard_map/ppermute | solution.py:216
  95.4 4.0 %collective-permute-start.8 = (bf16[1040,128]{1,0:T(8,128)(2,1)S(1)}, bf16[1040,128]{1,0:T(8,128)(2,1)S(1)}, u32[]{:S(2)}, u32[]{:S(2)}) collective-permute-start(bf16[1040,128]{1,0:T(8,128)(2,1)S(1)} %slice.119), channel_id=1, source_target_pairs={{0,28},{4,0},{8,4},{12,8},{16,12},{20,16},{24,20},{28,24},{1,29},{... | collective-permute-start | bytes 798728 | tf_op jit(solution)/shard_map/ppermute | solution.py:216
  99.4 5.4 %shard_map.66 = (f32[8,128,768]{2,1,0:T(8,128)S(1)}, bf16[8,2080,128]{2,1,0:T(8,128)(2,1)S(1)}, bf16[8,3104,128]{2,1,0:T(8,128)(2,1)S(1)}, s32[8,128]{1,0:T(8,128)}) custom-call(s32[19]{0:T(128)S(1)} %concatenate.25.refs_0_, bf16[2080,128]{1,0:T(8,128)(2,1)S(1)} %collective-permute-done.3.refs_1_, ...), custom_call_target="tpu_custom_call", output_to_operand_aliasing={{0}: (5, {}), {1}: (6, {}), {2}: (7, {})} | custom-call | flops 805306368 | bytes 1048576 | tf_op jit(solution)/shard_map/pallas_call | solution.py:133
  104.8 4.9 %shard_map.67 = (f32[8,128,768]{2,1,0:T(8,128)S(1)}, bf16[8,2080,128]{2,1,0:T(8,128)(2,1)S(1)}, bf16[8,3104,128]{2,1,0:T(8,128)(2,1)S(1)}, s32[8,128]{1,0:T(8,128)}) custom-call(s32[19]{0:T(128)S(1)} %concatenate.25.refs_0_, bf16[1040,128]{1,0:T(8,128)(2,1)S(1)} %collective-permute-done.4.refs_1_, ...), custom_call_target="tpu_custom_call", output_to_operand_aliasing={{0}: (5, {}), {1}: (6, {}), {2}: (7, {})} | custom-call | flops 805306368 | bytes 1048576 | tf_op jit(solution)/shard_map/pallas_call | solution.py:133
  109.9 1.9 %collective-permute-start.17 = (f32[4,128,768]{2,1,0:T(8,128)S(1)}, f32[4,128,768]{2,1,0:T(8,128)S(1)}, u32[]{:S(2)}, u32[]{:S(2)}) collective-permute-start(f32[4,128,768]{2,1,0:T(8,128)S(1)} %slice.107), channel_id=1, source_target_pairs={{0,1},{1,0},{2,3},{3,2},{4,5},{5,4},{6,7},{7,6},{8,9},{9,8},{10,11... | collective-permute-start | bytes 4718600 | tf_op jit(solution)/shard_map/ppermute | solution.py:235
  111.8 3.4 %collective-permute-done.17 = f32[4,128,768]{2,1,0:T(8,128)S(1)} collective-permute-done((f32[4,128,768]{2,1,0:T(8,128)S(1)}, f32[4,128,768]{2,1,0:T(8,128)S(1)}, u32[]{:S(2)}, u32[]{:S(2)}) %collective-permute-start.17) | collective-permute-done | bytes 1572896 | tf_op jit(solution)/shard_map/ppermute | solution.py:235
  116.0 3.3 %collective-permute-start.18 = (s16[128,896]{1,0:T(8,128)(2,1)S(1)}, s16[128,896]{1,0:T(8,128)(2,1)S(1)}, u32[]{:S(2)}, u32[]{:S(2)}) collective-permute-start(s16[128,896]{1,0:T(8,128)(2,1)S(1)} %pad_add_fusion), channel_id=1, source_target_pairs={{0,2},{2,0},{256,258},{258,256},{1,3},{3,1},{257,259},{259,257},{4... | collective-permute-start | bytes 688136 | tf_op jit(solution)/shard_map/ppermute | solution.py:239
  119.4 4.7 %collective-permute-start.19 = (s16[128,896]{1,0:T(8,128)(2,1)S(1)}, s16[128,896]{1,0:T(8,128)(2,1)S(1)}, u32[]{:S(2)}, u32[]{:S(2)}) collective-permute-start(s16[128,896]{1,0:T(8,128)(2,1)S(1)} %pad_add_fusion.1), channel_id=1, source_target_pairs={{0,256},{2,258},{256,2},{258,0},{1,257},{3,259},{257,3},{259,1},{4... | collective-permute-start | bytes 688136 | tf_op jit(solution)/shard_map/ppermute | solution.py:239
  124.2 1.9 %collective-permute-start.20 = (s16[128,896]{1,0:T(8,128)(2,1)S(1)}, s16[128,896]{1,0:T(8,128)(2,1)S(1)}, u32[]{:S(2)}, u32[]{:S(2)}) collective-permute-start(s16[128,896]{1,0:T(8,128)(2,1)S(1)} %pad_add_fusion.2), channel_id=1, source_target_pairs={{0,258},{2,256},{256,0},{258,2},{1,259},{3,257},{257,1},{259,3},{4... | collective-permute-start | bytes 688136 | tf_op jit(solution)/shard_map/ppermute | solution.py:239
  127.2 3.3 %collective-permute-done.19 = s16[128,896]{1,0:T(8,128)(2,1)S(1)} collective-permute-done((s16[128,896]{1,0:T(8,128)(2,1)S(1)}, s16[128,896]{1,0:T(8,128)(2,1)S(1)}, u32[]{:S(2)}, u32[]{:S(2)}) %collective-permute-start.19) | collective-permute-done | bytes 229408 | tf_op jit(solution)/shard_map/ppermute | solution.py:239
  130.6 3.9 %collective-permute-done.20 = s16[128,896]{1,0:T(8,128)(2,1)S(1)} collective-permute-done((s16[128,896]{1,0:T(8,128)(2,1)S(1)}, s16[128,896]{1,0:T(8,128)(2,1)S(1)}, u32[]{:S(2)}, u32[]{:S(2)}) %collective-permute-start.20) | collective-permute-done | bytes 229408 | tf_op jit(solution)/shard_map/ppermute | solution.py:239
  (60 shorter events, 9.5 us)
Async XLA Ops:
  0.0 4.9 %copy-start = (bf16[1,8,1,3,128,128]{5,4,3,2,1,0:T(8,128)(2,1)S(1)}, bf16[1,8,1,3,128,128]{5,4,3,2,1,0:T(8,128)(2,1)}, u32[]{:S(2)}) copy-start(bf16[1,8,1,3,128,128]{5,4,3,2,1,0:T(8,128)(2,1)} %param.12) | copy-start | bytes 2359300
  0.7 4.2 %copy-start.1 = (s32[1,8,1,3]{1,2,3,0:T(1,128)S(1)}, s32[1,8,1,3]{1,2,3,0:T(1,128)}, u32[]{:S(2)}) copy-start(s32[1,8,1,3]{1,2,3,0:T(1,128)} %param.13) | copy-start | bytes 292
  2.1 10.0 %collective-permute-start = (bf16[1040,128]{1,0:T(8,128)(2,1)S(1)}, bf16[1040,128]{1,0:T(8,128)(2,1)S(1)}, u32[]{:S(2)}, u32[]{:S(2)}) collective-permute-start(bf16[1040,128]{1,0:T(8,128)(2,1)S(1)} %pad_maximum_fusion.1), channel_id=1, source_target_pairs={{0,256},{256,0},{1,257},{257,1},{2,258},{258,2},{3,259},{259,3},{4... | collective-permute-start | bytes 798728 | tf_op jit(solution)/shard_map/ppermute | solution.py:187
  4.9 49.4 %copy-start.2 = (s32[8]{0:T(128)S(1)}, s32[8]{0:T(128)}, u32[]{:S(2)}) copy-start(s32[8]{0:T(128)} %constant.201.clone) | copy-start | bytes 100
  4.9 49.4 %copy-start.3 = (s32[8]{0:T(128)S(1)}, s32[8]{0:T(128)}, u32[]{:S(2)}) copy-start(s32[8]{0:T(128)} %constant.202.clone) | copy-start | bytes 100
  12.1 27.8 %collective-permute-start.9 = (bf16[3104,128]{1,0:T(8,128)(2,1)S(1)}, bf16[3104,128]{1,0:T(8,128)(2,1)S(1)}, u32[]{:S(2)}, u32[]{:S(2)}) collective-permute-start(bf16[3104,128]{1,0:T(8,128)(2,1)S(1)} %fusion.5.refs_4_), channel_id=1, source_target_pairs={{0,288},{32,64},{64,352},{96,128},{128,416},{160,192},{192,480},{2... | collective-permute-start | bytes 2383880 | tf_op jit(solution)/shard_map/ppermute | solution.py:213
  16.7 25.2 %collective-permute-start.11 = (bf16[3104,128]{1,0:T(8,128)(2,1)S(1)}, bf16[3104,128]{1,0:T(8,128)(2,1)S(1)}, u32[]{:S(2)}, u32[]{:S(2)}) collective-permute-start(bf16[3104,128]{1,0:T(8,128)(2,1)S(1)} %fusion.5.refs_4_), channel_id=1, source_target_pairs={{0,224},{32,256},{64,32},{96,320},{128,96},{160,384},{192,160},{22... | collective-permute-start | bytes 2383880 | tf_op jit(solution)/shard_map/ppermute | solution.py:213
  25.4 21.6 %collective-permute-start.1 = (bf16[2080,128]{1,0:T(8,128)(2,1)S(1)}, bf16[2080,128]{1,0:T(8,128)(2,1)}, u32[]{:S(2)}, u32[]{:S(2)}) collective-permute-start(bf16[2080,128]{1,0:T(8,128)(2,1)S(1)} %pad_maximum_fusion.refs_1_), channel_id=1, source_target_pairs={{0,4},{4,8},{8,12},{12,16},{16,20},{20,24},{24,28},{28,0},{1,5},{5... | collective-permute-start | bytes 1597448 | tf_op jit(solution)/shard_map/ppermute | solution.py:216
  28.9 21.6 %collective-permute-start.5 = (bf16[2080,128]{1,0:T(8,128)(2,1)S(1)}, bf16[2080,128]{1,0:T(8,128)(2,1)}, u32[]{:S(2)}, u32[]{:S(2)}) collective-permute-start(bf16[2080,128]{1,0:T(8,128)(2,1)S(1)} %pad_maximum_fusion.refs_1_), channel_id=1, source_target_pairs={{0,28},{4,0},{8,4},{12,8},{16,12},{20,16},{24,20},{28,24},{1,29},{... | collective-permute-start | bytes 1597448 | tf_op jit(solution)/shard_map/ppermute | solution.py:216
  39.9 21.2 %collective-permute-start.10 = (bf16[3104,128]{1,0:T(8,128)(2,1)S(1)}, bf16[3104,128]{1,0:T(8,128)(2,1)}, u32[]{:S(2)}, u32[]{:S(2)}) collective-permute-start(bf16[3104,128]{1,0:T(8,128)(2,1)S(1)} %collective-permute-done.9.refs_5_), channel_id=1, source_target_pairs={{0,288},{32,64},{64,352},{96,128},{128,416},{160,192},{192,480},{2... | collective-permute-start | bytes 2383880 | tf_op jit(solution)/shard_map/ppermute | solution.py:213
  41.8 20.9 %collective-permute-start.12 = (bf16[3104,128]{1,0:T(8,128)(2,1)S(1)}, bf16[3104,128]{1,0:T(8,128)(2,1)}, u32[]{:S(2)}, u32[]{:S(2)}) collective-permute-start(bf16[3104,128]{1,0:T(8,128)(2,1)S(1)} %collective-permute-done.11.refs_6_), channel_id=1, source_target_pairs={{0,224},{32,256},{64,32},{96,320},{128,96},{160,384},{192,160},{22... | collective-permute-start | bytes 2383880 | tf_op jit(solution)/shard_map/ppermute | solution.py:213
  47.0 22.9 %collective-permute-start.2 = (bf16[2080,128]{1,0:T(8,128)(2,1)}, bf16[2080,128]{1,0:T(8,128)(2,1)}, u32[]{:S(2)}, u32[]{:S(2)}) collective-permute-start(bf16[2080,128]{1,0:T(8,128)(2,1)} %collective-permute-done.1.refs_2_), channel_id=1, source_target_pairs={{0,4},{4,8},{8,12},{12,16},{16,20},{20,24},{24,28},{28,0},{1,5},{5... | collective-permute-start | bytes 1597448 | tf_op jit(solution)/shard_map/ppermute | solution.py:216
  50.5 22.8 %collective-permute-start.6 = (bf16[2080,128]{1,0:T(8,128)(2,1)}, bf16[2080,128]{1,0:T(8,128)(2,1)S(1)}, u32[]{:S(2)}, u32[]{:S(2)}) collective-permute-start(bf16[2080,128]{1,0:T(8,128)(2,1)} %collective-permute-done.5.refs_3_), channel_id=1, source_target_pairs={{0,28},{4,0},{8,4},{12,8},{16,12},{20,16},{24,20},{28,24},{1,29},{... | collective-permute-start | bytes 1597448 | tf_op jit(solution)/shard_map/ppermute | solution.py:216
  62.8 20.5 %collective-permute-start.13 = (bf16[3104,128]{1,0:T(8,128)(2,1)}, bf16[3104,128]{1,0:T(8,128)(2,1)S(1)}, u32[]{:S(2)}, u32[]{:S(2)}) collective-permute-start(bf16[3104,128]{1,0:T(8,128)(2,1)} %collective-permute-done.10.refs_3_), channel_id=1, source_target_pairs={{0,288},{32,64},{64,352},{96,128},{128,416},{160,192},{192,480},{2... | collective-permute-start | bytes 2383880 | tf_op jit(solution)/shard_map/ppermute | solution.py:213
  64.7 20.1 %collective-permute-start.14 = (bf16[3104,128]{1,0:T(8,128)(2,1)}, bf16[3104,128]{1,0:T(8,128)(2,1)S(1)}, u32[]{:S(2)}, u32[]{:S(2)}) collective-permute-start(bf16[3104,128]{1,0:T(8,128)(2,1)} %collective-permute-done.12.refs_4_), channel_id=1, source_target_pairs={{0,224},{32,256},{64,32},{96,320},{128,96},{160,384},{192,160},{22... | collective-permute-start | bytes 2383880 | tf_op jit(solution)/shard_map/ppermute | solution.py:213
  69.9 22.1 %collective-permute-start.3 = (bf16[2080,128]{1,0:T(8,128)(2,1)}, bf16[2080,128]{1,0:T(8,128)(2,1)S(1)}, u32[]{:S(2)}, u32[]{:S(2)}) collective-permute-start(bf16[2080,128]{1,0:T(8,128)(2,1)} %collective-permute-done.2.refs_1_), channel_id=1, source_target_pairs={{0,4},{4,8},{8,12},{12,16},{16,20},{20,24},{24,28},{28,0},{1,5},{5... | collective-permute-start | bytes 1597448 | tf_op jit(solution)/shard_map/ppermute | solution.py:216
  73.3 22.1 %collective-permute-start.7 = (bf16[2080,128]{1,0:T(8,128)(2,1)S(1)}, bf16[2080,128]{1,0:T(8,128)(2,1)S(1)}, u32[]{:S(2)}, u32[]{:S(2)}) collective-permute-start(bf16[2080,128]{1,0:T(8,128)(2,1)S(1)} %collective-permute-done.6.refs_2_), channel_id=1, source_target_pairs={{0,28},{4,0},{8,4},{12,8},{16,12},{20,16},{24,20},{28,24},{1,29},{... | collective-permute-start | bytes 1597448 | tf_op jit(solution)/shard_map/ppermute | solution.py:216
  84.9 20.0 %collective-permute-start.15 = (bf16[1552,128]{1,0:T(8,128)(2,1)S(1)}, bf16[1552,128]{1,0:T(8,128)(2,1)S(1)}, u32[]{:S(2)}, u32[]{:S(2)}) collective-permute-start(bf16[1552,128]{1,0:T(8,128)(2,1)S(1)} %slice.104), channel_id=1, source_target_pairs={{0,288},{32,64},{64,352},{96,128},{128,416},{160,192},{192,480},{2... | collective-permute-start | bytes 1191944 | tf_op jit(solution)/shard_map/ppermute | solution.py:213
  88.6 16.3 %collective-permute-start.16 = (bf16[1552,128]{1,0:T(8,128)(2,1)S(1)}, bf16[1552,128]{1,0:T(8,128)(2,1)S(1)}, u32[]{:S(2)}, u32[]{:S(2)}) collective-permute-start(bf16[1552,128]{1,0:T(8,128)(2,1)S(1)} %slice.105), channel_id=1, source_target_pairs={{0,224},{32,256},{64,32},{96,320},{128,96},{160,384},{192,160},{22... | collective-permute-start | bytes 1191944 | tf_op jit(solution)/shard_map/ppermute | solution.py:213
  92.1 12.7 %collective-permute-start.4 = (bf16[1040,128]{1,0:T(8,128)(2,1)S(1)}, bf16[1040,128]{1,0:T(8,128)(2,1)S(1)}, u32[]{:S(2)}, u32[]{:S(2)}) collective-permute-start(bf16[1040,128]{1,0:T(8,128)(2,1)S(1)} %slice.118), channel_id=1, source_target_pairs={{0,4},{4,8},{8,12},{12,16},{16,20},{20,24},{24,28},{28,0},{1,5},{5... | collective-permute-start | bytes 798728 | tf_op jit(solution)/shard_map/ppermute | solution.py:216
  95.4 9.4 %collective-permute-start.8 = (bf16[1040,128]{1,0:T(8,128)(2,1)S(1)}, bf16[1040,128]{1,0:T(8,128)(2,1)S(1)}, u32[]{:S(2)}, u32[]{:S(2)}) collective-permute-start(bf16[1040,128]{1,0:T(8,128)(2,1)S(1)} %slice.119), channel_id=1, source_target_pairs={{0,28},{4,0},{8,4},{12,8},{16,12},{20,16},{24,20},{28,24},{1,29},{... | collective-permute-start | bytes 798728 | tf_op jit(solution)/shard_map/ppermute | solution.py:216
  109.9 5.3 %collective-permute-start.17 = (f32[4,128,768]{2,1,0:T(8,128)S(1)}, f32[4,128,768]{2,1,0:T(8,128)S(1)}, u32[]{:S(2)}, u32[]{:S(2)}) collective-permute-start(f32[4,128,768]{2,1,0:T(8,128)S(1)} %slice.107), channel_id=1, source_target_pairs={{0,1},{1,0},{2,3},{3,2},{4,5},{5,4},{6,7},{7,6},{8,9},{9,8},{10,11... | collective-permute-start | bytes 4718600 | tf_op jit(solution)/shard_map/ppermute | solution.py:235
  116.0 11.0 %collective-permute-start.18 = (s16[128,896]{1,0:T(8,128)(2,1)S(1)}, s16[128,896]{1,0:T(8,128)(2,1)S(1)}, u32[]{:S(2)}, u32[]{:S(2)}) collective-permute-start(s16[128,896]{1,0:T(8,128)(2,1)S(1)} %pad_add_fusion), channel_id=1, source_target_pairs={{0,2},{2,0},{256,258},{258,256},{1,3},{3,1},{257,259},{259,257},{4... | collective-permute-start | bytes 688136 | tf_op jit(solution)/shard_map/ppermute | solution.py:239
  119.4 11.0 %collective-permute-start.19 = (s16[128,896]{1,0:T(8,128)(2,1)S(1)}, s16[128,896]{1,0:T(8,128)(2,1)S(1)}, u32[]{:S(2)}, u32[]{:S(2)}) collective-permute-start(s16[128,896]{1,0:T(8,128)(2,1)S(1)} %pad_add_fusion.1), channel_id=1, source_target_pairs={{0,256},{2,258},{256,2},{258,0},{1,257},{3,259},{257,3},{259,1},{4... | collective-permute-start | bytes 688136 | tf_op jit(solution)/shard_map/ppermute | solution.py:239
  124.2 10.2 %collective-permute-start.20 = (s16[128,896]{1,0:T(8,128)(2,1)S(1)}, s16[128,896]{1,0:T(8,128)(2,1)S(1)}, u32[]{:S(2)}, u32[]{:S(2)}) collective-permute-start(s16[128,896]{1,0:T(8,128)(2,1)S(1)} %pad_add_fusion.2), channel_id=1, source_target_pairs={{0,258},{2,256},{256,0},{258,2},{1,259},{3,257},{257,1},{259,3},{4... | collective-permute-start | bytes 688136 | tf_op jit(solution)/shard_map/ppermute | solution.py:239

commit v12 on v10

--- a/solution.py
+++ b/solution.py
@@ -238,7 +238,7 @@
     got = lax.ppermute(acc[4:], "core", [(0, 1), (1, 0)])
     total = acc[:4] + got
     out = total[0]
-    for step in (2, 1, 3):
+    for step in (1, 2, 3):
         moved = lax.ppermute(encode(total[step]), ("x_lo", "x_hi"), chip_pairs(step))
         out = out + decode(moved)
     return out

time: 135 us -> 137 us (1.015)
  the two profiles are of different devices: /device:TPU:30 before, /device:TPU:27 now
where the time goes in v12:
time: 137 us; the launch traced here: 136 us
  starting transfers between devices  79.9 us (58%)
  waiting for transfers between devices  33 us (24%)
  Pallas kernels  16.3 us (12%)
  other arithmetic  3.56 us (3%)
  local copies, waits for them, and re-layouts  2.81 us (2%)
    ppermute x8, starting transfers between devices, step_y(): return (lax.ppermute(fore, 'y', turn(1)), lax.ppermute(back, 'y', turn(-1)))  26 us
    ppermute x4, starting transfers between devices, step_z(): lax.ppermute(down, row, ring_pairs(-1))  21.5 us
    pallas_call x4, Pallas kernels, run_stage(): pl.pallas_call(lambda *refs: stage(number, new_left, new_right, slots, ch...  16.3 us
    ppermute x4, starting transfers between devices, step_z(): lax.ppermute(up, row, ring_pairs(1))  10.6 us
    ppermute x3, starting transfers between devices, per_device(): lax.ppermute(encode(total[step]), ('x_lo', 'x_hi'), chip_pairs(step))  9.65 us
    ppermute x3, waiting for transfers between devices, per_device(): lax.ppermute(encode(total[step]), ('x_lo', 'x_hi'), chip_pairs(step))  8.95 us
    ppermute x4, waiting for transfers between devices, step_z(): lax.ppermute(up, row, ring_pairs(1))  8.61 us
    ppermute x1, starting transfers between devices, per_device(): got = lax.ppermute(acc[4:], 'core', [(0, 1), (1, 0)])  7.82 us
  transfers between devices with their start and end apart: 22, of which 11 were waited for; matrix products, arithmetic and copies ran while one was open for 2% of the time, Pallas kernels for 9%

profile of v12, /device:TPU:27, one launch (start us, length us, event | category | flops | bytes accessed | tf_op | source)
XLA Modules:
  0.0 136.0 jit_solution(6657302722573038765)
XLA Ops:
  1.1 2.2 %collective-permute-start = (bf16[1024,128]{1,0:T(8,128)(2,1)S(1)}, bf16[1024,128]{1,0:T(8,128)(2,1)S(1)}, u32[]{:S(2)}, u32[]{:S(2)}) collective-permute-start(bf16[1024,128]{1,0:T(8,128)(2,1)S(1)} %get-tuple-element.108), channel_id=1, source_target_pairs={{0,256},{256,0},{1,257},{257,1},{2,258},{258,2},{3,259},{259,3},{4... | collective-permute-start | bytes 786440 | tf_op jit(solution)/shard_map/ppermute | solution.py:191
  5.9 4.3 %collective-permute-done = bf16[1024,128]{1,0:T(8,128)(2,1)S(1)} collective-permute-done((bf16[1024,128]{1,0:T(8,128)(2,1)S(1)}, bf16[1024,128]{1,0:T(8,128)(2,1)S(1)}, u32[]{:S(2)}, u32[]{:S(2)}) %collective-permute-start) | collective-permute-done | bytes 262176 | tf_op jit(solution)/shard_map/ppermute | solution.py:191
  10.2 4.0 %collective-permute-start.10 = (bf16[3104,128]{1,0:T(8,128)(2,1)S(1)}, bf16[3104,128]{1,0:T(8,128)(2,1)S(1)}, u32[]{:S(2)}, u32[]{:S(2)}) collective-permute-start(bf16[3104,128]{1,0:T(8,128)(2,1)S(1)} %fusion.7.refs_4_), channel_id=1, source_target_pairs={{0,288},{32,64},{64,352},{96,128},{128,416},{160,192},{192,480},{2... | collective-permute-start | bytes 2383880 | tf_op jit(solution)/shard_map/ppermute | solution.py:216
  14.2 8.6 %collective-permute-start.12 = (bf16[3104,128]{1,0:T(8,128)(2,1)S(1)}, bf16[3104,128]{1,0:T(8,128)(2,1)S(1)}, u32[]{:S(2)}, u32[]{:S(2)}) collective-permute-start(bf16[3104,128]{1,0:T(8,128)(2,1)S(1)} %fusion.7.refs_4_), channel_id=1, source_target_pairs={{0,224},{32,256},{64,32},{96,320},{128,96},{160,384},{192,160},{22... | collective-permute-start | bytes 2383880 | tf_op jit(solution)/shard_map/ppermute | solution.py:216
  22.8 2.2 %collective-permute-start.1 = (bf16[16,128]{1,0:T(8,128)(2,1)S(1)}, bf16[16,128]{1,0:T(8,128)(2,1)S(1)}, u32[]{:S(2)}, u32[]{:S(2)}) collective-permute-start(bf16[16,128]{1,0:T(8,128)(2,1)S(1)} %scatter.19), channel_id=1, source_target_pairs={{0,256},{256,0},{1,257},{257,1},{2,258},{258,2},{3,259},{259,3},{4... | collective-permute-start | bytes 12296 | tf_op jit(solution)/shard_map/ppermute | solution.py:193
  25.0 2.9 %collective-permute-done.1 = bf16[16,128]{1,0:T(8,128)(2,1)S(1)} collective-permute-done((bf16[16,128]{1,0:T(8,128)(2,1)S(1)}, bf16[16,128]{1,0:T(8,128)(2,1)S(1)}, u32[]{:S(2)}, u32[]{:S(2)}) %collective-permute-start.1) | collective-permute-done | bytes 4128 | tf_op jit(solution)/shard_map/ppermute | solution.py:193
  27.9 4.4 %collective-permute-start.2 = (bf16[2080,128]{1,0:T(8,128)(2,1)S(1)}, bf16[2080,128]{1,0:T(8,128)(2,1)}, u32[]{:S(2)}, u32[]{:S(2)}) collective-permute-start(bf16[2080,128]{1,0:T(8,128)(2,1)S(1)} %fusion.10.refs_1_), channel_id=1, source_target_pairs={{0,4},{4,8},{8,12},{12,16},{16,20},{20,24},{24,28},{28,0},{1,5},{5... | collective-permute-start | bytes 1597448 | tf_op jit(solution)/shard_map/ppermute | solution.py:219
  32.3 1.9 %collective-permute-start.6 = (bf16[2080,128]{1,0:T(8,128)(2,1)S(1)}, bf16[2080,128]{1,0:T(8,128)(2,1)}, u32[]{:S(2)}, u32[]{:S(2)}) collective-permute-start(bf16[2080,128]{1,0:T(8,128)(2,1)S(1)} %fusion.10.refs_1_), channel_id=1, source_target_pairs={{0,28},{4,0},{8,4},{12,8},{16,12},{20,16},{24,20},{28,24},{1,29},{... | collective-permute-start | bytes 1597448 | tf_op jit(solution)/shard_map/ppermute | solution.py:219
  34.3 3.1 %collective-permute-done.10.refs_5_ = bf16[3104,128]{1,0:T(8,128)(2,1)S(1)} collective-permute-done((bf16[3104,128]{1,0:T(8,128)(2,1)S(1)}, bf16[3104,128]{1,0:T(8,128)(2,1)S(1)}, u32[]{:S(2)}, u32[]{:S(2)}) %collective-permute-start.10) | collective-permute-done | bytes 794656 | tf_op jit(solution)/shard_map/ppermute | solution.py:216
  39.3 4.6 %collective-permute-start.13 = (bf16[3104,128]{1,0:T(8,128)(2,1)S(1)}, bf16[3104,128]{1,0:T(8,128)(2,1)}, u32[]{:S(2)}, u32[]{:S(2)}) collective-permute-start(bf16[3104,128]{1,0:T(8,128)(2,1)S(1)} %collective-permute-done.12.refs_6_), channel_id=1, source_target_pairs={{0,224},{32,256},{64,32},{96,320},{128,96},{160,384},{192,160},{22... | collective-permute-start | bytes 2383880 | tf_op jit(solution)/shard_map/ppermute | solution.py:216
  43.9 4.5 %collective-permute-start.3 = (bf16[2080,128]{1,0:T(8,128)(2,1)}, bf16[2080,128]{1,0:T(8,128)(2,1)}, u32[]{:S(2)}, u32[]{:S(2)}) collective-permute-start(bf16[2080,128]{1,0:T(8,128)(2,1)} %collective-permute-done.2.refs_2_), channel_id=1, source_target_pairs={{0,4},{4,8},{8,12},{12,16},{16,20},{20,24},{24,28},{28,0},{1,5},{5... | collective-permute-start | bytes 1597448 | tf_op jit(solution)/shard_map/ppermute | solution.py:219
  48.4 1.9 %collective-permute-start.7 = (bf16[2080,128]{1,0:T(8,128)(2,1)}, bf16[2080,128]{1,0:T(8,128)(2,1)S(1)}, u32[]{:S(2)}, u32[]{:S(2)}) collective-permute-start(bf16[2080,128]{1,0:T(8,128)(2,1)} %collective-permute-done.6.refs_3_), channel_id=1, source_target_pairs={{0,28},{4,0},{8,4},{12,8},{16,12},{20,16},{24,20},{28,24},{1,29},{... | collective-permute-start | bytes 1597448 | tf_op jit(solution)/shard_map/ppermute | solution.py:219
  50.5 3.4 %shard_map.64 = (f32[8,128,768]{2,1,0:T(8,128)S(1)}, bf16[8,2080,128]{2,1,0:T(8,128)(2,1)S(1)}, bf16[8,3104,128]{2,1,0:T(8,128)(2,1)S(1)}, s32[8,128]{1,0:T(8,128)S(1)}) custom-call(s32[19]{0:T(128)S(1)} %concatenate.26.refs_0_, bf16[2080,128]{1,0:T(8,128)(2,1)S(1)} %fusion.10.refs_1_, bf16[2080,128]{1,0:T(8,128)(2,1)} %collective-permute-done.2.refs_2_, ...), custom_call_target="tpu_custom_call" | custom-call | flops 805306368 | bytes 1048576 | tf_op jit(solution)/shard_map/pallas_call | solution.py:131
  53.9 3.6 %collective-permute-done.11.refs_3_ = bf16[3104,128]{1,0:T(8,128)(2,1)} collective-permute-done((bf16[3104,128]{1,0:T(8,128)(2,1)S(1)}, bf16[3104,128]{1,0:T(8,128)(2,1)}, u32[]{:S(2)}, u32[]{:S(2)}) %collective-permute-start.11) | collective-permute-done | bytes 794656 | tf_op jit(solution)/shard_map/ppermute | solution.py:216
  61.1 4.6 %collective-permute-start.15 = (bf16[3104,128]{1,0:T(8,128)(2,1)}, bf16[3104,128]{1,0:T(8,128)(2,1)S(1)}, u32[]{:S(2)}, u32[]{:S(2)}) collective-permute-start(bf16[3104,128]{1,0:T(8,128)(2,1)} %collective-permute-done.13.refs_4_), channel_id=1, source_target_pairs={{0,224},{32,256},{64,32},{96,320},{128,96},{160,384},{192,160},{22... | collective-permute-start | bytes 2383880 | tf_op jit(solution)/shard_map/ppermute | solution.py:216
  65.7 4.6 %collective-permute-start.4 = (bf16[2080,128]{1,0:T(8,128)(2,1)}, bf16[2080,128]{1,0:T(8,128)(2,1)S(1)}, u32[]{:S(2)}, u32[]{:S(2)}) collective-permute-start(bf16[2080,128]{1,0:T(8,128)(2,1)} %collective-permute-done.3.refs_1_), channel_id=1, source_target_pairs={{0,4},{4,8},{8,12},{12,16},{16,20},{20,24},{24,28},{28,0},{1,5},{5... | collective-permute-start | bytes 1597448 | tf_op jit(solution)/shard_map/ppermute | solution.py:219
  70.4 1.9 %collective-permute-start.8 = (bf16[2080,128]{1,0:T(8,128)(2,1)S(1)}, bf16[2080,128]{1,0:T(8,128)(2,1)S(1)}, u32[]{:S(2)}, u32[]{:S(2)}) collective-permute-start(bf16[2080,128]{1,0:T(8,128)(2,1)S(1)} %collective-permute-done.7.refs_2_), channel_id=1, source_target_pairs={{0,28},{4,0},{8,4},{12,8},{16,12},{20,16},{24,20},{28,24},{1,29},{... | collective-permute-start | bytes 1597448 | tf_op jit(solution)/shard_map/ppermute | solution.py:219
  72.3 4.5 %shard_map.65 = (f32[8,128,768]{2,1,0:T(8,128)S(1)}, bf16[8,2080,128]{2,1,0:T(8,128)(2,1)S(1)}, bf16[8,3104,128]{2,1,0:T(8,128)(2,1)S(1)}, s32[8,128]{1,0:T(8,128)S(1)}) custom-call(s32[19]{0:T(128)S(1)} %concatenate.26.refs_0_, bf16[2080,128]{1,0:T(8,128)(2,1)} %collective-permute-done.3.refs_1_, ...), custom_call_target="tpu_custom_call", output_to_operand_aliasing={{0}: (5, {}), {1}: (6, {}), {2}: (7, {})} | custom-call | flops 805306368 | bytes 1048576 | tf_op jit(solution)/shard_map/pallas_call | solution.py:131
  80.2 2.8 %collective-permute-start.16 = (bf16[1552,128]{1,0:T(8,128)(2,1)S(1)}, bf16[1552,128]{1,0:T(8,128)(2,1)S(1)}, u32[]{:S(2)}, u32[]{:S(2)}) collective-permute-start(bf16[1552,128]{1,0:T(8,128)(2,1)S(1)} %slice.136), channel_id=1, source_target_pairs={{0,288},{32,64},{64,352},{96,128},{128,416},{160,192},{192,480},{2... | collective-permute-start | bytes 1191944 | tf_op jit(solution)/shard_map/ppermute | solution.py:216
  83.1 3.7 %collective-permute-start.17 = (bf16[1552,128]{1,0:T(8,128)(2,1)S(1)}, bf16[1552,128]{1,0:T(8,128)(2,1)S(1)}, u32[]{:S(2)}, u32[]{:S(2)}) collective-permute-start(bf16[1552,128]{1,0:T(8,128)(2,1)S(1)} %slice.137), channel_id=1, source_target_pairs={{0,224},{32,256},{64,32},{96,320},{128,96},{160,384},{192,160},{22... | collective-permute-start | bytes 1191944 | tf_op jit(solution)/shard_map/ppermute | solution.py:216
  86.9 4.7 %collective-permute-start.5 = (bf16[1040,128]{1,0:T(8,128)(2,1)S(1)}, bf16[1040,128]{1,0:T(8,128)(2,1)S(1)}, u32[]{:S(2)}, u32[]{:S(2)}) collective-permute-start(bf16[1040,128]{1,0:T(8,128)(2,1)S(1)} %slice.152), channel_id=1, source_target_pairs={{0,4},{4,8},{8,12},{12,16},{16,20},{20,24},{24,28},{28,0},{1,5},{5... | collective-permute-start | bytes 798728 | tf_op jit(solution)/shard_map/ppermute | solution.py:219
  91.7 1.9 %collective-permute-start.9 = (bf16[1040,128]{1,0:T(8,128)(2,1)S(1)}, bf16[1040,128]{1,0:T(8,128)(2,1)S(1)}, u32[]{:S(2)}, u32[]{:S(2)}) collective-permute-start(bf16[1040,128]{1,0:T(8,128)(2,1)S(1)} %slice.153), channel_id=1, source_target_pairs={{0,28},{4,0},{8,4},{12,8},{16,12},{20,16},{24,20},{28,24},{1,29},{... | collective-permute-start | bytes 798728 | tf_op jit(solution)/shard_map/ppermute | solution.py:219
  93.6 4.4 %shard_map.66 = (f32[8,128,768]{2,1,0:T(8,128)S(1)}, bf16[8,2080,128]{2,1,0:T(8,128)(2,1)S(1)}, bf16[8,3104,128]{2,1,0:T(8,128)(2,1)S(1)}, s32[8,128]{1,0:T(8,128)}) custom-call(s32[19]{0:T(128)S(1)} %concatenate.26.refs_0_, bf16[2080,128]{1,0:T(8,128)(2,1)S(1)} %collective-permute-done.4.refs_1_, ...), custom_call_target="tpu_custom_call", output_to_operand_aliasing={{0}: (5, {}), {1}: (6, {}), {2}: (7, {})} | custom-call | flops 805306368 | bytes 1048576 | tf_op jit(solution)/shard_map/pallas_call | solution.py:131
  98.0 2.0 %collective-permute-done.9.refs_2_ = bf16[1040,128]{1,0:T(8,128)(2,1)S(1)} collective-permute-done((bf16[1040,128]{1,0:T(8,128)(2,1)S(1)}, bf16[1040,128]{1,0:T(8,128)(2,1)S(1)}, u32[]{:S(2)}, u32[]{:S(2)}) %collective-permute-start.9) | collective-permute-done | bytes 266272 | tf_op jit(solution)/shard_map/ppermute | solution.py:219
  100.0 4.0 %shard_map.67 = (f32[8,128,768]{2,1,0:T(8,128)S(1)}, bf16[8,2080,128]{2,1,0:T(8,128)(2,1)S(1)}, bf16[8,3104,128]{2,1,0:T(8,128)(2,1)S(1)}, s32[8,128]{1,0:T(8,128)}) custom-call(s32[19]{0:T(128)S(1)} %concatenate.26.refs_0_, bf16[1040,128]{1,0:T(8,128)(2,1)S(1)} %collective-permute-done.5.refs_1_, ...), custom_call_target="tpu_custom_call", output_to_operand_aliasing={{0}: (5, {}), {1}: (6, {}), {2}: (7, {})} | custom-call | flops 805306368 | bytes 1048576 | tf_op jit(solution)/shard_map/pallas_call | solution.py:131
  104.2 7.8 %collective-permute-start.18 = (f32[4,128,768]{2,1,0:T(8,128)S(1)}, f32[4,128,768]{2,1,0:T(8,128)S(1)}, u32[]{:S(2)}, u32[]{:S(2)}) collective-permute-start(f32[4,128,768]{2,1,0:T(8,128)S(1)} %slice.139), channel_id=1, source_target_pairs={{0,1},{1,0},{2,3},{3,2},{4,5},{5,4},{6,7},{7,6},{8,9},{9,8},{10,11... | collective-permute-start | bytes 4718600 | tf_op jit(solution)/shard_map/ppermute | solution.py:238
  112.0 3.0 %collective-permute-done.18 = f32[4,128,768]{2,1,0:T(8,128)S(1)} collective-permute-done((f32[4,128,768]{2,1,0:T(8,128)S(1)}, f32[4,128,768]{2,1,0:T(8,128)S(1)}, u32[]{:S(2)}, u32[]{:S(2)}) %collective-permute-start.18) | collective-permute-done | bytes 1572896 | tf_op jit(solution)/shard_map/ppermute | solution.py:238
  115.8 3.1 %collective-permute-start.19 = (s16[128,896]{1,0:T(8,128)(2,1)S(1)}, s16[128,896]{1,0:T(8,128)(2,1)S(1)}, u32[]{:S(2)}, u32[]{:S(2)}) collective-permute-start(s16[128,896]{1,0:T(8,128)(2,1)S(1)} %pad_add_fusion), channel_id=1, source_target_pairs={{0,256},{2,258},{256,2},{258,0},{1,257},{3,259},{257,3},{259,1},{4... | collective-permute-start | bytes 688136 | tf_op jit(solution)/shard_map/ppermute | solution.py:242
  119.1 2.7 %collective-permute-start.20 = (s16[128,896]{1,0:T(8,128)(2,1)S(1)}, s16[128,896]{1,0:T(8,128)(2,1)S(1)}, u32[]{:S(2)}, u32[]{:S(2)}) collective-permute-start(s16[128,896]{1,0:T(8,128)(2,1)S(1)} %pad_add_fusion.1), channel_id=1, source_target_pairs={{0,2},{2,0},{256,258},{258,256},{1,3},{3,1},{257,259},{259,257},{4... | collective-permute-start | bytes 688136 | tf_op jit(solution)/shard_map/ppermute | solution.py:242
  121.9 3.8 %collective-permute-start.21 = (s16[128,896]{1,0:T(8,128)(2,1)S(1)}, s16[128,896]{1,0:T(8,128)(2,1)S(1)}, u32[]{:S(2)}, u32[]{:S(2)}) collective-permute-start(s16[128,896]{1,0:T(8,128)(2,1)S(1)} %pad_add_fusion.2), channel_id=1, source_target_pairs={{0,258},{2,256},{256,0},{258,2},{1,259},{3,257},{257,1},{259,3},{4... | collective-permute-start | bytes 688136 | tf_op jit(solution)/shard_map/ppermute | solution.py:242
  125.8 3.2 %collective-permute-done.20 = s16[128,896]{1,0:T(8,128)(2,1)S(1)} collective-permute-done((s16[128,896]{1,0:T(8,128)(2,1)S(1)}, s16[128,896]{1,0:T(8,128)(2,1)S(1)}, u32[]{:S(2)}, u32[]{:S(2)}) %collective-permute-start.20) | collective-permute-done | bytes 229408 | tf_op jit(solution)/shard_map/ppermute | solution.py:242
  129.1 5.8 %collective-permute-done.21 = s16[128,896]{1,0:T(8,128)(2,1)S(1)} collective-permute-done((s16[128,896]{1,0:T(8,128)(2,1)S(1)}, s16[128,896]{1,0:T(8,128)(2,1)S(1)}, u32[]{:S(2)}, u32[]{:S(2)}) %collective-permute-start.21) | collective-permute-done | bytes 229408 | tf_op jit(solution)/shard_map/ppermute | solution.py:242
  (61 shorter events, 15.3 us)
Async XLA Ops:
  0.0 5.2 %copy-start = (bf16[1,8,1,3,128,128]{5,4,3,2,1,0:T(8,128)(2,1)S(1)}, bf16[1,8,1,3,128,128]{5,4,3,2,1,0:T(8,128)(2,1)}, u32[]{:S(2)}) copy-start(bf16[1,8,1,3,128,128]{5,4,3,2,1,0:T(8,128)(2,1)} %param.16) | copy-start | bytes 2359300
  0.0 5.3 %copy-start.1 = (s32[1,8,1,3]{1,2,3,0:T(1,128)S(1)}, s32[1,8,1,3]{1,2,3,0:T(1,128)}, u32[]{:S(2)}) copy-start(s32[1,8,1,3]{1,2,3,0:T(1,128)} %param.17) | copy-start | bytes 292
  1.1 9.1 %collective-permute-start = (bf16[1024,128]{1,0:T(8,128)(2,1)S(1)}, bf16[1024,128]{1,0:T(8,128)(2,1)S(1)}, u32[]{:S(2)}, u32[]{:S(2)}) collective-permute-start(bf16[1024,128]{1,0:T(8,128)(2,1)S(1)} %get-tuple-element.108), channel_id=1, source_target_pairs={{0,256},{256,0},{1,257},{257,1},{2,258},{258,2},{3,259},{259,3},{4... | collective-permute-start | bytes 786440 | tf_op jit(solution)/shard_map/ppermute | solution.py:191
  5.3 45.0 %copy-start.2 = (s32[8]{0:T(128)S(1)}, s32[8]{0:T(128)}, u32[]{:S(2)}) copy-start(s32[8]{0:T(128)} %constant.239.clone) | copy-start | bytes 100
  5.3 45.0 %copy-start.3 = (s32[8]{0:T(128)S(1)}, s32[8]{0:T(128)}, u32[]{:S(2)}) copy-start(s32[8]{0:T(128)} %constant.240.clone) | copy-start | bytes 100
  10.2 27.1 %collective-permute-start.10 = (bf16[3104,128]{1,0:T(8,128)(2,1)S(1)}, bf16[3104,128]{1,0:T(8,128)(2,1)S(1)}, u32[]{:S(2)}, u32[]{:S(2)}) collective-permute-start(bf16[3104,128]{1,0:T(8,128)(2,1)S(1)} %fusion.7.refs_4_), channel_id=1, source_target_pairs={{0,288},{32,64},{64,352},{96,128},{128,416},{160,192},{192,480},{2... | collective-permute-start | bytes 2383880 | tf_op jit(solution)/shard_map/ppermute | solution.py:216
  14.2 25.1 %collective-permute-start.12 = (bf16[3104,128]{1,0:T(8,128)(2,1)S(1)}, bf16[3104,128]{1,0:T(8,128)(2,1)S(1)}, u32[]{:S(2)}, u32[]{:S(2)}) collective-permute-start(bf16[3104,128]{1,0:T(8,128)(2,1)S(1)} %fusion.7.refs_4_), channel_id=1, source_target_pairs={{0,224},{32,256},{64,32},{96,320},{128,96},{160,384},{192,160},{22... | collective-permute-start | bytes 2383880 | tf_op jit(solution)/shard_map/ppermute | solution.py:216
  22.8 5.1 %collective-permute-start.1 = (bf16[16,128]{1,0:T(8,128)(2,1)S(1)}, bf16[16,128]{1,0:T(8,128)(2,1)S(1)}, u32[]{:S(2)}, u32[]{:S(2)}) collective-permute-start(bf16[16,128]{1,0:T(8,128)(2,1)S(1)} %scatter.19), channel_id=1, source_target_pairs={{0,256},{256,0},{1,257},{257,1},{2,258},{258,2},{3,259},{259,3},{4... | collective-permute-start | bytes 12296 | tf_op jit(solution)/shard_map/ppermute | solution.py:193
  27.9 16.0 %collective-permute-start.2 = (bf16[2080,128]{1,0:T(8,128)(2,1)S(1)}, bf16[2080,128]{1,0:T(8,128)(2,1)}, u32[]{:S(2)}, u32[]{:S(2)}) collective-permute-start(bf16[2080,128]{1,0:T(8,128)(2,1)S(1)} %fusion.10.refs_1_), channel_id=1, source_target_pairs={{0,4},{4,8},{8,12},{12,16},{16,20},{20,24},{24,28},{28,0},{1,5},{5... | collective-permute-start | bytes 1597448 | tf_op jit(solution)/shard_map/ppermute | solution.py:219
  32.3 16.1 %collective-permute-start.6 = (bf16[2080,128]{1,0:T(8,128)(2,1)S(1)}, bf16[2080,128]{1,0:T(8,128)(2,1)}, u32[]{:S(2)}, u32[]{:S(2)}) collective-permute-start(bf16[2080,128]{1,0:T(8,128)(2,1)S(1)} %fusion.10.refs_1_), channel_id=1, source_target_pairs={{0,28},{4,0},{8,4},{12,8},{16,12},{20,16},{24,20},{28,24},{1,29},{... | collective-permute-start | bytes 1597448 | tf_op jit(solution)/shard_map/ppermute | solution.py:219
  37.3 20.2 %collective-permute-start.11 = (bf16[3104,128]{1,0:T(8,128)(2,1)S(1)}, bf16[3104,128]{1,0:T(8,128)(2,1)}, u32[]{:S(2)}, u32[]{:S(2)}) collective-permute-start(bf16[3104,128]{1,0:T(8,128)(2,1)S(1)} %collective-permute-done.10.refs_5_), channel_id=1, source_target_pairs={{0,288},{32,64},{64,352},{96,128},{128,416},{160,192},{192,480},{2... | collective-permute-start | bytes 2383880 | tf_op jit(solution)/shard_map/ppermute | solution.py:216
  39.3 19.9 %collective-permute-start.13 = (bf16[3104,128]{1,0:T(8,128)(2,1)S(1)}, bf16[3104,128]{1,0:T(8,128)(2,1)}, u32[]{:S(2)}, u32[]{:S(2)}) collective-permute-start(bf16[3104,128]{1,0:T(8,128)(2,1)S(1)} %collective-permute-done.12.refs_6_), channel_id=1, source_target_pairs={{0,224},{32,256},{64,32},{96,320},{128,96},{160,384},{192,160},{22... | collective-permute-start | bytes 2383880 | tf_op jit(solution)/shard_map/ppermute | solution.py:216
  43.9 21.9 %collective-permute-start.3 = (bf16[2080,128]{1,0:T(8,128)(2,1)}, bf16[2080,128]{1,0:T(8,128)(2,1)}, u32[]{:S(2)}, u32[]{:S(2)}) collective-permute-start(bf16[2080,128]{1,0:T(8,128)(2,1)} %collective-permute-done.2.refs_2_), channel_id=1, source_target_pairs={{0,4},{4,8},{8,12},{12,16},{16,20},{20,24},{24,28},{28,0},{1,5},{5... | collective-permute-start | bytes 1597448 | tf_op jit(solution)/shard_map/ppermute | solution.py:219
  48.4 22.0 %collective-permute-start.7 = (bf16[2080,128]{1,0:T(8,128)(2,1)}, bf16[2080,128]{1,0:T(8,128)(2,1)S(1)}, u32[]{:S(2)}, u32[]{:S(2)}) collective-permute-start(bf16[2080,128]{1,0:T(8,128)(2,1)} %collective-permute-done.6.refs_3_), channel_id=1, source_target_pairs={{0,28},{4,0},{8,4},{12,8},{16,12},{20,16},{24,20},{28,24},{1,29},{... | collective-permute-start | bytes 1597448 | tf_op jit(solution)/shard_map/ppermute | solution.py:219
  59.2 19.4 %collective-permute-start.14 = (bf16[3104,128]{1,0:T(8,128)(2,1)}, bf16[3104,128]{1,0:T(8,128)(2,1)S(1)}, u32[]{:S(2)}, u32[]{:S(2)}) collective-permute-start(bf16[3104,128]{1,0:T(8,128)(2,1)} %collective-permute-done.11.refs_3_), channel_id=1, source_target_pairs={{0,288},{32,64},{64,352},{96,128},{128,416},{160,192},{192,480},{2... | collective-permute-start | bytes 2383880 | tf_op jit(solution)/shard_map/ppermute | solution.py:216
  61.1 19.1 %collective-permute-start.15 = (bf16[3104,128]{1,0:T(8,128)(2,1)}, bf16[3104,128]{1,0:T(8,128)(2,1)S(1)}, u32[]{:S(2)}, u32[]{:S(2)}) collective-permute-start(bf16[3104,128]{1,0:T(8,128)(2,1)} %collective-permute-done.13.refs_4_), channel_id=1, source_target_pairs={{0,224},{32,256},{64,32},{96,320},{128,96},{160,384},{192,160},{22... | collective-permute-start | bytes 2383880 | tf_op jit(solution)/shard_map/ppermute | solution.py:216
  65.7 21.1 %collective-permute-start.4 = (bf16[2080,128]{1,0:T(8,128)(2,1)}, bf16[2080,128]{1,0:T(8,128)(2,1)S(1)}, u32[]{:S(2)}, u32[]{:S(2)}) collective-permute-start(bf16[2080,128]{1,0:T(8,128)(2,1)} %collective-permute-done.3.refs_1_), channel_id=1, source_target_pairs={{0,4},{4,8},{8,12},{12,16},{16,20},{20,24},{24,28},{28,0},{1,5},{5... | collective-permute-start | bytes 1597448 | tf_op jit(solution)/shard_map/ppermute | solution.py:219
  70.4 21.3 %collective-permute-start.8 = (bf16[2080,128]{1,0:T(8,128)(2,1)S(1)}, bf16[2080,128]{1,0:T(8,128)(2,1)S(1)}, u32[]{:S(2)}, u32[]{:S(2)}) collective-permute-start(bf16[2080,128]{1,0:T(8,128)(2,1)S(1)} %collective-permute-done.7.refs_2_), channel_id=1, source_target_pairs={{0,28},{4,0},{8,4},{12,8},{16,12},{20,16},{24,20},{28,24},{1,29},{... | collective-permute-start | bytes 1597448 | tf_op jit(solution)/shard_map/ppermute | solution.py:219
  80.2 19.8 %collective-permute-start.16 = (bf16[1552,128]{1,0:T(8,128)(2,1)S(1)}, bf16[1552,128]{1,0:T(8,128)(2,1)S(1)}, u32[]{:S(2)}, u32[]{:S(2)}) collective-permute-start(bf16[1552,128]{1,0:T(8,128)(2,1)S(1)} %slice.136), channel_id=1, source_target_pairs={{0,288},{32,64},{64,352},{96,128},{128,416},{160,192},{192,480},{2... | collective-permute-start | bytes 1191944 | tf_op jit(solution)/shard_map/ppermute | solution.py:216
  83.1 16.9 %collective-permute-start.17 = (bf16[1552,128]{1,0:T(8,128)(2,1)S(1)}, bf16[1552,128]{1,0:T(8,128)(2,1)S(1)}, u32[]{:S(2)}, u32[]{:S(2)}) collective-permute-start(bf16[1552,128]{1,0:T(8,128)(2,1)S(1)} %slice.137), channel_id=1, source_target_pairs={{0,224},{32,256},{64,32},{96,320},{128,96},{160,384},{192,160},{22... | collective-permute-start | bytes 1191944 | tf_op jit(solution)/shard_map/ppermute | solution.py:216
  86.9 11.1 %collective-permute-start.5 = (bf16[1040,128]{1,0:T(8,128)(2,1)S(1)}, bf16[1040,128]{1,0:T(8,128)(2,1)S(1)}, u32[]{:S(2)}, u32[]{:S(2)}) collective-permute-start(bf16[1040,128]{1,0:T(8,128)(2,1)S(1)} %slice.152), channel_id=1, source_target_pairs={{0,4},{4,8},{8,12},{12,16},{16,20},{20,24},{24,28},{28,0},{1,5},{5... | collective-permute-start | bytes 798728 | tf_op jit(solution)/shard_map/ppermute | solution.py:219
  91.7 8.4 %collective-permute-start.9 = (bf16[1040,128]{1,0:T(8,128)(2,1)S(1)}, bf16[1040,128]{1,0:T(8,128)(2,1)S(1)}, u32[]{:S(2)}, u32[]{:S(2)}) collective-permute-start(bf16[1040,128]{1,0:T(8,128)(2,1)S(1)} %slice.153), channel_id=1, source_target_pairs={{0,28},{4,0},{8,4},{12,8},{16,12},{20,16},{24,20},{28,24},{1,29},{... | collective-permute-start | bytes 798728 | tf_op jit(solution)/shard_map/ppermute | solution.py:219
  104.2 10.8 %collective-permute-start.18 = (f32[4,128,768]{2,1,0:T(8,128)S(1)}, f32[4,128,768]{2,1,0:T(8,128)S(1)}, u32[]{:S(2)}, u32[]{:S(2)}) collective-permute-start(f32[4,128,768]{2,1,0:T(8,128)S(1)} %slice.139), channel_id=1, source_target_pairs={{0,1},{1,0},{2,3},{3,2},{4,5},{5,4},{6,7},{7,6},{8,9},{9,8},{10,11... | collective-permute-start | bytes 4718600 | tf_op jit(solution)/shard_map/ppermute | solution.py:238
  115.8 9.9 %collective-permute-start.19 = (s16[128,896]{1,0:T(8,128)(2,1)S(1)}, s16[128,896]{1,0:T(8,128)(2,1)S(1)}, u32[]{:S(2)}, u32[]{:S(2)}) collective-permute-start(s16[128,896]{1,0:T(8,128)(2,1)S(1)} %pad_add_fusion), channel_id=1, source_target_pairs={{0,256},{2,258},{256,2},{258,0},{1,257},{3,259},{257,3},{259,1},{4... | collective-permute-start | bytes 688136 | tf_op jit(solution)/shard_map/ppermute | solution.py:242
  119.1 9.9 %collective-permute-start.20 = (s16[128,896]{1,0:T(8,128)(2,1)S(1)}, s16[128,896]{1,0:T(8,128)(2,1)S(1)}, u32[]{:S(2)}, u32[]{:S(2)}) collective-permute-start(s16[128,896]{1,0:T(8,128)(2,1)S(1)} %pad_add_fusion.1), channel_id=1, source_target_pairs={{0,2},{2,0},{256,258},{258,256},{1,3},{3,1},{257,259},{259,257},{4... | collective-permute-start | bytes 688136 | tf_op jit(solution)/shard_map/ppermute | solution.py:242
  121.9 13.0 %collective-permute-start.21 = (s16[128,896]{1,0:T(8,128)(2,1)S(1)}, s16[128,896]{1,0:T(8,128)(2,1)S(1)}, u32[]{:S(2)}, u32[]{:S(2)}) collective-permute-start(s16[128,896]{1,0:T(8,128)(2,1)S(1)} %pad_add_fusion.2), channel_id=1, source_target_pairs={{0,258},{2,256},{256,0},{258,2},{1,259},{3,257},{257,1},{259,3},{4... | collective-permute-start | bytes 688136 | tf_op jit(solution)/shard_map/ppermute | solution.py:242
